TPU v7x, 32 devices: a whole 2x2x4 slice. The times are simulated.
32 devices in a mesh: shard: 4 (over x, core), replica: 8 (over z, y).
Axes of the slice: x: 2, y: 2, z: 4, core: 2. Of those that a mesh axis runs over, the one named last changes fastest.
Arguments:
- tokens: bfloat16 [32768, 896], P(('shard', 'replica')), may hold values from -6 to 6
- segments: int32 [32, 1024], P(('shard', 'replica')), may hold values from 0 to 3, never falling along the last dimension, each value on 1 to 768 neighbouring positions
- cotangent: bfloat16 [32768, 896], P(('shard', 'replica')), may hold values from -6 to 6
- gain_attn: float32 [896], replicated, may hold values from 0.1 to 1.9
- gain_ffn: float32 [896], replicated, may hold values from 0.1 to 1.9
- w_query: bfloat16 [896, 896], P('shard'), may hold values from -0.1875 to 0.1875
- bias_query: float32 [896], replicated, may hold values from -3 to 3
- w_key: bfloat16 [896, 128], P('shard'), may hold values from -0.1875 to 0.1875
- bias_key: float32 [128], replicated, may hold values from -3 to 3
- w_value: bfloat16 [896, 128], P('shard'), may hold values from -0.1875 to 0.1875
- bias_value: float32 [128], replicated, may hold values from -3 to 3
- w_output: bfloat16 [896, 896], P('shard'), may hold values from -1.5 to 1.5
- w_gate: bfloat16 [896, 4864], P('shard'), may hold values from -0.1875 to 0.1875
- w_up: bfloat16 [896, 4864], P('shard'), may hold values from -0.1875 to 0.1875
- w_down: bfloat16 [4864, 896], P('shard'), may hold values from -0.078125 to 0.078125
Outputs:
- output: bfloat16 [32768, 896], P(('shard', 'replica'))
- grad_tokens: float32 [32768, 896], P(('shard', 'replica'))
- grad_gain_attn: float32 [896], replicated
- grad_gain_ffn: float32 [896], replicated
- grad_w_query: float32 [896, 896], P('shard')
- grad_bias_query: float32 [896], replicated
- grad_w_key: float32 [896, 128], P('shard')
- grad_bias_key: float32 [128], replicated
- grad_w_value: float32 [896, 128], P('shard')
- grad_bias_value: float32 [128], replicated
- grad_w_output: float32 [896, 896], P('shard')
- grad_w_gate: float32 [896, 4864], P('shard')
- grad_w_up: float32 [896, 4864], P('shard')
- grad_w_down: float32 [4864, 896], P('shard')
Inputs may be any that keep to these rules, and one draw needn't show every extreme that they name: `segments`: each row is one device's pack: document numbers never fall along it, each document has 1 to 768 tokens, and one has exactly 768.
All inputs are finite; a program needn't handle non-finite values.
Results may differ from a plain program's by a relative error of at most 0.024.
Values may be sent and summed in bfloat16 or wider, within the bound.
No kernel may reach another device: no remote copies, remote signals or barrier semaphores. Data moves between devices by JAX's collectives and lax.ppermute only.
A program may use at most 256 MiB of HBM per device.

v0:
```python
import jax
import jax.numpy as jnp
from jax import lax
from jax.sharding import PartitionSpec as P

HEADS = 14
KVHEADS = 2
HD = 64


epsilon = 1e-06
rope_base = 1000000.0
masked_score = -1e30


def product(left, right):
    return jnp.dot(left, right, preferred_element_type=jnp.float32)


def product_right_t(left, right):
    return lax.dot_general(
        left, right, (((1,), (1,)), ((), ())), preferred_element_type=jnp.float32
    )


def product_left_t(left, right):
    return lax.dot_general(
        left, right, (((0,), (0,)), ((), ())), preferred_element_type=jnp.float32
    )


def rms_stats(values, gain_vector):
    inverse = lax.rsqrt(jnp.mean(values * values, axis=-1, keepdims=True) + epsilon)
    return (values * inverse * gain_vector, inverse)


def norm_back(values, inverse, gain_vector, upstream):
    scaled = upstream * gain_vector
    feature_count = values.shape[-1]
    grad_gain = jnp.sum(upstream * values * inverse, axis=0)
    correction = jnp.sum(scaled * values, axis=-1, keepdims=True) / feature_count
    grad_values = inverse * scaled - values * (inverse * inverse * inverse) * correction
    return (grad_values, grad_gain)


def rotate(values, cosine_table, sine_table):
    half_width = values.shape[-1] // 2
    first_half = values[..., :half_width]
    second_half = values[..., half_width:]
    return jnp.concatenate(
        [
            first_half * cosine_table - second_half * sine_table,
            second_half * cosine_table + first_half * sine_table,
        ],
        axis=-1,
    )


def rotate_back(gradients, cosine_table, sine_table):
    half_width = gradients.shape[-1] // 2
    first_half = gradients[..., :half_width]
    second_half = gradients[..., half_width:]
    return jnp.concatenate(
        [
            first_half * cosine_table + second_half * sine_table,
            second_half * cosine_table - first_half * sine_table,
        ],
        axis=-1,
    )


def pack_tables(doc_ids):
    row_count = doc_ids.shape[0]
    row_ids = jnp.arange(row_count, dtype=jnp.int32)
    same_doc = doc_ids[:, None] == doc_ids[None, :]
    before = row_ids[None, :] < row_ids[:, None]
    places = jnp.sum(jnp.where(same_doc & before, 1, 0).astype(jnp.int32), axis=1)
    allowed = same_doc & (row_ids[None, :] <= row_ids[:, None])
    frequency = rope_base ** (-jnp.arange(0, HD, 2).astype(jnp.float32) / HD)
    angles = places.astype(jnp.float32)[:, None] * frequency[None, :]
    return (allowed, jnp.cos(angles), jnp.sin(angles))


def block_scores(queries, key_rows, allowed, block_start, block_rows):
    query_block = lax.dynamic_slice_in_dim(queries, block_start, block_rows, 0)
    mask_block = lax.dynamic_slice_in_dim(allowed, block_start, block_rows, 0)
    scores = (
        jnp.einsum("bkgd,rkd->kgbr", query_block, key_rows, preferred_element_type=jnp.float32)
        * 0.125
    )
    return (jnp.where(mask_block[None, None], scores, masked_score), query_block)


def attention_forward(queries, key_rows, value_rows, allowed, block_rows):
    block_count = queries.shape[0] // block_rows

    def one_block(block_start):
        scores, query_block = block_scores(queries, key_rows, allowed, block_start, block_rows)
        largest = jnp.max(scores, axis=-1, keepdims=True)
        exponent = jnp.exp(scores - largest)
        exp_total = jnp.sum(exponent, axis=-1, keepdims=True)
        probabilities = (exponent / exp_total).astype(jnp.bfloat16)
        mixed_block = jnp.einsum(
            "kgbr,rkd->bkgd", probabilities, value_rows, preferred_element_type=jnp.float32
        )
        return (mixed_block.astype(jnp.bfloat16), largest + jnp.log(exp_total))

    starts = jnp.arange(block_count, dtype=jnp.int32) * block_rows
    return lax.map(one_block, starts)


def attention_backward(queries, key_rows, value_rows, allowed, log_totals, grad_mixed, block_rows):
    block_count = queries.shape[0] // block_rows

    def one_block(running, block_inputs):
        grad_keys, grad_values = running
        block_start, log_total = block_inputs
        scores, query_block = block_scores(queries, key_rows, allowed, block_start, block_rows)
        probabilities = jnp.exp(scores - log_total)
        grad_block = lax.dynamic_slice_in_dim(grad_mixed, block_start, block_rows, 0)
        grad_probs = jnp.einsum(
            "bkgd,rkd->kgbr", grad_block, value_rows, preferred_element_type=jnp.float32
        )
        inner_sum = jnp.sum(probabilities * grad_probs, axis=-1, keepdims=True)
        grad_scores = (probabilities * (grad_probs - inner_sum)).astype(jnp.bfloat16)
        grad_query = (
            jnp.einsum("kgbr,rkd->bkgd", grad_scores, key_rows, preferred_element_type=jnp.float32)
            * 0.125
        )
        grad_keys = (
            grad_keys
            + jnp.einsum(
                "kgbr,bkgd->rkd", grad_scores, query_block, preferred_element_type=jnp.float32
            )
            * 0.125
        )
        grad_values = grad_values + jnp.einsum(
            "kgbr,bkgd->rkd",
            probabilities.astype(jnp.bfloat16),
            grad_block,
            preferred_element_type=jnp.float32,
        )
        return ((grad_keys, grad_values), grad_query)

    starts = jnp.arange(block_count, dtype=jnp.int32) * block_rows
    zero_rows = jnp.zeros(key_rows.shape, jnp.float32)
    totals, grad_queries = lax.scan(one_block, (zero_rows, zero_rows), (starts, log_totals))
    return (grad_queries, totals[0], totals[1])


def on_device(
    tokens,
    segments,
    cotangent,
    gain_attn,
    gain_ffn,
    w_query,
    bias_query,
    w_key,
    bias_key,
    w_value,
    bias_value,
    w_output,
    w_gate,
    w_up,
    w_down,
):
    inputs = tokens.astype(jnp.float32)
    row_count = inputs.shape[0]
    group_size = HEADS // KVHEADS
    block_rows = min(512, row_count)
    allowed, cosine_table, sine_table = pack_tables(segments[0])
    cosine_heads = cosine_table[:, None, :]
    sine_heads = sine_table[:, None, :]
    full_query, full_key, full_value, full_output = (
        lax.all_gather(w_query, "shard", axis=0, tiled=True),
        lax.all_gather(w_key, "shard", axis=0, tiled=True),
        lax.all_gather(w_value, "shard", axis=0, tiled=True),
        lax.all_gather(w_output, "shard", axis=0, tiled=True),
    )
    normed, inverse_one = rms_stats(inputs, gain_attn)
    normed_low = normed.astype(jnp.bfloat16)
    query_proj = product(normed_low, full_query) + bias_query
    key_proj = product(normed_low, full_key) + bias_key
    value_proj = product(normed_low, full_value) + bias_value
    queries = (
        rotate(query_proj.reshape(row_count, HEADS, HD), cosine_heads, sine_heads)
        .astype(jnp.bfloat16)
        .reshape(row_count, KVHEADS, group_size, HD)
    )
    key_rows = rotate(key_proj.reshape(row_count, KVHEADS, HD), cosine_heads, sine_heads).astype(
        jnp.bfloat16
    )
    value_rows = value_proj.reshape(row_count, KVHEADS, HD).astype(jnp.bfloat16)
    mixed_heads, log_totals = attention_forward(queries, key_rows, value_rows, allowed, block_rows)
    mixed_low = mixed_heads.reshape(row_count, HEADS * HD)
    residual = inputs + product(mixed_low, full_output)
    normed_two, inverse_two = rms_stats(residual, gain_ffn)
    normed_two_low = normed_two.astype(jnp.bfloat16)
    full_gate, full_up, full_down = (
        lax.all_gather(w_gate, "shard", axis=0, tiled=True),
        lax.all_gather(w_up, "shard", axis=0, tiled=True),
        lax.all_gather(w_down, "shard", axis=0, tiled=True),
    )
    gate_proj = product(normed_two_low, full_gate)
    up_proj = product(normed_two_low, full_up)
    sigmoid_gate = jax.nn.sigmoid(gate_proj)
    silu_gate = gate_proj * sigmoid_gate
    hidden_low = (silu_gate * up_proj).astype(jnp.bfloat16)
    output = (residual + product(hidden_low, full_down)).astype(jnp.bfloat16)
    upstream = cotangent.astype(jnp.float32)
    back_gate, back_up, back_down = (
        lax.all_gather(w_gate, "shard", axis=0, tiled=True),
        lax.all_gather(w_up, "shard", axis=0, tiled=True),
        lax.all_gather(w_down, "shard", axis=0, tiled=True),
    )
    grad_branch = upstream.astype(jnp.bfloat16)
    grad_hidden = product_right_t(grad_branch, back_down)
    grad_w_down = product_left_t(hidden_low, grad_branch)
    grad_gate_low = (
        grad_hidden * up_proj * (sigmoid_gate + gate_proj * sigmoid_gate * (1.0 - sigmoid_gate))
    ).astype(jnp.bfloat16)
    grad_up_low = (grad_hidden * silu_gate).astype(jnp.bfloat16)
    grad_w_gate = product_left_t(normed_two_low, grad_gate_low)
    grad_w_up = product_left_t(normed_two_low, grad_up_low)
    grad_normed_two = product_right_t(grad_gate_low, back_gate) + product_right_t(
        grad_up_low, back_up
    )
    grad_from_two, grad_gain_ffn = norm_back(residual, inverse_two, gain_ffn, grad_normed_two)
    grad_residual = upstream + grad_from_two
    back_query, back_key, back_value, back_output = (
        lax.all_gather(w_query, "shard", axis=0, tiled=True),
        lax.all_gather(w_key, "shard", axis=0, tiled=True),
        lax.all_gather(w_value, "shard", axis=0, tiled=True),
        lax.all_gather(w_output, "shard", axis=0, tiled=True),
    )
    grad_attn_low = grad_residual.astype(jnp.bfloat16)
    grad_w_output = product_left_t(mixed_low, grad_attn_low)
    grad_mixed = (
        product_right_t(grad_attn_low, back_output)
        .astype(jnp.bfloat16)
        .reshape(row_count, KVHEADS, group_size, HD)
    )
    grad_queries, grad_keys, grad_values = attention_backward(
        queries, key_rows, value_rows, allowed, log_totals, grad_mixed, block_rows
    )
    grad_query_low = (
        rotate_back(grad_queries.reshape(row_count, HEADS, HD), cosine_heads, sine_heads)
        .reshape(row_count, HEADS * HD)
        .astype(jnp.bfloat16)
    )
    grad_key_low = (
        rotate_back(grad_keys, cosine_heads, sine_heads)
        .reshape(row_count, KVHEADS * HD)
        .astype(jnp.bfloat16)
    )
    grad_value_low = grad_values.reshape(row_count, KVHEADS * HD).astype(jnp.bfloat16)
    grad_w_query = product_left_t(normed_low, grad_query_low)
    grad_w_key = product_left_t(normed_low, grad_key_low)
    grad_w_value = product_left_t(normed_low, grad_value_low)
    grad_bias_query = jnp.sum(grad_query_low.astype(jnp.float32), axis=0)
    grad_bias_key = jnp.sum(grad_key_low.astype(jnp.float32), axis=0)
    grad_bias_value = jnp.sum(grad_value_low.astype(jnp.float32), axis=0)
    grad_normed = (
        product_right_t(grad_query_low, back_query)
        + product_right_t(grad_key_low, back_key)
        + product_right_t(grad_value_low, back_value)
    )
    grad_from_one, grad_gain_attn = norm_back(inputs, inverse_one, gain_attn, grad_normed)
    grad_tokens = grad_residual + grad_from_one
    full_grads = (
        grad_w_query,
        grad_w_key,
        grad_w_value,
        grad_w_output,
        grad_w_gate,
        grad_w_up,
        grad_w_down,
    )
    owned_rows = (
        lax.psum_scatter(
            full_grads[0].astype(jnp.bfloat16), "shard", scatter_dimension=0, tiled=True
        ).astype(jnp.float32),
        lax.psum_scatter(
            full_grads[1].astype(jnp.bfloat16), "shard", scatter_dimension=0, tiled=True
        ).astype(jnp.float32),
        lax.psum_scatter(
            full_grads[2].astype(jnp.bfloat16), "shard", scatter_dimension=0, tiled=True
        ).astype(jnp.float32),
        lax.psum_scatter(
            full_grads[3].astype(jnp.bfloat16), "shard", scatter_dimension=0, tiled=True
        ).astype(jnp.float32),
        lax.psum_scatter(
            full_grads[4].astype(jnp.bfloat16), "shard", scatter_dimension=0, tiled=True
        ).astype(jnp.float32),
        lax.psum_scatter(
            full_grads[5].astype(jnp.bfloat16), "shard", scatter_dimension=0, tiled=True
        ).astype(jnp.float32),
        lax.psum_scatter(
            full_grads[6].astype(jnp.bfloat16), "shard", scatter_dimension=0, tiled=True
        ).astype(jnp.float32),
    )
    summed = (
        lax.psum(owned_rows[0].astype(jnp.bfloat16), "replica").astype(jnp.float32),
        lax.psum(owned_rows[1].astype(jnp.bfloat16), "replica").astype(jnp.float32),
        lax.psum(owned_rows[2].astype(jnp.bfloat16), "replica").astype(jnp.float32),
        lax.psum(owned_rows[3].astype(jnp.bfloat16), "replica").astype(jnp.float32),
        lax.psum(owned_rows[4].astype(jnp.bfloat16), "replica").astype(jnp.float32),
        lax.psum(owned_rows[5].astype(jnp.bfloat16), "replica").astype(jnp.float32),
        lax.psum(owned_rows[6].astype(jnp.bfloat16), "replica").astype(jnp.float32),
    )
    small_sums = lax.psum(
        (grad_gain_attn, grad_gain_ffn, grad_bias_query, grad_bias_key, grad_bias_value),
        ("shard", "replica"),
    )
    return (
        output,
        grad_tokens,
        small_sums[0],
        small_sums[1],
        summed[0],
        small_sums[2],
        summed[1],
        small_sums[3],
        summed[2],
        small_sums[4],
        summed[3],
        summed[4],
        summed[5],
        summed[6],
    )


def solution(mesh):
    return jax.shard_map(
        on_device,
        mesh=mesh,
        in_specs=(
            P(("shard", "replica"), None),
            P(("shard", "replica"), None),
            P(("shard", "replica"), None),
            P(),
            P(),
            P("shard", None),
            P(),
            P("shard", None),
            P(),
            P("shard", None),
            P(),
            P("shard", None),
            P("shard", None),
            P("shard", None),
            P("shard", None),
        ),
        out_specs=(
            P(("shard", "replica"), None),
            P(("shard", "replica"), None),
            P(),
            P(),
            P("shard", None),
            P(),
            P("shard", None),
            P(),
            P("shard", None),
            P(),
            P("shard", None),
            P("shard", None),
            P("shard", None),
            P("shard", None),
        ),
        check_vma=False,
    )
```

profile of v0, /device:TPU:0, one launch (start us, length us, event | category | flops | bytes accessed | tf_op | source)
XLA Modules:
  0.0 1259.4 jit_solution(8313719846199733176)
XLA Ops:
  12.9 7.0 all_gather.29
  19.9 7.2 all_gather.30
  37.5 4.1 broadcast_add_fusion
  43.8 98.9 %while.27 = (s32[]{:T(128)}, bf16[2,512,2,7,64]{1,4,3,2,0:T(8,128)(2,1)}, f32[2,2,7,512,1]{3,2,1,4,0:T(8,128)}, s32[2]{0:T(128)S(1)}, pred[1024,1024]{1,0:T(8,12...) while((s32[]{:T(128)}, ...), condition=%wide.region_5.6_spmd, body=%wide.region_2.5_spmd.sunk | while | flops 1967580160 | bytes 210735312 | solution.py:109
  47.9 14.2 %bitcast_reduce_fusion.2 = (f32[2,7,512]{2,1,0:T(8,128)S(1)}, f32[2,512,7,1024]{3,1,2,0:T(8,128)}) fusion(pred[512,1024]{1,0:T(8,128)(4,1)S(1)} %constant_dynamic-slice_fusion.4, bf16[1024,2,64]{0,2,1:T(8,128)(2,1)S(1)} %get-tuple-element.422, bf16[1024,2,7,64]{0,3,2,1:T(8,128)(2,1)} %get-tuple-element.421, s32[]{:T(128)S(6)} %select_n.56), kind=kOutput, calls=%fused_computation.1.clone.1 | convolution fusion | flops 961537024 | bytes 31092740 | tf_op jit(solution)/shard_map/while/body/eval_jaxpr/bkgd,rkd->kgbr/dot_general | solution.py:88
  62.1 16.4 %fusion.117 = f32[2,7,512]{2,1,0:T(8,128)S(1)} fusion(f32[2,512,7,1024]{3,1,2,0:T(8,128)} %get-tuple-element.379, f32[2,7,512]{2,1,0:T(8,128)S(1)} %get-tuple-element.380, pred[512,1024]{1,0:T(8,128)(4,1)S(1)} %constant_dynamic-slice_fusion.4), kind=kLoop, calls=%fused_computation.5.clone.1 | loop fusion | flops 29352960 | bytes 29941760 | tf_op jit(solution)/shard_map/while/body/eval_jaxpr/reduce_sum | solution.py:101
  78.6 4.2 copy-done
  82.8 9.7 fusion.118
  97.0 14.1 %bitcast_reduce_fusion.2 = (f32[2,7,512]{2,1,0:T(8,128)S(1)}, f32[2,512,7,1024]{3,1,2,0:T(8,128)}) fusion(pred[512,1024]{1,0:T(8,128)(4,1)S(1)} %constant_dynamic-slice_fusion.4, bf16[1024,2,64]{0,2,1:T(8,128)(2,1)S(1)} %get-tuple-element.422, bf16[1024,2,7,64]{0,3,2,1:T(8,128)(2,1)} %get-tuple-element.421, s32[]{:T(128)S(6)} %select_n.56), kind=kOutput, calls=%fused_computation.1.clone.1 | convolution fusion | flops 961537024 | bytes 31092740 | tf_op jit(solution)/shard_map/while/body/eval_jaxpr/bkgd,rkd->kgbr/dot_general | solution.py:88
  111.1 15.3 %fusion.117 = f32[2,7,512]{2,1,0:T(8,128)S(1)} fusion(f32[2,512,7,1024]{3,1,2,0:T(8,128)} %get-tuple-element.379, f32[2,7,512]{2,1,0:T(8,128)S(1)} %get-tuple-element.380, pred[512,1024]{1,0:T(8,128)(4,1)S(1)} %constant_dynamic-slice_fusion.4), kind=kLoop, calls=%fused_computation.5.clone.1 | loop fusion | flops 29352960 | bytes 29941760 | tf_op jit(solution)/shard_map/while/body/eval_jaxpr/reduce_sum | solution.py:101
  126.4 5.5 copy-done
  131.9 9.7 fusion.118
  147.9 4.5 multiply_reduce_fusion.2
  155.8 17.2 %fusion.54 = f32[1024,4864]{1,0:T(8,128)} fusion(bf16[1024,896]{0,1:T(8,128)(2,1)S(1)} %multiply_convert_fusion.3, bf16[896,4864]{1,0:T(8,128)(2,1)} %all-gather.12.cloned.1.call-done), kind=kOutput, calls=%fused_computation.122 | convolution fusion | flops 8925478912 | bytes 30474240 | tf_op jit(solution)/shard_map/dot_general | solution.py:17
  173.0 5.2 all-gather.10.cloned.1.call-done
  178.2 17.9 %fusion.53 = f32[1024,4864]{1,0:T(8,128)} fusion(bf16[1024,896]{0,1:T(8,128)(2,1)} %copy-done.26, bf16[896,4864]{1,0:T(8,128)(2,1)} %all-gather.10.cloned.1.call-done), kind=kOutput, calls=%fused_computation.121 | convolution fusion | flops 8925478912 | bytes 30474240 | tf_op jit(solution)/shard_map/dot_general | solution.py:17
  196.2 43.6 %all-gather.14.cloned.1.call-done = bf16[4864,896]{1,0:T(8,128)(2,1)} async-done(((bf16[1216,896]{1,0:T(8,128)(2,1)}), bf16[4864,896]{1,0:T(8,128)(2,1)}) %all-gather.14.cloned.1.call-update) | async-done | bytes 8716304 | tf_op jit(solution)/shard_map/all_gather | solution.py:203
  239.8 33.1 %multiply_convert_fusion = (bf16[1024,4864]{1,0:T(8,128)(2,1)}, bf16[1024,4864]{1,0:T(8,128)(2,1)}, bf16[1024,4864]{1,0:T(8,128)(2,1)}) fusion(f32[1024,4864]{1,0:T(8,128)} %fusion.53, f32[1024,4864]{1,0:T(8,128)} %fusion.54, bf16[1024,896]{1,0:T(8,128)(2,1)S(1)} %copy-done.22, bf16[4864,896]{1,0:T(8,128)(2,1)} %all-gather.14.cloned.1.call-done), kind=kOutput, calls=%fused_computation.49 | convolution fusion | flops 8995209216 | bytes 80281600 | tf_op jit(solution)/shard_map/dot_general | solution.py:21
  272.9 15.7 %fusion.55 = f32[1024,896]{0,1:T(8,128)} fusion(bf16[1024,4864]{1,0:T(8,128)(2,1)} %get-tuple-element.250, bf16[896,4864]{1,0:T(8,128)(2,1)} %all-gather.10.cloned.1.call-done), kind=kOutput, calls=%fused_computation.123 | convolution fusion | flops 8925478912 | bytes 22347776 | tf_op jit(solution)/shard_map/dot_general | solution.py:21
  288.6 15.1 %multiply_reduce_fusion = (f32[896]{0:T(1024)}, f32[1024]{0:T(1024)S(1)}, f32[1024,896]{0,1:T(8,128)S(1)}) fusion(f32[1024,896]{0,1:T(8,128)S(1)} %copy-done.9, f32[1024]{0:T(1024)S(1)} %get-tuple-element.265, f32[896]{0:T(1024)S(1)} %copy-done.39, f32[1024,896]{0,1:T(8,128)} %fusion.55, bf16[1024,4864]{1,0:T(8,128)(2,1)S(1)} %copy-done.46, ...), kind=kOutput, calls=%fused_computation.79 | convolution fusion | flops 8931899392 | bytes 29703168 | tf_op jit(solution)/shard_map/dot_general | solution.py:21
  308.4 271.2 %while.28 = (s32[]{:T(128)}, f32[1024,2,64]{0,2,1:T(8,128)S(1)}, f32[1024,2,64]{0,2,1:T(8,128)S(1)}, f32[2,512,2,7,64]{1,0,4,3,2:T(2,128)}, s32[2]{0:T(128)S(1)}...) while((s32[]{:T(128)}, f32[1024,2,64]{0,2,1:T(8,128)S(1)}, ...), condition=%wide.region_10.11_spmd.clone, body=%wide.region_8.10_spmd.clone.sunk | while | flops 4764787712 | bytes 237646048 | solution.py:147
  312.8 15.0 %fusion.127 = f32[2,512,7,1024]{3,1,2,0:T(8,128)} fusion(bf16[1024,2,7,64]{0,3,2,1:T(8,128)(2,1)} %get-tuple-element.464, s32[]{:T(128)S(6)} %select_n.57, bf16[1024,2,64]{0,2,1:T(8,128)(2,1)S(1)} %get-tuple-element.465), kind=kOutput, calls=%fused_computation.36.clone.1 | convolution fusion | flops 939524096 | bytes 30539780 | tf_op jit(solution)/shard_map/while/body/eval_jaxpr/bkgd,rkd->kgbr/dot_general | solution.py:121
  327.8 23.5 %fusion.128 = (f32[2,7,512]{2,1,0:T(8,128)S(1)}, f32[2,7,512,1024]{3,2,1,0:T(8,128)}) fusion(f32[2,512,7,1024]{3,1,2,0:T(8,128)} %fusion.127, f32[2,7,512]{2,1,0:T(8,128)S(1)} %dynamic-slice_bitcast_fusion.2, bf16[1024,2,64]{0,2,1:T(8,128)(2,1)S(1)} %get-tuple-element.462, bf16[1024,2,7,64]{0,3,2,1:T(8,128)(2,1)} %get-tuple-element.460, ...), kind=kOutput, calls=%fused_computation.21.clone.1 | convolution fusion | flops 976217088 | bytes 60481540 | tf_op jit(solution)/shard_map/while/body/eval_jaxpr/bkgd,rkd->kgbr/dot_general | solution.py:88
  351.3 24.3 %fusion.129 = bf16[2,7,512,1024]{3,2,1,0:T(8,128)(2,1)} fusion(f32[2,7,512,1024]{3,2,1,0:T(8,128)} %get-tuple-element.392, f32[2,512,7,1024]{3,1,2,0:T(8,128)} %fusion.127, f32[2,7,512]{2,1,0:T(8,128)S(1)} %get-tuple-element.393), kind=kLoop, calls=%fused_computation.23.clone.1 | loop fusion | flops 22020096 | bytes 73428992 | tf_op jit(solution)/shard_map/while/body/eval_jaxpr/convert_element_type | solution.py:125
  375.6 12.5 fusion.131
  388.1 8.3 fusion.130
  396.5 11.0 multiply_bitcast_fusion.2
  410.8 33.4 %dynamic_update_slice.20 = f32[2,512,2,7,64]{1,0,4,3,2:T(2,128)} dynamic-update-slice(f32[2,512,2,7,64]{1,0,4,3,2:T(2,128)} %get-tuple-element.444, f32[1,512,2,7,64]{1,0,4,3,2:T(1,128)S(1)} %copy.76, s32[]{:T(128)S(6)} %copy.93, s32[]{:T(128)} %constant.41.clone.1..sunk.1, s32[]{:T(128)} %constant.41.clone.1..sunk.1, s32[]{:T(128)} %constant.41.clone.1..sunk.1, s32[]{:T(128)} %constant.41.clone.1..sunk.1) | dynamic-update-slice | bytes 3670020 | tf_op jit(solution)/shard_map/while/body/jit(dynamic_update_index_in_dim)/dynamic_update_slice | solution.py:147
  448.2 14.9 %fusion.127 = f32[2,512,7,1024]{3,1,2,0:T(8,128)} fusion(bf16[1024,2,7,64]{0,3,2,1:T(8,128)(2,1)} %get-tuple-element.464, s32[]{:T(128)S(6)} %select_n.57, bf16[1024,2,64]{0,2,1:T(8,128)(2,1)S(1)} %get-tuple-element.465), kind=kOutput, calls=%fused_computation.36.clone.1 | convolution fusion | flops 939524096 | bytes 30539780 | tf_op jit(solution)/shard_map/while/body/eval_jaxpr/bkgd,rkd->kgbr/dot_general | solution.py:121
  463.2 23.5 %fusion.128 = (f32[2,7,512]{2,1,0:T(8,128)S(1)}, f32[2,7,512,1024]{3,2,1,0:T(8,128)}) fusion(f32[2,512,7,1024]{3,1,2,0:T(8,128)} %fusion.127, f32[2,7,512]{2,1,0:T(8,128)S(1)} %dynamic-slice_bitcast_fusion.2, bf16[1024,2,64]{0,2,1:T(8,128)(2,1)S(1)} %get-tuple-element.462, bf16[1024,2,7,64]{0,3,2,1:T(8,128)(2,1)} %get-tuple-element.460, ...), kind=kOutput, calls=%fused_computation.21.clone.1 | convolution fusion | flops 976217088 | bytes 60481540 | tf_op jit(solution)/shard_map/while/body/eval_jaxpr/bkgd,rkd->kgbr/dot_general | solution.py:88
  486.6 24.3 %fusion.129 = bf16[2,7,512,1024]{3,2,1,0:T(8,128)(2,1)} fusion(f32[2,7,512,1024]{3,2,1,0:T(8,128)} %get-tuple-element.392, f32[2,512,7,1024]{3,1,2,0:T(8,128)} %fusion.127, f32[2,7,512]{2,1,0:T(8,128)S(1)} %get-tuple-element.393), kind=kLoop, calls=%fused_computation.23.clone.1 | loop fusion | flops 22020096 | bytes 73428992 | tf_op jit(solution)/shard_map/while/body/eval_jaxpr/convert_element_type | solution.py:125
  510.9 12.4 fusion.131
  523.4 8.3 fusion.130
  531.6 11.0 multiply_bitcast_fusion.2
  546.0 33.4 %dynamic_update_slice.20 = f32[2,512,2,7,64]{1,0,4,3,2:T(2,128)} dynamic-update-slice(f32[2,512,2,7,64]{1,0,4,3,2:T(2,128)} %get-tuple-element.444, f32[1,512,2,7,64]{1,0,4,3,2:T(1,128)S(1)} %copy.76, s32[]{:T(128)S(6)} %copy.93, s32[]{:T(128)} %constant.41.clone.1..sunk.1, s32[]{:T(128)} %constant.41.clone.1..sunk.1, s32[]{:T(128)} %constant.41.clone.1..sunk.1, s32[]{:T(128)} %constant.41.clone.1..sunk.1) | dynamic-update-slice | bytes 3670020 | tf_op jit(solution)/shard_map/while/body/jit(dynamic_update_index_in_dim)/dynamic_update_slice | solution.py:147
  585.4 5.9 convolution_convert_fusion.4
  591.3 6.0 reshape.189
  604.8 15.6 %convolution_convert_fusion.1 = bf16[896,4864]{1,0:T(8,128)(2,1)} fusion(bf16[1024,896]{0,1:T(8,128)(2,1)} %copy-done.26, bf16[1024,4864]{1,0:T(8,128)(2,1)} %get-tuple-element.250), kind=kOutput, calls=%fused_computation.55 | convolution fusion | flops 8929837056 | bytes 20512768 | tf_op jit(solution)/shard_map/dot_general | solution.py:27
  621.9 15.0 %convolution_convert_fusion = bf16[896,4864]{1,0:T(8,128)(2,1)} fusion(bf16[1024,896]{0,1:T(8,128)(2,1)S(1)} %copy-done.27, bf16[1024,4864]{1,0:T(8,128)(2,1)} %get-tuple-element.249), kind=kOutput, calls=%fused_computation.54 | convolution fusion | flops 8929837056 | bytes 20512768 | tf_op jit(solution)/shard_map/dot_general | solution.py:27
  638.5 16.3 %convolution_convert_fusion.2 = bf16[4864,896]{1,0:T(8,128)(2,1)} fusion(bf16[1024,4864]{1,0:T(8,128)(2,1)} %get-tuple-element.251, bf16[1024,896]{1,0:T(8,128)(2,1)S(1)} %copy-done.23), kind=kOutput, calls=%fused_computation.56 | convolution fusion | flops 8929837056 | bytes 20512768 | tf_op jit(solution)/shard_map/dot_general | solution.py:27
  657.7 31.8 %reduce-scatter.8.cloned.1.call-done = bf16[224,896]{1,0:T(8,128)(2,1)} async-done(((bf16[896,896]{1,0:T(8,128)(2,1)}), bf16[224,896]{1,0:T(8,128)(2,1)}) %reduce-scatter.8.cloned.1.call-update) | async-done | bytes 401424 | tf_op jit(solution)/shard_map/reduce_scatter | solution.py:281
  689.5 76.2 %reduce-scatter.16.cloned.1.call-done = bf16[224,4864]{1,0:T(8,128)(2,1)} async-done(((bf16[896,4864]{1,0:T(8,128)(2,1)}), bf16[224,4864]{1,0:T(8,128)(2,1)}) %reduce-scatter.16.cloned.1.call-update) | async-done | bytes 2179088 | tf_op jit(solution)/shard_map/reduce_scatter | solution.py:293
  765.7 76.4 %reduce-scatter.18.cloned.1.call-done = bf16[224,4864]{1,0:T(8,128)(2,1)} async-done(((bf16[896,4864]{1,0:T(8,128)(2,1)}), bf16[224,4864]{1,0:T(8,128)(2,1)}) %reduce-scatter.18.cloned.1.call-update) | async-done | bytes 2179088 | tf_op jit(solution)/shard_map/reduce_scatter | solution.py:296
  842.1 76.2 %reduce-scatter.20.cloned.1.call-done = bf16[1216,896]{1,0:T(8,128)(2,1)} async-done(((bf16[4864,896]{1,0:T(8,128)(2,1)}), bf16[1216,896]{1,0:T(8,128)(2,1)}) %reduce-scatter.20.cloned.1.call-update) | async-done | bytes 2179088 | tf_op jit(solution)/shard_map/reduce_scatter | solution.py:299
  918.4 16.3 %add_convert_fusion = bf16[1024,896]{0,1:T(8,128)(2,1)} fusion(f32[1024,896]{0,1:T(8,128)} %copy-done.8, bf16[1024,4864]{1,0:T(8,128)(2,1)} %get-tuple-element.251, bf16[4864,896]{1,0:T(8,128)(2,1)} %all-gather.14.cloned.1.call-done), kind=kOutput, calls=%fused_computation.83 | convolution fusion | flops 8927313920 | bytes 24182784 | tf_op jit(solution)/shard_map/dot_general | solution.py:17
  947.3 5.0 copy.50
  952.3 39.6 %all-reduce = (f32[896]{0:T(1024)}, f32[896]{0:T(1024)}, f32[896]{0:T(1024)}, f32[128]{0:T(128)}, f32[128]{0:T(128)}) all-reduce(f32[896]{0:T(1024)S(1)} %get-tuple-element.187, f32[896]{0:T(1024)S(1)} %copy-done.40, f32[896]{0:T(1024)S(1)} %reduce_sum.122, ...), channel_id=1, replica_groups=mesh['shard'=4,'replica'=8] {'shard','replica'}, use_global_device_ids=true, to_apply=%region_13.14 | all-reduce | flops 2944 | bytes 23552 | tf_op jit(solution)/shard_map/psum | solution.py:312
  994.8 246.4 %all-reduce.8.cloned.1.call-done = (bf16[224,896]{1,0:T(8,128)(2,1)}, bf16[224,896]{1,0:T(8,128)(2,1)}, bf16[224,4864]{1,0:T(8,128)(2,1)}, bf16[224,4864]{1,0:T(8,128)(2,1)}, bf16[1216,896]{1,0:T(8,128)(2,1)}) async-done(((bf16[224,896]{1,0:T(8,128)(2,1)}, bf16[224,896]{1,0:T(8,128)(2,1)}, bf16[224,4864]{1,0:T(8,128)(2,1)}, bf16[224,4864]{1,0:T(8,128)(2,1)}, bf16[1216,896]{1,0:T(8,128)(2,1)}), ...) | async-done | bytes 7340048 | tf_op jit(solution)/shard_map/psum | solution.py:304
  (196 shorter events, 93.2 us)
Async XLA Ops:
  7.2 3.5 copy-start.37
  7.2 30.3 %all-gather.6.cloned.1.call-start = ((), (), s32[]{:S(2)}) async-start(), calls=%async_computation.7 | async-start | bytes 2007040 | tf_op jit(solution)/shard_map/all_gather | solution.py:176
  7.9 140.0 %all-gather.8.cloned.1.call-start = ((), (), s32[]{:S(2)}) async-start(), calls=%async_computation.8 | async-start | bytes 2007040 | tf_op jit(solution)/shard_map/all_gather | solution.py:179
  8.7 4.2 copy-start.33
  8.7 11.2 copy-start.34
  8.7 145.9 %all-gather.12.cloned.1.call-start = ((), (), s32[]{:S(2)}) async-start(), calls=%async_computation.10 | async-start | bytes 10895360 | tf_op jit(solution)/shard_map/all_gather | solution.py:202
  9.4 168.8 %all-gather.10.cloned.1.call-start = ((), (), s32[]{:S(2)}) async-start(), calls=%async_computation.9 | async-start | bytes 10895360 | tf_op jit(solution)/shard_map/all_gather | solution.py:201
  10.0 229.8 %all-gather.14.cloned.1.call-start = ((), (), s32[]{:S(2)}) async-start(), calls=%async_computation.11 | async-start | bytes 10895360 | tf_op jit(solution)/shard_map/all_gather | solution.py:203
  10.6 644.3 %reduce-scatter.10.cloned.1.call-start = ((), (), s32[]{:S(2)}) async-start(), calls=%async_computation.13 | async-start | bytes 286720 | tf_op jit(solution)/shard_map/reduce_scatter | solution.py:284
  19.9 16.9 %copy-start.20 = (bf16[896,128]{1,0:T(8,128)(2,1)}, bf16[896,128]{1,0:T(8,128)(2,1)S(1)}, u32[]{:S(2)}) copy-start(bf16[896,128]{1,0:T(8,128)(2,1)S(1)} %all_gather.29) | copy-start | bytes 688132
  27.1 9.1 copy-start.28
  30.1 6.1 copy-start.3
  30.1 5.6 copy-start.35
  31.3 4.9 copy-start.31
  31.3 4.9 copy-start.45
  35.7 6.0 copy-start.13
  35.7 6.0 copy-start.15
  62.1 20.6 %copy-start = (f32[2,512,7,1024]{3,1,2,0:T(8,128)S(1)}, f32[2,512,7,1024]{3,1,2,0:T(8,128)}, u32[]{:S(2)}) copy-start(f32[2,512,7,1024]{3,1,2,0:T(8,128)} %get-tuple-element.379) | copy-start | bytes 88080384 | tf_op jit(solution)/shard_map/while
  111.1 20.7 %copy-start = (f32[2,512,7,1024]{3,1,2,0:T(8,128)S(1)}, f32[2,512,7,1024]{3,1,2,0:T(8,128)}, u32[]{:S(2)}) copy-start(f32[2,512,7,1024]{3,1,2,0:T(8,128)} %get-tuple-element.379) | copy-start | bytes 88080384 | tf_op jit(solution)/shard_map/while
  142.6 5.3 copy-start.4
  147.9 6.3 copy-start.39
  173.0 66.8 %copy-start.22 = (bf16[1024,896]{1,0:T(8,128)(2,1)S(1)}, bf16[1024,896]{1,0:T(8,128)(2,1)}, u32[]{:S(2)}) copy-start(bf16[1024,896]{1,0:T(8,128)(2,1)} %param.21) | copy-start | bytes 5505028
  272.9 15.7 %copy-start.9 = (f32[1024,896]{0,1:T(8,128)S(1)}, f32[1024,896]{0,1:T(8,128)}, u32[]{:S(2)}) copy-start(f32[1024,896]{0,1:T(8,128)} %copy-done.8) | copy-start | bytes 11010052
  272.9 15.7 %copy-start.46 = (bf16[1024,4864]{1,0:T(8,128)(2,1)S(1)}, bf16[1024,4864]{1,0:T(8,128)(2,1)}, u32[]{:S(2)}) copy-start(bf16[1024,4864]{1,0:T(8,128)(2,1)} %get-tuple-element.249) | copy-start | bytes 29884420
  288.6 15.1 %copy-start.12 = (bf16[1024,896]{0,1:T(8,128)(2,1)S(1)}, bf16[1024,896]{0,1:T(8,128)(2,1)}, u32[]{:S(2)}) copy-start(bf16[1024,896]{0,1:T(8,128)(2,1)} %copy.42) | copy-start | bytes 5505028
  305.1 3.3 copy-start.10
  305.1 3.3 copy-start.1
  305.1 3.3 copy-start.2
  305.1 3.3 copy-start.30
  579.6 4.3 copy-start.7
  583.8 71.2 %reduce-scatter.12.cloned.1.call-start = ((), (), s32[]{:S(2)}) async-start(), calls=%async_computation.14 | async-start | bytes 286720 | tf_op jit(solution)/shard_map/reduce_scatter | solution.py:287
  585.3 72.4 %reduce-scatter.14.cloned.1.call-start = ((), (), s32[]{:S(2)}) async-start(), calls=%async_computation.15 | async-start | bytes 2007040 | tf_op jit(solution)/shard_map/reduce_scatter | solution.py:290
  591.3 98.2 %reduce-scatter.8.cloned.1.call-start = ((), (), s32[]{:S(2)}) async-start(), calls=%async_computation.12 | async-start | bytes 2007040 | tf_op jit(solution)/shard_map/reduce_scatter | solution.py:281
  591.3 6.0 copy-start.14
  591.3 6.0 copy-start.16
  604.8 160.9 %reduce-scatter.16.cloned.1.call-start = ((), (), s32[]{:S(2)}) async-start(), calls=%async_computation.16 | async-start | bytes 10895360 | tf_op jit(solution)/shard_map/reduce_scatter | solution.py:293
  620.4 221.7 %reduce-scatter.18.cloned.1.call-start = ((), (), s32[]{:S(2)}) async-start(), calls=%async_computation.17 | async-start | bytes 10895360 | tf_op jit(solution)/shard_map/reduce_scatter | solution.py:296
  637.0 281.4 %reduce-scatter.20.cloned.1.call-start = ((), (), s32[]{:S(2)}) async-start(), calls=%async_computation.18 | async-start | bytes 10895360 | tf_op jit(solution)/shard_map/reduce_scatter | solution.py:299
  654.9 337.0 %all-reduce.6.cloned.1.call-start = ((), (), s32[]{:S(2)}) async-start(), calls=%async_computation.19 | async-start | bytes 229376 | tf_op jit(solution)/shard_map/psum | solution.py:305
  655.6 585.6 %all-reduce.8.cloned.1.call-start = ((), (), s32[]{:S(2)}) async-start(), calls=%async_computation.20 | async-start | bytes 14680064 | tf_op jit(solution)/shard_map/psum | solution.py:304
  934.7 4.2 copy-start.21
  934.7 4.8 copy-start.25
  940.3 2.1 copy-start.32
  940.3 2.1 copy-start.36
  947.3 5.0 copy-start.40
  1241.2 4.2 copy-start.19
  1243.3 4.4 copy-start.18
  1247.7 2.5 copy-start.17
  (14 other events, 22.7 us)
Sparse Core Ops, SparseCore 0:
  9.6 23.7 all-gather.5
  34.9 19.8 all-gather.7
  56.4 60.1 all-gather.11
  118.0 60.1 all-gather.9
  179.6 60.1 all-gather.13
  583.9 19.8 reduce-scatter.9
  606.9 19.8 reduce-scatter.11
  629.3 28.3 reduce-scatter.13
  661.0 28.4 reduce-scatter.7
  692.0 73.7 reduce-scatter.15
  768.4 73.7 reduce-scatter.17
  844.6 73.7 reduce-scatter.19
  921.8 69.2 all-reduce.5
  996.8 244.3 all-reduce.7
where the time goes:
time: 1270 us; the launch traced here: 1260 us
  waiting for transfers between devices  562 us (44%)
  matrix products  381 us (30%)
  local copies, waits for them, and re-layouts  128 us (10%)
  other arithmetic  111 us (9%)
  blocking collectives  53.8 us (4%)
  between operations  14.9 us (1%)
    psum x1, waiting for transfers between devices, on_device(): lax.psum(owned_rows[0].astype(jnp.bfloat16), 'replica').astype(jnp.float32)  246 us
    reduce_scatter x1, waiting for transfers between devices, on_device(): lax.psum_scatter(full_grads[5].astype(jnp.bfloat16), 'shard', scatter_dim...  76.4 us
    reduce_scatter x1, waiting for transfers between devices, on_device(): lax.psum_scatter(full_grads[6].astype(jnp.bfloat16), 'shard', scatter_dim...  76.2 us
    reduce_scatter x1, waiting for transfers between devices, on_device(): lax.psum_scatter(full_grads[4].astype(jnp.bfloat16), 'shard', scatter_dim...  76.2 us
    dot_general x4, matrix products, block_scores(): jnp.einsum('bkgd,rkd->kgbr', query_block, key_rows, preferred_element_typ...  75.4 us
    dynamic_update_slice x4, local copies, waits for them, and re-layouts, attention_backward(): lax.scan(one_block, (zero_rows, zero_rows), (starts, log_totals))  73.7 us
    dot_general x7, matrix products, product_right_t(): lax.dot_general(left, right, (((1,), (1,)), ((), ())), preferred_element_...  71.3 us
    dot_general x7, matrix products, product(): return jnp.dot(left, right, preferred_element_type=jnp.float32)  61 us
  transfers between devices with their start and end apart: 14, of which 8 were waited for; matrix products, arithmetic and copies ran while one was open for 20% of the time, Pallas kernels for 0%

commit v1 on v0

v1 whole, which is shorter than its diff:
```python
import functools

import jax
import jax.numpy as jnp
from jax import lax
from jax.experimental import pallas as pl
from jax.experimental.pallas import tpu as pltpu
from jax.sharding import PartitionSpec as P

HEADS,KVHEADS,HD=14,2,64
GROUP=HEADS//KVHEADS
PAIRS=HEADS//2
TILE=256
VMEM_CAP=56<<20
bf16,f32=jnp.bfloat16,jnp.float32
def nn(a,b): return lax.dot_general(a,b,(((1,),(0,)),((),())),preferred_element_type=f32)
def nt(a,b): return lax.dot_general(a,b,(((1,),(1,)),((),())),preferred_element_type=f32)
def tn(a,b): return lax.dot_general(a,b,(((0,),(0,)),((),())),preferred_element_type=f32)

def left_half(rows):
    return lax.broadcasted_iota(jnp.int32,(rows,2*HD),1)<HD

def attend_kernel(tiles,segc,segr,q,kx,vx,o,linv,*rest):
    probs,bias=rest[:tiles],rest[tiles]
    pair=pl.program_id(0)
    @pl.when(pair==0)
    def _():
        for i in range(tiles):
            w=(i+1)*TILE
            rows=lax.broadcasted_iota(jnp.int32,(TILE,w),0)+i*TILE
            cols=lax.broadcasted_iota(jnp.int32,(TILE,w),1)
            ok=(segc[i*TILE:w,:]==segr[:,:w])&(cols<=rows)
            bias[i*TILE:w,:w]=jnp.where(ok,0.0,-1e30)
    left=left_half(TILE)
    kinds=[2*(2*pair+side>=GROUP).astype(jnp.int32)+side for side in (0,1)]
    for i in range(tiles):
        w=(i+1)*TILE
        block=q[i*TILE:w,:]
        mixed=[]
        for side in (0,1):
            s=nt(block,kx[kinds[side],:w,:])+bias[i*TILE:w,:w]
            e=jnp.exp(s-jnp.max(s,axis=-1,keepdims=True)).astype(bf16)
            for j in range(i+1):
                probs[j][side,(i-j)*TILE:(i-j+1)*TILE,:]=e[:,j*TILE:(j+1)*TILE]
            mixed.append(nn(e,vx[kinds[side],:w,:]))
        totals=jnp.where(left,pltpu.roll(mixed[0],HD,1),pltpu.roll(mixed[1],HD,1))
        inverse=1.0/totals
        o[i*TILE:w,:]=(jnp.where(left,mixed[0],mixed[1])*inverse).astype(bf16)
        linv[i*TILE:w,:]=inverse

def attend(segments,q,kx,vx):
    t=q.shape[0]; tiles=t//TILE
    whole=lambda *s: pl.BlockSpec(s,lambda p:(0,)*len(s))
    lane=pl.BlockSpec((t,2*HD),lambda p:(0,p))
    pshape=[(HEADS,t-j*TILE,TILE) for j in range(tiles)]
    return pl.pallas_call(functools.partial(attend_kernel,tiles),grid=(PAIRS,),
        in_specs=[whole(t,1),whole(1,t),lane,whole(4,t,2*HD),whole(4,t,2*HD)],
        out_specs=[lane,lane]+[pl.BlockSpec((2,)+s[1:],lambda p:(p,0,0)) for s in pshape],
        out_shape=[jax.ShapeDtypeStruct(q.shape,bf16),jax.ShapeDtypeStruct(q.shape,f32)]+[jax.ShapeDtypeStruct(s,bf16) for s in pshape],
        scratch_shapes=[pltpu.VMEM((t,t),f32)],
        compiler_params=pltpu.CompilerParams(vmem_limit_bytes=VMEM_CAP),
        cost_estimate=pl.CostEstimate(flops=20*10**9,bytes_accessed=40*10**6,transcendentals=9*10**6),
        name="attend")(segments.reshape(t,1),segments.reshape(1,t),q,kx,vx)

def swap_halves(v,lanes):
    half=HD//2
    return jnp.where(lanes%HD<half,pltpu.roll(v,v.shape[1]-half,1),pltpu.roll(v,half,1))

def attend_back_kernel(tiles,q,do,o,kx,vz,cos,sin,*rest):
    probs=rest[:tiles]
    dq,dk,dv,ds0,ds1,dkacc,dvacc=rest[tiles:]
    pair=pl.program_id(0)
    t=q.shape[0]
    @pl.when(pair==0)
    def _():
        dkacc[...]=jnp.zeros_like(dkacc)
        dvacc[...]=jnp.zeros_like(dvacc)
    left=left_half(t)
    t_=do[...].astype(f32)*o[...].astype(f32)
    inner=[jnp.sum(jnp.where(left,t_,0.0),axis=-1,keepdims=True),jnp.sum(jnp.where(left,0.0,t_),axis=-1,keepdims=True)]
    kinds=[2*(2*pair+side>=GROUP).astype(jnp.int32)+side for side in (0,1)]
    for side,ds in ((0,ds0),(1,ds1)):
        kind=kinds[side]
        for j in range(tiles):
            lo=j*TILE
            p=probs[j][side]
            dp=nt(do[lo:,:],vz[kind,lo:lo+TILE,:])
            d=(p.astype(f32)*(dp-inner[side][lo:])).astype(bf16)
            ds[lo:,lo:lo+TILE]=d
            dkacc[kind,lo:lo+TILE,:]+=tn(d,q[lo:,:])
            dvacc[kind,lo:lo+TILE,:]+=tn(p,do[lo:,:])
    lanes=lax.broadcasted_iota(jnp.int32,(TILE,2*HD),1)
    for i in range(tiles):
        w=(i+1)*TILE
        g=(nn(ds0[i*TILE:w,:w],kx[kinds[0],:w,:])+nn(ds1[i*TILE:w,:w],kx[kinds[1],:w,:]))*0.125
        dq[i*TILE:w,:]=(g*cos[i*TILE:w,:]-swap_halves(g,lanes)*sin[i*TILE:w,:]).astype(bf16)
    @pl.when(pair==PAIRS-1)
    def _():
        lanes=lax.broadcasted_iota(jnp.int32,(t,2*HD),1)
        g=jnp.where(left,dkacc[0]+pltpu.roll(dkacc[1],HD,1),pltpu.roll(dkacc[2],HD,1)+dkacc[3])
        dk[...]=(g*cos[...]-swap_halves(g,lanes)*sin[...]).astype(bf16)
        dv[...]=jnp.where(left,dvacc[0]+pltpu.roll(dvacc[1],HD,1),pltpu.roll(dvacc[2],HD,1)+dvacc[3]).astype(bf16)

def attend_back(q,do,o,kx,vz,cos,sin,probs):
    t=q.shape[0]; tiles=t//TILE
    whole=lambda *s: pl.BlockSpec(s,lambda p:(0,)*len(s))
    lane=pl.BlockSpec((t,2*HD),lambda p:(0,p))
    return pl.pallas_call(functools.partial(attend_back_kernel,tiles),grid=(PAIRS,),
        in_specs=[lane,lane,lane,whole(4,t,2*HD),whole(4,t,2*HD),whole(t,2*HD),whole(t,2*HD)]+[pl.BlockSpec((2,)+p.shape[1:],lambda p:(p,0,0)) for p in probs],
        out_specs=[lane,whole(t,2*HD),whole(t,2*HD)],
        out_shape=[jax.ShapeDtypeStruct(q.shape,bf16)]+[jax.ShapeDtypeStruct((t,2*HD),bf16)]*2,
        scratch_shapes=[pltpu.VMEM((t,t),bf16)]*2+[pltpu.VMEM((4,t,2*HD),f32)]*2,
        compiler_params=pltpu.CompilerParams(vmem_limit_bytes=VMEM_CAP),
        cost_estimate=pl.CostEstimate(flops=30*10**9,bytes_accessed=40*10**6,transcendentals=0),
        name="attend_back")(q,do,o,kx,vz,cos,sin,*probs)

def pad_heads(rows,other):
    t=rows.shape[0]
    fill=jnp.full((t,HD),other,rows.dtype)
    out=[]
    for kv in range(KVHEADS):
        one=rows[:,kv*HD:(kv+1)*HD]
        out+= [jnp.concatenate([one,fill],1),jnp.concatenate([fill,one],1)]
    return jnp.stack(out)

BLK=256
def cuts(n):
    return [(a,min(a+BLK,n)) for a in range(0,n,BLK)]
def ffn_kernel(steps,place,n2,dy,gu0,gu1,gu2,gu3,d0,d1,d2,hid,dg,du,keep_gu,send_gu,keep_d,send_d,wgu,wd,ag,au,ad):
    step=pl.program_id(0)
    rows=gu0.shape[1]; half=d0.shape[0]; part=d1.shape[0]
    width=wgu.shape[2]
    @pl.when(step==0)
    def _():
        for n,piece in enumerate((gu0,gu1,gu2,gu3)):
            at=pl.ds(pl.multiple_of(place[n]*rows,16),rows)
            wgu[0,at,:]=piece[0]
            wgu[1,at,:]=piece[1]
        wd[pl.ds(pl.multiple_of(place[4]*half,16),half),:]=d0[...]
        wd[pl.ds(pl.multiple_of(place[5]*part,16),part),:]=d1[...]
        wd[pl.ds(pl.multiple_of(place[6]*part,16),part),:]=d2[...]
        ag[...]=jnp.zeros_like(ag); au[...]=jnp.zeros_like(au); ad[...]=jnp.zeros_like(ad)
    x=n2[...]; y=dy[...]
    for lo,hi in cuts(width):
        gate=nn(x,wgu[0,:,lo:hi]); up=nn(x,wgu[1,:,lo:hi]); dh=nt(y,wd[lo:hi,:])
        sig=jax.nn.sigmoid(gate); silu=gate*sig
        h=(silu*up).astype(bf16)
        g=(dh*up*(sig+silu*(1.0-sig))).astype(bf16)
        u=(dh*silu).astype(bf16)
        hid[:,lo:hi]=h; dg[:,lo:hi]=g; du[:,lo:hi]=u
        ad[lo:hi,:]+=tn(h,y)
        ag[:,lo:hi]+=tn(x,g)
        au[:,lo:hi]+=tn(x,u)
    @pl.when(step==steps-1)
    def _():
        mine,other=place[7],1-place[7]
        for ref,side in ((keep_gu,mine),(send_gu,other)):
            at=pl.ds(pl.multiple_of(side*2*rows,16),2*rows)
            ref[0]=ag[at,:].astype(bf16); ref[1]=au[at,:].astype(bf16)
        for ref,side in ((keep_d,mine),(send_d,other)):
            ref[...]=ad[pl.ds(pl.multiple_of(side*half,16),half),:].astype(bf16)
def ffn_part(place,n2,dy,gus,ds,tt=512):
    t,d=n2.shape; width=gus[0].shape[2]; half=ds[0].shape[0]; steps=t//tt
    whole=lambda *s: pl.BlockSpec(s,lambda i:(0,)*len(s))
    tok=lambda c: pl.BlockSpec((tt,c),lambda i:(i,0))
    S=jax.ShapeDtypeStruct
    return pl.pallas_call(functools.partial(ffn_kernel,steps),grid=(steps,),
      in_specs=[pl.BlockSpec(memory_space=pltpu.SMEM),tok(d),tok(d)]+[whole(*g.shape) for g in gus]+[whole(*g.shape) for g in ds],
      out_specs=[tok(width)]*3+[whole(2,d//2,width)]*2+[whole(half,d)]*2+[whole(2,d,width),whole(width,d)],
      out_shape=[S((t,width),bf16)]*3+[S((2,d//2,width),bf16)]*2+[S((half,d),bf16)]*2+[S((2,d,width),bf16),S((width,d),bf16)],
      scratch_shapes=[pltpu.VMEM((d,width),f32)]*2+[pltpu.VMEM((width,d),f32)],
      compiler_params=pltpu.CompilerParams(vmem_limit_bytes=VMEM_CAP),
      cost_estimate=pl.CostEstimate(flops=12*t*d*width,bytes_accessed=20*10**6,transcendentals=t*width),
      name="ffn_part")(place,n2,dy,*gus,*ds)
def tokens_sum_kernel(parts,*refs):
    out=refs[-1]
    total=None
    for n in range(parts):
        dg,du,w=refs[3*n:3*n+3]
        s=nt(dg[...],w[0])+nt(du[...],w[1])
        total=s if total is None else total+s
    out[...]=total.astype(out.dtype)
def back_tokens(dgs,dus,wgus,first,rows,dtype,tt=512):
    d=wgus[0].shape[1]; n0=first//tt
    ops,specs=[],[]
    fl=0
    for g,u,w in zip(dgs,dus,wgus):
        ops+=[g,u,w]; fl+=4*rows*d*g.shape[1]
        specs+=[pl.BlockSpec((tt,g.shape[1]),lambda i:(i+n0,0))]*2+[pl.BlockSpec(w.shape,lambda i:(0,0,0))]
    return pl.pallas_call(functools.partial(tokens_sum_kernel,len(dgs)),grid=(rows//tt,),in_specs=specs,
      out_specs=pl.BlockSpec((tt,d),lambda i:(i,0)),out_shape=jax.ShapeDtypeStruct((rows,d),dtype),
      compiler_params=pltpu.CompilerParams(vmem_limit_bytes=VMEM_CAP),
      cost_estimate=pl.CostEstimate(flops=fl,bytes_accessed=30*10**6,transcendentals=0),name="back_tokens")(*ops)
def down_kernel(parts,*refs):
    total=None
    for n in range(parts):
        s=nn(refs[2*n][...],refs[2*n+1][...])
        total=s if total is None else total+s
    refs[-1][...]=total.astype(refs[-1].dtype)
def down_tokens(hids,wds,first,rows,dtype,tt=512):
    d=wds[0].shape[1]; n0=first//tt
    ops,specs=[],[]
    fl=0
    for h,w in zip(hids,wds):
        ops+=[h,w]; fl+=2*rows*d*h.shape[1]
        specs+=[pl.BlockSpec((tt,h.shape[1]),lambda i:(i+n0,0)),pl.BlockSpec(w.shape,lambda i:(0,0))]
    return pl.pallas_call(functools.partial(down_kernel,len(hids)),grid=(rows//tt,),in_specs=specs,
      out_specs=pl.BlockSpec((tt,d),lambda i:(i,0)),out_shape=jax.ShapeDtypeStruct((rows,d),dtype),
      compiler_params=pltpu.CompilerParams(vmem_limit_bytes=VMEM_CAP),
      cost_estimate=pl.CostEstimate(flops=fl,bytes_accessed=20*10**6,transcendentals=0),name="down_tokens")(*ops)

epsilon = 1e-06
rope_base = 1000000.0


def rms_stats(values, gain_vector):
    inverse = lax.rsqrt(jnp.mean(values * values, axis=-1, keepdims=True) + epsilon)
    return (values * inverse * gain_vector, inverse)


def norm_back(values, inverse, gain_vector, upstream):
    scaled = upstream * gain_vector
    grad_gain = jnp.sum(upstream * values * inverse, axis=0)
    correction = jnp.sum(scaled * values, axis=-1, keepdims=True) / values.shape[-1]
    grad_values = inverse * scaled - values * (inverse * inverse * inverse) * correction
    return (grad_values, grad_gain)


def rotate(values, cosine_table, sine_table):
    half = values.shape[-1] // 2
    a, b = values[..., :half], values[..., half:]
    return jnp.concatenate([a * cosine_table - b * sine_table, b * cosine_table + a * sine_table], axis=-1)


def angles_of(doc_ids):
    t = doc_ids.shape[0]
    earlier = jnp.sum((doc_ids[None, :] < doc_ids[:, None]).astype(jnp.int32), axis=1)
    places = jnp.arange(t, dtype=jnp.int32) - earlier
    frequency = rope_base ** (-jnp.arange(0, HD, 2).astype(jnp.float32) / HD)
    return places.astype(jnp.float32)[:, None] * frequency[None, :]


def widths_of(rows):
    big = [256] * (rows // 256)
    rest = rows - sum(big)
    return big + ([rest] if rest else [])


class Links:
    def __init__(self, shards, replicas):
        self.shards, self.replicas = shards, replicas
        s, r = lax.axis_index("shard"), lax.axis_index("replica")
        self.x, self.c, self.y, self.z = s // 2, s % 2, r % 2, r // 2

    def core(self, v):
        return lax.ppermute(v, "shard", [(i, i ^ 1) for i in range(self.shards)])

    def across(self, v):
        return lax.ppermute(v, "shard", [(i, i ^ 2) for i in range(self.shards)])

    def beside(self, v):
        return lax.ppermute(v, "replica", [(i, i ^ 1) for i in range(self.replicas)])

    def line(self, v):
        if self.replicas == 8:
            v = v + lax.ppermute(v, "replica", [(0, 2), (1, 3), (6, 4), (7, 5)])
            v = v + lax.ppermute(v, "replica", [(2, 4), (4, 2), (3, 5), (5, 3)])
            ends = lax.ppermute(v, "replica", [(2, 0), (3, 1), (4, 6), (5, 7)])
            return jnp.where((self.z == 0) | (self.z == 3), ends, v)
        bit = 2
        while bit < self.replicas:
            v = v + lax.ppermute(v, "replica", [(i, i ^ bit) for i in range(self.replicas)])
            bit *= 2
        return v

    def both(self, v, axis):
        half = v.shape[axis] // 2
        take = lambda n: lax.dynamic_slice_in_dim(v, n * half, half, axis)
        return take(self.y), take(1 - self.y)

    def replica_sum(self, v, axis):
        keep, send = self.both(v, axis)
        total = self.line(keep + self.beside(send))
        return total, self.beside(total)

    def in_order(self, mine, other, axis):
        first = jnp.where(self.y == 0, mine, other)
        second = jnp.where(self.y == 0, other, mine)
        return jnp.concatenate([first, second], axis)

    def everywhere(self, v):
        v = v + self.core(v)
        v = v + self.across(v)
        v = v + self.beside(v)
        return self.line(v)


def product(left, right):
    return jnp.dot(left, right, preferred_element_type=jnp.float32)


def on_device(
    links_shape,
    tokens,
    segments,
    cotangent,
    gain_attn,
    gain_ffn,
    w_query,
    bias_query,
    w_key,
    bias_key,
    w_value,
    bias_value,
    w_output,
    w_gate,
    w_up,
    w_down,
):
    links = Links(*links_shape)
    x, c, y = links.x, links.c, links.y
    t, d = tokens.shape
    own = w_query.shape[0]
    inputs = tokens.astype(f32)
    doc_ids = segments[0]

    def gathered(local):
        opposite = links.across(local)
        pair = jnp.stack([local, opposite])
        partner = links.core(pair)
        rows = []
        for s in range(4):
            from_mine = jnp.where(x == s // 2, pair[0], pair[1])
            from_partner = jnp.where(x == s // 2, partner[0], partner[1])
            rows.append(jnp.where(c == s % 2, from_mine, from_partner))
        return jnp.concatenate(rows, 0)

    full_qkv = gathered(jnp.concatenate([w_query, w_key, w_value], 1))
    full_output = gathered(w_output)

    ff_rows = w_down.shape[0]
    widths = widths_of(ff_rows)
    offsets = [sum(widths[:n]) for n in range(len(widths))]

    def section(core, off, w):
        return jnp.stack(
            [
                jnp.concatenate(
                    [m[:, (2 * side + core) * ff_rows + off : (2 * side + core) * ff_rows + off + w] for side in (0, 1)], 1
                )
                for m in (w_gate, w_up)
            ]
        )

    gathered_parts = []
    for off, w in zip(offsets, widths):
        sec0, sec1 = section(0, off, w), section(1, off, w)
        mine = jnp.where(c == 0, sec0, sec1)
        core_rows = links.core(jnp.where(c == 0, sec1, sec0))
        x_rows = links.across(jnp.where(y == c, mine, core_rows))
        y_rows = links.beside(x_rows)
        down = w_down[off : off + w]
        x_down = links.across(lax.dynamic_slice_in_dim(down, y * (w // 2), w // 2, 0))
        y_down = links.beside(x_down)
        gathered_parts.append(([mine, core_rows, x_rows, y_rows], [down, x_down, y_down]))
    place = jnp.stack(
        [2 * x + c, 2 * x + 1 - c, 2 * (1 - x) + y, 2 * (1 - x) + 1 - y, x, 2 * (1 - x) + y, 2 * (1 - x) + 1 - y, x]
    ).astype(jnp.int32)

    dy_all = jnp.concatenate([cotangent, links.core(cotangent)], 0)

    angle = angles_of(doc_ids)
    cosine, sine = jnp.cos(angle), jnp.sin(angle)
    normed, inverse_one = rms_stats(inputs, gain_attn)
    normed_low = normed.astype(bf16)
    proj = product(normed_low, full_qkv) + jnp.concatenate([bias_query, bias_key, bias_value])
    qw, kw = w_query.shape[1], w_key.shape[1]
    cos_heads, sin_heads = cosine[:, None, :], sine[:, None, :]
    queries = rotate(proj[:, :qw].reshape(t, HEADS, HD), cos_heads, sin_heads).astype(bf16)
    queries = (queries.astype(f32) * 0.125).astype(bf16).reshape(t, qw)
    key_rows = rotate(proj[:, qw : qw + kw].reshape(t, KVHEADS, HD), cos_heads, sin_heads).astype(bf16).reshape(t, kw)
    value_rows = proj[:, qw + kw :].astype(bf16)
    kx, vx, vz = pad_heads(key_rows, 0), pad_heads(value_rows, 1), pad_heads(value_rows, 0)
    mixed_low, inverse_sums, *probs = attend(doc_ids, queries, kx, vx)
    residual = inputs + product(mixed_low, full_output)
    normed_two, inverse_two = rms_stats(residual, gain_ffn)
    normed_two_low = normed_two.astype(bf16)
    n2_all = jnp.concatenate([normed_two_low, links.core(normed_two_low)], 0)

    hids, dgs, dus, wgus, wds, gate_up, downs = [], [], [], [], [], [], []
    for gus, ds in gathered_parts:
        hid, dg, du, keep_gu, send_gu, keep_d, send_d, wgu, wd = ffn_part(place, n2_all, dy_all, gus, ds)
        hids.append(hid), dgs.append(dg), dus.append(du), wgus.append(wgu), wds.append(wd)
        half_gu, other_gu = links.replica_sum(keep_gu + links.across(send_gu), 1)
        own_rows = jnp.where(c == y, half_gu, other_gu)
        send_rows = jnp.where(c == y, other_gu, half_gu)
        gate_up.append((own_rows, links.core(send_rows)))
        half_d, other_d = links.replica_sum(keep_d + links.across(send_d), 0)
        downs.append(links.in_order(half_d, other_d, 0))

    send_dn2 = back_tokens(dgs, dus, wgus, t, t, bf16)
    grad_normed_two = back_tokens(dgs, dus, wgus, 0, t, f32) + links.core(send_dn2).astype(f32)
    send_out = down_tokens(hids, wds, t, t, bf16)
    output = (residual + down_tokens(hids, wds, 0, t, f32) + links.core(send_out).astype(f32)).astype(bf16)

    upstream = cotangent.astype(f32)
    grad_from_two, grad_gain_ffn = norm_back(residual, inverse_two, gain_ffn, grad_normed_two)
    grad_residual = upstream + grad_from_two
    grad_attn_low = grad_residual.astype(bf16)

    def product_right_t(left, right):
        return lax.dot_general(left, right, (((1,), (1,)), ((), ())), preferred_element_type=f32)

    def product_left_t(left, right):
        return lax.dot_general(left, right, (((0,), (0,)), ((), ())), preferred_element_type=f32)

    def owned(full):
        quarters = full.reshape(2, 2, own, full.shape[1])
        pick = lambda v, n, axis: lax.dynamic_index_in_dim(v, n, axis, keepdims=False)
        pair = pick(quarters, c, 1) + links.core(pick(quarters, 1 - c, 1))
        rows = pick(pair, x, 0) + links.across(pick(pair, 1 - x, 0))
        return links.in_order(*links.replica_sum(rows, 0), 0).astype(f32)

    grad_w_output = owned(product_left_t(mixed_low, grad_attn_low).astype(bf16))
    grad_mixed = product_right_t(grad_attn_low, full_output).astype(bf16)
    scaled_mixed = (grad_mixed.astype(f32) * inverse_sums).astype(bf16)
    cos_lanes = jnp.tile(cosine, (1, 4))
    sin_lanes = jnp.tile(jnp.concatenate([-sine, sine], 1), (1, 2))
    d_query, d_key, d_value = attend_back(queries, scaled_mixed, mixed_low, kx, vz, cos_lanes, sin_lanes, probs)
    d_qkv = jnp.concatenate([d_query, d_key, d_value], 1)
    grad_qkv = owned(product_left_t(normed_low, d_qkv).astype(bf16))
    grad_biases = jnp.sum(d_qkv.astype(f32), axis=0)
    grad_normed = product_right_t(d_qkv, full_qkv)
    grad_from_one, grad_gain_attn = norm_back(inputs, inverse_one, gain_attn, grad_normed)
    grad_tokens = grad_residual + grad_from_one

    small = links.everywhere(jnp.concatenate([grad_gain_attn, grad_gain_ffn, grad_biases])[None, :])[0]

    def assembled(which):
        columns = []
        for s in range(4):
            side, core = s // 2, s % 2
            for (mine, other), w in zip(gate_up, widths):
                piece = jnp.where(c == core, mine[which], other[which])
                columns.append(piece[:, side * w : (side + 1) * w])
        return jnp.concatenate(columns, 1).astype(f32)

    return (
        output,
        grad_tokens,
        small[:d],
        small[d : 2 * d],
        grad_qkv[:, :qw],
        small[2 * d : 2 * d + qw],
        grad_qkv[:, qw : qw + kw],
        small[2 * d + qw : 2 * d + qw + kw],
        grad_qkv[:, qw + kw :],
        small[2 * d + qw + kw :],
        grad_w_output,
        assembled(0),
        assembled(1),
        jnp.concatenate(downs, 0).astype(f32),
    )


def solution(mesh):
    tokens, rows, whole = P(("shard", "replica"), None), P("shard", None), P()
    return jax.shard_map(
        functools.partial(on_device, (mesh.shape["shard"], mesh.shape["replica"])),
        mesh=mesh,
        in_specs=(tokens, tokens, tokens, whole, whole, rows, whole, rows, whole, rows, whole, rows, rows, rows, rows),
        out_specs=(tokens, tokens, whole, whole, rows, whole, rows, whole, rows, whole, rows, rows, rows, rows),
        check_vma=False,
    )
```

time: 1270 us -> 802 us (0.63)
  matrix products: 381 us -> 19.8 us
  waiting for transfers between devices: 562 us -> 267 us
  Pallas kernels: 0 us -> 220 us
  starting transfers between devices: 0.56 us -> 141 us
  local copies, waits for them, and re-layouts: 128 us -> 64.3 us
  blocking collectives: 53.8 us -> 0 us
  other arithmetic: 111 us -> 73.1 us
    ppermute x0 -> x118, waiting for transfers between devices: none -> 267 us  [the longest x35 105 us: beside(): lax.ppermute(v, 'replica', [(i, i ^ 1) for i in range(self.replicas)])]
    reduce_scatter x7 -> x0, waiting for transfers between devices: 263 us -> none  [the longest x1 76.4 us: on_device(): lax.psum_scatter(full_grads[5].astype(jnp.bfloat16), 'shard', scatter_dim...]
    psum x2 -> x0, waiting for transfers between devices: 246 us -> none  [the longest x1 246 us: on_device(): lax.psum(owned_rows[0].astype(jnp.bfloat16), 'replica').astype(jnp.float32)]
    pallas_call x0 -> x11, Pallas kernels: none -> 220 us  [the longest x5 101 us: ffn_part(): pl.pallas_call(functools.partial(ffn_kernel, steps), grid=(steps,), in_sp...]
    dot_general x14 -> x0, matrix products: 188 us -> none  [the longest x4 75.4 us: block_scores(): jnp.einsum('bkgd,rkd->kgbr', query_block, key_rows, preferred_element_typ...]
    ppermute x0 -> x118, starting transfers between devices: none -> 141 us  [the longest x13 46.3 us: line(): v = v + lax.ppermute(v, 'replica', [(0, 2), (1, 3), (6, 4), (7, 5)])]
    dynamic_update_slice x4 -> x0, local copies, waits for them, and re-layouts: 73.7 us -> none  [attention_backward(): lax.scan(one_block, (zero_rows, zero_rows), (starts, log_totals))]
    dot_general x7 -> x2, matrix products: 71.3 us -> 6.69 us  [product_right_t(): lax.dot_general(left, right, (((1,), (1,)), ((), ())), preferred_element_...]
  transfers between devices with their start and end apart: 14 -> 118, of which waited for: 8 -> 39; matrix products, arithmetic and copies ran while one was open for 20% -> 19% of each run, Pallas kernels for 0% -> 21%
where the time goes in v1:
time: 802 us; the launch traced here: 789 us
  waiting for transfers between devices  267 us (33%)
  Pallas kernels  220 us (27%)
  starting transfers between devices  141 us (18%)
  other arithmetic  73.1 us (9%)
  local copies, waits for them, and re-layouts  64.3 us (8%)
  matrix products  19.8 us (2%)
    ppermute x35, waiting for transfers between devices, beside(): lax.ppermute(v, 'replica', [(i, i ^ 1) for i in range(self.replicas)])  105 us
    pallas_call x5, Pallas kernels, ffn_part(): pl.pallas_call(functools.partial(ffn_kernel, steps), grid=(steps,), in_sp...  101 us
    ppermute x25, waiting for transfers between devices, across(): return lax.ppermute(v, 'shard', [(i, i ^ 2) for i in range(self.shards)])  84.9 us
    ppermute x13, waiting for transfers between devices, line(): ends = lax.ppermute(v, 'replica', [(2, 0), (3, 1), (4, 6), (5, 7)])  68.1 us
    ppermute x13, starting transfers between devices, line(): v = v + lax.ppermute(v, 'replica', [(0, 2), (1, 3), (6, 4), (7, 5)])  46.3 us
    ppermute x35, starting transfers between devices, beside(): lax.ppermute(v, 'replica', [(i, i ^ 1) for i in range(self.replicas)])  36 us
    pallas_call x2, Pallas kernels, back_tokens(): pl.pallas_call(functools.partial(tokens_sum_kernel, len(dgs)), grid=(rows...  35.9 us
    pallas_call x1, Pallas kernels, attend_back(): pl.pallas_call(functools.partial(attend_back_kernel, tiles), grid=(PAIRS,...  34.5 us
  transfers between devices with their start and end apart: 118, of which 39 were waited for; matrix products, arithmetic and copies ran while one was open for 19% of the time, Pallas kernels for 21%

profile of v1, /device:TPU:0, one launch (start us, length us, event | category | flops | bytes accessed | tf_op | source)
XLA Modules:
  0.0 789.0 jit_solution(10466126766652467336)
XLA Ops:
  43.5 4.3 fusion.46
  50.0 5.2 copy.39
  74.0 27.5 %attend.1 = (bf16[1024,896]{1,0:T(8,128)(2,1)}, f32[1024,896]{1,0:T(8,128)}, bf16[14,1024,256]{2,1,0:T(8,128)(2,1)}, bf16[14,768,256]{2,1,0:T(8,128)(2,1)}, bf16...) custom-call(s32[1024,1]{1,0:T(8,128)} %copy.44.segc, s32[1,1024]{1,0:T(1,128)} %segr.1, ...), custom_call_target="tpu_custom_call" | custom-call | flops 20000000000 | bytes 40000000 | tf_op jit(solution)/shard_map/attend/pallas_call | solution.py:56
  101.6 4.0 multiply_reduce_fusion.2
  123.4 8.4 %collective-permute-done.22.gu2 = bf16[2,224,512]{2,1,0:T(8,128)(2,1)S(1)} collective-permute-done((bf16[2,224,512]{2,1,0:T(8,128)(2,1)S(1)}, bf16[2,224,512]{2,1,0:T(8,128)(2,1)S(1)}, u32[]{:S(2)}, u32[]{:S(2)}) %collective-permute-start.22) | collective-permute-done | bytes 458784 | tf_op jit(solution)/shard_map/ppermute | solution.py:259
  139.8 4.2 pad_maximum_fusion.n2
  144.0 7.2 collective-permute-done.19.d1
  155.3 20.6 %ffn_part.8 = (bf16[2048,512]{1,0:T(8,128)(2,1)}, bf16[2048,512]{1,0:T(8,128)(2,1)}, bf16[2048,512]{1,0:T(8,128)(2,1)}, bf16[2,448,512]{2,1,0:T(8,128)(2,1)}, bf...) custom-call(s32[8]{0:T(128)} %stack.192.place, ...), custom_call_target="tpu_custom_call" | custom-call | flops 11274289152 | bytes 20000000 | tf_op jit(solution)/shard_map/ffn_part/pallas_call | solution.py:167
  181.3 20.7 %ffn_part.7 = (bf16[2048,512]{1,0:T(8,128)(2,1)}, bf16[2048,512]{1,0:T(8,128)(2,1)}, bf16[2048,512]{1,0:T(8,128)(2,1)}, bf16[2,448,512]{2,1,0:T(8,128)(2,1)}, bf...) custom-call(s32[8]{0:T(128)} %stack.192.place, ...), custom_call_target="tpu_custom_call" | custom-call | flops 11274289152 | bytes 20000000 | tf_op jit(solution)/shard_map/ffn_part/pallas_call | solution.py:167
  207.0 20.5 %ffn_part.6 = (bf16[2048,512]{1,0:T(8,128)(2,1)}, bf16[2048,512]{1,0:T(8,128)(2,1)}, bf16[2048,512]{1,0:T(8,128)(2,1)}, bf16[2,448,512]{2,1,0:T(8,128)(2,1)}, bf...) custom-call(s32[8]{0:T(128)} %stack.192.place, ...), custom_call_target="tpu_custom_call" | custom-call | flops 11274289152 | bytes 20000000 | tf_op jit(solution)/shard_map/ffn_part/pallas_call | solution.py:167
  228.3 18.4 %ffn_part.9 = (bf16[2048,384]{1,0:T(8,128)(2,1)}, bf16[2048,384]{1,0:T(8,128)(2,1)}, bf16[2048,384]{1,0:T(8,128)(2,1)}, bf16[2,448,384]{2,1,0:T(8,128)(2,1)}, bf...) custom-call(s32[8]{0:T(128)} %stack.192.place, ...), custom_call_target="tpu_custom_call" | custom-call | flops 8455716864 | bytes 20000000 | tf_op jit(solution)/shard_map/ffn_part/pallas_call | solution.py:167
  247.6 20.7 %ffn_part.5 = (bf16[2048,512]{1,0:T(8,128)(2,1)}, bf16[2048,512]{1,0:T(8,128)(2,1)}, bf16[2048,512]{1,0:T(8,128)(2,1)}, bf16[2,448,512]{2,1,0:T(8,128)(2,1)}, bf...) custom-call(s32[8]{0:T(128)} %stack.192.place, ...), custom_call_target="tpu_custom_call" | custom-call | flops 11274289152 | bytes 20000000 | tf_op jit(solution)/shard_map/ffn_part/pallas_call | solution.py:167
  268.3 17.7 %back_tokens.3 = bf16[1024,896]{1,0:T(8,128)(2,1)} custom-call(bf16[2048,512]{1,0:T(8,128)(2,1)} %get-tuple-element.79.refs_0_, bf16[2048,512]{1,0:T(8,128)(2,1)} %get-tuple-element.80.refs_1_, bf16[2,896,512]{2,1,0:T(8,128)(2,1)} %get-tuple-element.81.refs_2_, bf16[2048,512]{1,0:T(8,128)(2,1)} %get-tuple-element.82.refs_3_, ...), custom_call_target="tpu_custom_call" | custom-call | flops 8925478912 | bytes 30000000 | tf_op jit(solution)/shard_map/back_tokens/pallas_call | solution.py:190
  286.0 18.2 %back_tokens.2 = f32[1024,896]{1,0:T(8,128)} custom-call(bf16[2048,512]{1,0:T(8,128)(2,1)} %get-tuple-element.79.refs_0_, bf16[2048,512]{1,0:T(8,128)(2,1)} %get-tuple-element.80.refs_1_, bf16[2,896,512]{2,1,0:T(8,128)(2,1)} %get-tuple-element.81.refs_2_, bf16[2048,512]{1,0:T(8,128)(2,1)} %get-tuple-element.82.refs_3_, ...), custom_call_target="tpu_custom_call" | custom-call | flops 8925478912 | bytes 30000000 | tf_op jit(solution)/shard_map/back_tokens/pallas_call | solution.py:190
  309.3 10.4 %down_tokens.3 = bf16[1024,896]{1,0:T(8,128)(2,1)} custom-call(bf16[2048,512]{1,0:T(8,128)(2,1)} %get-tuple-element.69.refs_0_, bf16[512,896]{1,0:T(8,128)(2,1)} %get-tuple-element.70.refs_1_, bf16[2048,512]{1,0:T(8,128)(2,1)} %get-tuple-element.71.refs_2_, bf16[512,896]{1,0:T(8,128)(2,1)} %get-tuple-element.72.refs_3_, ...), custom_call_target="tpu_custom_call" | custom-call | flops 4462739456 | bytes 20000000 | tf_op jit(solution)/shard_map/down_tokens/pallas_call | solution.py:207
  319.7 10.4 %down_tokens.2 = f32[1024,896]{1,0:T(8,128)} custom-call(bf16[2048,512]{1,0:T(8,128)(2,1)} %get-tuple-element.69.refs_0_, bf16[512,896]{1,0:T(8,128)(2,1)} %get-tuple-element.70.refs_1_, bf16[2048,512]{1,0:T(8,128)(2,1)} %get-tuple-element.71.refs_2_, bf16[512,896]{1,0:T(8,128)(2,1)} %get-tuple-element.72.refs_3_, ...), custom_call_target="tpu_custom_call" | custom-call | flops 4462739456 | bytes 20000000 | tf_op jit(solution)/shard_map/down_tokens/pallas_call | solution.py:207
  331.4 8.6 %collective-permute-done.106 = bf16[256,896]{1,0:T(8,128)(2,1)S(1)} collective-permute-done((bf16[256,896]{1,0:T(8,128)(2,1)S(1)}, bf16[256,896]{1,0:T(8,128)(2,1)S(1)}, u32[]{:S(2)}, u32[]{:S(2)}) %collective-permute-start.106) | collective-permute-done | bytes 458784 | tf_op jit(solution)/shard_map/ppermute | solution.py:259
  341.3 8.6 %collective-permute-done.100 = bf16[256,896]{1,0:T(8,128)(2,1)S(1)} collective-permute-done((bf16[256,896]{1,0:T(8,128)(2,1)S(1)}, bf16[256,896]{1,0:T(8,128)(2,1)S(1)}, u32[]{:S(2)}, u32[]{:S(2)}) %collective-permute-start.100) | collective-permute-done | bytes 458784 | tf_op jit(solution)/shard_map/ppermute | solution.py:259
  351.0 8.7 %collective-permute-done.94 = bf16[256,896]{1,0:T(8,128)(2,1)S(1)} collective-permute-done((bf16[256,896]{1,0:T(8,128)(2,1)S(1)}, bf16[256,896]{1,0:T(8,128)(2,1)S(1)}, u32[]{:S(2)}, u32[]{:S(2)}) %collective-permute-start.94) | collective-permute-done | bytes 458784 | tf_op jit(solution)/shard_map/ppermute | solution.py:259
  364.6 40.6 %collective-permute-done.88 = bf16[256,896]{1,0:T(8,128)(2,1)S(1)} collective-permute-done((bf16[256,896]{1,0:T(8,128)(2,1)S(1)}, bf16[256,896]{1,0:T(8,128)(2,1)S(1)}, u32[]{:S(2)}, u32[]{:S(2)}) %collective-permute-start.88) | collective-permute-done | bytes 458784 | tf_op jit(solution)/shard_map/ppermute | solution.py:259
  413.0 5.1 collective-permute-done.101
  419.0 5.0 collective-permute-done.95
  425.0 5.3 collective-permute-done.89
  432.1 9.9 %collective-permute-start.108 = (bf16[128,896]{1,0:T(8,128)(2,1)S(1)}, bf16[128,896]{1,0:T(8,128)(2,1)S(1)}, u32[]{:S(2)}, u32[]{:S(2)}) collective-permute-start(bf16[128,896]{1,0:T(8,128)(2,1)S(1)} %dynamic-slice_add_fusion.6), channel_id=1, source_target_pairs={{0,2},{1,3},{6,4},{7,5},{8,10},{9,11},{14,12},{15,13},{16,18},{17,... | collective-permute-start | bytes 688136 | tf_op jit(solution)/shard_map/ppermute | solution.py:266
  453.5 8.1 %collective-permute-start.83 = (bf16[2,224,384]{2,1,0:T(8,128)(2,1)S(1)}, bf16[2,224,384]{2,1,0:T(8,128)(2,1)S(1)}, u32[]{:S(2)}, u32[]{:S(2)}) collective-permute-start(bf16[2,224,384]{2,1,0:T(8,128)(2,1)S(1)} %dynamic-slice_add_fusion.4), channel_id=1, source_target_pairs={{0,2},{1,3},{6,4},{7,5},{8,10},{9,11},{14,12},{15,13},{16,18},{17,... | collective-permute-start | bytes 1032200 | tf_op jit(solution)/shard_map/ppermute | solution.py:266
  468.6 4.3 collective-permute-done.68
  473.3 9.4 %collective-permute-done.61 = bf16[2,224,512]{2,1,0:T(8,128)(2,1)S(1)} collective-permute-done((bf16[2,224,512]{2,1,0:T(8,128)(2,1)S(1)}, bf16[2,224,512]{2,1,0:T(8,128)(2,1)S(1)}, u32[]{:S(2)}, u32[]{:S(2)}) %collective-permute-start.61) | collective-permute-done | bytes 458784 | tf_op jit(solution)/shard_map/ppermute | solution.py:262
  484.2 7.6 collective-permute-done.54
  497.2 9.9 %collective-permute-done.104 = bf16[128,896]{1,0:T(8,128)(2,1)S(1)} collective-permute-done((bf16[128,896]{1,0:T(8,128)(2,1)S(1)}, bf16[128,896]{1,0:T(8,128)(2,1)S(1)}, u32[]{:S(2)}, u32[]{:S(2)}) %collective-permute-start.104) | collective-permute-done | bytes 229408 | tf_op jit(solution)/shard_map/ppermute | solution.py:268
  508.5 7.1 collective-permute-done.92
  517.2 5.6 collective-permute-done.93
  523.7 6.6 collective-permute-done.99
  531.2 7.4 collective-permute-done.105
  539.5 5.1 collective-permute-done.111
  544.6 5.1 collective-permute-start.76
  566.9 34.5 %attend_back.1 = (bf16[1024,896]{1,0:T(8,128)(2,1)}, bf16[1024,128]{1,0:T(8,128)(2,1)}, bf16[1024,128]{1,0:T(8,128)(2,1)}) custom-call(bf16[1024,896]{1,0:T(8,128)(2,1)} %copy.45.q, bf16[1024,896]{1,0:T(8,128)(2,1)} %multiply_convert_fusion.do, bf16[1024,896]{1,0:T(8,128)(2,1)} %get-tuple-element.68.o, bf16[4,1024,128]{2,1,0:T(8,128)(2,1)} %pad_maximum_fusion.3.kx, ...), custom_call_target="tpu_custom_call" | custom-call | flops 30000001024 | bytes 40000000 | tf_op jit(solution)/shard_map/attend_back/pallas_call | solution.py:108
  633.8 14.6 %collective-permute-done.38 = f32[1,2944]{1,0:T(1,128)S(1)} collective-permute-done((f32[1,2944]{1,0:T(1,128)S(1)}, f32[1,2944]{1,0:T(1,128)S(1)}, u32[]{:S(2)}, u32[]{:S(2)}) %collective-permute-start.38) | collective-permute-done | bytes 11808 | tf_op jit(solution)/shard_map/ppermute | solution.py:268
  653.8 5.1 collective-permute-done.86
  664.0 7.2 collective-permute-done.78
  672.4 9.9 %collective-permute-done.71 = bf16[2,224,512]{2,1,0:T(8,128)(2,1)S(1)} collective-permute-done((bf16[2,224,512]{2,1,0:T(8,128)(2,1)S(1)}, bf16[2,224,512]{2,1,0:T(8,128)(2,1)S(1)}, u32[]{:S(2)}, u32[]{:S(2)}) %collective-permute-start.71) | collective-permute-done | bytes 458784 | tf_op jit(solution)/shard_map/ppermute | solution.py:268
  683.5 8.5 %collective-permute-done.64 = bf16[2,224,512]{2,1,0:T(8,128)(2,1)S(1)} collective-permute-done((bf16[2,224,512]{2,1,0:T(8,128)(2,1)S(1)}, bf16[2,224,512]{2,1,0:T(8,128)(2,1)S(1)}, u32[]{:S(2)}, u32[]{:S(2)}) %collective-permute-start.64) | collective-permute-done | bytes 458784 | tf_op jit(solution)/shard_map/ppermute | solution.py:268
  693.3 6.3 collective-permute-done.57
  704.3 8.8 %collective-permute-done.65 = bf16[2,224,512]{2,1,0:T(8,128)(2,1)S(1)} collective-permute-done((bf16[2,224,512]{2,1,0:T(8,128)(2,1)S(1)}, bf16[2,224,512]{2,1,0:T(8,128)(2,1)S(1)}, u32[]{:S(2)}, u32[]{:S(2)}) %collective-permute-start.65) | collective-permute-done | bytes 458784 | tf_op jit(solution)/shard_map/ppermute | solution.py:262
  713.2 11.3 %collective-permute-done.48 = bf16[112,896]{1,0:T(8,128)(2,1)S(1)} collective-permute-done((bf16[112,896]{1,0:T(8,128)(2,1)S(1)}, bf16[112,896]{1,0:T(8,128)(2,1)S(1)}, u32[]{:S(2)}, u32[]{:S(2)}) %collective-permute-start.48) | collective-permute-done | bytes 200736 | tf_op jit(solution)/shard_map/ppermute | solution.py:262
  726.2 4.9 collective-permute-done.49
  733.2 5.7 collective-permute-done.41
  740.3 6.8 collective-permute-start.42
  777.3 4.7 collective-permute-done.52
  (746 shorter events, 270.1 us)
Async XLA Ops:
  2.5 173.5 %collective-permute-start.29 = (bf16[96,896]{1,0:T(8,128)(2,1)}, bf16[96,896]{1,0:T(8,128)(2,1)}, u32[]{:S(2)}, u32[]{:S(2)}) collective-permute-start(bf16[96,896]{1,0:T(8,128)(2,1)} %constant_dynamic-slice_fusion.12), channel_id=1, source_target_pairs={{0,16},{8,24},{16,0},{24,8},{1,17},{9,25},{17,1},{25,9},{2,18},{10... | collective-permute-start | bytes 516104 | tf_op jit(solution)/shard_map/ppermute | solution.py:259
  9.2 102.7 %collective-permute-start.26 = (bf16[2,224,384]{2,1,0:T(8,128)(2,1)}, bf16[2,224,384]{2,1,0:T(8,128)(2,1)}, u32[]{:S(2)}, u32[]{:S(2)}) collective-permute-start(bf16[2,224,384]{2,1,0:T(8,128)(2,1)} %broadcast_select_fusion.36), channel_id=1, source_target_pairs={{0,8},{8,0},{16,24},{24,16},{1,9},{9,1},{17,25},{25,17},{2,10},{10... | collective-permute-start | bytes 1032200 | tf_op jit(solution)/shard_map/ppermute | solution.py:256
  15.9 98.7 %collective-permute-start.6 = (bf16[2,224,512]{2,1,0:T(8,128)(2,1)}, bf16[2,224,512]{2,1,0:T(8,128)(2,1)}, u32[]{:S(2)}, u32[]{:S(2)}) collective-permute-start(bf16[2,224,512]{2,1,0:T(8,128)(2,1)} %broadcast_select_fusion.26), channel_id=1, source_target_pairs={{0,8},{8,0},{16,24},{24,16},{1,9},{9,1},{17,25},{25,17},{2,10},{10... | collective-permute-start | bytes 1376264 | tf_op jit(solution)/shard_map/ppermute | solution.py:256
  38.9 93.9 %collective-permute-start.5 = (bf16[1024,896]{1,0:T(8,128)(2,1)S(1)}, bf16[1024,896]{1,0:T(8,128)(2,1)}, u32[]{:S(2)}, u32[]{:S(2)}) collective-permute-start(bf16[1024,896]{1,0:T(8,128)(2,1)S(1)} %copy-done.4), channel_id=1, source_target_pairs={{0,8},{8,0},{16,24},{24,16},{1,9},{9,1},{17,25},{25,17},{2,10},{10... | collective-permute-start | bytes 5505032 | tf_op jit(solution)/shard_map/ppermute | solution.py:256
  108.0 29.8 %collective-permute-start.4 = (bf16[1024,896]{1,0:T(8,128)(2,1)}, bf16[1024,896]{1,0:T(8,128)(2,1)}, u32[]{:S(2)}, u32[]{:S(2)}) collective-permute-start(bf16[1024,896]{1,0:T(8,128)(2,1)} %multiply_convert_fusion.1), channel_id=1, source_target_pairs={{0,8},{8,0},{16,24},{24,16},{1,9},{9,1},{17,25},{25,17},{2,10},{10... | collective-permute-start | bytes 5505032 | tf_op jit(solution)/shard_map/ppermute | solution.py:256
  151.2 25.9 %collective-permute-start.14 = (bf16[128,896]{1,0:T(8,128)(2,1)S(1)}, bf16[128,896]{1,0:T(8,128)(2,1)S(1)}, u32[]{:S(2)}, u32[]{:S(2)}) collective-permute-start(bf16[128,896]{1,0:T(8,128)(2,1)S(1)} %copy-done.103), channel_id=1, source_target_pairs={{0,16},{8,24},{16,0},{24,8},{1,17},{9,25},{17,1},{25,9},{2,18},{10... | collective-permute-start | bytes 688136 | tf_op jit(solution)/shard_map/ppermute | solution.py:259
  152.3 25.9 %collective-permute-start.20 = (bf16[128,896]{1,0:T(8,128)(2,1)S(1)}, bf16[128,896]{1,0:T(8,128)(2,1)S(1)}, u32[]{:S(2)}, u32[]{:S(2)}) collective-permute-start(bf16[128,896]{1,0:T(8,128)(2,1)S(1)} %collective-permute-done.19.d1), channel_id=1, source_target_pairs={{0,1},{1,0},{2,3},{3,2},{4,5},{5,4},{6,7},{7,6},{8,9},{9,8},{10,11... | collective-permute-start | bytes 688136 | tf_op jit(solution)/shard_map/ppermute | solution.py:262
  153.4 25.9 %collective-permute-start.12 = (bf16[2,224,512]{2,1,0:T(8,128)(2,1)S(1)}, bf16[2,224,512]{2,1,0:T(8,128)(2,1)S(1)}, u32[]{:S(2)}, u32[]{:S(2)}) collective-permute-start(bf16[2,224,512]{2,1,0:T(8,128)(2,1)S(1)} %get-tuple-element.135), channel_id=1, source_target_pairs={{0,16},{8,24},{16,0},{24,8},{1,17},{9,25},{17,1},{25,9},{2,18},{10... | collective-permute-start | bytes 1376264 | tf_op jit(solution)/shard_map/ppermute | solution.py:259
  154.4 26.0 %collective-permute-start.18 = (bf16[2,224,512]{2,1,0:T(8,128)(2,1)S(1)}, bf16[2,224,512]{2,1,0:T(8,128)(2,1)S(1)}, u32[]{:S(2)}, u32[]{:S(2)}) collective-permute-start(bf16[2,224,512]{2,1,0:T(8,128)(2,1)S(1)} %collective-permute-done.17.gu2), channel_id=1, source_target_pairs={{0,1},{1,0},{2,3},{3,2},{4,5},{5,4},{6,7},{7,6},{8,9},{9,8},{10,11... | collective-permute-start | bytes 1376264 | tf_op jit(solution)/shard_map/ppermute | solution.py:262
  176.0 26.0 %collective-permute-start.9 = (bf16[128,896]{1,0:T(8,128)(2,1)S(1)}, bf16[128,896]{1,0:T(8,128)(2,1)S(1)}, u32[]{:S(2)}, u32[]{:S(2)}) collective-permute-start(bf16[128,896]{1,0:T(8,128)(2,1)S(1)} %copy-done.106), channel_id=1, source_target_pairs={{0,16},{8,24},{16,0},{24,8},{1,17},{9,25},{17,1},{25,9},{2,18},{10... | collective-permute-start | bytes 688136 | tf_op jit(solution)/shard_map/ppermute | solution.py:259
  177.1 26.1 %collective-permute-start.15 = (bf16[128,896]{1,0:T(8,128)(2,1)S(1)}, bf16[128,896]{1,0:T(8,128)(2,1)S(1)}, u32[]{:S(2)}, u32[]{:S(2)}) collective-permute-start(bf16[128,896]{1,0:T(8,128)(2,1)S(1)} %collective-permute-done.14.d1), channel_id=1, source_target_pairs={{0,1},{1,0},{2,3},{3,2},{4,5},{5,4},{6,7},{7,6},{8,9},{9,8},{10,11... | collective-permute-start | bytes 688136 | tf_op jit(solution)/shard_map/ppermute | solution.py:262
  178.2 25.9 %collective-permute-start.27 = (bf16[2,224,384]{2,1,0:T(8,128)(2,1)S(1)}, bf16[2,224,384]{2,1,0:T(8,128)(2,1)S(1)}, u32[]{:S(2)}, u32[]{:S(2)}) collective-permute-start(bf16[2,224,384]{2,1,0:T(8,128)(2,1)S(1)} %copy-done.99), channel_id=1, source_target_pairs={{0,16},{8,24},{16,0},{24,8},{1,17},{9,25},{17,1},{25,9},{2,18},{10... | collective-permute-start | bytes 1032200 | tf_op jit(solution)/shard_map/ppermute | solution.py:259
  179.3 26.0 %collective-permute-start.7 = (bf16[2,224,512]{2,1,0:T(8,128)(2,1)S(1)}, bf16[2,224,512]{2,1,0:T(8,128)(2,1)S(1)}, u32[]{:S(2)}, u32[]{:S(2)}) collective-permute-start(bf16[2,224,512]{2,1,0:T(8,128)(2,1)S(1)} %copy-done.84), channel_id=1, source_target_pairs={{0,16},{8,24},{16,0},{24,8},{1,17},{9,25},{17,1},{25,9},{2,18},{10... | collective-permute-start | bytes 1376264 | tf_op jit(solution)/shard_map/ppermute | solution.py:259
  180.4 25.8 %collective-permute-start.13 = (bf16[2,224,512]{2,1,0:T(8,128)(2,1)S(1)}, bf16[2,224,512]{2,1,0:T(8,128)(2,1)S(1)}, u32[]{:S(2)}, u32[]{:S(2)}) collective-permute-start(bf16[2,224,512]{2,1,0:T(8,128)(2,1)S(1)} %collective-permute-done.12.gu2), channel_id=1, source_target_pairs={{0,1},{1,0},{2,3},{3,2},{4,5},{5,4},{6,7},{7,6},{8,9},{9,8},{10,11... | collective-permute-start | bytes 1376264 | tf_op jit(solution)/shard_map/ppermute | solution.py:262
  202.0 25.5 %collective-permute-start.30 = (bf16[96,896]{1,0:T(8,128)(2,1)}, bf16[96,896]{1,0:T(8,128)(2,1)S(1)}, u32[]{:S(2)}, u32[]{:S(2)}) collective-permute-start(bf16[96,896]{1,0:T(8,128)(2,1)} %collective-permute-done.29.d1), channel_id=1, source_target_pairs={{0,1},{1,0},{2,3},{3,2},{4,5},{5,4},{6,7},{7,6},{8,9},{9,8},{10,11... | collective-permute-start | bytes 516104 | tf_op jit(solution)/shard_map/ppermute | solution.py:262
  203.2 43.5 %collective-permute-start.10 = (bf16[128,896]{1,0:T(8,128)(2,1)S(1)}, bf16[128,896]{1,0:T(8,128)(2,1)S(1)}, u32[]{:S(2)}, u32[]{:S(2)}) collective-permute-start(bf16[128,896]{1,0:T(8,128)(2,1)S(1)} %collective-permute-done.9.d1), channel_id=1, source_target_pairs={{0,1},{1,0},{2,3},{3,2},{4,5},{5,4},{6,7},{7,6},{8,9},{9,8},{10,11... | collective-permute-start | bytes 688136 | tf_op jit(solution)/shard_map/ppermute | solution.py:262
  205.3 41.5 %collective-permute-start.8 = (bf16[2,224,512]{2,1,0:T(8,128)(2,1)S(1)}, bf16[2,224,512]{2,1,0:T(8,128)(2,1)S(1)}, u32[]{:S(2)}, u32[]{:S(2)}) collective-permute-start(bf16[2,224,512]{2,1,0:T(8,128)(2,1)S(1)} %collective-permute-done.7.gu2), channel_id=1, source_target_pairs={{0,1},{1,0},{2,3},{3,2},{4,5},{5,4},{6,7},{7,6},{8,9},{9,8},{10,11... | collective-permute-start | bytes 1376264 | tf_op jit(solution)/shard_map/ppermute | solution.py:262
  304.2 26.0 %collective-permute-start.112 = (bf16[192,896]{1,0:T(8,128)(2,1)}, bf16[192,896]{1,0:T(8,128)(2,1)S(1)}, u32[]{:S(2)}, u32[]{:S(2)}) collective-permute-start(bf16[192,896]{1,0:T(8,128)(2,1)} %get-tuple-element.121), channel_id=1, source_target_pairs={{0,16},{8,24},{16,0},{24,8},{1,17},{9,25},{17,1},{25,9},{2,18},{10... | collective-permute-start | bytes 1032200 | tf_op jit(solution)/shard_map/ppermute | solution.py:259
  305.2 102.1 %collective-permute-start.81 = (bf16[2,448,384]{2,1,0:T(8,128)(2,1)S(1)}, bf16[2,448,384]{2,1,0:T(8,128)(2,1)S(1)}, u32[]{:S(2)}, u32[]{:S(2)}) collective-permute-start(bf16[2,448,384]{2,1,0:T(8,128)(2,1)S(1)} %copy-done.131), channel_id=1, source_target_pairs={{0,16},{8,24},{16,0},{24,8},{1,17},{9,25},{17,1},{25,9},{2,18},{10... | collective-permute-start | bytes 2064392 | tf_op jit(solution)/shard_map/ppermute | solution.py:259
  306.3 33.8 %collective-permute-start.106 = (bf16[256,896]{1,0:T(8,128)(2,1)S(1)}, bf16[256,896]{1,0:T(8,128)(2,1)S(1)}, u32[]{:S(2)}, u32[]{:S(2)}) collective-permute-start(bf16[256,896]{1,0:T(8,128)(2,1)S(1)} %copy-done.132), channel_id=1, source_target_pairs={{0,16},{8,24},{16,0},{24,8},{1,17},{9,25},{17,1},{25,9},{2,18},{10... | collective-permute-start | bytes 1376264 | tf_op jit(solution)/shard_map/ppermute | solution.py:259
  307.3 42.6 %collective-permute-start.100 = (bf16[256,896]{1,0:T(8,128)(2,1)S(1)}, bf16[256,896]{1,0:T(8,128)(2,1)S(1)}, u32[]{:S(2)}, u32[]{:S(2)}) collective-permute-start(bf16[256,896]{1,0:T(8,128)(2,1)S(1)} %copy-done.133), channel_id=1, source_target_pairs={{0,16},{8,24},{16,0},{24,8},{1,17},{9,25},{17,1},{25,9},{2,18},{10... | collective-permute-start | bytes 1376264 | tf_op jit(solution)/shard_map/ppermute | solution.py:259
  308.3 51.4 %collective-permute-start.94 = (bf16[256,896]{1,0:T(8,128)(2,1)S(1)}, bf16[256,896]{1,0:T(8,128)(2,1)S(1)}, u32[]{:S(2)}, u32[]{:S(2)}) collective-permute-start(bf16[256,896]{1,0:T(8,128)(2,1)S(1)} %copy-done.134), channel_id=1, source_target_pairs={{0,16},{8,24},{16,0},{24,8},{1,17},{9,25},{17,1},{25,9},{2,18},{10... | collective-permute-start | bytes 1376264 | tf_op jit(solution)/shard_map/ppermute | solution.py:259
  330.2 101.9 %collective-permute-start.74 = (bf16[2,448,512]{2,1,0:T(8,128)(2,1)S(1)}, bf16[2,448,512]{2,1,0:T(8,128)(2,1)S(1)}, u32[]{:S(2)}, u32[]{:S(2)}) collective-permute-start(bf16[2,448,512]{2,1,0:T(8,128)(2,1)S(1)} %copy-done.127), channel_id=1, source_target_pairs={{0,16},{8,24},{16,0},{24,8},{1,17},{9,25},{17,1},{25,9},{2,18},{10... | collective-permute-start | bytes 2752520 | tf_op jit(solution)/shard_map/ppermute | solution.py:259
  349.9 92.4 %collective-permute-start.67 = (bf16[2,448,512]{2,1,0:T(8,128)(2,1)S(1)}, bf16[2,448,512]{2,1,0:T(8,128)(2,1)S(1)}, u32[]{:S(2)}, u32[]{:S(2)}) collective-permute-start(bf16[2,448,512]{2,1,0:T(8,128)(2,1)S(1)} %copy-done.128), channel_id=1, source_target_pairs={{0,16},{8,24},{16,0},{24,8},{1,17},{9,25},{17,1},{25,9},{2,18},{10... | collective-permute-start | bytes 2752520 | tf_op jit(solution)/shard_map/ppermute | solution.py:259
  359.7 45.5 %collective-permute-start.88 = (bf16[256,896]{1,0:T(8,128)(2,1)S(1)}, bf16[256,896]{1,0:T(8,128)(2,1)S(1)}, u32[]{:S(2)}, u32[]{:S(2)}) collective-permute-start(bf16[256,896]{1,0:T(8,128)(2,1)S(1)} %copy-done.138), channel_id=1, source_target_pairs={{0,16},{8,24},{16,0},{24,8},{1,17},{9,25},{17,1},{25,9},{2,18},{10... | collective-permute-start | bytes 1376264 | tf_op jit(solution)/shard_map/ppermute | solution.py:259
  360.9 45.3 %collective-permute-start.114 = (bf16[96,896]{1,0:T(8,128)(2,1)S(1)}, bf16[96,896]{1,0:T(8,128)(2,1)S(1)}, u32[]{:S(2)}, u32[]{:S(2)}) collective-permute-start(bf16[96,896]{1,0:T(8,128)(2,1)S(1)} %dynamic-slice_add_fusion.11), channel_id=1, source_target_pairs={{0,2},{1,3},{6,4},{7,5},{8,10},{9,11},{14,12},{15,13},{16,18},{17,... | collective-permute-start | bytes 516104 | tf_op jit(solution)/shard_map/ppermute | solution.py:266
  406.3 37.6 %collective-permute-start.60 = (bf16[2,448,512]{2,1,0:T(8,128)(2,1)S(1)}, bf16[2,448,512]{2,1,0:T(8,128)(2,1)S(1)}, u32[]{:S(2)}, u32[]{:S(2)}) collective-permute-start(bf16[2,448,512]{2,1,0:T(8,128)(2,1)S(1)} %copy-done.129), channel_id=1, source_target_pairs={{0,16},{8,24},{16,0},{24,8},{1,17},{9,25},{17,1},{25,9},{2,18},{10... | collective-permute-start | bytes 2752520 | tf_op jit(solution)/shard_map/ppermute | solution.py:259
  407.4 38.1 %collective-permute-start.53 = (bf16[2,448,512]{2,1,0:T(8,128)(2,1)S(1)}, bf16[2,448,512]{2,1,0:T(8,128)(2,1)S(1)}, u32[]{:S(2)}, u32[]{:S(2)}) collective-permute-start(bf16[2,448,512]{2,1,0:T(8,128)(2,1)S(1)} %copy-done.130), channel_id=1, source_target_pairs={{0,16},{8,24},{16,0},{24,8},{1,17},{9,25},{17,1},{25,9},{2,18},{10... | collective-permute-start | bytes 2752520 | tf_op jit(solution)/shard_map/ppermute | solution.py:259
  464.2 92.2 %collective-permute-start.32 = (bf16[1024,896]{1,0:T(8,128)(2,1)S(1)}, bf16[1024,896]{1,0:T(8,128)(2,1)S(1)}, u32[]{:S(2)}, u32[]{:S(2)}) collective-permute-start(bf16[1024,896]{1,0:T(8,128)(2,1)S(1)} %copy-done.125), channel_id=1, source_target_pairs={{0,8},{8,0},{16,24},{24,16},{1,9},{9,1},{17,25},{25,17},{2,10},{10... | collective-permute-start | bytes 5505032 | tf_op jit(solution)/shard_map/ppermute | solution.py:256
  464.3 96.1 %collective-permute-start.31 = (bf16[1024,896]{1,0:T(8,128)(2,1)S(1)}, bf16[1024,896]{1,0:T(8,128)(2,1)S(1)}, u32[]{:S(2)}, u32[]{:S(2)}) collective-permute-start(bf16[1024,896]{1,0:T(8,128)(2,1)S(1)} %copy-done.126), channel_id=1, source_target_pairs={{0,8},{8,0},{16,24},{24,16},{1,9},{9,1},{17,25},{25,17},{2,10},{10... | collective-permute-start | bytes 5505032 | tf_op jit(solution)/shard_map/ppermute | solution.py:256
  467.2 24.6 %collective-permute-start.54 = (bf16[2,224,512]{2,1,0:T(8,128)(2,1)S(1)}, bf16[2,224,512]{2,1,0:T(8,128)(2,1)S(1)}, u32[]{:S(2)}, u32[]{:S(2)}) collective-permute-start(bf16[2,224,512]{2,1,0:T(8,128)(2,1)S(1)} %constant_dynamic-slice_fusion.9), channel_id=1, source_target_pairs={{0,1},{1,0},{2,3},{3,2},{4,5},{5,4},{6,7},{7,6},{8,9},{9,8},{10,11... | collective-permute-start | bytes 1376264 | tf_op jit(solution)/shard_map/ppermute | solution.py:262
  472.9 77.0 %collective-permute-start.117 = (bf16[96,896]{1,0:T(8,128)(2,1)S(1)}, bf16[96,896]{1,0:T(8,128)(2,1)S(1)}, u32[]{:S(2)}, u32[]{:S(2)}) collective-permute-start(bf16[96,896]{1,0:T(8,128)(2,1)S(1)} %broadcast_select_fusion.49), channel_id=1, source_target_pairs={{0,1},{1,0},{2,3},{3,2},{4,5},{5,4},{6,7},{7,6},{8,9},{9,8},{10,11... | collective-permute-start | bytes 516104 | tf_op jit(solution)/shard_map/ppermute | solution.py:262
  515.6 38.3 %collective-permute-start.84 = (bf16[2,224,384]{2,1,0:T(8,128)(2,1)S(1)}, bf16[2,224,384]{2,1,0:T(8,128)(2,1)S(1)}, u32[]{:S(2)}, u32[]{:S(2)}) collective-permute-start(bf16[2,224,384]{2,1,0:T(8,128)(2,1)S(1)} %add.388), channel_id=1, source_target_pairs={{2,4},{4,2},{3,5},{5,3},{10,12},{12,10},{11,13},{13,11},{18,20},{2... | collective-permute-start | bytes 1032200 | tf_op jit(solution)/shard_map/ppermute | solution.py:267
  544.6 77.5 %collective-permute-start.76 = (bf16[2,224,512]{2,1,0:T(8,128)(2,1)S(1)}, bf16[2,224,512]{2,1,0:T(8,128)(2,1)}, u32[]{:S(2)}, u32[]{:S(2)}) collective-permute-start(bf16[2,224,512]{2,1,0:T(8,128)(2,1)S(1)} %dynamic-slice_add_fusion), channel_id=1, source_target_pairs={{0,2},{1,3},{6,4},{7,5},{8,10},{9,11},{14,12},{15,13},{16,18},{17,... | collective-permute-start | bytes 1376264 | tf_op jit(solution)/shard_map/ppermute | solution.py:266
  549.9 75.5 %collective-permute-start.69 = (bf16[2,224,512]{2,1,0:T(8,128)(2,1)S(1)}, bf16[2,224,512]{2,1,0:T(8,128)(2,1)S(1)}, u32[]{:S(2)}, u32[]{:S(2)}) collective-permute-start(bf16[2,224,512]{2,1,0:T(8,128)(2,1)S(1)} %dynamic-slice_add_fusion.1), channel_id=1, source_target_pairs={{0,2},{1,3},{6,4},{7,5},{8,10},{9,11},{14,12},{15,13},{16,18},{17,... | collective-permute-start | bytes 1376264 | tf_op jit(solution)/shard_map/ppermute | solution.py:266
  553.9 72.4 %collective-permute-start.62 = (bf16[2,224,512]{2,1,0:T(8,128)(2,1)S(1)}, bf16[2,224,512]{2,1,0:T(8,128)(2,1)}, u32[]{:S(2)}, u32[]{:S(2)}) collective-permute-start(bf16[2,224,512]{2,1,0:T(8,128)(2,1)S(1)} %dynamic-slice_add_fusion.2), channel_id=1, source_target_pairs={{0,2},{1,3},{6,4},{7,5},{8,10},{9,11},{14,12},{15,13},{16,18},{17,... | collective-permute-start | bytes 1376264 | tf_op jit(solution)/shard_map/ppermute | solution.py:266
  556.3 71.8 %collective-permute-start.55 = (bf16[2,224,512]{2,1,0:T(8,128)(2,1)S(1)}, bf16[2,224,512]{2,1,0:T(8,128)(2,1)}, u32[]{:S(2)}, u32[]{:S(2)}) collective-permute-start(bf16[2,224,512]{2,1,0:T(8,128)(2,1)S(1)} %dynamic-slice_add_fusion.3), channel_id=1, source_target_pairs={{0,2},{1,3},{6,4},{7,5},{8,10},{9,11},{14,12},{15,13},{16,18},{17,... | collective-permute-start | bytes 1376264 | tf_op jit(solution)/shard_map/ppermute | solution.py:266
  626.2 24.2 %collective-permute-start.70 = (bf16[2,224,512]{2,1,0:T(8,128)(2,1)S(1)}, bf16[2,224,512]{2,1,0:T(8,128)(2,1)S(1)}, u32[]{:S(2)}, u32[]{:S(2)}) collective-permute-start(bf16[2,224,512]{2,1,0:T(8,128)(2,1)S(1)} %add.380), channel_id=1, source_target_pairs={{2,4},{4,2},{3,5},{5,3},{10,12},{12,10},{11,13},{13,11},{18,20},{2... | collective-permute-start | bytes 1376264 | tf_op jit(solution)/shard_map/ppermute | solution.py:267
  650.5 50.0 %collective-permute-start.39 = (bf16[2,224,1152]{2,1,0:T(8,128)(2,1)S(1)}, bf16[2,224,1152]{2,1,0:T(8,128)(2,1)S(1)}, u32[]{:S(2)}, u32[]{:S(2)}) collective-permute-start(bf16[2,224,1152]{2,1,0:T(8,128)(2,1)S(1)} %dynamic-slice_bitcast_fusion), channel_id=1, source_target_pairs={{0,8},{8,0},{16,24},{24,16},{1,9},{9,1},{17,25},{25,17},{2,10},{10... | collective-permute-start | bytes 3096584 | tf_op jit(solution)/shard_map/ppermute | solution.py:256
  652.3 29.9 %collective-permute-start.71 = (bf16[2,224,512]{2,1,0:T(8,128)(2,1)S(1)}, bf16[2,224,512]{2,1,0:T(8,128)(2,1)S(1)}, u32[]{:S(2)}, u32[]{:S(2)}) collective-permute-start(bf16[2,224,512]{2,1,0:T(8,128)(2,1)S(1)} %add.381), channel_id=1, source_target_pairs={{2,0},{3,1},{4,6},{5,7},{10,8},{11,9},{12,14},{13,15},{18,16},{19,... | collective-permute-start | bytes 1376264 | tf_op jit(solution)/shard_map/ppermute | solution.py:268
  658.9 33.2 %collective-permute-start.64 = (bf16[2,224,512]{2,1,0:T(8,128)(2,1)S(1)}, bf16[2,224,512]{2,1,0:T(8,128)(2,1)S(1)}, u32[]{:S(2)}, u32[]{:S(2)}) collective-permute-start(bf16[2,224,512]{2,1,0:T(8,128)(2,1)S(1)} %add.377), channel_id=1, source_target_pairs={{2,0},{3,1},{4,6},{5,7},{10,8},{11,9},{12,14},{13,15},{18,16},{19,... | collective-permute-start | bytes 1376264 | tf_op jit(solution)/shard_map/ppermute | solution.py:268
  662.0 37.7 %collective-permute-start.57 = (bf16[2,224,512]{2,1,0:T(8,128)(2,1)S(1)}, bf16[2,224,512]{2,1,0:T(8,128)(2,1)S(1)}, u32[]{:S(2)}, u32[]{:S(2)}) collective-permute-start(bf16[2,224,512]{2,1,0:T(8,128)(2,1)S(1)} %add.373), channel_id=1, source_target_pairs={{2,0},{3,1},{4,6},{5,7},{10,8},{11,9},{12,14},{13,15},{18,16},{19,... | collective-permute-start | bytes 1376264 | tf_op jit(solution)/shard_map/ppermute | solution.py:268
  671.3 30.8 %collective-permute-start.47 = (bf16[224,896]{1,0:T(8,128)(2,1)S(1)}, bf16[224,896]{1,0:T(8,128)(2,1)S(1)}, u32[]{:S(2)}, u32[]{:S(2)}) collective-permute-start(bf16[224,896]{1,0:T(8,128)(2,1)S(1)} %dynamic-slice_bitcast_fusion.3), channel_id=1, source_target_pairs={{0,16},{8,24},{16,0},{24,8},{1,17},{9,25},{17,1},{25,9},{2,18},{10... | collective-permute-start | bytes 1204232 | tf_op jit(solution)/shard_map/ppermute | solution.py:259
  700.5 31.8 %collective-permute-start.58 = (bf16[2,224,512]{2,1,0:T(8,128)(2,1)S(1)}, bf16[2,224,512]{2,1,0:T(8,128)(2,1)S(1)}, u32[]{:S(2)}, u32[]{:S(2)}) collective-permute-start(bf16[2,224,512]{2,1,0:T(8,128)(2,1)S(1)} %broadcast_select_fusion.7), channel_id=1, source_target_pairs={{0,1},{1,0},{2,3},{3,2},{4,5},{5,4},{6,7},{7,6},{8,9},{9,8},{10,11... | collective-permute-start | bytes 1376264 | tf_op jit(solution)/shard_map/ppermute | solution.py:262
  704.2 36.1 %collective-permute-start.80 = (bf16[2,224,512]{2,1,0:T(8,128)(2,1)S(1)}, bf16[2,224,512]{2,1,0:T(8,128)(2,1)S(1)}, u32[]{:S(2)}, u32[]{:S(2)}) collective-permute-start(bf16[2,224,512]{2,1,0:T(8,128)(2,1)S(1)} %get-tuple-element.216), channel_id=1, source_target_pairs={{0,8},{8,0},{16,24},{24,16},{1,9},{9,1},{17,25},{25,17},{2,10},{10... | collective-permute-start | bytes 1376264 | tf_op jit(solution)/shard_map/ppermute | solution.py:256
  713.1 37.0 %collective-permute-start.73 = (bf16[2,224,512]{2,1,0:T(8,128)(2,1)S(1)}, bf16[2,224,512]{2,1,0:T(8,128)(2,1)S(1)}, u32[]{:S(2)}, u32[]{:S(2)}) collective-permute-start(bf16[2,224,512]{2,1,0:T(8,128)(2,1)S(1)} %get-tuple-element.218), channel_id=1, source_target_pairs={{0,8},{8,0},{16,24},{24,16},{1,9},{9,1},{17,25},{25,17},{2,10},{10... | collective-permute-start | bytes 1376264 | tf_op jit(solution)/shard_map/ppermute | solution.py:256
  724.5 28.5 %collective-permute-start.66 = (bf16[2,224,512]{2,1,0:T(8,128)(2,1)S(1)}, bf16[2,224,512]{2,1,0:T(8,128)(2,1)S(1)}, u32[]{:S(2)}, u32[]{:S(2)}) collective-permute-start(bf16[2,224,512]{2,1,0:T(8,128)(2,1)S(1)} %get-tuple-element.220), channel_id=1, source_target_pairs={{0,8},{8,0},{16,24},{24,16},{1,9},{9,1},{17,25},{25,17},{2,10},{10... | collective-permute-start | bytes 1376264 | tf_op jit(solution)/shard_map/ppermute | solution.py:256
  738.9 34.2 %collective-permute-start.51 = (bf16[112,896]{1,0:T(8,128)(2,1)S(1)}, bf16[112,896]{1,0:T(8,128)(2,1)}, u32[]{:S(2)}, u32[]{:S(2)}) collective-permute-start(bf16[112,896]{1,0:T(8,128)(2,1)S(1)} %add.367), channel_id=1, source_target_pairs={{2,0},{3,1},{4,6},{5,7},{10,8},{11,9},{12,14},{13,15},{18,16},{19,... | collective-permute-start | bytes 602120 | tf_op jit(solution)/shard_map/ppermute | solution.py:268
  (227 other events, 2234.4 us)

commit v2 on v0

v2 whole, which is shorter than its diff:
```python
import functools

import jax
import jax.numpy as jnp
from jax import lax
from jax.experimental import pallas as pl
from jax.experimental.pallas import tpu as pltpu
from jax.sharding import PartitionSpec as P

HEADS, KVHEADS, HD = 14, 2, 64
GROUP = HEADS // KVHEADS
PAIRS = HEADS // 2
TILE = 256
BLK = 256
VMEM_CAP = 63 << 20
bf16, f32 = jnp.bfloat16, jnp.float32
epsilon = 1e-06
rope_base = 1000000.0


def nn(a, b):
    return lax.dot_general(a, b, (((1,), (0,)), ((), ())), preferred_element_type=f32)


def nt(a, b):
    return lax.dot_general(a, b, (((1,), (1,)), ((), ())), preferred_element_type=f32)


def tn(a, b):
    return lax.dot_general(a, b, (((0,), (0,)), ((), ())), preferred_element_type=f32)


def shaped(shape, dtype=bf16):
    return jax.ShapeDtypeStruct(shape, dtype)


def fixed(shape):
    return pl.BlockSpec(shape, lambda i: (0,) * len(shape))


def by_rows(rows, columns, first=0):
    return pl.BlockSpec((rows, columns), lambda i: (i + first, 0))


SCALARS = pl.BlockSpec(memory_space=pltpu.SMEM)
X, CORE, Y, Z = range(4)


FLOPS_PER_US = 500 * 10**6


class Order:
    def __init__(self):
        self.due = []

    def wait(self, *arrays):
        self.due += arrays


def call(order, body, name, us, grid, ins, outs, scratch=(), aliases=()):
    after = order.due
    n = len(after)

    def kernel(*refs):
        body(*refs[n:])

    result = pl.pallas_call(
        kernel,
        grid=(grid,),
        in_specs=[pl.BlockSpec(memory_space=pl.ANY)] * n + [s for _, s in ins],
        out_specs=[s for _, s in outs],
        out_shape=[s for s, _ in outs],
        scratch_shapes=list(scratch),
        input_output_aliases={n + a: b for a, b in aliases},
        compiler_params=pltpu.CompilerParams(vmem_limit_bytes=VMEM_CAP),
        cost_estimate=pl.CostEstimate(flops=int(us * FLOPS_PER_US), bytes_accessed=10**5, transcendentals=0),
        name=name,
    )(*after, *[a for a, _ in ins])
    order.due = [result[0]]
    return result


def gate(order, v):
    anywhere = pl.BlockSpec(memory_space=pl.ANY)

    def body(v, out):
        pass

    return call(order, body, "gate", 1, 1, [(v, anywhere)], [(shaped(v.shape, v.dtype), anywhere)], (), [(0, 0)])[0]


def widths_of(rows):
    if rows == 1216:
        return [(256, 0), (384, 256), (384, 640), (192, 1024)]
    cuts, at = [], 0
    while at < rows:
        w = min(256, rows - at)
        cuts.append((w, at))
        at += w
    return cuts


def split_weights(order, where, w_gate, w_up, w_down, cuts):
    own, d = w_gate.shape[0], w_down.shape[1]
    ff = w_down.shape[0]
    n = len(cuts)

    def body(where, gate, up, down, *refs):
        sends, mine, downs = refs[: 2 * n], refs[2 * n : 3 * n], refs[3 * n :]

        def put(targets, core, cut):
            w, off = cut
            for src, (ref, start) in zip((gate, up), targets):
                for side in (0, 1):
                    a = (2 * side + core) * ff + off
                    ref[:, start + side * w : start + side * w + w] = src[:, a : a + w]

        for core in (0, 1):

            @pl.when(where[CORE] == core)
            def _():
                for k, (cut, ref) in enumerate(zip(cuts, mine)):
                    put(((ref, 0), (ref, 2 * cut[0])), core, cut)
                    put(((sends[2 * k], 0), (sends[2 * k + 1], 0)), 1 - core, cut)

        for (w, off), part in zip(cuts, downs):
            for lo in range(0, w, 128):
                hi = min(lo + 128, w)
                part[:, lo:hi] = down[off + lo : off + hi, :].T

    whole = lambda a: (a, fixed(a.shape))
    return call(
        order,
        body,
        "split_weights",
        2 + 2 * n,
        1,
        [(where, SCALARS)] + [whole(a) for a in (w_gate, w_up, w_down)],
        [(shaped((own, 2 * w)), fixed((own, 2 * w))) for w, _ in cuts for _ in (0, 1)]
        + [(shaped((own, 4 * w)), fixed((own, 4 * w))) for w, _ in cuts]
        + [(shaped((d, w)), fixed((d, w))) for w, _ in cuts],
    )


def pack_weights(order, where, core_rows, mine, downs, groups, extra=()):
    own = mine[0].shape[0]
    widths = [m.shape[1] // 4 for m in mine]
    n = len(mine)

    def body(where, *refs):
        cores, refs = refs[: 2 * n], refs[2 * n :]
        mine, downs, extras, outs = refs[:n], refs[n : 2 * n], refs[2 * n : 2 * n + len(extra)], refs[2 * n + len(extra) :]
        for group, out in zip(groups, outs):
            at6 = 0
            for k in group:
                w = widths[k]

                @pl.when(where[CORE] == where[Y])
                def _():
                    out[:, at6 : at6 + 4 * w] = mine[k][...]

                @pl.when(where[CORE] != where[Y])
                def _():
                    out[:, at6 : at6 + 2 * w] = cores[2 * k][...]
                    out[:, at6 + 2 * w : at6 + 4 * w] = cores[2 * k + 1][...]

                for h in (0, 1):
                    rows = pl.ds(pl.multiple_of((2 * where[Y] + h) * own, 16), own)
                    out[:, at6 + (4 + h) * w : at6 + (5 + h) * w] = downs[k][rows, :]
                at6 += 6 * w
        if extras:
            outs[-1][:own, :] = extras[0][...]
            outs[-1][own:, :] = extras[1][...]

    whole = lambda a: (a, fixed(a.shape))
    totals = [sum(6 * widths[k] for k in group) for group in groups]
    return call(
        order,
        body,
        "pack_weights",
        2 + n,
        1,
        [(where, SCALARS)] + [whole(a) for a in (*core_rows, *mine, *downs, *extra)],
        [(shaped((own, m)), fixed((own, m))) for m in totals]
        + [(shaped((2 * own, e.shape[1])), fixed((2 * own, e.shape[1]))) for e in extra[:1]],
    )


def place_rows(where, refs, rows, target):
    x, c = where[0], where[1]
    for ref, s in zip(refs, (2 * x + c, 2 * (1 - x) + c, 2 * x + 1 - c, 2 * (1 - x) + 1 - c)):
        target[pl.ds(pl.multiple_of(s * rows, 16), rows), :] = ref


def project(order, where, tokens, gain, own_w, across_w, core_w, far_w, bias, cos, sin):
    t, d = tokens.shape
    rows, width = own_w.shape
    kw = KVHEADS * HD
    qw = width - 2 * kw

    def body(where, tokens, gain, own_w, across_w, core_w, far_w, bias, cos, sin, normed, q, kx, vx, vz, w):
        @pl.when(pl.program_id(0) == 0)
        def _():
            place_rows(where, (own_w[...], across_w[...], core_w[...], far_w[...]), rows, w)

        v = tokens[...].astype(f32)
        inverse = lax.rsqrt(jnp.mean(v * v, axis=-1, keepdims=True) + epsilon)
        n = (v * inverse * gain[...]).astype(bf16)
        normed[...] = n
        lanes = lax.broadcasted_iota(jnp.int32, (TILE, 2 * HD), 1)
        left = lanes < HD
        c, s = cos[...], sin[...]
        for p in range(width // 128):
            at = slice(p * 128, p * 128 + 128)
            u = nn(n, w[:, at]) + bias[:, at]
            if p * 128 < qw + kw:
                u = (u * c + swap_halves(u, lanes) * s).astype(bf16)
            if p * 128 < qw:
                q[:, at] = (u.astype(f32) * 0.125).astype(bf16)
                continue
            u = u.astype(f32)
            turned = pltpu.roll(u, HD, 1)
            first, second = (kx, 0.0), (vx, 1.0)
            for ref, fill in (first,) if p * 128 < qw + kw else (second, (vz, 0.0)):
                ref[0] = jnp.where(left, u, fill).astype(bf16)
                ref[1] = jnp.where(left, fill, turned).astype(bf16)
                ref[2] = jnp.where(left, turned, fill).astype(bf16)
                ref[3] = jnp.where(left, fill, u).astype(bf16)

    heads = (shaped((4, t, 2 * HD)), pl.BlockSpec((4, TILE, 2 * HD), lambda i: (0, i, 0)))
    return call(
        order,
        body,
        "project",
        10,
        t // TILE,
        [
            (where, SCALARS),
            (tokens, by_rows(TILE, d)),
            (gain, fixed(gain.shape)),
            (own_w, fixed(own_w.shape)),
            (across_w, fixed(across_w.shape)),
            (core_w, fixed(core_w.shape)),
            (far_w, fixed(far_w.shape)),
            (bias, fixed(bias.shape)),
            (cos, by_rows(TILE, 2 * HD)),
            (sin, by_rows(TILE, 2 * HD)),
        ],
        [
            (shaped((t, d)), by_rows(TILE, d)),
            (shaped((t, qw)), by_rows(TILE, qw)),
            heads,
            heads,
            heads,
            (shaped((d, width)), fixed((d, width))),
        ],
    )


def swap_halves(v, lanes):
    half = HD // 2
    return jnp.where(lanes % HD < half, pltpu.roll(v, v.shape[1] - half, 1), pltpu.roll(v, half, 1))


def kinds_of(pair):
    return [2 * (2 * pair + side >= GROUP).astype(jnp.int32) + side for side in (0, 1)]


def attend(order, segments, q, kx, vx, first, last):
    t = q.shape[0]
    tiles = t // TILE

    def body(segc, segr, q, kx, vx, o, o_rest, linv, *rest):
        probs, bias = rest[:tiles], rest[tiles]
        step = pl.program_id(0)
        pair = step + first

        @pl.when(step == 0)
        def _():
            for i in range(tiles):
                w = (i + 1) * TILE
                rows = lax.broadcasted_iota(jnp.int32, (TILE, w), 0) + i * TILE
                cols = lax.broadcasted_iota(jnp.int32, (TILE, w), 1)
                ok = (segc[i * TILE : w, :] == segr[:, :w]) & (cols <= rows)
                bias[i * TILE : w, :w] = jnp.where(ok, 0.0, -1e30)

        left = lax.broadcasted_iota(jnp.int32, (TILE, 2 * HD), 1) < HD
        kinds = kinds_of(pair)
        for i in range(tiles):
            w = (i + 1) * TILE
            block = q[i * TILE : w, :]
            mixed = []
            for side in (0, 1):
                s = nt(block, kx[kinds[side], :w, :]) + bias[i * TILE : w, :w]
                e = jnp.exp(s - jnp.max(s, axis=-1, keepdims=True)).astype(bf16)
                for j in range(i + 1):
                    probs[j][side, (i - j) * TILE : (i - j + 1) * TILE, :] = e[:, j * TILE : (j + 1) * TILE]
                mixed.append(nn(e, vx[kinds[side], :w, :]))
            totals = jnp.where(left, pltpu.roll(mixed[0], HD, 1), pltpu.roll(mixed[1], HD, 1))
            inverse = 1.0 / totals
            out = jnp.where(left, mixed[0], mixed[1]) * inverse
            low = out.astype(bf16)
            o[i * TILE : w, :] = low
            o_rest[i * TILE : w, :] = (out - low.astype(f32)).astype(bf16)
            linv[i * TILE : w, :] = inverse

    count = last - first
    lane = pl.BlockSpec((t, 2 * HD), lambda p: (0, p + first))
    out_lane = pl.BlockSpec((t, 2 * HD), lambda p: (0, p))
    out = (t, count * 2 * HD)
    pshape = [(2 * count, t - j * TILE, TILE) for j in range(tiles)]
    return call(
        order,
        body,
        "attend",
        4 * count,
        count,
        [
            (segments.reshape(t, 1), fixed((t, 1))),
            (segments.reshape(1, t), fixed((1, t))),
            (q, lane),
            (kx, fixed(kx.shape)),
            (vx, fixed(vx.shape)),
        ],
        [(shaped(out), out_lane), (shaped(out), out_lane), (shaped(out, f32), out_lane)]
        + [(shaped(s), pl.BlockSpec((2,) + s[1:], lambda p: (p, 0, 0))) for s in pshape],
        [pltpu.VMEM((t, t), f32)],
    )


def attend_back(order, q, do, o, o_rest, kx, vz, cos, sin, probs, first, last, running=()):
    t = q.shape[0]
    tiles = t // TILE
    count = last - first

    def body(q, do, o, o_rest, kx, vz, cos, sin, *rest):
        probs, rest = rest[:tiles], rest[tiles:]
        if running:
            dk_in, dv_in, rest = rest[0], rest[1], rest[2:]
        dq, dk, dv, ds0, ds1, dkacc, dvacc = rest
        step = pl.program_id(0)
        pair = step + first

        @pl.when(step == 0)
        def _():
            if running:
                dkacc[...] = dk_in[...]
                dvacc[...] = dv_in[...]
            else:
                dkacc[...] = jnp.zeros_like(dkacc)
                dvacc[...] = jnp.zeros_like(dvacc)

        left = lax.broadcasted_iota(jnp.int32, (t, 2 * HD), 1) < HD
        along = do[...].astype(f32) * (o[...].astype(f32) + o_rest[...].astype(f32))
        inner = [
            jnp.sum(jnp.where(left, along, 0.0), axis=-1, keepdims=True),
            jnp.sum(jnp.where(left, 0.0, along), axis=-1, keepdims=True),
        ]
        kinds = kinds_of(pair)
        for side, ds in ((0, ds0), (1, ds1)):
            kind = kinds[side]
            for j in range(tiles):
                lo = j * TILE
                p = probs[j][side]
                dp = nt(do[lo:, :], vz[kind, lo : lo + TILE, :])
                d = (p.astype(f32) * (dp - inner[side][lo:])).astype(bf16)
                ds[lo:, lo : lo + TILE] = d
                dkacc[kind, lo : lo + TILE, :] += tn(d, q[lo:, :])
                dvacc[kind, lo : lo + TILE, :] += tn(p, do[lo:, :])
        lanes = lax.broadcasted_iota(jnp.int32, (TILE, 2 * HD), 1)
        for i in range(tiles):
            w = (i + 1) * TILE
            at = slice(i * TILE, w)
            g = (nn(ds0[at, :w], kx[kinds[0], :w, :]) + nn(ds1[at, :w], kx[kinds[1], :w, :])) * 0.125
            dq[at, :] = (g * cos[at, :] - swap_halves(g, lanes) * sin[at, :]).astype(bf16)

        @pl.when(step == count - 1)
        def _():
            if not running:
                dk[...] = dkacc[...]
                dv[...] = dvacc[...]
                return
            lanes = lax.broadcasted_iota(jnp.int32, (t, 2 * HD), 1)
            one = lambda a: jnp.where(left, a[0] + pltpu.roll(a[1], HD, 1), pltpu.roll(a[2], HD, 1) + a[3])
            g = one(dkacc)
            dk[...] = (g * cos[...] - swap_halves(g, lanes) * sin[...]).astype(bf16)
            dv[...] = one(dvacc).astype(bf16)

    lane = pl.BlockSpec((t, 2 * HD), lambda p: (0, p + first))
    out_lane = pl.BlockSpec((t, 2 * HD), lambda p: (0, p))
    wide = (4, t, 2 * HD)
    sums = (shaped((t, 2 * HD)), fixed((t, 2 * HD))) if running else (shaped(wide, f32), fixed(wide))
    return call(
        order,
        body,
        "attend_back",
        6 * count,
        count,
        [(q, lane), (do, out_lane), (o, out_lane), (o_rest, out_lane), (kx, fixed(wide)), (vz, fixed(wide))]
        + [(cos, fixed(cos.shape)), (sin, fixed(sin.shape))]
        + [(p, pl.BlockSpec((2,) + p.shape[1:], lambda i: (i, 0, 0))) for p in probs]
        + [(r, fixed(wide)) for r in running],
        [(shaped((t, count * 2 * HD)), out_lane), sums, sums],
        [pltpu.VMEM((t, t), bf16)] * 2 + [pltpu.VMEM(wide, f32)] * 2,
    )


def join_output(order, where, tokens, mixed, own_w, across, core, gain):
    t, d = tokens.shape
    rows = own_w.shape[0]
    n = len(mixed)

    def body(where, tokens, own_w, across, core, gain, *refs):
        mixed, (resid, normed, w) = refs[:n], refs[n:]

        @pl.when(pl.program_id(0) == 0)
        def _():
            place_rows(where, (own_w[...], across[:rows, :], core[...], across[rows:, :]), rows, w)

        v, lo = tokens[...].astype(f32), 0
        for m in mixed:
            v = v + nn(m[...], w[lo : lo + m.shape[1], :])
            lo += m.shape[1]
        resid[...] = v
        inverse = lax.rsqrt(jnp.mean(v * v, axis=-1, keepdims=True) + epsilon)
        normed[...] = (v * inverse * gain[...]).astype(bf16)

    return call(
        order,
        body,
        "join_output",
        7,
        t // TILE,
        [(where, SCALARS), (tokens, by_rows(TILE, d))]
        + [(a, fixed(a.shape)) for a in (own_w, across, core, gain)]
        + [(m, by_rows(TILE, m.shape[1])) for m in mixed],
        [
            (shaped((t, d), f32), by_rows(TILE, d)),
            (shaped((t, d)), by_rows(TILE, d)),
            (shaped((4 * rows, d)), fixed((4 * rows, d))),
        ],
    )


def ffn_part(order, where, n2, dy, mine, core_rows, x_rows, y_rows, down, cut, at6, tt=512):
    t, d = n2[0].shape
    w, off = cut
    own = mine.shape[0]
    half = d // 2
    steps = t // tt

    def body(where, n2a, n2b, dya, dyb, mine, core_gate, core_up, x_rows, y_rows, down, hid, dgu, keep, send, wt, acc):
        step = pl.program_id(0)
        x, c, y = where[0], where[1], where[2]

        @pl.when(step == 0)
        def _():
            def put(ref, s, at=at6):
                wt[pl.ds(pl.multiple_of(s * own, 16), own), : 4 * w] = ref[:, at : at + 4 * w]

            put(mine, 2 * x + c, 0)
            other = pl.ds(pl.multiple_of((2 * x + 1 - c) * own, 16), own)
            wt[other, : 2 * w] = core_gate[...]
            wt[other, 2 * w : 4 * w] = core_up[...]
            put(x_rows, 2 * (1 - x) + y)
            put(y_rows, 2 * (1 - x) + 1 - y)
            for side in (0, 1):

                @pl.when(x == side)
                def _():
                    wt[:, (4 + side) * w : (5 + side) * w] = down[...]
                    lo = (5 - side) * w
                    for ref, h in ((x_rows, y), (y_rows, 1 - y)):
                        for part in (0, 1):
                            at = pl.ds(pl.multiple_of((2 * h + part) * own, 16), own)
                            wt[at, lo : lo + w] = ref[:, at6 + (4 + part) * w : at6 + (5 + part) * w]

            acc[...] = jnp.zeros_like(acc)

        first = step < steps
        a = jnp.where(first, n2a[...], n2b[...])
        b = jnp.where(first, dya[...], dyb[...])
        for lo in range(0, 2 * w, BLK):
            hi = min(lo + BLK, 2 * w)
            g, u, v = slice(lo, hi), slice(2 * w + lo, 2 * w + hi), slice(4 * w + lo, 4 * w + hi)
            gate, up, dh = nn(a, wt[:, g]), nn(a, wt[:, u]), nn(b, wt[:, v])
            sig = jax.nn.sigmoid(gate)
            silu = gate * sig
            h = (silu * up).astype(bf16)
            d_gate = (dh * up * (sig + silu * (1.0 - sig))).astype(bf16)
            d_up = (dh * silu).astype(bf16)
            hid[:, g] = h
            dgu[:, g] = d_gate
            dgu[:, u] = d_up
            acc[:, v] += tn(b, h)
            acc[:, g] += tn(a, d_gate)
            acc[:, u] += tn(a, d_up)

        @pl.when(step == 2 * steps - 1)
        def _():
            for ref, side in ((keep, x), (send, 1 - x)):
                at = pl.ds(pl.multiple_of(side * half, 16), half)
                ref[:, : 4 * w] = acc[at, : 4 * w].astype(bf16)
            for side in (0, 1):

                @pl.when(x == side)
                def _():
                    for ref, s in ((keep, side), (send, 1 - side)):
                        lanes = slice((4 + s) * w, (5 + s) * w)
                        ref[:, 4 * w : 5 * w] = acc[:half, lanes].astype(bf16)
                        ref[:, 5 * w :] = acc[half:, lanes].astype(bf16)

    whole = lambda a: (a, fixed(a.shape))
    early = pl.BlockSpec((tt, d), lambda i: (jnp.minimum(i, steps - 1), 0))
    late = pl.BlockSpec((tt, d), lambda i: (jnp.maximum(i - steps, 0), 0))
    return call(
        order,
        body,
        "ffn_part",
        5 + w // 16,
        2 * steps,
        [(where, SCALARS), (n2[0], early), (n2[1], late), (dy[0], early), (dy[1], late)]
        + [whole(a) for a in (mine, *core_rows, x_rows, y_rows, down)],
        [
            (shaped((2 * t, 2 * w)), by_rows(tt, 2 * w)),
            (shaped((2 * t, 4 * w)), by_rows(tt, 4 * w)),
            (shaped((half, 6 * w)), fixed((half, 6 * w))),
            (shaped((half, 6 * w)), fixed((half, 6 * w))),
            (shaped((d, 6 * w)), fixed((d, 6 * w))),
        ],
        [pltpu.VMEM((d, 6 * w), f32)],
    )


def sum_parts(order, name, us, parts, weights, lanes, block, tokens, apart=False, tt=256):
    d = weights[0].shape[0]
    t = parts[0].shape[0] // 2
    n = len(parts)
    steps = t // tt
    k = len(tokens)

    def body(*refs):
        step = pl.program_id(0)
        total = None
        for part, weight in zip(refs[:n], refs[n : 2 * n]):
            s = nt(part[...], weight[...])
            total = s if total is None else total + s
        for out, (first, count, _) in zip(refs[2 * n :], outs):

            @pl.when((step >= first) & (step < first + count))
            def _():
                out[...] = total.astype(out.dtype)

    def spec(first, count):
        return pl.BlockSpec((tt, d), lambda i: (jnp.clip(i - first, 0, count - 1), 0))

    outs = []
    for at, half in enumerate(tokens):
        if half and apart:
            outs += [(at * steps + k, 1, bf16) for k in range(steps)]
        else:
            outs.append((at * steps, steps, bf16 if half else f32))

    start = tokens[0] * steps
    return call(
        order,
        body,
        name,
        us,
        k * steps,
        [(p, pl.BlockSpec((tt, p.shape[1]), lambda i: ((i + start) % (2 * steps), 0))) for p in parts]
        + [(w, pl.BlockSpec((d, n), lambda i: (0, block))) for w, n in zip(weights, lanes)],
        [(shaped((count * tt, d), kind), spec(first, count)) for first, count, kind in outs],
    )


def turn_back(order, dn2, dn2_other, residual, cotangent, gain, full_output, inverse_sums):
    t, d = residual.shape
    n = len(inverse_sums)

    steps = len(dn2_other)

    def body(dn2, resid, dy, gain, w, *refs):
        others, refs = refs[:steps], refs[steps:]
        sums, (d_resid, d_attn, grad_gain), scaled, other = refs[:n], refs[n : n + 3], refs[n + 3 : -1], refs[-1]
        step = pl.program_id(0)
        for k, ref in enumerate(others):

            @pl.when(step == k)
            def _():
                other[...] = ref[...]

        @pl.when(step == 0)
        def _():
            grad_gain[...] = jnp.zeros_like(grad_gain)

        up = dn2[...] + other[...].astype(f32)
        grad, gains = norm_back(resid[...], gain[...], up)
        grad_gain[...] += gains
        total = dy[...].astype(f32) + grad
        d_resid[...] = total
        low = total.astype(bf16)
        d_attn[...] = low
        d_mixed = nt(low, w[...]).astype(bf16).astype(f32)
        lo = 0
        for linv, out in zip(sums, scaled):
            hi = lo + linv.shape[1]
            out[...] = (d_mixed[:, lo:hi] * linv[...]).astype(bf16)
            lo = hi

    rows = by_rows(TILE, d)
    return call(
        order,
        body,
        "turn_back",
        8,
        steps,
        [(a, rows) for a in (dn2, residual, cotangent)]
        + [(gain, fixed(gain.shape)), (full_output, fixed(full_output.shape))]
        + [(a, fixed(a.shape)) for a in dn2_other]
        + [(a, by_rows(TILE, a.shape[1])) for a in inverse_sums],
        [(shaped((t, d), f32), rows), (shaped((t, d)), rows), (shaped((1, d), f32), fixed((1, d)))]
        + [(shaped((t, a.shape[1])), by_rows(TILE, a.shape[1])) for a in inverse_sums],
        [pltpu.VMEM((TILE, d), bf16)],
    )


def weight_grads(order, where, us, pairs):
    d = sum(a.shape[1] for a in pairs[0][0])
    width = sum(g.shape[1] for _, g in pairs)
    own = d // 4
    lefts = []
    for pieces, _ in pairs:
        lefts += [a for a in pieces if not any(a is b for b in lefts)]
    rights = [g for _, g in pairs]
    place = [[next(i for i, b in enumerate(lefts) if b is a) for a in pieces] for pieces, _ in pairs]

    def body(where, *refs):
        left, right, (keep, send) = refs[: len(lefts)], refs[len(lefts) : -2], refs[-2:]
        c = where[CORE]
        lo = 0
        for spots, g in zip(place, right):
            hi = lo + g.shape[1]
            grad = jnp.concatenate([tn(left[i][...], g[...]).astype(bf16) for i in spots], 0)
            for core in (0, 1):
                rows = jnp.concatenate([grad[core * own : (core + 1) * own], grad[(2 + core) * own : (3 + core) * own]], 0)

                @pl.when(c == core)
                def _():
                    keep[:, lo:hi] = rows

                @pl.when(c != core)
                def _():
                    send[:, lo:hi] = rows

            lo = hi

    out = (shaped((2 * own, width)), fixed((2 * own, width)))
    return call(
        order, body, "weight_grads", us, 1, [(where, SCALARS)] + [(a, fixed(a.shape)) for a in (*lefts, *rights)], [out, out]
    )


def finish_tokens(order, tokens, gain, d_parts, full_qkv, d_resid):
    t, d = tokens.shape
    n = len(d_parts)
    width = full_qkv.shape[1]

    def body(tokens, gain, w, d_resid, *refs):
        parts, out, grad_gain, sums = refs[:n], refs[n], refs[n + 1], refs[n + 2]

        @pl.when(pl.program_id(0) == 0)
        def _():
            grad_gain[...] = jnp.zeros_like(grad_gain)
            sums[...] = jnp.zeros_like(sums)

        total, lo = None, 0
        for part in parts:
            hi = lo + part.shape[1]
            p = part[...]
            sums[:, lo:hi] += jnp.sum(p.astype(f32), axis=0, keepdims=True)
            s = nt(p, w[:, lo:hi])
            total = s if total is None else total + s
            lo = hi
        grad, gains = norm_back(tokens[...].astype(f32), gain[...], total)
        grad_gain[...] += gains
        out[...] = d_resid[...] + grad

    rows = by_rows(TILE, d)
    return call(
        order,
        body,
        "finish_tokens",
        8,
        t // TILE,
        [(tokens, rows), (gain, fixed(gain.shape)), (full_qkv, fixed(full_qkv.shape)), (d_resid, rows)]
        + [(p, by_rows(TILE, p.shape[1])) for p in d_parts],
        [(shaped((t, d), f32), rows), (shaped((1, d), f32), fixed((1, d))), (shaped((1, width), f32), fixed((1, width)))],
    )


def assemble(order, where, halves, others, cores, cuts, ff):
    own = halves[0].shape[0]
    d = 4 * own
    n = len(cuts)
    steps = d // 128
    block = own // steps

    def body(where, *refs):
        halves, others, cores = refs[:n], refs[n : 2 * n], refs[2 * n : 3 * n]
        gate, up, down, down_t = refs[3 * n :]
        step = pl.program_id(0)
        c, y = where[1], where[2]
        rows = pl.ds(pl.multiple_of(step * block, 16), block)

        @pl.when(step == 0)
        def _():
            for (w, off), a, b in zip(cuts, halves, others):
                for ref, h in ((a, y), (b, 1 - y)):
                    for part in (0, 1):
                        at = pl.ds(pl.multiple_of((2 * part + h) * own, 16), own)
                        down_t[at, off : off + w] = ref[:, (4 + part) * w : (5 + part) * w]

        for core in (0, 1):
            for (w, off), a, b, o in zip(cuts, halves, others, cores):

                def put(ref, to):
                    for m, out in enumerate((gate, up)):
                        for side in (0, 1):
                            at = (2 * side + to) * ff + off
                            lo = (2 * m + side) * w
                            out[:, at : at + w] = ref[rows, lo : lo + w].astype(f32)

                @pl.when((c == core) & (c == y))
                def _():
                    put(a, core)

                @pl.when((c == core) & (c != y))
                def _():
                    put(b, core)

                @pl.when(c != core)
                def _():
                    put(o, core)

        down[...] = down_t[pl.ds(pl.multiple_of(step * 128, 128), 128), :].astype(f32).T

    whole = lambda a: (a, fixed(a.shape))
    return call(
        order,
        body,
        "assemble",
        11,
        steps,
        [(where, SCALARS)] + [whole(a) for a in (*halves, *others, *cores)],
        [
            (shaped((own, 4 * ff), f32), by_rows(block, 4 * ff)),
            (shaped((own, 4 * ff), f32), by_rows(block, 4 * ff)),
            (shaped((ff, d), f32), pl.BlockSpec((ff, 128), lambda i: (0, i))),
        ],
        [pltpu.VMEM((d, ff), bf16)],
    )


class Links:
    def __init__(self, shards, replicas):
        self.shards, self.replicas = shards, replicas
        s, r = lax.axis_index("shard"), lax.axis_index("replica")
        self.where = jnp.stack([s // 2, s % 2, r % 2, r // 2 % 2]).astype(jnp.int32)

    def core(self, v):
        return lax.ppermute(v, "shard", [(i, i ^ 1) for i in range(self.shards)])

    def across(self, v):
        return lax.ppermute(v, "shard", [(i, i ^ 2) for i in range(self.shards)])

    def beside(self, v):
        return lax.ppermute(v, "replica", [(i, i ^ 1) for i in range(self.replicas)])

    def far(self, v, bit):
        return lax.ppermute(v, "replica", [(i, i ^ bit) for i in range(self.replicas)])

    def along(self, v):
        return lax.psum(v, "replica", axis_index_groups=[list(range(y, self.replicas, 2)) for y in (0, 1)])

    def bits(self):
        bit = 2
        while bit < self.replicas:
            yield bit
            bit *= 2


def split_sum(axis, keep, got):
    half = keep.shape[0] // 2
    shape = shaped((half, keep.shape[1]), keep.dtype)

    def body(where, keep, got, mine, send):
        n = where[axis]
        for ref, h in ((mine, n), (send, 1 - n)):
            at = pl.ds(pl.multiple_of(h * half, 16), half)
            ref[...] = (keep[at, :].astype(f32) + got[at, :].astype(f32)).astype(ref.dtype)

    return body, [(keep, fixed(keep.shape)), (got, fixed(got.shape))], [shape, shape]


def whole_sum(v, got):
    def body(where, v, got, out):
        out[...] = (v[...].astype(f32) + got[...].astype(f32)).astype(out.dtype)

    return body, [(v, fixed(v.shape)), (got, fixed(got.shape))], [shaped(v.shape, v.dtype)]


def in_order(axis, mine, other, dtype=bf16):
    rows, width = mine.shape

    def body(where, mine, other, out):
        n = where[axis]
        out[pl.ds(pl.multiple_of(n * rows, 16), rows), :] = mine[...].astype(dtype)
        out[pl.ds(pl.multiple_of((1 - n) * rows, 16), rows), :] = other[...].astype(dtype)

    return body, [(mine, fixed(mine.shape)), (other, fixed(other.shape))], [shaped((2 * rows, width), dtype)]


def rows_for_core(half, other, lanes):
    spec = fixed((half.shape[0], lanes))

    def body(where, half, other, out):
        same = where[CORE] == where[Y]

        @pl.when(same)
        def _():
            out[...] = other[...]

        @pl.when(jnp.logical_not(same))
        def _():
            out[...] = half[...]

    return body, [(half, spec), (other, spec)], [shaped((half.shape[0], lanes))]


GATE = "gate"


def advance(order, where, chains):
    chains = [chain for chain in chains if chain.asked is not None]
    for chain in [chain for chain in chains if chain.asked[0] == GATE]:
        chains.remove(chain)
        chain.give([gate(order, chain.asked[1])])
    if not chains:
        return
    asked = [chain.asked for chain in chains]
    n_in = sum(len(ins) for _, ins, _ in asked)

    def body(where, *refs):
        ins, outs = refs[:n_in], refs[n_in:]
        for part, i, o in asked:
            part(where, *ins[: len(i)], *outs[: len(o)])
            ins, outs = ins[len(i) :], outs[len(o) :]

    results = call(
        order,
        body,
        "sums",
        2,
        1,
        [(where, SCALARS)] + [pair for _, i, _ in asked for pair in i],
        [(shape, fixed(shape.shape)) for _, _, o in asked for shape in o],
    )
    for chain, (_, _, o) in zip(chains, asked):
        chain.give(results[: len(o)])
        results = results[len(o) :]


class Chain:
    def __init__(self, steps):
        self.steps = steps
        self.result = None
        self.asked = next(steps)

    def give(self, results):
        try:
            self.asked = self.steps.send(results)
        except StopIteration as stop:
            self.asked, self.result = None, stop.value


def replica_steps(order, links, mine, send, how):
    bits = list(links.bits())
    if how == "halves" and bits:
        mine, send = yield split_sum(Z, mine, links.beside(send))
        (mine,) = yield whole_sum(mine, links.far(send, bits[0]))
        for bit in bits[1:]:
            (mine,) = yield whole_sum(mine, links.far(mine, bit))
        (mine,) = yield in_order(Z, mine, links.far(mine, bits[0]))
    else:
        (mine,) = yield whole_sum(mine, links.beside(send))
        if how == "offload":
            (mine,) = yield GATE, links.along(mine)
        else:
            for bit in bits:
                (mine,) = yield whole_sum(mine, links.far(mine, bit))
    return mine, links.beside(mine)


def ffn_steps(order, links, keep, send, w, how):
    mine, send = yield split_sum(Y, keep, links.across(send))
    half, other = yield from replica_steps(order, links, mine, send, how)
    (rows,) = yield rows_for_core(half, other, 4 * w)
    return half, other, links.core(rows)


def owned_steps(order, links, keep, send, how):
    mine, send = yield split_sum(X, keep, links.core(send))
    mine, send = yield split_sum(Y, mine, links.across(send))
    half, other = yield from replica_steps(order, links, mine, send, how)
    (rows,) = yield in_order(Y, half, other, f32)
    return rows


def small_steps(links, v):
    for move in (links.core, links.across, links.beside):
        (v,) = yield whole_sum(v, move(v))
    for bit in links.bits():
        (v,) = yield whole_sum(v, links.far(v, bit))
    return v


def norm_back(values, gain_vector, upstream):
    inverse = lax.rsqrt(jnp.mean(values * values, axis=-1, keepdims=True) + epsilon)
    scaled = upstream * gain_vector
    grad_gain = jnp.sum(upstream * values * inverse, axis=0, keepdims=True)
    correction = jnp.sum(scaled * values, axis=-1, keepdims=True) / values.shape[-1]
    return inverse * scaled - values * (inverse * inverse * inverse) * correction, grad_gain


def position_tables(doc_ids):
    t = doc_ids.shape[0]
    earlier = jnp.sum((doc_ids[None, :] < doc_ids[:, None]).astype(jnp.int32), axis=1)
    places = jnp.arange(t, dtype=jnp.int32) - earlier
    frequency = rope_base ** (-jnp.arange(0, HD, 2).astype(f32) / HD)
    angles = places.astype(f32)[:, None] * frequency[None, :]
    cosine, sine = jnp.cos(angles), jnp.sin(angles)
    return jnp.tile(cosine, (1, 4)), jnp.tile(jnp.concatenate([-sine, sine], 1), (1, 2))


def on_device(
    links_shape,
    tokens,
    segments,
    cotangent,
    gain_attn,
    gain_ffn,
    w_query,
    bias_query,
    w_key,
    bias_key,
    w_value,
    bias_value,
    w_output,
    w_gate,
    w_up,
    w_down,
):
    links = Links(*links_shape)
    order = Order()
    where = links.where
    t, d = tokens.shape
    qw, kw = w_query.shape[1], w_key.shape[1]
    doc_ids = segments[0]
    ff = w_down.shape[0]
    cuts = widths_of(ff)
    cos, sin = position_tables(doc_ids)
    gain_attn, gain_ffn = gain_attn[None, :], gain_ffn[None, :]
    pieces = range(len(cuts))
    stages = [[[0]], [[1], list(pieces[2:])]] if len(cuts) > 2 else [[[n] for n in pieces]]
    group_of = [number for number, group in enumerate(g for stage in stages for g in stage) for _ in group]

    own_qkv = jnp.concatenate([w_query, w_key, w_value], 1)
    across_qkv, core_qkv = links.across(own_qkv), links.core(own_qkv)
    dy = (cotangent, links.core(cotangent))
    core_output = links.core(w_output)
    mine, downs, core_rows, at6 = [], [], [], []
    order.wait(cos, sin)
    for number, stage in enumerate(stages):
        chosen = [cuts[n] for group in stage for n in group]
        k = len(chosen)
        parts = split_weights(order, where, w_gate, w_up, w_down, chosen)
        core_rows.append([links.core(v) for v in parts[: 2 * k]])
        mine.append(parts[2 * k : 3 * k])
        downs.append(parts[3 * k :])
        for group in stage:
            at6 += [sum(6 * cuts[m][0] for m in group[:k]) for k in range(len(group))]
        if number == 0:
            across_qkv = gate(order, across_qkv)
            far_qkv = links.core(across_qkv)
    x_rows = []
    for number, stage in enumerate(stages):
        sizes = [len(group) for group in stage]
        local = [list(range(sum(sizes[:k]), sum(sizes[: k + 1]))) for k in range(len(sizes))]
        packed = pack_weights(
            order,
            where,
            core_rows[number],
            mine[number],
            downs[number],
            local,
            [w_output, core_output] if number == 0 else [],
        )
        if number == 0:
            *packed, joined = packed
            across_output = links.across(joined)
        x_rows += [links.across(v) for v in packed]
    mine, downs, core_rows = ([v for part in parts for v in part] for parts in (mine, downs, core_rows))

    bias = jnp.concatenate([bias_query, bias_key, bias_value])[None, :]
    order.wait(dy[1])
    normed, queries, kx, vx, vz, full_qkv = project(
        order, where, tokens, gain_attn, own_qkv, across_qkv, core_qkv, far_qkv, bias, cos, sin
    )
    middle = 3
    y_rows = []

    def forward_rows(*groups):
        for g in groups:
            if g < len(x_rows) and g == len(y_rows):
                x_rows[g] = gate(order, x_rows[g])
                y_rows.append(links.beside(x_rows[g]))

    first_part = attend(order, doc_ids, queries, kx, vx, 0, middle)
    forward_rows(0)
    second_part = attend(order, doc_ids, queries, kx, vx, middle, PAIRS)
    forward_rows(1)
    order.wait(y_rows[0])
    mixed, mixed_rest, inverse_sums = zip(first_part[:3], second_part[:3])
    probs = (first_part[3:], second_part[3:])
    residual, normed_two, full_output = join_output(
        order, where, tokens, mixed, w_output, across_output, core_output, gain_ffn
    )
    n2 = (normed_two, links.core(normed_two))

    chains, hids, dgus, weights = [], [], [], []
    how = ["whole"] * len(cuts)

    def step(*which):
        advance(order, where, [chains[n] for n in which if n < len(chains)])

    for n in pieces:
        g = group_of[n]
        forward_rows(g)
        if n >= 2:
            step(0)
        hid, dgu, keep, send, weight = ffn_part(
            order, where, n2, dy, mine[n], core_rows[2 * n : 2 * n + 2], x_rows[g], y_rows[g], downs[n], cuts[n], at6[n]
        )
        hids.append(hid), dgus.append(dgu), weights.append(weight)
        chains.append(Chain(ffn_steps(order, links, keep, send, cuts[n][0], how[n])))
        if n == 0:
            forward_rows(2)

    step(0, 1)
    *dn2_send, dn2 = sum_parts(order, "back_tokens", 24, dgus, weights, [4 * w for w, _ in cuts], 0, (1, 0), True)
    dn2_other = [links.core(v) for v in dn2_send]
    step(0, 1, 2)
    d_resid, d_attn, grad_gain_ffn, *scaled = turn_back(
        order, dn2, dn2_other, residual, cotangent, gain_ffn, full_output, inverse_sums
    )
    step(0, 1, 3)

    both = [
        (queries, scaled[n], mixed[n], mixed_rest[n], kx, vz, cos, sin, probs[n], *span)
        for n, span in enumerate(((0, middle), (middle, PAIRS)))
    ]
    dq_first, *running = attend_back(order, *both[0], ())
    step(2, 3)
    chains.append(
        Chain(owned_steps(order, links, *weight_grads(order, where, 5, [(mixed, d_attn)]), "whole"))
    )
    out_n = len(chains) - 1
    dq_second, d_key, d_value = attend_back(order, *both[1], running)
    step(1, 2, out_n)
    d_parts = [dq_first, dq_second, d_key, d_value]
    chains.append(
        Chain(owned_steps(order, links, *weight_grads(order, where, 8, [((normed,), p) for p in d_parts]), "whole"))
    )
    qkv_n = out_n + 1
    step(1, 3, out_n, qkv_n)
    grad_tokens, grad_gain_attn, grad_biases = finish_tokens(order, tokens, gain_attn, d_parts, full_qkv, d_resid)
    chains.append(Chain(small_steps(links, jnp.concatenate([grad_gain_attn, grad_gain_ffn, grad_biases], 1))))
    small_n = qkv_n + 1
    step(2, out_n, qkv_n)
    down_lanes = [2 * w for w, _ in cuts]
    (out_send,) = sum_parts(order, "down_tokens", 11, hids, weights, down_lanes, 2, (1,))
    out_other = links.core(out_send)
    step(2, 3, out_n, qkv_n, small_n)
    (out,) = sum_parts(order, "down_tokens", 11, hids, weights, down_lanes, 2, (0,))
    output = (residual + out + out_other.astype(f32)).astype(bf16)
    while any(chain.result is None for chain in chains[: len(cuts)]):
        step(*range(len(chains)))
    grad_gate, grad_up, grad_down = assemble(order, where, *zip(*(chain.result for chain in chains[: len(cuts)])), cuts, ff)
    while any(chain.result is None for chain in chains):
        step(*range(len(chains)))
    grad_output, grad_qkv, small = (chain.result for chain in chains[len(cuts) :])
    small = small[0]
    return (
        output,
        grad_tokens,
        small[:d],
        small[d : 2 * d],
        grad_qkv[:, :qw],
        small[2 * d : 2 * d + qw],
        grad_qkv[:, qw : qw + kw],
        small[2 * d + qw : 2 * d + qw + kw],
        grad_qkv[:, qw + kw :],
        small[2 * d + qw + kw :],
        grad_output,
        grad_gate,
        grad_up,
        grad_down,
    )


def solution(mesh):
    tokens, rows, whole = P(("shard", "replica"), None), P("shard", None), P()
    return jax.shard_map(
        functools.partial(on_device, (mesh.shape["shard"], mesh.shape["replica"])),
        mesh=mesh,
        in_specs=(tokens, tokens, tokens, whole, whole, rows, whole, rows, whole, rows, whole, rows, rows, rows, rows),
        out_specs=(tokens, tokens, whole, whole, rows, whole, rows, whole, rows, whole, rows, rows, rows, rows),
        check_vma=False,
    )
```

time: 1270 us -> 548 us (0.43)
  waiting for transfers between devices: 562 us -> 108 us
  matrix products: 381 us -> 0 us
  Pallas kernels: 0 us -> 348 us
  other arithmetic: 111 us -> 7.88 us
  local copies, waits for them, and re-layouts: 128 us -> 27.9 us
  blocking collectives: 53.8 us -> 0 us
  starting transfers between devices: 0.56 us -> 48.4 us
  between operations: 14.9 us -> 1.3 us
    dot_general x35 -> x0, matrix products: 381 us -> none  [the longest x4 75.4 us: block_scores(): jnp.einsum('bkgd,rkd->kgbr', query_block, key_rows, preferred_element_typ...]
    pallas_call x0 -> x40, Pallas kernels: none -> 348 us  [call(): pl.pallas_call(kernel, grid=(grid,), in_specs=[pl.BlockSpec(memory_space=...]
    reduce_scatter x7 -> x0, waiting for transfers between devices: 263 us -> none  [the longest x1 76.4 us: on_device(): lax.psum_scatter(full_grads[5].astype(jnp.bfloat16), 'shard', scatter_dim...]
    psum x2 -> x0, waiting for transfers between devices: 246 us -> none  [the longest x1 246 us: on_device(): lax.psum(owned_rows[0].astype(jnp.bfloat16), 'replica').astype(jnp.float32)]
    ppermute x0 -> x67, waiting for transfers between devices: none -> 108 us  [the longest x14 63.4 us: far(): lax.ppermute(v, 'replica', [(i, i ^ bit) for i in range(self.replicas)])]
    dynamic_update_slice x4 -> x0, local copies, waits for them, and re-layouts: 73.7 us -> none  [attention_backward(): lax.scan(one_block, (zero_rows, zero_rows), (starts, log_totals))]
    convert_element_type x12 -> x2, other arithmetic: 63.6 us -> 5.4 us  [the longest x1 5.39 us: on_device(): output = (residual + out + out_other.astype(f32)).astype(bf16)]
    all_gather x5 -> x0, waiting for transfers between devices: 48.9 us -> none  [the longest x1 43.6 us: on_device(): lax.all_gather(w_down, 'shard', axis=0, tiled=True)]
  transfers between devices with their start and end apart: 14 -> 67, of which waited for: 8 -> 25; matrix products, arithmetic and copies ran while one was open for 20% -> 4% of each run, Pallas kernels for 0% -> 59%
where the time goes in v2:
time: 548 us; the launch traced here: 542 us
  Pallas kernels  348 us (64%)
  waiting for transfers between devices  108 us (20%)
  starting transfers between devices  48.4 us (9%)
  local copies, waits for them, and re-layouts  27.9 us (5%)
  other arithmetic  7.88 us (1%)
    pallas_call x40, Pallas kernels, call(): pl.pallas_call(kernel, grid=(grid,), in_specs=[pl.BlockSpec(memory_space=...  348 us
    ppermute x14, waiting for transfers between devices, far(): lax.ppermute(v, 'replica', [(i, i ^ bit) for i in range(self.replicas)])  63.4 us
    ppermute x12, waiting for transfers between devices, across(): return lax.ppermute(v, 'shard', [(i, i ^ 2) for i in range(self.shards)])  28.1 us
    ppermute x16, starting transfers between devices, beside(): lax.ppermute(v, 'replica', [(i, i ^ 1) for i in range(self.replicas)])  16.2 us
    unnamed x82, local copies, waits for them, and re-layouts  14.8 us
    ppermute x12, starting transfers between devices, across(): return lax.ppermute(v, 'shard', [(i, i ^ 2) for i in range(self.shards)])  14.4 us
    ppermute x16, waiting for transfers between devices, beside(): lax.ppermute(v, 'replica', [(i, i ^ 1) for i in range(self.replicas)])  13 us
    ppermute x14, starting transfers between devices, far(): lax.ppermute(v, 'replica', [(i, i ^ bit) for i in range(self.replicas)])  13 us
  transfers between devices with their start and end apart: 67, of which 25 were waited for; matrix products, arithmetic and copies ran while one was open for 4% of the time, Pallas kernels for 59%

profile of v2, /device:TPU:0, one launch (start us, length us, event | category | flops | bytes accessed | tf_op | source)
XLA Modules:
  0.0 542.5 jit_solution(6360950596758975230)
XLA Ops:
  5.8 2.5 collective-permute-start
  13.2 4.4 split_weights.2
  18.1 2.9 collective-permute-done.refs_1_
  21.1 6.1 %split_weights.3 = (bf16[224,768]{1,0:T(8,128)(2,1)}, bf16[224,768]{1,0:T(8,128)(2,1)}, bf16[224,768]{1,0:T(8,128)(2,1)}, bf16[224,768]{1,0:T(8,128)(2,1)}, bf16...) custom-call(bf16[224,1152]{1,0:T(8,128)(2,1)} %gate.4.refs_0_.refs_6, ...), custom_call_target="tpu_custom_call" | custom-call | flops 4000000000 | bytes 100000 | tf_op jit(solution)/shard_map/split_weights/pallas_call | solution.py:67
  33.8 2.8 pack_weights.2
  38.6 4.5 pack_weights.3
  44.9 9.7 %project.1 = (bf16[1024,896]{1,0:T(8,128)(2,1)}, bf16[1024,896]{1,0:T(8,128)(2,1)}, bf16[4,1024,128]{2,1,0:T(8,128)(2,1)}, bf16[4,1024,128]{2,1,0:T(8,128)(2,1)}...) custom-call(bf16[224,2304]{1,0:T(8,128)(2,1)} %get-tuple-element.163.refs_0_, ...), custom_call_target="tpu_custom_call" | custom-call | flops 5000000000 | bytes 100000 | tf_op jit(solution)/shard_map/project/pallas_call | solution.py:67
  54.6 13.7 %attend.2 = (bf16[1024,384]{1,0:T(8,128)(2,1)}, bf16[1024,384]{1,0:T(8,128)(2,1)}, f32[1024,384]{1,0:T(8,128)}, bf16[6,1024,256]{2,1,0:T(8,128)(2,1)}, bf16[6,76...) custom-call(bf16[1024,896]{1,0:T(8,128)(2,1)} %get-tuple-element.164.refs_0_.refs_2_, ...), custom_call_target="tpu_custom_call" | custom-call | flops 6000000000 | bytes 100000 | tf_op jit(solution)/shard_map/attend/pallas_call | solution.py:67
  70.8 17.1 %attend.3 = (bf16[1024,512]{1,0:T(8,128)(2,1)}, bf16[1024,512]{1,0:T(8,128)(2,1)}, f32[1024,512]{1,0:T(8,128)}, bf16[8,1024,256]{2,1,0:T(8,128)(2,1)}, bf16[8,76...) custom-call(bf16[224,1536]{1,0:T(8,128)(2,1)} %gate.5.refs_0_.refs_9_, ...), custom_call_target="tpu_custom_call" | custom-call | flops 8000000000 | bytes 100000 | tf_op jit(solution)/shard_map/attend/pallas_call | solution.py:67
  87.9 5.9 %collective-permute-done.14.refs_1_ = bf16[224,2304]{1,0:T(8,128)(2,1)} collective-permute-done((bf16[224,2304]{1,0:T(8,128)(2,1)}, bf16[224,2304]{1,0:T(8,128)(2,1)}, u32[]{:S(2)}, u32[]{:S(2)}) %collective-permute-start.14) | collective-permute-done | bytes 1032224 | tf_op jit(solution)/shard_map/ppermute | solution.py:775
  94.7 7.0 %join_output.1 = (f32[1024,896]{1,0:T(8,128)}, bf16[1024,896]{1,0:T(8,128)(2,1)}, bf16[896,896]{1,0:T(8,128)(2,1)}) custom-call(bf16[224,2304]{1,0:T(8,128)(2,1)} %gate.6.refs_0_.refs_9_, bf16[224,1536]{1,0:T(8,128)(2,1)} %copy-done.31, s32[4]{0:T(128)} %pad_add_fusion.refs_2_.refs_1_, bf16[1024,896]{1,0:T(8,128)(2,1)} %refs_1_.1, bf16[224,896]{1,0:T(8,128)(2,1)} %refs_4_.9, ...), custom_call_target="tpu_custom_call" | custom-call | flops 3500000000 | bytes 100000 | tf_op jit(solution)/shard_map/join_output/pallas_call | solution.py:67
  105.8 21.5 %ffn_part.4 = (bf16[2048,512]{1,0:T(8,128)(2,1)}, bf16[2048,1024]{1,0:T(8,128)(2,1)}, bf16[448,1536]{1,0:T(8,128)(2,1)}, bf16[448,1536]{1,0:T(8,128)(2,1)}, bf16[896,1536]{1,0:T(8,128)(2,1)}) custom-call(f32[1024,896]{1,0:T(8,128)} %get-tuple-element.171.refs_0_.refs_2_, s32[4]{0:T(128)} %pad_add_fusion.refs_2_.refs_1_, ...), custom_call_target="tpu_custom_call" | custom-call | flops 10499999744 | bytes 100000 | tf_op jit(solution)/shard_map/ffn_part/pallas_call | solution.py:67
  127.4 10.9 %collective-permute-done.18.refs_1_ = bf16[224,3456]{1,0:T(8,128)(2,1)} collective-permute-done((bf16[224,3456]{1,0:T(8,128)(2,1)}, bf16[224,3456]{1,0:T(8,128)(2,1)}, u32[]{:S(2)}, u32[]{:S(2)}) %collective-permute-start.18) | collective-permute-done | bytes 1548320 | tf_op jit(solution)/shard_map/ppermute | solution.py:775
  141.5 29.5 %ffn_part.5 = (bf16[2048,768]{1,0:T(8,128)(2,1)}, bf16[2048,1536]{1,0:T(8,128)(2,1)}, bf16[448,2304]{1,0:T(8,128)(2,1)}, bf16[448,2304]{1,0:T(8,128)(2,1)}, bf16[896,2304]{1,0:T(8,128)(2,1)}) custom-call(bf16[224,3456]{1,0:T(8,128)(2,1)} %gate.7.refs_0_.refs_9_, s32[4]{0:T(128)} %pad_add_fusion.refs_2_.refs_1_, ...), custom_call_target="tpu_custom_call" | custom-call | flops 14499999744 | bytes 100000 | tf_op jit(solution)/shard_map/ffn_part/pallas_call | solution.py:67
  171.8 3.1 sums.14
  175.2 30.0 %ffn_part.6 = (bf16[2048,768]{1,0:T(8,128)(2,1)}, bf16[2048,1536]{1,0:T(8,128)(2,1)}, bf16[448,2304]{1,0:T(8,128)(2,1)}, bf16[448,2304]{1,0:T(8,128)(2,1)}, bf16[896,2304]{1,0:T(8,128)(2,1)}) custom-call(bf16[224,1536]{1,0:T(8,128)(2,1)} %get-tuple-element.178.refs_0_.refs_2_, s32[4]{0:T(128)} %pad_add_fusion.refs_2_.refs_1_, ...), custom_call_target="tpu_custom_call" | custom-call | flops 14499999744 | bytes 100000 | tf_op jit(solution)/shard_map/ffn_part/pallas_call | solution.py:67
  211.7 20.4 %ffn_part.7 = (bf16[2048,384]{1,0:T(8,128)(2,1)}, bf16[2048,768]{1,0:T(8,128)(2,1)}, bf16[448,1152]{1,0:T(8,128)(2,1)}, bf16[448,1152]{1,0:T(8,128)(2,1)}, bf16[896,1152]{1,0:T(8,128)(2,1)}) custom-call(bf16[224,1536]{1,0:T(8,128)(2,1)} %sums.15.refs_0_.refs_2_, s32[4]{0:T(128)} %pad_add_fusion.refs_2_.refs_1_, ...), custom_call_target="tpu_custom_call" | custom-call | flops 8499999744 | bytes 100000 | tf_op jit(solution)/shard_map/ffn_part/pallas_call | solution.py:67
  233.0 4.4 sums.16
  237.4 2.6 collective-permute-start.25
  241.5 29.5 %back_tokens.1 = (bf16[256,896]{1,0:T(8,128)(2,1)}, bf16[256,896]{1,0:T(8,128)(2,1)}, bf16[256,896]{1,0:T(8,128)(2,1)}, bf16[256,896]{1,0:T(8,128)(2,1)}, f32[1024,896]{1,0:T(8,128)}) custom-call(bf16[224,1536]{1,0:T(8,128)(2,1)} %get-tuple-element.184.refs_0_.refs_2_, bf16[2048,1024]{1,0:T(8,128)(2,1)} %get-tuple-element.185.refs_1_, ...), custom_call_target="tpu_custom_call" | custom-call | flops 12000000000 | bytes 100000 | tf_op jit(solution)/shard_map/back_tokens/pallas_call | solution.py:67
  272.3 5.6 %sums.17 = (bf16[224,1536]{1,0:T(8,128)(2,1)}, bf16[224,2304]{1,0:T(8,128)(2,1)}, bf16[224,2304]{1,0:T(8,128)(2,1)}, bf16[224,2304]{1,0:T(8,128)(2,1)}) custom-call(bf16[256,896]{1,0:T(8,128)(2,1)} %get-tuple-element.193.refs_0_, s32[4]{0:T(128)} %pad_add_fusion.refs_2_.refs_1_, bf16[224,1536]{1,0:T(8,128)(2,1)} %get-tuple-element.184.refs_0_.refs_2_, ...), custom_call_target="tpu_custom_call" | custom-call | flops 1000000000 | bytes 100000 | tf_op jit(solution)/shard_map/sums/pallas_call | solution.py:67
  281.2 10.1 %turn_back.1 = (f32[1024,896]{1,0:T(8,128)}, bf16[1024,896]{1,0:T(8,128)(2,1)}, f32[1,896]{1,0:T(1,128)}, bf16[1024,384]{1,0:T(8,128)(2,1)}, bf16[1024,512]{1,0:T(8,128)(2,1)}) custom-call(bf16[224,1536]{1,0:T(8,128)(2,1)} %get-tuple-element.198.refs_0_.refs_2_, f32[1024,896]{1,0:T(8,128)} %get-tuple-element.199.refs_1_, ...), custom_call_target="tpu_custom_call" | custom-call | flops 4000000000 | bytes 100000 | tf_op jit(solution)/shard_map/turn_back/pallas_call | solution.py:67
  291.3 5.3 collective-permute-done.34.refs_7_
  297.4 5.6 %collective-permute-done.33.refs_5_ = bf16[224,2304]{1,0:T(8,128)(2,1)} collective-permute-done((bf16[224,2304]{1,0:T(8,128)(2,1)}, bf16[224,2304]{1,0:T(8,128)(2,1)}, u32[]{:S(2)}, u32[]{:S(2)}) %collective-permute-start.33) | collective-permute-done | bytes 1032224 | tf_op jit(solution)/shard_map/ppermute | solution.py:781
  303.0 4.1 sums.18
  308.0 18.2 %attend_back.2 = (bf16[1024,384]{1,0:T(8,128)(2,1)}, f32[4,1024,128]{2,1,0:T(8,128)}, f32[4,1024,128]{2,1,0:T(8,128)}) custom-call(bf16[224,1024]{1,0:T(8,128)(2,1)} %get-tuple-element.210.refs_0_, bf16[1024,896]{1,0:T(8,128)(2,1)} %get-tuple-element.165.refs_3_.refs_1_, bf16[1024,384]{1,0:T(8,128)(2,1)} %get-tuple-element.211.refs_2_, ...), custom_call_target="tpu_custom_call" | custom-call | flops 8999999488 | bytes 100000 | tf_op jit(solution)/shard_map/attend_back/pallas_call | solution.py:67
  326.2 3.4 collective-permute-done.36.refs_5_
  330.5 3.3 sums.19
  335.3 5.5 %weight_grads.2 = (bf16[448,896]{1,0:T(8,128)(2,1)}, bf16[448,896]{1,0:T(8,128)(2,1)}) custom-call(bf16[224,2304]{1,0:T(8,128)(2,1)} %get-tuple-element.223.refs_0_.refs_4_, s32[4]{0:T(128)} %pad_add_fusion.refs_2_.refs_1_, bf16[1024,384]{1,0:T(8,128)(2,1)} %get-tuple-element.168.refs_0_.refs_8_.refs_3_.refs_2_, ...), custom_call_target="tpu_custom_call" | custom-call | flops 2500000000 | bytes 100000 | tf_op jit(solution)/shard_map/weight_grads/pallas_call | solution.py:67
  340.8 23.6 %attend_back.3 = (bf16[1024,512]{1,0:T(8,128)(2,1)}, bf16[1024,128]{1,0:T(8,128)(2,1)}, bf16[1024,128]{1,0:T(8,128)(2,1)}) custom-call(bf16[448,896]{1,0:T(8,128)(2,1)} %get-tuple-element.225.refs_0_.refs_6_, bf16[1024,896]{1,0:T(8,128)(2,1)} %get-tuple-element.165.refs_3_.refs_1_, bf16[1024,512]{1,0:T(8,128)(2,1)} %get-tuple-element.226.refs_2_, ...), custom_call_target="tpu_custom_call" | custom-call | flops 12000000000 | bytes 100000 | tf_op jit(solution)/shard_map/attend_back/pallas_call | solution.py:67
  364.4 12.2 %collective-permute-done.38.refs_5_ = bf16[224,2304]{1,0:T(8,128)(2,1)} collective-permute-done((bf16[224,2304]{1,0:T(8,128)(2,1)}, bf16[224,2304]{1,0:T(8,128)(2,1)}, u32[]{:S(2)}, u32[]{:S(2)}) %collective-permute-start.38) | collective-permute-done | bytes 1032224 | tf_op jit(solution)/shard_map/ppermute | solution.py:781
  376.6 4.4 sums.20
  381.1 8.2 %weight_grads.3 = (bf16[448,1152]{1,0:T(8,128)(2,1)}, bf16[448,1152]{1,0:T(8,128)(2,1)}) custom-call(bf16[224,2304]{1,0:T(8,128)(2,1)} %get-tuple-element.237.refs_0_.refs_2_.refs_3_, s32[4]{0:T(128)} %pad_add_fusion.refs_2_.refs_1_, bf16[1024,896]{1,0:T(8,128)(2,1)} %get-tuple-element.164.refs_0_.refs_2_, ...), custom_call_target="tpu_custom_call" | custom-call | flops 4000000000 | bytes 100000 | tf_op jit(solution)/shard_map/weight_grads/pallas_call | solution.py:67
  392.4 21.0 %collective-permute-done.41.refs_5_ = bf16[224,1152]{1,0:T(8,128)(2,1)S(1)} collective-permute-done((bf16[224,1152]{1,0:T(8,128)(2,1)S(1)}, bf16[224,1152]{1,0:T(8,128)(2,1)S(1)}, u32[]{:S(2)}, u32[]{:S(2)}) %collective-permute-start.41) | collective-permute-done | bytes 516128 | tf_op jit(solution)/shard_map/ppermute | solution.py:781
  414.9 4.2 sums.21
  421.2 9.3 %finish_tokens.1 = (f32[1024,896]{1,0:T(8,128)}, f32[1,896]{1,0:T(1,128)}, f32[1,1152]{1,0:T(1,128)}) custom-call(bf16[224,1536]{1,0:T(8,128)(2,1)} %get-tuple-element.245.refs_0_, bf16[1024,896]{1,0:T(8,128)(2,1)} %refs_1_.1, f32[1,896]{1,0:T(1,128)} %broadcast_in_dim.11.refs_4_.refs_2_, bf16[896,1152]{1,0:T(8,128)(2,1)} %get-tuple-element.246.refs_3_, ...), custom_call_target="tpu_custom_call" | custom-call | flops 4000000000 | bytes 100000 | tf_op jit(solution)/shard_map/finish_tokens/pallas_call | solution.py:67
  430.5 8.6 %collective-permute-done.44.refs_3_ = bf16[224,2304]{1,0:T(8,128)(2,1)} collective-permute-done((bf16[224,2304]{1,0:T(8,128)(2,1)}, bf16[224,2304]{1,0:T(8,128)(2,1)}, u32[]{:S(2)}, u32[]{:S(2)}) %collective-permute-start.44) | collective-permute-done | bytes 1032224 | tf_op jit(solution)/shard_map/ppermute | solution.py:781
  440.0 3.4 sums.22
  449.3 10.1 %down_tokens.2.refs_0_ = bf16[1024,896]{1,0:T(8,128)(2,1)} custom-call(bf16[224,2304]{1,0:T(8,128)(2,1)} %get-tuple-element.253.refs_0_.refs_2_.refs_4_, bf16[2048,512]{1,0:T(8,128)(2,1)} %get-tuple-element.173.refs_0_.refs_1_, bf16[2048,768]{1,0:T(8,128)(2,1)} %get-tuple-element.175.refs_0_.refs_2_, bf16[2048,768]{1,0:T(8,128)(2,1)} %get-tuple-element.179.refs_0_.refs_3_, ...), custom_call_target="tpu_custom_call" | custom-call | flops 5500000256 | bytes 100000 | tf_op jit(solution)/shard_map/down_tokens/pallas_call | solution.py:67
  459.5 8.2 %collective-permute-done.48.refs_5_ = bf16[224,1152]{1,0:T(8,128)(2,1)S(1)} collective-permute-done((bf16[224,1152]{1,0:T(8,128)(2,1)}, bf16[224,1152]{1,0:T(8,128)(2,1)S(1)}, u32[]{:S(2)}, u32[]{:S(2)}) %collective-permute-start.48) | collective-permute-done | bytes 516128 | tf_op jit(solution)/shard_map/ppermute | solution.py:781
  467.7 5.6 %collective-permute-done.50.refs_9_ = bf16[112,1152]{1,0:T(8,128)(2,1)S(1)} collective-permute-done((bf16[112,1152]{1,0:T(8,128)(2,1)}, bf16[112,1152]{1,0:T(8,128)(2,1)S(1)}, u32[]{:S(2)}, u32[]{:S(2)}) %collective-permute-start.50) | collective-permute-done | bytes 258080 | tf_op jit(solution)/shard_map/ppermute | solution.py:778
  474.0 3.1 sums.23
  480.2 2.8 collective-permute-done.56.refs_9_
  483.0 5.1 collective-permute-done.54.refs_5_
  488.7 10.2 %down_tokens.3.refs_0_ = f32[1024,896]{1,0:T(8,128)} custom-call(bf16[224,1536]{1,0:T(8,128)(2,1)} %get-tuple-element.261.refs_0_, bf16[2048,512]{1,0:T(8,128)(2,1)} %get-tuple-element.173.refs_0_.refs_1_, bf16[2048,768]{1,0:T(8,128)(2,1)} %get-tuple-element.175.refs_0_.refs_2_, bf16[2048,768]{1,0:T(8,128)(2,1)} %get-tuple-element.179.refs_0_.refs_3_, ...), custom_call_target="tpu_custom_call" | custom-call | flops 5500000256 | bytes 100000 | tf_op jit(solution)/shard_map/down_tokens/pallas_call | solution.py:67
  506.3 10.7 %assemble.1 = (f32[224,4864]{1,0:T(8,128)}, f32[224,4864]{1,0:T(8,128)}, f32[1216,896]{1,0:T(8,128)}) custom-call(bf16[224,768]{1,0:T(8,128)(2,1)} %get-tuple-element.266.refs_0_, s32[4]{0:T(128)} %pad_add_fusion.refs_2_.refs_1_, bf16[224,1536]{1,0:T(8,128)(2,1)} %get-tuple-element.198.refs_0_.refs_2_, ...), custom_call_target="tpu_custom_call" | custom-call | flops 5500000256 | bytes 100000 | tf_op jit(solution)/shard_map/assemble/pallas_call | solution.py:67
  522.4 5.4 add_convert_fusion
  527.8 2.5 collective-permute-done.64.refs_3_
  (230 shorter events, 92.7 us)
Async XLA Ops:
  0.6 27.2 %collective-permute-start.3 = (bf16[224,896]{1,0:T(8,128)(2,1)}, bf16[224,896]{1,0:T(8,128)(2,1)S(1)}, u32[]{:S(2)}, u32[]{:S(2)}) collective-permute-start(bf16[224,896]{1,0:T(8,128)(2,1)} %refs_4_.9), channel_id=1, source_target_pairs={{0,8},{8,0},{16,24},{24,16},{1,9},{9,1},{17,25},{25,17},{2,10},{10... | collective-permute-start | bytes 1204232 | tf_op jit(solution)/shard_map/ppermute | solution.py:772
  5.8 15.2 %collective-permute-start = (bf16[224,1152]{1,0:T(8,128)(2,1)}, bf16[224,1152]{1,0:T(8,128)(2,1)}, u32[]{:S(2)}, u32[]{:S(2)}) collective-permute-start(bf16[224,1152]{1,0:T(8,128)(2,1)} %constant_dynamic-update-slice_fusion.refs_5_), channel_id=1, source_target_pairs={{0,16},{8,24},{16,0},{24,8},{1,17},{9,25},{17,1},{25,9},{2,18},{10... | collective-permute-start | bytes 1548296 | tf_op jit(solution)/shard_map/ppermute | solution.py:775
  8.3 36.6 %collective-permute-start.10 = (bf16[1024,896]{1,0:T(8,128)(2,1)}, bf16[1024,896]{1,0:T(8,128)(2,1)}, u32[]{:S(2)}, u32[]{:S(2)}) collective-permute-start(bf16[1024,896]{1,0:T(8,128)(2,1)} %refs_3_.9), channel_id=1, source_target_pairs={{0,8},{8,0},{16,24},{24,16},{1,9},{9,1},{17,25},{25,17},{2,10},{10... | collective-permute-start | bytes 5505032 | tf_op jit(solution)/shard_map/ppermute | solution.py:772
  30.5 12.6 %collective-permute-start.11 = (bf16[224,1152]{1,0:T(8,128)(2,1)}, bf16[224,1152]{1,0:T(8,128)(2,1)}, u32[]{:S(2)}, u32[]{:S(2)}) collective-permute-start(bf16[224,1152]{1,0:T(8,128)(2,1)} %constant_dynamic-update-slice_fusion.refs_5_), channel_id=1, source_target_pairs={{0,8},{8,0},{16,24},{24,16},{1,9},{9,1},{17,25},{25,17},{2,10},{10... | collective-permute-start | bytes 1548296 | tf_op jit(solution)/shard_map/ppermute | solution.py:772
  30.7 14.2 %collective-permute-start.12 = (bf16[224,1152]{1,0:T(8,128)(2,1)}, bf16[224,1152]{1,0:T(8,128)(2,1)}, u32[]{:S(2)}, u32[]{:S(2)}) collective-permute-start(bf16[224,1152]{1,0:T(8,128)(2,1)} %gate.4.refs_0_.refs_6_), channel_id=1, source_target_pairs={{0,8},{8,0},{16,24},{24,16},{1,9},{9,1},{17,25},{25,17},{2,10},{10... | collective-permute-start | bytes 1548296 | tf_op jit(solution)/shard_map/ppermute | solution.py:772
  36.6 31.8 %collective-permute-start.13 = (bf16[224,1536]{1,0:T(8,128)(2,1)}, bf16[224,1536]{1,0:T(8,128)(2,1)S(1)}, u32[]{:S(2)}, u32[]{:S(2)}) collective-permute-start(bf16[224,1536]{1,0:T(8,128)(2,1)} %get-tuple-element.151.refs_0_), channel_id=1, source_target_pairs={{0,16},{8,24},{16,0},{24,8},{1,17},{9,25},{17,1},{25,9},{2,18},{10... | collective-permute-start | bytes 2064392 | tf_op jit(solution)/shard_map/ppermute | solution.py:775
  38.3 55.5 %collective-permute-start.16 = (bf16[448,896]{1,0:T(8,128)(2,1)}, bf16[448,896]{1,0:T(8,128)(2,1)}, u32[]{:S(2)}, u32[]{:S(2)}) collective-permute-start(bf16[448,896]{1,0:T(8,128)(2,1)} %get-tuple-element.170), channel_id=1, source_target_pairs={{0,16},{8,24},{16,0},{24,8},{1,17},{9,25},{17,1},{25,9},{2,18},{10... | collective-permute-start | bytes 2408456 | tf_op jit(solution)/shard_map/ppermute | solution.py:775
  43.1 50.7 %collective-permute-start.14 = (bf16[224,2304]{1,0:T(8,128)(2,1)}, bf16[224,2304]{1,0:T(8,128)(2,1)}, u32[]{:S(2)}, u32[]{:S(2)}) collective-permute-start(bf16[224,2304]{1,0:T(8,128)(2,1)} %get-tuple-element.163.refs_0_), channel_id=1, source_target_pairs={{0,16},{8,24},{16,0},{24,8},{1,17},{9,25},{17,1},{25,9},{2,18},{10... | collective-permute-start | bytes 3096584 | tf_op jit(solution)/shard_map/ppermute | solution.py:775
  69.2 24.6 %collective-permute-start.15 = (bf16[224,1536]{1,0:T(8,128)(2,1)}, bf16[224,1536]{1,0:T(8,128)(2,1)S(1)}, u32[]{:S(2)}, u32[]{:S(2)}) collective-permute-start(bf16[224,1536]{1,0:T(8,128)(2,1)} %gate.5.refs_0_.refs_9_), channel_id=1, source_target_pairs={{0,1},{1,0},{2,3},{3,2},{4,5},{5,4},{6,7},{7,6},{8,9},{9,8},{10,11... | collective-permute-start | bytes 2064392 | tf_op jit(solution)/shard_map/ppermute | solution.py:778
  101.7 36.6 %collective-permute-start.18 = (bf16[224,3456]{1,0:T(8,128)(2,1)}, bf16[224,3456]{1,0:T(8,128)(2,1)}, u32[]{:S(2)}, u32[]{:S(2)}) collective-permute-start(bf16[224,3456]{1,0:T(8,128)(2,1)} %get-tuple-element.174), channel_id=1, source_target_pairs={{0,16},{8,24},{16,0},{24,8},{1,17},{9,25},{17,1},{25,9},{2,18},{10... | collective-permute-start | bytes 4644872 | tf_op jit(solution)/shard_map/ppermute | solution.py:775
  103.5 38.0 %collective-permute-start.19 = (bf16[224,2304]{1,0:T(8,128)(2,1)}, bf16[224,2304]{1,0:T(8,128)(2,1)}, u32[]{:S(2)}, u32[]{:S(2)}) collective-permute-start(bf16[224,2304]{1,0:T(8,128)(2,1)} %gate.6.refs_0_.refs_9_), channel_id=1, source_target_pairs={{0,1},{1,0},{2,3},{3,2},{4,5},{5,4},{6,7},{7,6},{8,9},{9,8},{10,11... | collective-permute-start | bytes 3096584 | tf_op jit(solution)/shard_map/ppermute | solution.py:778
  138.3 36.9 %collective-permute-start.21 = (bf16[224,3456]{1,0:T(8,128)(2,1)}, bf16[224,3456]{1,0:T(8,128)(2,1)}, u32[]{:S(2)}, u32[]{:S(2)}) collective-permute-start(bf16[224,3456]{1,0:T(8,128)(2,1)} %gate.7.refs_0_.refs_9_), channel_id=1, source_target_pairs={{0,1},{1,0},{2,3},{3,2},{4,5},{5,4},{6,7},{7,6},{8,9},{9,8},{10,11... | collective-permute-start | bytes 4644872 | tf_op jit(solution)/shard_map/ppermute | solution.py:778
  140.0 31.8 %collective-permute-start.20 = (bf16[448,1536]{1,0:T(8,128)(2,1)}, bf16[448,1536]{1,0:T(8,128)(2,1)}, u32[]{:S(2)}, u32[]{:S(2)}) collective-permute-start(bf16[448,1536]{1,0:T(8,128)(2,1)} %get-tuple-element.177), channel_id=1, source_target_pairs={{0,16},{8,24},{16,0},{24,8},{1,17},{9,25},{17,1},{25,9},{2,18},{10... | collective-permute-start | bytes 4128776 | tf_op jit(solution)/shard_map/ppermute | solution.py:775
  171.1 61.1 %collective-permute-start.24 = (bf16[448,2304]{1,0:T(8,128)(2,1)}, bf16[448,2304]{1,0:T(8,128)(2,1)}, u32[]{:S(2)}, u32[]{:S(2)}) collective-permute-start(bf16[448,2304]{1,0:T(8,128)(2,1)} %get-tuple-element.183), channel_id=1, source_target_pairs={{0,16},{8,24},{16,0},{24,8},{1,17},{9,25},{17,1},{25,9},{2,18},{10... | collective-permute-start | bytes 6193160 | tf_op jit(solution)/shard_map/ppermute | solution.py:775
  174.9 32.0 %collective-permute-start.22 = (bf16[224,1536]{1,0:T(8,128)(2,1)}, bf16[224,1536]{1,0:T(8,128)(2,1)S(1)}, u32[]{:S(2)}, u32[]{:S(2)}) collective-permute-start(bf16[224,1536]{1,0:T(8,128)(2,1)} %get-tuple-element.180), channel_id=1, source_target_pairs={{0,1},{1,0},{2,3},{3,2},{4,5},{5,4},{6,7},{7,6},{8,9},{9,8},{10,11... | collective-permute-start | bytes 2064392 | tf_op jit(solution)/shard_map/ppermute | solution.py:778
  205.1 67.0 %collective-permute-start.27 = (bf16[448,2304]{1,0:T(8,128)(2,1)}, bf16[448,2304]{1,0:T(8,128)(2,1)}, u32[]{:S(2)}, u32[]{:S(2)}) collective-permute-start(bf16[448,2304]{1,0:T(8,128)(2,1)} %get-tuple-element.197), channel_id=1, source_target_pairs={{0,16},{8,24},{16,0},{24,8},{1,17},{9,25},{17,1},{25,9},{2,18},{10... | collective-permute-start | bytes 6193160 | tf_op jit(solution)/shard_map/ppermute | solution.py:775
  210.1 22.0 %collective-permute-start.23 = (bf16[224,1536]{1,0:T(8,128)(2,1)}, bf16[224,1536]{1,0:T(8,128)(2,1)S(1)}, u32[]{:S(2)}, u32[]{:S(2)}) collective-permute-start(bf16[224,1536]{1,0:T(8,128)(2,1)} %sums.15.refs_0_.refs_2_), channel_id=1, source_target_pairs={{0,2},{1,3},{2,0},{3,1},{4,6},{5,7},{6,4},{7,5},{8,10},{9,11},{10,... | collective-permute-start | bytes 2064392 | tf_op jit(solution)/shard_map/ppermute | solution.py:781
  237.4 34.1 %collective-permute-start.25 = (bf16[224,1536]{1,0:T(8,128)(2,1)}, bf16[224,1536]{1,0:T(8,128)(2,1)S(1)}, u32[]{:S(2)}, u32[]{:S(2)}) collective-permute-start(bf16[224,1536]{1,0:T(8,128)(2,1)} %get-tuple-element.184.refs_0_.refs_2_), channel_id=1, source_target_pairs={{0,4},{1,5},{2,6},{3,7},{4,0},{5,1},{6,2},{7,3},{8,12},{9,13},{10,... | collective-permute-start | bytes 2064392 | tf_op jit(solution)/shard_map/ppermute | solution.py:781
  240.0 32.1 %collective-permute-start.26 = (bf16[224,2304]{1,0:T(8,128)(2,1)}, bf16[224,2304]{1,0:T(8,128)(2,1)}, u32[]{:S(2)}, u32[]{:S(2)}) collective-permute-start(bf16[224,2304]{1,0:T(8,128)(2,1)} %get-tuple-element.195), channel_id=1, source_target_pairs={{0,1},{1,0},{2,3},{3,2},{4,5},{5,4},{6,7},{7,6},{8,9},{9,8},{10,11... | collective-permute-start | bytes 3096584 | tf_op jit(solution)/shard_map/ppermute | solution.py:778
  271.5 25.1 %collective-permute-start.34 = (bf16[448,1152]{1,0:T(8,128)(2,1)}, bf16[448,1152]{1,0:T(8,128)(2,1)}, u32[]{:S(2)}, u32[]{:S(2)}) collective-permute-start(bf16[448,1152]{1,0:T(8,128)(2,1)} %get-tuple-element.209), channel_id=1, source_target_pairs={{0,16},{8,24},{16,0},{24,8},{1,17},{9,25},{17,1},{25,9},{2,18},{10... | collective-permute-start | bytes 3096584 | tf_op jit(solution)/shard_map/ppermute | solution.py:775
  277.9 25.1 %collective-permute-start.33 = (bf16[224,2304]{1,0:T(8,128)(2,1)}, bf16[224,2304]{1,0:T(8,128)(2,1)}, u32[]{:S(2)}, u32[]{:S(2)}) collective-permute-start(bf16[224,2304]{1,0:T(8,128)(2,1)} %get-tuple-element.207.refs_4_), channel_id=1, source_target_pairs={{0,2},{1,3},{2,0},{3,1},{4,6},{5,7},{6,4},{7,5},{8,10},{9,11},{10,... | collective-permute-start | bytes 3096584 | tf_op jit(solution)/shard_map/ppermute | solution.py:781
  278.9 18.5 %collective-permute-start.32 = (bf16[224,1536]{1,0:T(8,128)(2,1)}, bf16[224,1536]{1,0:T(8,128)(2,1)S(1)}, u32[]{:S(2)}, u32[]{:S(2)}) collective-permute-start(bf16[224,1536]{1,0:T(8,128)(2,1)} %get-tuple-element.198.refs_0_.refs_2_), channel_id=1, source_target_pairs={{0,1},{1,0},{2,3},{3,2},{4,5},{5,4},{6,7},{7,6},{8,9},{9,8},{10,11... | collective-permute-start | bytes 2064392 | tf_op jit(solution)/shard_map/ppermute | solution.py:778
  280.5 45.7 %collective-permute-start.35 = (bf16[224,2304]{1,0:T(8,128)(2,1)}, bf16[224,2304]{1,0:T(8,128)(2,1)}, u32[]{:S(2)}, u32[]{:S(2)}) collective-permute-start(bf16[224,2304]{1,0:T(8,128)(2,1)} %get-tuple-element.220), channel_id=1, source_target_pairs={{0,1},{1,0},{2,3},{3,2},{4,5},{5,4},{6,7},{7,6},{8,9},{9,8},{10,11... | collective-permute-start | bytes 3096584 | tf_op jit(solution)/shard_map/ppermute | solution.py:778
  307.1 22.5 %collective-permute-start.36 = (bf16[224,1152]{1,0:T(8,128)(2,1)}, bf16[224,1152]{1,0:T(8,128)(2,1)S(1)}, u32[]{:S(2)}, u32[]{:S(2)}) collective-permute-start(bf16[224,1152]{1,0:T(8,128)(2,1)} %get-tuple-element.222), channel_id=1, source_target_pairs={{0,1},{1,0},{2,3},{3,2},{4,5},{5,4},{6,7},{7,6},{8,9},{9,8},{10,11... | collective-permute-start | bytes 1548296 | tf_op jit(solution)/shard_map/ppermute | solution.py:778
  307.6 56.7 %collective-permute-start.37 = (bf16[224,2304]{1,0:T(8,128)(2,1)}, bf16[224,2304]{1,0:T(8,128)(2,1)}, u32[]{:S(2)}, u32[]{:S(2)}) collective-permute-start(bf16[224,2304]{1,0:T(8,128)(2,1)} %get-tuple-element.235.refs_2_), channel_id=1, source_target_pairs={{0,4},{1,5},{2,6},{3,7},{4,0},{5,1},{6,2},{7,3},{8,12},{9,13},{10,... | collective-permute-start | bytes 3096584 | tf_op jit(solution)/shard_map/ppermute | solution.py:781
  333.7 42.9 %collective-permute-start.38 = (bf16[224,2304]{1,0:T(8,128)(2,1)}, bf16[224,2304]{1,0:T(8,128)(2,1)}, u32[]{:S(2)}, u32[]{:S(2)}) collective-permute-start(bf16[224,2304]{1,0:T(8,128)(2,1)} %get-tuple-element.223.refs_0_.refs_4_), channel_id=1, source_target_pairs={{0,2},{1,3},{2,0},{3,1},{4,6},{5,7},{6,4},{7,5},{8,10},{9,11},{10,... | collective-permute-start | bytes 3096584 | tf_op jit(solution)/shard_map/ppermute | solution.py:781
  340.8 23.6 %collective-permute-start.39 = (bf16[448,896]{1,0:T(8,128)(2,1)}, bf16[448,896]{1,0:T(8,128)(2,1)S(1)}, u32[]{:S(2)}, u32[]{:S(2)}) collective-permute-start(bf16[448,896]{1,0:T(8,128)(2,1)} %get-tuple-element.236), channel_id=1, source_target_pairs={{0,8},{8,0},{16,24},{24,16},{1,9},{9,1},{17,25},{25,17},{2,10},{10... | collective-permute-start | bytes 2408456 | tf_op jit(solution)/shard_map/ppermute | solution.py:772
  389.3 24.8 %collective-permute-start.43 = (bf16[448,1152]{1,0:T(8,128)(2,1)}, bf16[448,1152]{1,0:T(8,128)(2,1)}, u32[]{:S(2)}, u32[]{:S(2)}) collective-permute-start(bf16[448,1152]{1,0:T(8,128)(2,1)} %get-tuple-element.244), channel_id=1, source_target_pairs={{0,8},{8,0},{16,24},{24,16},{1,9},{9,1},{17,25},{25,17},{2,10},{10... | collective-permute-start | bytes 3096584 | tf_op jit(solution)/shard_map/ppermute | solution.py:772
  389.3 25.5 %collective-permute-start.40 = (bf16[224,2304]{1,0:T(8,128)(2,1)}, bf16[224,2304]{1,0:T(8,128)(2,1)}, u32[]{:S(2)}, u32[]{:S(2)}) collective-permute-start(bf16[224,2304]{1,0:T(8,128)(2,1)} %get-tuple-element.237.refs_0_.refs_2_.refs_3_), channel_id=1, source_target_pairs={{0,1},{1,0},{2,3},{3,2},{4,5},{5,4},{6,7},{7,6},{8,9},{9,8},{10,11... | collective-permute-start | bytes 3096584 | tf_op jit(solution)/shard_map/ppermute | solution.py:778
  390.9 22.5 %collective-permute-start.41 = (bf16[224,1152]{1,0:T(8,128)(2,1)S(1)}, bf16[224,1152]{1,0:T(8,128)(2,1)S(1)}, u32[]{:S(2)}, u32[]{:S(2)}) collective-permute-start(bf16[224,1152]{1,0:T(8,128)(2,1)S(1)} %copy-done.8), channel_id=1, source_target_pairs={{0,2},{1,3},{2,0},{3,1},{4,6},{5,7},{6,4},{7,5},{8,10},{9,11},{10,... | collective-permute-start | bytes 1548296 | tf_op jit(solution)/shard_map/ppermute | solution.py:781
  390.9 48.3 %collective-permute-start.44 = (bf16[224,2304]{1,0:T(8,128)(2,1)}, bf16[224,2304]{1,0:T(8,128)(2,1)}, u32[]{:S(2)}, u32[]{:S(2)}) collective-permute-start(bf16[224,2304]{1,0:T(8,128)(2,1)} %get-tuple-element.248.refs_2_), channel_id=1, source_target_pairs={{0,4},{1,5},{2,6},{3,7},{4,0},{5,1},{6,2},{7,3},{8,12},{9,13},{10,... | collective-permute-start | bytes 3096584 | tf_op jit(solution)/shard_map/ppermute | solution.py:781
  391.8 22.3 %collective-permute-start.42 = (bf16[224,896]{1,0:T(8,128)(2,1)}, bf16[224,896]{1,0:T(8,128)(2,1)S(1)}, u32[]{:S(2)}, u32[]{:S(2)}) collective-permute-start(bf16[224,896]{1,0:T(8,128)(2,1)} %get-tuple-element.243), channel_id=1, source_target_pairs={{0,16},{8,24},{16,0},{24,8},{1,17},{9,25},{17,1},{25,9},{2,18},{10... | collective-permute-start | bytes 1204232 | tf_op jit(solution)/shard_map/ppermute | solution.py:775
  419.1 20.1 %collective-permute-start.46 = (bf16[224,1152]{1,0:T(8,128)(2,1)}, bf16[224,1152]{1,0:T(8,128)(2,1)S(1)}, u32[]{:S(2)}, u32[]{:S(2)}) collective-permute-start(bf16[224,1152]{1,0:T(8,128)(2,1)} %get-tuple-element.252), channel_id=1, source_target_pairs={{0,16},{8,24},{16,0},{24,8},{1,17},{9,25},{17,1},{25,9},{2,18},{10... | collective-permute-start | bytes 1548296 | tf_op jit(solution)/shard_map/ppermute | solution.py:775
  419.7 19.5 %collective-permute-start.45 = (bf16[112,896]{1,0:T(8,128)(2,1)}, bf16[112,896]{1,0:T(8,128)(2,1)S(1)}, u32[]{:S(2)}, u32[]{:S(2)}) collective-permute-start(bf16[112,896]{1,0:T(8,128)(2,1)} %get-tuple-element.250), channel_id=1, source_target_pairs={{0,1},{1,0},{2,3},{3,2},{4,5},{5,4},{6,7},{7,6},{8,9},{9,8},{10,11... | collective-permute-start | bytes 602120 | tf_op jit(solution)/shard_map/ppermute | solution.py:778
  443.4 29.8 %collective-permute-start.47 = (bf16[224,2304]{1,0:T(8,128)(2,1)}, bf16[224,2304]{1,0:T(8,128)(2,1)}, u32[]{:S(2)}, u32[]{:S(2)}) collective-permute-start(bf16[224,2304]{1,0:T(8,128)(2,1)} %get-tuple-element.253.refs_0_.refs_2_.refs_4_), channel_id=1, source_target_pairs={{0,1},{1,0},{2,3},{3,2},{4,5},{5,4},{6,7},{7,6},{8,9},{9,8},{10,11... | collective-permute-start | bytes 3096584 | tf_op jit(solution)/shard_map/ppermute | solution.py:778
  443.9 23.7 %collective-permute-start.48 = (bf16[224,1152]{1,0:T(8,128)(2,1)}, bf16[224,1152]{1,0:T(8,128)(2,1)S(1)}, u32[]{:S(2)}, u32[]{:S(2)}) collective-permute-start(bf16[224,1152]{1,0:T(8,128)(2,1)} %get-tuple-element.254.refs_4_), channel_id=1, source_target_pairs={{0,4},{1,5},{2,6},{3,7},{4,0},{5,1},{6,2},{7,3},{8,12},{9,13},{10,... | collective-permute-start | bytes 1548296 | tf_op jit(solution)/shard_map/ppermute | solution.py:781
  445.7 13.7 %collective-permute-start.51 = (f32[1,2944]{1,0:T(1,128)}, f32[1,2944]{1,0:T(1,128)}, u32[]{:S(2)}, u32[]{:S(2)}) collective-permute-start(f32[1,2944]{1,0:T(1,128)} %constant_dynamic-update-slice_fusion.3.refs_10_), channel_id=1, source_target_pairs={{0,8},{8,0},{16,24},{24,16},{1,9},{9,1},{17,25},{25,17},{2,10},{10... | collective-permute-start | bytes 35336 | tf_op jit(solution)/shard_map/ppermute | solution.py:772
  445.7 22.0 %collective-permute-start.49 = (bf16[112,896]{1,0:T(8,128)(2,1)}, bf16[112,896]{1,0:T(8,128)(2,1)S(1)}, u32[]{:S(2)}, u32[]{:S(2)}) collective-permute-start(bf16[112,896]{1,0:T(8,128)(2,1)} %get-tuple-element.255.refs_6_), channel_id=1, source_target_pairs={{0,2},{1,3},{2,0},{3,1},{4,6},{5,7},{6,4},{7,5},{8,10},{9,11},{10,... | collective-permute-start | bytes 602120 | tf_op jit(solution)/shard_map/ppermute | solution.py:781
  447.7 25.5 %collective-permute-start.50 = (bf16[112,1152]{1,0:T(8,128)(2,1)}, bf16[112,1152]{1,0:T(8,128)(2,1)S(1)}, u32[]{:S(2)}, u32[]{:S(2)}) collective-permute-start(bf16[112,1152]{1,0:T(8,128)(2,1)} %get-tuple-element.257), channel_id=1, source_target_pairs={{0,1},{1,0},{2,3},{3,2},{4,5},{5,4},{6,7},{7,6},{8,9},{9,8},{10,11... | collective-permute-start | bytes 774152 | tf_op jit(solution)/shard_map/ppermute | solution.py:778
  459.4 62.9 %collective-permute-start.52 = (bf16[1024,896]{1,0:T(8,128)(2,1)}, bf16[1024,896]{1,0:T(8,128)(2,1)}, u32[]{:S(2)}, u32[]{:S(2)}) collective-permute-start(bf16[1024,896]{1,0:T(8,128)(2,1)} %down_tokens.2.refs_0_), channel_id=1, source_target_pairs={{0,8},{8,0},{16,24},{24,16},{1,9},{9,1},{17,25},{25,17},{2,10},{10... | collective-permute-start | bytes 5505032 | tf_op jit(solution)/shard_map/ppermute | solution.py:772
  477.1 11.1 %collective-permute-start.55 = (bf16[112,1152]{1,0:T(8,128)(2,1)}, bf16[112,1152]{1,0:T(8,128)(2,1)S(1)}, u32[]{:S(2)}, u32[]{:S(2)}) collective-permute-start(bf16[112,1152]{1,0:T(8,128)(2,1)} %get-tuple-element.264.refs_6_), channel_id=1, source_target_pairs={{0,2},{1,3},{2,0},{3,1},{4,6},{5,7},{6,4},{7,5},{8,10},{9,11},{10,... | collective-permute-start | bytes 774152 | tf_op jit(solution)/shard_map/ppermute | solution.py:781
  479.7 19.2 %collective-permute-start.53 = (bf16[224,1152]{1,0:T(8,128)(2,1)}, bf16[224,1152]{1,0:T(8,128)(2,1)S(1)}, u32[]{:S(2)}, u32[]{:S(2)}) collective-permute-start(bf16[224,1152]{1,0:T(8,128)(2,1)} %get-tuple-element.262.refs_2_.refs_5_), channel_id=1, source_target_pairs={{0,1},{1,0},{2,3},{3,2},{4,5},{5,4},{6,7},{7,6},{8,9},{9,8},{10,11... | collective-permute-start | bytes 1548296 | tf_op jit(solution)/shard_map/ppermute | solution.py:778
  483.0 19.2 %collective-permute-start.57 = (bf16[224,1024]{1,0:T(8,128)(2,1)}, bf16[224,1024]{1,0:T(8,128)(2,1)}, u32[]{:S(2)}, u32[]{:S(2)}) collective-permute-start(bf16[224,1024]{1,0:T(8,128)(2,1)} %get-tuple-element.210.refs_0_), channel_id=1, source_target_pairs={{0,8},{8,0},{16,24},{24,16},{1,9},{9,1},{17,25},{25,17},{2,10},{10... | collective-permute-start | bytes 1376264 | tf_op jit(solution)/shard_map/ppermute | solution.py:772
  488.1 14.6 %collective-permute-start.58 = (bf16[224,1536]{1,0:T(8,128)(2,1)}, bf16[224,1536]{1,0:T(8,128)(2,1)}, u32[]{:S(2)}, u32[]{:S(2)}) collective-permute-start(bf16[224,1536]{1,0:T(8,128)(2,1)} %get-tuple-element.245.refs_0_), channel_id=1, source_target_pairs={{0,8},{8,0},{16,24},{24,16},{1,9},{9,1},{17,25},{25,17},{2,10},{10... | collective-permute-start | bytes 2064392 | tf_op jit(solution)/shard_map/ppermute | solution.py:772
  488.2 16.1 %collective-permute-start.59 = (bf16[224,1536]{1,0:T(8,128)(2,1)}, bf16[224,1536]{1,0:T(8,128)(2,1)}, u32[]{:S(2)}, u32[]{:S(2)}) collective-permute-start(bf16[224,1536]{1,0:T(8,128)(2,1)} %get-tuple-element.261.refs_0_), channel_id=1, source_target_pairs={{0,8},{8,0},{16,24},{24,16},{1,9},{9,1},{17,25},{25,17},{2,10},{10... | collective-permute-start | bytes 2064392 | tf_op jit(solution)/shard_map/ppermute | solution.py:772
  502.2 14.8 %collective-permute-start.63 = (f32[1,2944]{1,0:T(1,128)}, f32[1,2944]{1,0:T(1,128)S(1)}, u32[]{:S(2)}, u32[]{:S(2)}) collective-permute-start(f32[1,2944]{1,0:T(1,128)} %get-tuple-element.270.refs_6_), channel_id=1, source_target_pairs={{0,1},{1,0},{2,3},{3,2},{4,5},{5,4},{6,7},{7,6},{8,9},{9,8},{10,11... | collective-permute-start | bytes 35336 | tf_op jit(solution)/shard_map/ppermute | solution.py:778
  502.7 14.3 %collective-permute-start.61 = (bf16[112,896]{1,0:T(8,128)(2,1)}, bf16[112,896]{1,0:T(8,128)(2,1)S(1)}, u32[]{:S(2)}, u32[]{:S(2)}) collective-permute-start(bf16[112,896]{1,0:T(8,128)(2,1)} %get-tuple-element.268.refs_2_), channel_id=1, source_target_pairs={{0,1},{1,0},{2,3},{3,2},{4,5},{5,4},{6,7},{7,6},{8,9},{9,8},{10,11... | collective-permute-start | bytes 602120 | tf_op jit(solution)/shard_map/ppermute | solution.py:778
  504.3 14.5 %collective-permute-start.62 = (bf16[112,1152]{1,0:T(8,128)(2,1)}, bf16[112,1152]{1,0:T(8,128)(2,1)S(1)}, u32[]{:S(2)}, u32[]{:S(2)}) collective-permute-start(bf16[112,1152]{1,0:T(8,128)(2,1)} %get-tuple-element.269.refs_4_), channel_id=1, source_target_pairs={{0,4},{1,5},{2,6},{3,7},{4,0},{5,1},{6,2},{7,3},{8,12},{9,13},{10,... | collective-permute-start | bytes 774152 | tf_op jit(solution)/shard_map/ppermute | solution.py:781
  (58 other events, 288.9 us)

commit v3 on v2

--- a/solution.py
+++ b/solution.py
@@ -12,7 +12,7 @@
 PAIRS = HEADS // 2
 TILE = 256
 BLK = 256
-VMEM_CAP = 63 << 20
+VMEM_CAP = (64 << 20) - (1 << 16)
 bf16, f32 = jnp.bfloat16, jnp.float32
 epsilon = 1e-06
 rope_base = 1000000.0
@@ -80,6 +80,14 @@
     return result
 
 
+def first_lanes(order, v, lanes):
+    def body(v, out):
+        out[...] = v[...]
+
+    spec = fixed((v.shape[0], lanes))
+    return call(order, body, "first_lanes", 0.1, 1, [(v, spec)], [(shaped((v.shape[0], lanes)), spec)])[0]
+
+
 def gate(order, v):
     anywhere = pl.BlockSpec(memory_space=pl.ANY)
 
@@ -106,22 +114,23 @@
     n = len(cuts)
 
     def body(where, gate, up, down, *refs):
-        sends, mine, downs = refs[: 2 * n], refs[2 * n : 3 * n], refs[3 * n :]
-
-        def put(targets, core, cut):
+        sends, mine, downs = refs[:n], refs[n : 2 * n], refs[2 * n :]
+
+        def put(ref, core, cut):
             w, off = cut
-            for src, (ref, start) in zip((gate, up), targets):
+            for m, src in enumerate((gate, up)):
                 for side in (0, 1):
+                    lo = (2 * m + side) * w
                     a = (2 * side + core) * ff + off
-                    ref[:, start + side * w : start + side * w + w] = src[:, a : a + w]
+                    ref[:, lo : lo + w] = src[:, a : a + w]
 
         for core in (0, 1):
 
             @pl.when(where[CORE] == core)
             def _():
-                for k, (cut, ref) in enumerate(zip(cuts, mine)):
-                    put(((ref, 0), (ref, 2 * cut[0])), core, cut)
-                    put(((sends[2 * k], 0), (sends[2 * k + 1], 0)), 1 - core, cut)
+                for cut, ref, send in zip(cuts, mine, sends):
+                    put(ref, core, cut)
+                    put(send, 1 - core, cut)
 
         for (w, off), part in zip(cuts, downs):
             for lo in range(0, w, 128):
@@ -133,10 +142,10 @@
         order,
         body,
         "split_weights",
-        2 + 2 * n,
+        0.1,
         1,
         [(where, SCALARS)] + [whole(a) for a in (w_gate, w_up, w_down)],
-        [(shaped((own, 2 * w)), fixed((own, 2 * w))) for w, _ in cuts for _ in (0, 1)]
+        [(shaped((own, 4 * w)), fixed((own, 4 * w))) for w, _ in cuts]
         + [(shaped((own, 4 * w)), fixed((own, 4 * w))) for w, _ in cuts]
         + [(shaped((d, w)), fixed((d, w))) for w, _ in cuts],
     )
@@ -148,7 +157,7 @@
     n = len(mine)
 
     def body(where, *refs):
-        cores, refs = refs[: 2 * n], refs[2 * n :]
+        cores, refs = refs[:n], refs[n:]
         mine, downs, extras, outs = refs[:n], refs[n : 2 * n], refs[2 * n : 2 * n + len(extra)], refs[2 * n + len(extra) :]
         for group, out in zip(groups, outs):
             at6 = 0
@@ -161,29 +170,49 @@
 
                 @pl.when(where[CORE] != where[Y])
                 def _():
-                    out[:, at6 : at6 + 2 * w] = cores[2 * k][...]
-                    out[:, at6 + 2 * w : at6 + 4 * w] = cores[2 * k + 1][...]
+                    out[:, at6 : at6 + 4 * w] = cores[k][...]
 
                 for h in (0, 1):
                     rows = pl.ds(pl.multiple_of((2 * where[Y] + h) * own, 16), own)
                     out[:, at6 + (4 + h) * w : at6 + (5 + h) * w] = downs[k][rows, :]
                 at6 += 6 * w
-        if extras:
-            outs[-1][:own, :] = extras[0][...]
-            outs[-1][own:, :] = extras[1][...]
+        at6 = sum(6 * widths[k] for k in groups[0])
+        for e in extras:
+            outs[0][:, at6 : at6 + e.shape[1]] = e[...]
+            at6 += e.shape[1]
 
     whole = lambda a: (a, fixed(a.shape))
     totals = [sum(6 * widths[k] for k in group) for group in groups]
+    totals[0] += sum(e.shape[1] for e in extra)
     return call(
         order,
         body,
         "pack_weights",
-        2 + n,
+        0.1,
         1,
         [(where, SCALARS)] + [whole(a) for a in (*core_rows, *mine, *downs, *extra)],
-        [(shaped((own, m)), fixed((own, m))) for m in totals]
-        + [(shaped((2 * own, e.shape[1])), fixed((2 * own, e.shape[1]))) for e in extra[:1]],
-    )
+        [(shaped((own, m)), fixed((own, m))) for m in totals],
+    )
+
+
+def side_by_side(order, parts):
+    rows, width = parts[0].shape[0], sum(p.shape[1] for p in parts)
+
+    def body(*refs):
+        lo = 0
+        for ref in refs[:-1]:
+            refs[-1][:, lo : lo + ref.shape[1]] = ref[...]
+            lo += ref.shape[1]
+
+    return call(
+        order,
+        body,
+        "side_by_side",
+        1,
+        1,
+        [(p, fixed(p.shape)) for p in parts],
+        [(shaped((rows, width)), fixed((rows, width)))],
+    )[0]
 
 
 def place_rows(where, refs, rows, target):
@@ -232,7 +261,7 @@
         order,
         body,
         "project",
-        10,
+        0.1,
         t // TILE,
         [
             (where, SCALARS),
@@ -313,7 +342,7 @@
         order,
         body,
         "attend",
-        4 * count,
+        0.1,
         count,
         [
             (segments.reshape(t, 1), fixed((t, 1))),
@@ -343,12 +372,8 @@
 
         @pl.when(step == 0)
         def _():
-            if running:
-                dkacc[...] = dk_in[...]
-                dvacc[...] = dv_in[...]
-            else:
-                dkacc[...] = jnp.zeros_like(dkacc)
-                dvacc[...] = jnp.zeros_like(dvacc)
+            dkacc[...] = jnp.zeros_like(dkacc)
+            dvacc[...] = jnp.zeros_like(dvacc)
 
         left = lax.broadcasted_iota(jnp.int32, (t, 2 * HD), 1) < HD
         along = do[...].astype(f32) * (o[...].astype(f32) + o_rest[...].astype(f32))
@@ -376,30 +401,30 @@
 
         @pl.when(step == count - 1)
         def _():
+            one = lambda a: jnp.where(left, a[0] + pltpu.roll(a[1], HD, 1), pltpu.roll(a[2], HD, 1) + a[3])
             if not running:
-                dk[...] = dkacc[...]
-                dv[...] = dvacc[...]
+                dk[...] = one(dkacc)
+                dv[...] = one(dvacc)
                 return
             lanes = lax.broadcasted_iota(jnp.int32, (t, 2 * HD), 1)
-            one = lambda a: jnp.where(left, a[0] + pltpu.roll(a[1], HD, 1), pltpu.roll(a[2], HD, 1) + a[3])
-            g = one(dkacc)
+            g = one(dkacc) + dk_in[...]
             dk[...] = (g * cos[...] - swap_halves(g, lanes) * sin[...]).astype(bf16)
-            dv[...] = one(dvacc).astype(bf16)
+            dv[...] = (one(dvacc) + dv_in[...]).astype(bf16)
 
     lane = pl.BlockSpec((t, 2 * HD), lambda p: (0, p + first))
     out_lane = pl.BlockSpec((t, 2 * HD), lambda p: (0, p))
     wide = (4, t, 2 * HD)
-    sums = (shaped((t, 2 * HD)), fixed((t, 2 * HD))) if running else (shaped(wide, f32), fixed(wide))
+    sums = (shaped((t, 2 * HD), bf16 if running else f32), fixed((t, 2 * HD)))
     return call(
         order,
         body,
         "attend_back",
-        6 * count,
+        1 + count,
         count,
         [(q, lane), (do, out_lane), (o, out_lane), (o_rest, out_lane), (kx, fixed(wide)), (vz, fixed(wide))]
         + [(cos, fixed(cos.shape)), (sin, fixed(sin.shape))]
         + [(p, pl.BlockSpec((2,) + p.shape[1:], lambda i: (i, 0, 0))) for p in probs]
-        + [(r, fixed(wide)) for r in running],
+        + [(r, fixed(r.shape)) for r in running],
         [(shaped((t, count * 2 * HD)), out_lane), sums, sums],
         [pltpu.VMEM((t, t), bf16)] * 2 + [pltpu.VMEM(wide, f32)] * 2,
     )
@@ -407,15 +432,17 @@
 
 def join_output(order, where, tokens, mixed, own_w, across, core, gain):
     t, d = tokens.shape
+    steps = t // TILE
     rows = own_w.shape[0]
     n = len(mixed)
 
     def body(where, tokens, own_w, across, core, gain, *refs):
-        mixed, (resid, normed, w) = refs[:n], refs[n:]
+        mixed, resid, w, normed = refs[:n], refs[n], refs[n + 1], refs[n + 2 :]
 
         @pl.when(pl.program_id(0) == 0)
         def _():
-            place_rows(where, (own_w[...], across[:rows, :], core[...], across[rows:, :]), rows, w)
+            lo = across.shape[1] - 2 * d
+            place_rows(where, (own_w[...], across[:, lo : lo + d], core[...], across[:, lo + d :]), rows, w)
 
         v, lo = tokens[...].astype(f32), 0
         for m in mixed:
@@ -423,35 +450,51 @@
             lo += m.shape[1]
         resid[...] = v
         inverse = lax.rsqrt(jnp.mean(v * v, axis=-1, keepdims=True) + epsilon)
-        normed[...] = (v * inverse * gain[...]).astype(bf16)
+        low = (v * inverse * gain[...]).astype(bf16)
+        for k, out in enumerate(normed):
+
+            @pl.when(pl.program_id(0) // (steps // 2) == k)
+            def _():
+                out[...] = low
 
     return call(
         order,
         body,
         "join_output",
-        7,
-        t // TILE,
+        0.1,
+        steps,
         [(where, SCALARS), (tokens, by_rows(TILE, d))]
         + [(a, fixed(a.shape)) for a in (own_w, across, core, gain)]
         + [(m, by_rows(TILE, m.shape[1])) for m in mixed],
         [
             (shaped((t, d), f32), by_rows(TILE, d)),
-            (shaped((t, d)), by_rows(TILE, d)),
             (shaped((4 * rows, d)), fixed((4 * rows, d))),
+        ]
+        + [
+            (shaped((t // 2, d)), pl.BlockSpec((TILE, d), lambda i, k=k: (jnp.clip(i - k * steps // 2, 0, steps // 2 - 1), 0)))
+            for k in (0, 1)
         ],
     )
 
 
-def ffn_part(order, where, n2, dy, mine, core_rows, x_rows, y_rows, down, cut, at6, tt=512):
-    t, d = n2[0].shape
+def ffn_part(order, where, n2, dy, mine, core_rows, x_rows, y_rows, down, cut, at6):
+    t, d = dy[0].shape
     w, off = cut
+    tt = t // 2
     own = mine.shape[0]
     half = d // 2
     steps = t // tt
 
-    def body(where, n2a, n2b, dya, dyb, mine, core_gate, core_up, x_rows, y_rows, down, hid, dgu, keep, send, wt, acc):
+    def body(where, dya, dyb, mine, core_rows, x_rows, y_rows, down, *refs):
+        n2, (hid, dgu, keep, send, weights, acc, wt, tokens, copied) = refs[: len(refs) - 9], refs[-9:]
         step = pl.program_id(0)
         x, c, y = where[0], where[1], where[2]
+        copy_out = pltpu.make_async_copy(wt, weights, copied)
+        for k, ref in enumerate(n2):
+
+            @pl.when(step == k)
+            def _():
+                tokens[...] = ref[...]
 
         @pl.when(step == 0)
         def _():
@@ -459,9 +502,7 @@
                 wt[pl.ds(pl.multiple_of(s * own, 16), own), : 4 * w] = ref[:, at : at + 4 * w]
 
             put(mine, 2 * x + c, 0)
-            other = pl.ds(pl.multiple_of((2 * x + 1 - c) * own, 16), own)
-            wt[other, : 2 * w] = core_gate[...]
-            wt[other, 2 * w : 4 * w] = core_up[...]
+            put(core_rows, 2 * x + 1 - c, 0)
             put(x_rows, 2 * (1 - x) + y)
             put(y_rows, 2 * (1 - x) + 1 - y)
             for side in (0, 1):
@@ -475,11 +516,11 @@
                             at = pl.ds(pl.multiple_of((2 * h + part) * own, 16), own)
                             wt[at, lo : lo + w] = ref[:, at6 + (4 + part) * w : at6 + (5 + part) * w]
 
+            copy_out.start()
             acc[...] = jnp.zeros_like(acc)
 
-        first = step < steps
-        a = jnp.where(first, n2a[...], n2b[...])
-        b = jnp.where(first, dya[...], dyb[...])
+        a = tokens[...]
+        b = jnp.where(step < steps, dya[...], dyb[...])
         for lo in range(0, 2 * w, BLK):
             hi = min(lo + BLK, 2 * w)
             g, u, v = slice(lo, hi), slice(2 * w + lo, 2 * w + hi), slice(4 * w + lo, 4 * w + hi)
@@ -498,6 +539,7 @@
 
         @pl.when(step == 2 * steps - 1)
         def _():
+            copy_out.wait()
             for ref, side in ((keep, x), (send, 1 - x)):
                 at = pl.ds(pl.multiple_of(side * half, 16), half)
                 ref[:, : 4 * w] = acc[at, : 4 * w].astype(bf16)
@@ -517,22 +559,27 @@
         order,
         body,
         "ffn_part",
-        5 + w // 16,
+        5 + w // 16 if off else 0.1,
         2 * steps,
-        [(where, SCALARS), (n2[0], early), (n2[1], late), (dy[0], early), (dy[1], late)]
-        + [whole(a) for a in (mine, *core_rows, x_rows, y_rows, down)],
+        [(where, SCALARS), (dy[0], early), (dy[1], late)]
+        + [whole(a) for a in (mine, core_rows, x_rows, y_rows, down, *n2)],
         [
             (shaped((2 * t, 2 * w)), by_rows(tt, 2 * w)),
             (shaped((2 * t, 4 * w)), by_rows(tt, 4 * w)),
             (shaped((half, 6 * w)), fixed((half, 6 * w))),
             (shaped((half, 6 * w)), fixed((half, 6 * w))),
-            (shaped((d, 6 * w)), fixed((d, 6 * w))),
+            (shaped((d, 6 * w)), pl.BlockSpec(memory_space=pl.ANY)),
         ],
-        [pltpu.VMEM((d, 6 * w), f32)],
-    )
-
-
-def sum_parts(order, name, us, parts, weights, lanes, block, tokens, apart=False, tt=256):
+        [
+            pltpu.VMEM((d, 6 * w), f32),
+            pltpu.VMEM((d, 6 * w), bf16),
+            pltpu.VMEM((tt, d), bf16),
+            pltpu.SemaphoreType.DMA(()),
+        ],
+    )
+
+
+def sum_parts(order, name, us, parts, weights, lanes, block, tokens, apart=False, add=None, pieces=(), tt=256):
     d = weights[0].shape[0]
     t = parts[0].shape[0] // 2
     n = len(parts)
@@ -545,7 +592,18 @@
         for part, weight in zip(refs[:n], refs[n : 2 * n]):
             s = nt(part[...], weight[...])
             total = s if total is None else total + s
-        for out, (first, count, _) in zip(refs[2 * n :], outs):
+        refs = refs[2 * n :]
+        if pieces:
+            more, others, refs = refs[0], refs[1 : 1 + len(pieces)], refs[1 + len(pieces) :]
+            other = refs[-1]
+            for at, ref in enumerate(others):
+
+                @pl.when(step == at)
+                def _():
+                    other[...] = ref[...]
+
+            total = total + more[...] + other[...].astype(f32)
+        for out, (first, count, _) in zip(refs, outs):
 
             @pl.when((step >= first) & (step < first + count))
             def _():
@@ -559,7 +617,7 @@
         if half and apart:
             outs += [(at * steps + k, 1, bf16) for k in range(steps)]
         else:
-            outs.append((at * steps, steps, bf16 if half else f32))
+            outs.append((at * steps, steps, bf16 if half or pieces else f32))
 
     start = tokens[0] * steps
     return call(
@@ -569,8 +627,11 @@
         us,
         k * steps,
         [(p, pl.BlockSpec((tt, p.shape[1]), lambda i: ((i + start) % (2 * steps), 0))) for p in parts]
-        + [(w, pl.BlockSpec((d, n), lambda i: (0, block))) for w, n in zip(weights, lanes)],
+        + [(w, pl.BlockSpec((d, n), lambda i: (0, block))) for w, n in zip(weights, lanes)]
+        + ([(add, by_rows(tt, d))] if pieces else [])
+        + [(p, fixed(p.shape)) for p in pieces],
         [(shaped((count * tt, d), kind), spec(first, count)) for first, count, kind in outs],
+        [pltpu.VMEM((tt, d), bf16)] if pieces else [],
     )
 
 
@@ -625,7 +686,7 @@
     )
 
 
-def weight_grads(order, where, us, pairs):
+def weight_grads(order, where, pairs, shares):
     d = sum(a.shape[1] for a in pairs[0][0])
     width = sum(g.shape[1] for _, g in pairs)
     own = d // 4
@@ -636,28 +697,36 @@
     place = [[next(i for i, b in enumerate(lefts) if b is a) for a in pieces] for pieces, _ in pairs]
 
     def body(where, *refs):
-        left, right, (keep, send) = refs[: len(lefts)], refs[len(lefts) : -2], refs[-2:]
+        left, right, refs = refs[: len(lefts)], refs[len(lefts) : len(lefts) + len(rights)], refs[len(lefts) + len(rights) :]
+        keep, sends, grad = refs[0], refs[1:-1], refs[-1]
         c = where[CORE]
         lo = 0
         for spots, g in zip(place, right):
             hi = lo + g.shape[1]
-            grad = jnp.concatenate([tn(left[i][...], g[...]).astype(bf16) for i in spots], 0)
-            for core in (0, 1):
-                rows = jnp.concatenate([grad[core * own : (core + 1) * own], grad[(2 + core) * own : (3 + core) * own]], 0)
-
-                @pl.when(c == core)
-                def _():
-                    keep[:, lo:hi] = rows
-
-                @pl.when(c != core)
-                def _():
-                    send[:, lo:hi] = rows
-
+            at = 0
+            for i in spots:
+                grad[at : at + left[i].shape[1], lo:hi] = tn(left[i][...], g[...]).astype(bf16)
+                at += left[i].shape[1]
             lo = hi
-
-    out = (shaped((2 * own, width)), fixed((2 * own, width)))
+        for side in (0, 1):
+            rows = lambda core: pl.ds(pl.multiple_of((2 * side + core) * own, 16), own)
+            at = slice(side * own, (side + 1) * own)
+            keep[at, :] = grad[rows(c), :]
+            lo = 0
+            for ref in sends:
+                ref[at, :] = grad[rows(1 - c), lo : lo + ref.shape[1]]
+                lo += ref.shape[1]
+
+    out = lambda lanes: (shaped((2 * own, lanes)), fixed((2 * own, lanes)))
     return call(
-        order, body, "weight_grads", us, 1, [(where, SCALARS)] + [(a, fixed(a.shape)) for a in (*lefts, *rights)], [out, out]
+        order,
+        body,
+        "weight_grads",
+        0.1,
+        1,
+        [(where, SCALARS)] + [(a, fixed(a.shape)) for a in (*lefts, *rights)],
+        [out(lanes) for lanes in (width, *shares)],
+        [pltpu.VMEM((d, width), bf16)],
     )
 
 
@@ -691,7 +760,7 @@
         order,
         body,
         "finish_tokens",
-        8,
+        0.1,
         t // TILE,
         [(tokens, rows), (gain, fixed(gain.shape)), (full_qkv, fixed(full_qkv.shape)), (d_resid, rows)]
         + [(p, by_rows(TILE, p.shape[1])) for p in d_parts],
@@ -790,17 +859,22 @@
             bit *= 2
 
 
-def split_sum(axis, keep, got):
+def split_sum(axis, keep, *got):
     half = keep.shape[0] // 2
     shape = shaped((half, keep.shape[1]), keep.dtype)
 
-    def body(where, keep, got, mine, send):
+    def body(where, keep, *refs):
+        *got, mine, send = refs
         n = where[axis]
         for ref, h in ((mine, n), (send, 1 - n)):
             at = pl.ds(pl.multiple_of(h * half, 16), half)
-            ref[...] = (keep[at, :].astype(f32) + got[at, :].astype(f32)).astype(ref.dtype)
-
-    return body, [(keep, fixed(keep.shape)), (got, fixed(got.shape))], [shape, shape]
+            lo = 0
+            for g in got:
+                hi = lo + g.shape[1]
+                ref[:, lo:hi] = (keep[at, lo:hi].astype(f32) + g[at, :].astype(f32)).astype(ref.dtype)
+                lo = hi
+
+    return body, [(a, fixed(a.shape)) for a in (keep, *got)], [shape, shape]
 
 
 def whole_sum(v, got):
@@ -819,6 +893,36 @@
         out[pl.ds(pl.multiple_of((1 - n) * rows, 16), rows), :] = other[...].astype(dtype)
 
     return body, [(mine, fixed(mine.shape)), (other, fixed(other.shape))], [shaped((2 * rows, width), dtype)]
+
+
+def in_order_lanes(axis, mine, other, widths):
+    rows = mine.shape[0]
+
+    def body(where, mine, other, *outs):
+        n = where[axis]
+        lo = 0
+        for out in outs:
+            hi = lo + out.shape[1]
+            out[pl.ds(pl.multiple_of(n * rows, 16), rows), :] = mine[:, lo:hi].astype(f32)
+            out[pl.ds(pl.multiple_of((1 - n) * rows, 16), rows), :] = other[:, lo:hi].astype(f32)
+            lo = hi
+
+    return (
+        body,
+        [(mine, fixed(mine.shape)), (other, fixed(other.shape))],
+        [shaped((2 * rows, w), f32) for w in widths],
+    )
+
+
+def lanes_sum(v, got, widths):
+    def body(where, v, got, *outs):
+        lo = 0
+        for out in outs:
+            hi = lo + out.shape[0]
+            out[...] = (v[:, lo:hi] + got[:, lo:hi])[0]
+            lo = hi
+
+    return body, [(v, fixed(v.shape)), (got, fixed(got.shape))], [shaped((w,), v.dtype) for w in widths]
 
 
 def rows_for_core(half, other, lanes):
@@ -909,20 +1013,19 @@
     return half, other, links.core(rows)
 
 
-def owned_steps(order, links, keep, send, how):
-    mine, send = yield split_sum(X, keep, links.core(send))
+def owned_steps(order, links, keep, sends, how, widths):
+    mine, send = yield split_sum(X, keep, *[links.core(send) for send in sends])
     mine, send = yield split_sum(Y, mine, links.across(send))
     half, other = yield from replica_steps(order, links, mine, send, how)
-    (rows,) = yield in_order(Y, half, other, f32)
-    return rows
-
-
-def small_steps(links, v):
-    for move in (links.core, links.across, links.beside):
+    return (yield in_order_lanes(Y, half, other, widths))
+
+
+def small_steps(links, v, widths):
+    moves = [links.core, links.beside, links.across]
+    moves += [functools.partial(links.far, bit=bit) for bit in links.bits()]
+    for move in moves[:-1]:
         (v,) = yield whole_sum(v, move(v))
-    for bit in links.bits():
-        (v,) = yield whole_sum(v, links.far(v, bit))
-    return v
+    return (yield lanes_sum(v, moves[-1](v), widths))
 
 
 def norm_back(values, gain_vector, upstream):
@@ -975,42 +1078,50 @@
     stages = [[[0]], [[1], list(pieces[2:])]] if len(cuts) > 2 else [[[n] for n in pieces]]
     group_of = [number for number, group in enumerate(g for stage in stages for g in stage) for _ in group]
 
-    own_qkv = jnp.concatenate([w_query, w_key, w_value], 1)
+    own_qkv = side_by_side(order, [w_query, w_key, w_value])
     across_qkv, core_qkv = links.across(own_qkv), links.core(own_qkv)
     dy = (cotangent, links.core(cotangent))
-    core_output = links.core(w_output)
-    mine, downs, core_rows, at6 = [], [], [], []
     order.wait(cos, sin)
-    for number, stage in enumerate(stages):
+    mine, downs, core_rows, x_rows, y_rows, at6 = [], [], [], [], [], []
+
+    def split_stage(stage):
         chosen = [cuts[n] for group in stage for n in group]
         k = len(chosen)
         parts = split_weights(order, where, w_gate, w_up, w_down, chosen)
-        core_rows.append([links.core(v) for v in parts[: 2 * k]])
-        mine.append(parts[2 * k : 3 * k])
-        downs.append(parts[3 * k :])
-        for group in stage:
-            at6 += [sum(6 * cuts[m][0] for m in group[:k]) for k in range(len(group))]
-        if number == 0:
-            across_qkv = gate(order, across_qkv)
-            far_qkv = links.core(across_qkv)
-    x_rows = []
-    for number, stage in enumerate(stages):
-        sizes = [len(group) for group in stage]
-        local = [list(range(sum(sizes[:k]), sum(sizes[: k + 1]))) for k in range(len(sizes))]
+        core_rows.extend(links.core(v) for v in parts[:k])
+        mine.extend(parts[k : 2 * k])
+        downs.extend(parts[2 * k :])
+
+    def pack_stage(stage, extra=()):
+        chosen = [n for group in stage for n in group]
+        first = chosen[0]
         packed = pack_weights(
             order,
             where,
-            core_rows[number],
-            mine[number],
-            downs[number],
-            local,
-            [w_output, core_output] if number == 0 else [],
+            [core_rows[n] for n in chosen],
+            [mine[n] for n in chosen],
+            [downs[n] for n in chosen],
+            [[n - first for n in group] for group in stage],
+            extra,
         )
-        if number == 0:
-            *packed, joined = packed
-            across_output = links.across(joined)
-        x_rows += [links.across(v) for v in packed]
-    mine, downs, core_rows = ([v for part in parts for v in part] for parts in (mine, downs, core_rows))
+        for group in stage:
+            at6.extend(sum(6 * cuts[m][0] for m in group[:k]) for k in range(len(group)))
+        x_rows.extend(links.across(v) for v in packed)
+
+    def forward_rows(*groups):
+        for g in groups:
+            if g < len(x_rows) and g == len(y_rows):
+                if g == 0:
+                    forwarded = first_lanes(order, x_rows[0], sum(6 * cuts[n][0] for n in stages[0][0]))
+                else:
+                    forwarded = x_rows[g] = gate(order, x_rows[g])
+                y_rows.append(links.beside(forwarded))
+
+    split_stage(stages[0])
+    core_output = links.core(w_output)
+    across_qkv = gate(order, across_qkv)
+    far_qkv = links.core(across_qkv)
+    pack_stage(stages[0], [w_output, core_output])
 
     bias = jnp.concatenate([bias_query, bias_key, bias_value])[None, :]
     order.wait(dy[1])
@@ -1018,28 +1129,25 @@
         order, where, tokens, gain_attn, own_qkv, across_qkv, core_qkv, far_qkv, bias, cos, sin
     )
     middle = 3
-    y_rows = []
-
-    def forward_rows(*groups):
-        for g in groups:
-            if g < len(x_rows) and g == len(y_rows):
-                x_rows[g] = gate(order, x_rows[g])
-                y_rows.append(links.beside(x_rows[g]))
-
+    for stage in stages[1:]:
+        split_stage(stage)
     first_part = attend(order, doc_ids, queries, kx, vx, 0, middle)
     forward_rows(0)
+    for stage in stages[1:]:
+        pack_stage(stage)
     second_part = attend(order, doc_ids, queries, kx, vx, middle, PAIRS)
-    forward_rows(1)
     order.wait(y_rows[0])
     mixed, mixed_rest, inverse_sums = zip(first_part[:3], second_part[:3])
     probs = (first_part[3:], second_part[3:])
-    residual, normed_two, full_output = join_output(
-        order, where, tokens, mixed, w_output, across_output, core_output, gain_ffn
-    )
-    n2 = (normed_two, links.core(normed_two))
+    residual, full_output, *normed_two = join_output(
+        order, where, tokens, mixed, w_output, x_rows[0], core_output, gain_ffn
+    )
+    n2 = [*normed_two, *[links.core(v) for v in normed_two]]
+
+    forward_rows(1)
 
     chains, hids, dgus, weights = [], [], [], []
-    how = ["whole"] * len(cuts)
+    how = ["whole"] + ["halves"] * (len(cuts) - 2) + ["whole"]
 
     def step(*which):
         advance(order, where, [chains[n] for n in which if n < len(chains)])
@@ -1050,7 +1158,7 @@
         if n >= 2:
             step(0)
         hid, dgu, keep, send, weight = ffn_part(
-            order, where, n2, dy, mine[n], core_rows[2 * n : 2 * n + 2], x_rows[g], y_rows[g], downs[n], cuts[n], at6[n]
+            order, where, n2, dy, mine[n], core_rows[n], x_rows[g], y_rows[g], downs[n], cuts[n], at6[n]
         )
         hids.append(hid), dgus.append(dgu), weights.append(weight)
         chains.append(Chain(ffn_steps(order, links, keep, send, cuts[n][0], how[n])))
@@ -1064,54 +1172,58 @@
     d_resid, d_attn, grad_gain_ffn, *scaled = turn_back(
         order, dn2, dn2_other, residual, cotangent, gain_ffn, full_output, inverse_sums
     )
-    step(0, 1, 3)
+    step(1)
 
     both = [
         (queries, scaled[n], mixed[n], mixed_rest[n], kx, vz, cos, sin, probs[n], *span)
         for n, span in enumerate(((0, middle), (middle, PAIRS)))
     ]
     dq_first, *running = attend_back(order, *both[0], ())
-    step(2, 3)
+    step(1, 2, 3)
+    out_keep, *out_sends = weight_grads(order, where, [(mixed, d_attn)], [d // 2 // 128 * 128, d - d // 2 // 128 * 128])
+    out_chain = Chain(owned_steps(order, links, out_keep, out_sends, "whole", [d]))
+    dq_second, d_key, d_value = attend_back(order, *both[1], running)
+    chains.append(out_chain)
+    n_out = len(chains) - 1
+    step(0, 1, 2, 3, n_out)
+    d_parts = [dq_first, dq_second, d_key, d_value]
+    share = (qw + 2 * kw) // 3 // 128 * 128
+    qkv_keep, *qkv_sends = weight_grads(
+        order, where, [((normed,), p) for p in d_parts], [share, share, qw + 2 * kw - 2 * share]
+    )
+    chains.append(Chain(owned_steps(order, links, qkv_keep, qkv_sends, "whole", [qw, kw, kw])))
+    n_qkv = n_out + 1
+    step(3, n_out, n_qkv)
+    grad_tokens, grad_gain_attn, grad_biases = finish_tokens(order, tokens, gain_attn, d_parts, full_qkv, d_resid)
     chains.append(
-        Chain(owned_steps(order, links, *weight_grads(order, where, 5, [(mixed, d_attn)]), "whole"))
-    )
-    out_n = len(chains) - 1
-    dq_second, d_key, d_value = attend_back(order, *both[1], running)
-    step(1, 2, out_n)
-    d_parts = [dq_first, dq_second, d_key, d_value]
-    chains.append(
-        Chain(owned_steps(order, links, *weight_grads(order, where, 8, [((normed,), p) for p in d_parts]), "whole"))
-    )
-    qkv_n = out_n + 1
-    step(1, 3, out_n, qkv_n)
-    grad_tokens, grad_gain_attn, grad_biases = finish_tokens(order, tokens, gain_attn, d_parts, full_qkv, d_resid)
-    chains.append(Chain(small_steps(links, jnp.concatenate([grad_gain_attn, grad_gain_ffn, grad_biases], 1))))
-    small_n = qkv_n + 1
-    step(2, out_n, qkv_n)
+        Chain(small_steps(links, jnp.concatenate([grad_gain_attn, grad_gain_ffn, grad_biases], 1), [d, d, qw, kw, kw]))
+    )
+    n_small = n_qkv + 1
+    step(1, 2, n_qkv, n_small)
     down_lanes = [2 * w for w, _ in cuts]
-    (out_send,) = sum_parts(order, "down_tokens", 11, hids, weights, down_lanes, 2, (1,))
-    out_other = links.core(out_send)
-    step(2, 3, out_n, qkv_n, small_n)
-    (out,) = sum_parts(order, "down_tokens", 11, hids, weights, down_lanes, 2, (0,))
-    output = (residual + out + out_other.astype(f32)).astype(bf16)
+    out_other = [links.core(v) for v in sum_parts(order, "down_tokens", 0.1, hids, weights, down_lanes, 2, (1,), True)]
+    step(2, n_out, n_qkv)
+    (output,) = sum_parts(order, "down_tokens", 0.1, hids, weights, down_lanes, 2, (0,), False, residual, out_other)
+    step(3, n_out, n_qkv, n_small)
+    step(2, n_small)
+    step(3, n_out, n_qkv, n_small)
     while any(chain.result is None for chain in chains[: len(cuts)]):
         step(*range(len(chains)))
     grad_gate, grad_up, grad_down = assemble(order, where, *zip(*(chain.result for chain in chains[: len(cuts)])), cuts, ff)
     while any(chain.result is None for chain in chains):
         step(*range(len(chains)))
-    grad_output, grad_qkv, small = (chain.result for chain in chains[len(cuts) :])
-    small = small[0]
+    (grad_output,), grad_qkv, small = (chain.result for chain in chains[len(cuts) :])
     return (
         output,
         grad_tokens,
-        small[:d],
-        small[d : 2 * d],
-        grad_qkv[:, :qw],
-        small[2 * d : 2 * d + qw],
-        grad_qkv[:, qw : qw + kw],
-        small[2 * d + qw : 2 * d + qw + kw],
-        grad_qkv[:, qw + kw :],
-        small[2 * d + qw + kw :],
+        small[0],
+        small[1],
+        grad_qkv[0],
+        small[2],
+        grad_qkv[1],
+        small[3],
+        grad_qkv[2],
+        small[4],
         grad_output,
         grad_gate,
         grad_up,

time: 548 us -> 490 us (0.89)
  waiting for transfers between devices: 108 us -> 69.8 us
  local copies, waits for them, and re-layouts: 27.9 us -> 10.2 us
    ppermute x14 -> x16, waiting for transfers between devices: 63.4 us -> 45.3 us  [far(): lax.ppermute(v, 'replica', [(i, i ^ bit) for i in range(self.replicas)])]
    ppermute x16, waiting for transfers between devices: 13 us -> 0.68 us  [beside(): lax.ppermute(v, 'replica', [(i, i ^ 1) for i in range(self.replicas)])]
    unnamed x82 -> x6, local copies, waits for them, and re-layouts: 14.8 us -> 2.58 us
    ppermute x12 -> x11, waiting for transfers between devices: 28.1 us -> 17.3 us  [across(): return lax.ppermute(v, 'shard', [(i, i ^ 2) for i in range(self.shards)])]
    slice x4 -> x0, local copies, waits for them, and re-layouts: 6.23 us -> none  [the longest x1 2.07 us: on_device(): grad_qkv[:, :qw]]
    pallas_call x40 -> x41, Pallas kernels: 348 us -> 350 us  [call(): pl.pallas_call(kernel, grid=(grid,), in_specs=[pl.BlockSpec(memory_space=...]
    ppermute x14 -> x16, starting transfers between devices: 13 us -> 11.8 us  [far(): lax.ppermute(v, 'replica', [(i, i ^ bit) for i in range(self.replicas)])]
    ppermute x12 -> x11, starting transfers between devices: 14.4 us -> 14.1 us  [across(): return lax.ppermute(v, 'shard', [(i, i ^ 2) for i in range(self.shards)])]
  transfers between devices with their start and end apart: 67 -> 71, of which waited for: 25 -> 19; matrix products, arithmetic and copies ran while one was open for 4% -> 3% of each run, Pallas kernels for 59% -> 68%
where the time goes in v3:
time: 490 us; the launch traced here: 482 us
  Pallas kernels  350 us (71%)
  waiting for transfers between devices  69.8 us (14%)
  starting transfers between devices  46.8 us (10%)
  local copies, waits for them, and re-layouts  10.2 us (2%)
    pallas_call x41, Pallas kernels, call(): pl.pallas_call(kernel, grid=(grid,), in_specs=[pl.BlockSpec(memory_space=...  350 us
    ppermute x16, waiting for transfers between devices, far(): lax.ppermute(v, 'replica', [(i, i ^ bit) for i in range(self.replicas)])  45.3 us
    ppermute x11, waiting for transfers between devices, across(): return lax.ppermute(v, 'shard', [(i, i ^ 2) for i in range(self.shards)])  17.3 us
    ppermute x16, starting transfers between devices, beside(): lax.ppermute(v, 'replica', [(i, i ^ 1) for i in range(self.replicas)])  16.1 us
    ppermute x11, starting transfers between devices, across(): return lax.ppermute(v, 'shard', [(i, i ^ 2) for i in range(self.shards)])  14.1 us
    ppermute x16, starting transfers between devices, far(): lax.ppermute(v, 'replica', [(i, i ^ bit) for i in range(self.replicas)])  11.8 us
  transfers between devices with their start and end apart: 71, of which 19 were waited for; matrix products, arithmetic and copies ran while one was open for 3% of the time, Pallas kernels for 68%

profile of v3, /device:TPU:0, one launch (start us, length us, event | category | flops | bytes accessed | tf_op | source)
XLA Modules:
  0.0 481.6 jit_solution(2662765768064651675)
XLA Ops:
  2.5 2.9 collective-permute-start
  10.1 4.4 split_weights.2
  15.0 2.5 collective-permute-done.refs_1_
  17.5 2.8 pack_weights.2.refs_0_
  25.2 9.7 %project.1 = (bf16[1024,896]{1,0:T(8,128)(2,1)}, bf16[1024,896]{1,0:T(8,128)(2,1)}, bf16[4,1024,128]{2,1,0:T(8,128)(2,1)}, bf16[4,1024,128]{2,1,0:T(8,128)(2,1)}...) custom-call(bf16[224,3328]{1,0:T(8,128)(2,1)} %pack_weights.2.refs_0_, ...), custom_call_target="tpu_custom_call" | custom-call | flops 50000000 | bytes 100000 | tf_op jit(solution)/shard_map/project/pallas_call | solution.py:67
  34.9 6.1 %split_weights.3 = (bf16[224,1536]{1,0:T(8,128)(2,1)}, bf16[224,1536]{1,0:T(8,128)(2,1)}, bf16[224,768]{1,0:T(8,128)(2,1)}, bf16[224,1536]{1,0:T(8,128)(2,1)}, b...) custom-call(bf16[1024,896]{1,0:T(8,128)(2,1)} %get-tuple-element.161, ...), custom_call_target="tpu_custom_call" | custom-call | flops 50000000 | bytes 100000 | tf_op jit(solution)/shard_map/split_weights/pallas_call | solution.py:67
  43.2 13.8 %attend.2 = (bf16[1024,384]{1,0:T(8,128)(2,1)}, bf16[1024,384]{1,0:T(8,128)(2,1)}, f32[1024,384]{1,0:T(8,128)}, bf16[6,1024,256]{2,1,0:T(8,128)(2,1)}, bf16[6,76...) custom-call(bf16[224,1536]{1,0:T(8,128)(2,1)} %get-tuple-element.162.refs_0_, ...), custom_call_target="tpu_custom_call" | custom-call | flops 50000000 | bytes 100000 | tf_op jit(solution)/shard_map/attend/pallas_call | solution.py:67
  59.0 4.6 pack_weights.3
  68.4 17.1 %attend.3 = (bf16[1024,512]{1,0:T(8,128)(2,1)}, bf16[1024,512]{1,0:T(8,128)(2,1)}, f32[1024,512]{1,0:T(8,128)}, bf16[8,1024,256]{2,1,0:T(8,128)(2,1)}, bf16[8,76...) custom-call(bf16[224,2304]{1,0:T(8,128)(2,1)} %get-tuple-element.175.refs_0_, ...), custom_call_target="tpu_custom_call" | custom-call | flops 50000000 | bytes 100000 | tf_op jit(solution)/shard_map/attend/pallas_call | solution.py:67
  85.5 8.3 %join_output.1 = (f32[1024,896]{1,0:T(8,128)}, bf16[896,896]{1,0:T(8,128)(2,1)}, bf16[512,896]{1,0:T(8,128)(2,1)}, bf16[512,896]{1,0:T(8,128)(2,1)}) custom-call(bf16[1024,512]{1,0:T(8,128)(2,1)} %get-tuple-element.176.refs_0_.refs_9_.refs_3_, bf16[224,1536]{1,0:T(8,128)(2,1)} %collective-permute-done.10.refs_1_.refs_7_, ...), custom_call_target="tpu_custom_call" | custom-call | flops 50000000 | bytes 100000 | tf_op jit(solution)/shard_map/join_output/pallas_call | solution.py:67
  98.0 21.3 %ffn_part.4 = (bf16[2048,512]{1,0:T(8,128)(2,1)}, bf16[2048,1024]{1,0:T(8,128)(2,1)}, bf16[448,1536]{1,0:T(8,128)(2,1)}, bf16[448,1536]{1,0:T(8,128)(2,1)}, bf16[896,1536]{1,0:T(8,128)(2,1)}) custom-call(bf16[224,2304]{1,0:T(8,128)(2,1)} %gate.4.refs_0_.refs_6_, s32[4]{0:T(128)} %pad_add_fusion.refs_3_.refs_1_.refs_2_, bf16[1024,896]{1,0:T(8,128)(2,1)} %refs_3_.7, ...), custom_call_target="tpu_custom_call" | custom-call | flops 50000000 | bytes 100000 | tf_op jit(solution)/shard_map/ffn_part/pallas_call | solution.py:67
  119.3 3.0 collective-permute-done.14.refs_1_
  124.4 29.1 %ffn_part.5 = (bf16[2048,768]{1,0:T(8,128)(2,1)}, bf16[2048,1536]{1,0:T(8,128)(2,1)}, bf16[448,2304]{1,0:T(8,128)(2,1)}, bf16[448,2304]{1,0:T(8,128)(2,1)}, bf16[896,2304]{1,0:T(8,128)(2,1)}) custom-call(bf16[224,3456]{1,0:T(8,128)(2,1)} %gate.5.refs_0_.refs_6_, s32[4]{0:T(128)} %pad_add_fusion.refs_3_.refs_1_.refs_2_, bf16[1024,896]{1,0:T(8,128)(2,1)} %refs_3_.7, ...), custom_call_target="tpu_custom_call" | custom-call | flops 14499999744 | bytes 100000 | tf_op jit(solution)/shard_map/ffn_part/pallas_call | solution.py:67
  155.7 3.1 sums.14
  159.5 29.4 %ffn_part.6 = (bf16[2048,768]{1,0:T(8,128)(2,1)}, bf16[2048,1536]{1,0:T(8,128)(2,1)}, bf16[448,2304]{1,0:T(8,128)(2,1)}, bf16[448,2304]{1,0:T(8,128)(2,1)}, bf16[896,2304]{1,0:T(8,128)(2,1)}) custom-call(bf16[224,1536]{1,0:T(8,128)(2,1)} %get-tuple-element.185.refs_0_.refs_2_, s32[4]{0:T(128)} %pad_add_fusion.refs_3_.refs_1_.refs_2_, ...), custom_call_target="tpu_custom_call" | custom-call | flops 14499999744 | bytes 100000 | tf_op jit(solution)/shard_map/ffn_part/pallas_call | solution.py:67
  189.1 2.3 sums.15.refs_0_.refs_2_
  193.3 20.6 %ffn_part.7 = (bf16[2048,384]{1,0:T(8,128)(2,1)}, bf16[2048,768]{1,0:T(8,128)(2,1)}, bf16[448,1152]{1,0:T(8,128)(2,1)}, bf16[448,1152]{1,0:T(8,128)(2,1)}, bf16[896,1152]{1,0:T(8,128)(2,1)}) custom-call(bf16[224,1536]{1,0:T(8,128)(2,1)} %sums.15.refs_0_.refs_2_, s32[4]{0:T(128)} %pad_add_fusion.refs_3_.refs_1_.refs_2_, bf16[1024,896]{1,0:T(8,128)(2,1)} %refs_3_.7, ...), custom_call_target="tpu_custom_call" | custom-call | flops 8499999744 | bytes 100000 | tf_op jit(solution)/shard_map/ffn_part/pallas_call | solution.py:67
  213.9 4.4 sums.16
  218.3 2.6 collective-permute-start.21
  222.4 29.4 %back_tokens.1 = (bf16[256,896]{1,0:T(8,128)(2,1)}, bf16[256,896]{1,0:T(8,128)(2,1)}, bf16[256,896]{1,0:T(8,128)(2,1)}, bf16[256,896]{1,0:T(8,128)(2,1)}, f32[1024,896]{1,0:T(8,128)}) custom-call(bf16[224,1536]{1,0:T(8,128)(2,1)} %get-tuple-element.191.refs_0_.refs_2_, bf16[2048,1024]{1,0:T(8,128)(2,1)} %get-tuple-element.192.refs_1_, ...), custom_call_target="tpu_custom_call" | custom-call | flops 12000000000 | bytes 100000 | tf_op jit(solution)/shard_map/back_tokens/pallas_call | solution.py:67
  252.9 5.4 %sums.17 = (bf16[224,1536]{1,0:T(8,128)(2,1)}, bf16[112,2304]{1,0:T(8,128)(2,1)}, bf16[112,2304]{1,0:T(8,128)(2,1)}, bf16[224,2304]{1,0:T(8,128)(2,1)}, bf16[224,2304]{1,0:T(8,128)(2,1)}) custom-call(bf16[256,896]{1,0:T(8,128)(2,1)} %get-tuple-element.200.refs_0_, s32[4]{0:T(128)} %pad_add_fusion.refs_3_.refs_1_.refs_2_, ...), custom_call_target="tpu_custom_call" | custom-call | flops 1000000000 | bytes 100000 | tf_op jit(solution)/shard_map/sums/pallas_call | solution.py:67
  260.9 10.1 %turn_back.1 = (f32[1024,896]{1,0:T(8,128)}, bf16[1024,896]{1,0:T(8,128)(2,1)}, f32[1,896]{1,0:T(1,128)}, bf16[1024,384]{1,0:T(8,128)(2,1)}, bf16[1024,512]{1,0:T(8,128)(2,1)}) custom-call(bf16[224,1536]{1,0:T(8,128)(2,1)} %get-tuple-element.205.refs_0_.refs_2_, f32[1024,896]{1,0:T(8,128)} %get-tuple-element.206.refs_1_, ...), custom_call_target="tpu_custom_call" | custom-call | flops 4000000000 | bytes 100000 | tf_op jit(solution)/shard_map/turn_back/pallas_call | solution.py:67
  275.3 18.0 %attend_back.2 = (bf16[1024,384]{1,0:T(8,128)(2,1)}, f32[1024,128]{1,0:T(8,128)}, f32[1024,128]{1,0:T(8,128)}) custom-call(bf16[112,2304]{1,0:T(8,128)(2,1)} %sums.18.refs_0_.refs_2_, bf16[1024,896]{1,0:T(8,128)(2,1)} %get-tuple-element.163.refs_3_.refs_1_, bf16[1024,384]{1,0:T(8,128)(2,1)} %get-tuple-element.216.refs_2_, ...), custom_call_target="tpu_custom_call" | custom-call | flops 2000000000 | bytes 100000 | tf_op jit(solution)/shard_map/attend_back/pallas_call | solution.py:67
  293.3 6.2 %collective-permute-done.29.refs_3_ = bf16[112,2304]{1,0:T(8,128)(2,1)} collective-permute-done((bf16[112,2304]{1,0:T(8,128)(2,1)}, bf16[112,2304]{1,0:T(8,128)(2,1)}, u32[]{:S(2)}, u32[]{:S(2)}) %collective-permute-start.29) | collective-permute-done | bytes 516128 | tf_op jit(solution)/shard_map/ppermute | solution.py:850
  299.5 4.1 sums.19
  306.3 5.3 %weight_grads.2 = (bf16[448,896]{1,0:T(8,128)(2,1)}, bf16[448,384]{1,0:T(8,128)(2,1)}, bf16[448,512]{1,0:T(8,128)(2,1)}) custom-call(bf16[112,2304]{1,0:T(8,128)(2,1)} %get-tuple-element.228.refs_0_.refs_4_, s32[4]{0:T(128)} %pad_add_fusion.refs_3_.refs_1_.refs_2_, bf16[1024,384]{1,0:T(8,128)(2,1)} %get-tuple-element.166.refs_0_.refs_8_.refs_3_.refs_2_, ...), custom_call_target="tpu_custom_call" | custom-call | flops 50000000 | bytes 100000 | tf_op jit(solution)/shard_map/weight_grads/pallas_call | solution.py:67
  312.2 22.2 %attend_back.3 = (bf16[1024,512]{1,0:T(8,128)(2,1)}, bf16[1024,128]{1,0:T(8,128)(2,1)}, bf16[1024,128]{1,0:T(8,128)(2,1)}) custom-call(bf16[448,896]{1,0:T(8,128)(2,1)} %get-tuple-element.230.refs_0_.refs_10_, bf16[1024,896]{1,0:T(8,128)(2,1)} %get-tuple-element.163.refs_3_.refs_1_, bf16[1024,512]{1,0:T(8,128)(2,1)} %get-tuple-element.231.refs_2_, ...), custom_call_target="tpu_custom_call" | custom-call | flops 2500000000 | bytes 100000 | tf_op jit(solution)/shard_map/attend_back/pallas_call | solution.py:67
  334.4 4.4 sums.20
  338.8 6.5 %weight_grads.3 = (bf16[448,1152]{1,0:T(8,128)(2,1)}, bf16[448,384]{1,0:T(8,128)(2,1)}, bf16[448,384]{1,0:T(8,128)(2,1)}, bf16[448,384]{1,0:T(8,128)(2,1)}) custom-call(bf16[224,1024]{1,0:T(8,128)(2,1)} %get-tuple-element.246.refs_0_, s32[4]{0:T(128)} %pad_add_fusion.refs_3_.refs_1_.refs_2_, bf16[1024,896]{1,0:T(8,128)(2,1)} %get-tuple-element.161.refs_0_.refs_2_, ...), custom_call_target="tpu_custom_call" | custom-call | flops 50000000 | bytes 100000 | tf_op jit(solution)/shard_map/weight_grads/pallas_call | solution.py:67
  351.3 7.2 %collective-permute-done.39.refs_5_ = bf16[224,896]{1,0:T(8,128)(2,1)} collective-permute-done((bf16[224,896]{1,0:T(8,128)(2,1)}, bf16[224,896]{1,0:T(8,128)(2,1)}, u32[]{:S(2)}, u32[]{:S(2)}) %collective-permute-start.39) | collective-permute-done | bytes 401440 | tf_op jit(solution)/shard_map/ppermute | solution.py:844
  358.5 6.1 %collective-permute-done.38.refs_3_ = bf16[224,1152]{1,0:T(8,128)(2,1)} collective-permute-done((bf16[224,1152]{1,0:T(8,128)(2,1)}, bf16[224,1152]{1,0:T(8,128)(2,1)}, u32[]{:S(2)}, u32[]{:S(2)}) %collective-permute-start.38) | collective-permute-done | bytes 516128 | tf_op jit(solution)/shard_map/ppermute | solution.py:850
  364.6 3.4 sums.21
  370.2 9.3 %finish_tokens.1 = (f32[1024,896]{1,0:T(8,128)}, f32[1,896]{1,0:T(1,128)}, f32[1,1152]{1,0:T(1,128)}) custom-call(bf16[224,1152]{1,0:T(8,128)(2,1)} %get-tuple-element.256.refs_0_.refs_2_, bf16[1024,896]{1,0:T(8,128)(2,1)} %refs_1_.3, f32[1,896]{1,0:T(1,128)} %broadcast_in_dim.11.refs_4_.refs_2_, bf16[896,1152]{1,0:T(8,128)(2,1)} %get-tuple-element.257.refs_3_, ...), custom_call_target="tpu_custom_call" | custom-call | flops 50000000 | bytes 100000 | tf_op jit(solution)/shard_map/finish_tokens/pallas_call | solution.py:67
  384.0 3.2 sums.22
  387.2 2.4 collective-permute-start.49
  389.7 10.6 %down_tokens.2 = (bf16[256,896]{1,0:T(8,128)(2,1)}, bf16[256,896]{1,0:T(8,128)(2,1)}, bf16[256,896]{1,0:T(8,128)(2,1)}, bf16[256,896]{1,0:T(8,128)(2,1)}) custom-call(bf16[224,1536]{1,0:T(8,128)(2,1)} %get-tuple-element.266.refs_0_, bf16[2048,512]{1,0:T(8,128)(2,1)} %get-tuple-element.180.refs_0_.refs_1_, ...), custom_call_target="tpu_custom_call" | custom-call | flops 50000000 | bytes 100000 | tf_op jit(solution)/shard_map/down_tokens/pallas_call | solution.py:67
  401.3 2.7 sums.23
  404.0 2.4 collective-permute-start.58
  410.6 12.1 %down_tokens.3.refs_0_ = bf16[1024,896]{1,0:T(8,128)(2,1)} custom-call(bf16[224,2304]{1,0:T(8,128)(2,1)} %get-tuple-element.273.refs_0_.refs_2_.refs_4_, bf16[2048,512]{1,0:T(8,128)(2,1)} %get-tuple-element.180.refs_0_.refs_1_, bf16[2048,768]{1,0:T(8,128)(2,1)} %get-tuple-element.182.refs_0_.refs_2_, bf16[2048,768]{1,0:T(8,128)(2,1)} %get-tuple-element.186.refs_0_.refs_3_, ...), custom_call_target="tpu_custom_call" | custom-call | flops 50000000 | bytes 100000 | tf_op jit(solution)/shard_map/down_tokens/pallas_call | solution.py:67
  422.8 10.1 %collective-permute-done.54.refs_3_ = bf16[224,1152]{1,0:T(8,128)(2,1)} collective-permute-done((bf16[224,1152]{1,0:T(8,128)(2,1)}, bf16[224,1152]{1,0:T(8,128)(2,1)}, u32[]{:S(2)}, u32[]{:S(2)}) %collective-permute-start.54) | collective-permute-done | bytes 516128 | tf_op jit(solution)/shard_map/ppermute | solution.py:850
  432.9 2.6 sums.24
  435.7 3.8 collective-permute-done.59.refs_5_
  439.5 2.2 sums.25
  441.9 16.9 %collective-permute-done.61.refs_5_ = bf16[112,896]{1,0:T(8,128)(2,1)} collective-permute-done((bf16[112,896]{1,0:T(8,128)(2,1)}, bf16[112,896]{1,0:T(8,128)(2,1)}, u32[]{:S(2)}, u32[]{:S(2)}) %collective-permute-start.61) | collective-permute-done | bytes 200736 | tf_op jit(solution)/shard_map/ppermute | solution.py:850
  458.9 4.0 collective-permute-done.63.refs_9_
  462.9 2.3 sums.26
  467.8 10.8 %assemble.1 = (f32[224,4864]{1,0:T(8,128)}, f32[224,4864]{1,0:T(8,128)}, f32[1216,896]{1,0:T(8,128)}) custom-call(bf16[224,768]{1,0:T(8,128)(2,1)} %get-tuple-element.286.refs_0_, s32[4]{0:T(128)} %pad_add_fusion.refs_3_.refs_1_.refs_2_, bf16[224,1536]{1,0:T(8,128)(2,1)} %get-tuple-element.205.refs_0_.refs_2_, ...), custom_call_target="tpu_custom_call" | custom-call | flops 5500000256 | bytes 100000 | tf_op jit(solution)/shard_map/assemble/pallas_call | solution.py:67
  478.8 2.6 sums.27
  (157 shorter events, 65.7 us)
Async XLA Ops:
  2.5 15.0 %collective-permute-start = (bf16[224,1152]{1,0:T(8,128)(2,1)}, bf16[224,1152]{1,0:T(8,128)(2,1)}, u32[]{:S(2)}, u32[]{:S(2)}) collective-permute-start(bf16[224,1152]{1,0:T(8,128)(2,1)} %side_by_side.1.refs_0_.refs_5_), channel_id=1, source_target_pairs={{0,16},{8,24},{16,0},{24,8},{1,17},{9,25},{17,1},{25,9},{2,18},{10... | collective-permute-start | bytes 1548296 | tf_op jit(solution)/shard_map/ppermute | solution.py:844
  5.5 19.7 %collective-permute-start.3 = (bf16[1024,896]{1,0:T(8,128)(2,1)}, bf16[1024,896]{1,0:T(8,128)(2,1)}, u32[]{:S(2)}, u32[]{:S(2)}) collective-permute-start(bf16[1024,896]{1,0:T(8,128)(2,1)} %refs_3_.7), channel_id=1, source_target_pairs={{0,8},{8,0},{16,24},{24,16},{1,9},{9,1},{17,25},{25,17},{2,10},{10... | collective-permute-start | bytes 5505032 | tf_op jit(solution)/shard_map/ppermute | solution.py:841
  20.3 36.7 %collective-permute-start.6 = (bf16[224,3328]{1,0:T(8,128)(2,1)}, bf16[224,3328]{1,0:T(8,128)(2,1)}, u32[]{:S(2)}, u32[]{:S(2)}) collective-permute-start(bf16[224,3328]{1,0:T(8,128)(2,1)} %pack_weights.2.refs_0_), channel_id=1, source_target_pairs={{0,16},{8,24},{16,0},{24,8},{1,17},{9,25},{17,1},{25,9},{2,18},{10... | collective-permute-start | bytes 4472840 | tf_op jit(solution)/shard_map/ppermute | solution.py:844
  41.0 18.0 %collective-permute-start.8 = (bf16[224,1536]{1,0:T(8,128)(2,1)}, bf16[224,1536]{1,0:T(8,128)(2,1)}, u32[]{:S(2)}, u32[]{:S(2)}) collective-permute-start(bf16[224,1536]{1,0:T(8,128)(2,1)} %get-tuple-element.167), channel_id=1, source_target_pairs={{0,8},{8,0},{16,24},{24,16},{1,9},{9,1},{17,25},{25,17},{2,10},{10... | collective-permute-start | bytes 2064392 | tf_op jit(solution)/shard_map/ppermute | solution.py:841
  41.0 18.0 %collective-permute-start.7 = (bf16[224,1536]{1,0:T(8,128)(2,1)}, bf16[224,1536]{1,0:T(8,128)(2,1)}, u32[]{:S(2)}, u32[]{:S(2)}) collective-permute-start(bf16[224,1536]{1,0:T(8,128)(2,1)} %get-tuple-element.162.refs_0_), channel_id=1, source_target_pairs={{0,8},{8,0},{16,24},{24,16},{1,9},{9,1},{17,25},{25,17},{2,10},{10... | collective-permute-start | bytes 2064392 | tf_op jit(solution)/shard_map/ppermute | solution.py:841
  41.5 17.5 %collective-permute-start.9 = (bf16[224,768]{1,0:T(8,128)(2,1)}, bf16[224,768]{1,0:T(8,128)(2,1)}, u32[]{:S(2)}, u32[]{:S(2)}) collective-permute-start(bf16[224,768]{1,0:T(8,128)(2,1)} %get-tuple-element.168), channel_id=1, source_target_pairs={{0,8},{8,0},{16,24},{24,16},{1,9},{9,1},{17,25},{25,17},{2,10},{10... | collective-permute-start | bytes 1032200 | tf_op jit(solution)/shard_map/ppermute | solution.py:841
  63.6 30.7 %collective-permute-start.11 = (bf16[224,2304]{1,0:T(8,128)(2,1)}, bf16[224,2304]{1,0:T(8,128)(2,1)}, u32[]{:S(2)}, u32[]{:S(2)}) collective-permute-start(bf16[224,2304]{1,0:T(8,128)(2,1)} %get-tuple-element.175.refs_0_), channel_id=1, source_target_pairs={{0,16},{8,24},{16,0},{24,8},{1,17},{9,25},{17,1},{25,9},{2,18},{10... | collective-permute-start | bytes 3096584 | tf_op jit(solution)/shard_map/ppermute | solution.py:844
  63.9 21.6 %collective-permute-start.10 = (bf16[224,1536]{1,0:T(8,128)(2,1)}, bf16[224,1536]{1,0:T(8,128)(2,1)}, u32[]{:S(2)}, u32[]{:S(2)}) collective-permute-start(bf16[224,1536]{1,0:T(8,128)(2,1)} %first_lanes.1.refs_0_), channel_id=1, source_target_pairs={{0,1},{1,0},{2,3},{3,2},{4,5},{5,4},{6,7},{7,6},{8,9},{9,8},{10,11... | collective-permute-start | bytes 2064392 | tf_op jit(solution)/shard_map/ppermute | solution.py:847
  65.7 56.7 %collective-permute-start.14 = (bf16[224,3456]{1,0:T(8,128)(2,1)}, bf16[224,3456]{1,0:T(8,128)(2,1)}, u32[]{:S(2)}, u32[]{:S(2)}) collective-permute-start(bf16[224,3456]{1,0:T(8,128)(2,1)} %get-tuple-element.181), channel_id=1, source_target_pairs={{0,16},{8,24},{16,0},{24,8},{1,17},{9,25},{17,1},{25,9},{2,18},{10... | collective-permute-start | bytes 4644872 | tf_op jit(solution)/shard_map/ppermute | solution.py:844
  94.4 30.0 %collective-permute-start.15 = (bf16[224,2304]{1,0:T(8,128)(2,1)}, bf16[224,2304]{1,0:T(8,128)(2,1)}, u32[]{:S(2)}, u32[]{:S(2)}) collective-permute-start(bf16[224,2304]{1,0:T(8,128)(2,1)} %gate.4.refs_0_.refs_6_), channel_id=1, source_target_pairs={{0,1},{1,0},{2,3},{3,2},{4,5},{5,4},{6,7},{7,6},{8,9},{9,8},{10,11... | collective-permute-start | bytes 3096584 | tf_op jit(solution)/shard_map/ppermute | solution.py:847
  122.3 37.2 %collective-permute-start.17 = (bf16[224,3456]{1,0:T(8,128)(2,1)}, bf16[224,3456]{1,0:T(8,128)(2,1)}, u32[]{:S(2)}, u32[]{:S(2)}) collective-permute-start(bf16[224,3456]{1,0:T(8,128)(2,1)} %gate.5.refs_0_.refs_6_), channel_id=1, source_target_pairs={{0,1},{1,0},{2,3},{3,2},{4,5},{5,4},{6,7},{7,6},{8,9},{9,8},{10,11... | collective-permute-start | bytes 4644872 | tf_op jit(solution)/shard_map/ppermute | solution.py:847
  123.9 31.9 %collective-permute-start.16 = (bf16[448,1536]{1,0:T(8,128)(2,1)}, bf16[448,1536]{1,0:T(8,128)(2,1)}, u32[]{:S(2)}, u32[]{:S(2)}) collective-permute-start(bf16[448,1536]{1,0:T(8,128)(2,1)} %get-tuple-element.184), channel_id=1, source_target_pairs={{0,16},{8,24},{16,0},{24,8},{1,17},{9,25},{17,1},{25,9},{2,18},{10... | collective-permute-start | bytes 4128776 | tf_op jit(solution)/shard_map/ppermute | solution.py:844
  153.5 60.4 %collective-permute-start.20 = (bf16[448,2304]{1,0:T(8,128)(2,1)}, bf16[448,2304]{1,0:T(8,128)(2,1)}, u32[]{:S(2)}, u32[]{:S(2)}) collective-permute-start(bf16[448,2304]{1,0:T(8,128)(2,1)} %get-tuple-element.190), channel_id=1, source_target_pairs={{0,16},{8,24},{16,0},{24,8},{1,17},{9,25},{17,1},{25,9},{2,18},{10... | collective-permute-start | bytes 6193160 | tf_op jit(solution)/shard_map/ppermute | solution.py:844
  158.8 30.3 %collective-permute-start.18 = (bf16[224,1536]{1,0:T(8,128)(2,1)}, bf16[224,1536]{1,0:T(8,128)(2,1)}, u32[]{:S(2)}, u32[]{:S(2)}) collective-permute-start(bf16[224,1536]{1,0:T(8,128)(2,1)} %get-tuple-element.187), channel_id=1, source_target_pairs={{0,1},{1,0},{2,3},{3,2},{4,5},{5,4},{6,7},{7,6},{8,9},{9,8},{10,11... | collective-permute-start | bytes 2064392 | tf_op jit(solution)/shard_map/ppermute | solution.py:847
  189.0 63.9 %collective-permute-start.23 = (bf16[448,2304]{1,0:T(8,128)(2,1)}, bf16[448,2304]{1,0:T(8,128)(2,1)}, u32[]{:S(2)}, u32[]{:S(2)}) collective-permute-start(bf16[448,2304]{1,0:T(8,128)(2,1)} %get-tuple-element.204), channel_id=1, source_target_pairs={{0,16},{8,24},{16,0},{24,8},{1,17},{9,25},{17,1},{25,9},{2,18},{10... | collective-permute-start | bytes 6193160 | tf_op jit(solution)/shard_map/ppermute | solution.py:844
  191.5 22.4 %collective-permute-start.19 = (bf16[224,1536]{1,0:T(8,128)(2,1)}, bf16[224,1536]{1,0:T(8,128)(2,1)}, u32[]{:S(2)}, u32[]{:S(2)}) collective-permute-start(bf16[224,1536]{1,0:T(8,128)(2,1)} %sums.15.refs_0_.refs_2_), channel_id=1, source_target_pairs={{0,2},{1,3},{2,0},{3,1},{4,6},{5,7},{6,4},{7,5},{8,10},{9,11},{10,... | collective-permute-start | bytes 2064392 | tf_op jit(solution)/shard_map/ppermute | solution.py:850
  218.3 34.1 %collective-permute-start.21 = (bf16[224,1536]{1,0:T(8,128)(2,1)}, bf16[224,1536]{1,0:T(8,128)(2,1)}, u32[]{:S(2)}, u32[]{:S(2)}) collective-permute-start(bf16[224,1536]{1,0:T(8,128)(2,1)} %get-tuple-element.191.refs_0_.refs_2_), channel_id=1, source_target_pairs={{0,4},{1,5},{2,6},{3,7},{4,0},{5,1},{6,2},{7,3},{8,12},{9,13},{10,... | collective-permute-start | bytes 2064392 | tf_op jit(solution)/shard_map/ppermute | solution.py:850
  220.9 31.6 %collective-permute-start.22 = (bf16[224,2304]{1,0:T(8,128)(2,1)}, bf16[224,2304]{1,0:T(8,128)(2,1)}, u32[]{:S(2)}, u32[]{:S(2)}) collective-permute-start(bf16[224,2304]{1,0:T(8,128)(2,1)} %get-tuple-element.202), channel_id=1, source_target_pairs={{0,1},{1,0},{2,3},{3,2},{4,5},{5,4},{6,7},{7,6},{8,9},{9,8},{10,11... | collective-permute-start | bytes 3096584 | tf_op jit(solution)/shard_map/ppermute | solution.py:847
  258.3 14.0 %collective-permute-start.28 = (bf16[112,2304]{1,0:T(8,128)(2,1)}, bf16[112,2304]{1,0:T(8,128)(2,1)}, u32[]{:S(2)}, u32[]{:S(2)}) collective-permute-start(bf16[112,2304]{1,0:T(8,128)(2,1)} %get-tuple-element.215), channel_id=1, source_target_pairs={{0,2},{1,3},{2,0},{3,1},{4,6},{5,7},{6,4},{7,5},{8,10},{9,11},{10,... | collective-permute-start | bytes 1548296 | tf_op jit(solution)/shard_map/ppermute | solution.py:850
  258.8 34.5 %collective-permute-start.31 = (bf16[448,1152]{1,0:T(8,128)(2,1)}, bf16[448,1152]{1,0:T(8,128)(2,1)}, u32[]{:S(2)}, u32[]{:S(2)}) collective-permute-start(bf16[448,1152]{1,0:T(8,128)(2,1)} %get-tuple-element.227), channel_id=1, source_target_pairs={{0,16},{8,24},{16,0},{24,8},{1,17},{9,25},{17,1},{25,9},{2,18},{10... | collective-permute-start | bytes 3096584 | tf_op jit(solution)/shard_map/ppermute | solution.py:844
  260.3 39.2 %collective-permute-start.30 = (bf16[224,2304]{1,0:T(8,128)(2,1)}, bf16[224,2304]{1,0:T(8,128)(2,1)}, u32[]{:S(2)}, u32[]{:S(2)}) collective-permute-start(bf16[224,2304]{1,0:T(8,128)(2,1)} %get-tuple-element.225), channel_id=1, source_target_pairs={{0,1},{1,0},{2,3},{3,2},{4,5},{5,4},{6,7},{7,6},{8,9},{9,8},{10,11... | collective-permute-start | bytes 3096584 | tf_op jit(solution)/shard_map/ppermute | solution.py:847
  274.5 25.0 %collective-permute-start.29 = (bf16[112,2304]{1,0:T(8,128)(2,1)}, bf16[112,2304]{1,0:T(8,128)(2,1)}, u32[]{:S(2)}, u32[]{:S(2)}) collective-permute-start(bf16[112,2304]{1,0:T(8,128)(2,1)} %sums.18.refs_0_.refs_2_), channel_id=1, source_target_pairs={{0,4},{1,5},{2,6},{3,7},{4,0},{5,1},{6,2},{7,3},{8,12},{9,13},{10,... | collective-permute-start | bytes 1548296 | tf_op jit(solution)/shard_map/ppermute | solution.py:850
  274.8 36.9 %collective-permute-start.32 = (bf16[224,1536]{1,0:T(8,128)(2,1)}, bf16[224,1536]{1,0:T(8,128)(2,1)}, u32[]{:S(2)}, u32[]{:S(2)}) collective-permute-start(bf16[224,1536]{1,0:T(8,128)(2,1)} %get-tuple-element.205.refs_0_.refs_2_), channel_id=1, source_target_pairs={{0,1},{1,0},{2,3},{3,2},{4,5},{5,4},{6,7},{7,6},{8,9},{9,8},{10,11... | collective-permute-start | bytes 2064392 | tf_op jit(solution)/shard_map/ppermute | solution.py:847
  303.7 30.7 %collective-permute-start.34 = (bf16[112,2304]{1,0:T(8,128)(2,1)}, bf16[112,2304]{1,0:T(8,128)(2,1)}, u32[]{:S(2)}, u32[]{:S(2)}) collective-permute-start(bf16[112,2304]{1,0:T(8,128)(2,1)} %get-tuple-element.241), channel_id=1, source_target_pairs={{0,2},{1,3},{2,0},{3,1},{4,6},{5,7},{6,4},{7,5},{8,10},{9,11},{10,... | collective-permute-start | bytes 1548296 | tf_op jit(solution)/shard_map/ppermute | solution.py:850
  303.7 30.7 %collective-permute-start.35 = (bf16[224,1152]{1,0:T(8,128)(2,1)}, bf16[224,1152]{1,0:T(8,128)(2,1)}, u32[]{:S(2)}, u32[]{:S(2)}) collective-permute-start(bf16[224,1152]{1,0:T(8,128)(2,1)} %get-tuple-element.243), channel_id=1, source_target_pairs={{0,1},{1,0},{2,3},{3,2},{4,5},{5,4},{6,7},{7,6},{8,9},{9,8},{10,11... | collective-permute-start | bytes 1548296 | tf_op jit(solution)/shard_map/ppermute | solution.py:847
  304.3 30.1 %collective-permute-start.33 = (bf16[112,2304]{1,0:T(8,128)(2,1)}, bf16[112,2304]{1,0:T(8,128)(2,1)}, u32[]{:S(2)}, u32[]{:S(2)}) collective-permute-start(bf16[112,2304]{1,0:T(8,128)(2,1)} %get-tuple-element.228.refs_0_.refs_4_), channel_id=1, source_target_pairs={{0,2},{1,3},{2,0},{3,1},{4,6},{5,7},{6,4},{7,5},{8,10},{9,11},{10,... | collective-permute-start | bytes 1548296 | tf_op jit(solution)/shard_map/ppermute | solution.py:850
  311.7 22.7 %collective-permute-start.37 = (bf16[448,512]{1,0:T(8,128)(2,1)}, bf16[448,512]{1,0:T(8,128)(2,1)}, u32[]{:S(2)}, u32[]{:S(2)}) collective-permute-start(bf16[448,512]{1,0:T(8,128)(2,1)} %get-tuple-element.245), channel_id=1, source_target_pairs={{0,8},{8,0},{16,24},{24,16},{1,9},{9,1},{17,25},{25,17},{2,10},{10... | collective-permute-start | bytes 1376264 | tf_op jit(solution)/shard_map/ppermute | solution.py:841
  311.7 22.7 %collective-permute-start.36 = (bf16[448,384]{1,0:T(8,128)(2,1)}, bf16[448,384]{1,0:T(8,128)(2,1)}, u32[]{:S(2)}, u32[]{:S(2)}) collective-permute-start(bf16[448,384]{1,0:T(8,128)(2,1)} %get-tuple-element.244), channel_id=1, source_target_pairs={{0,8},{8,0},{16,24},{24,16},{1,9},{9,1},{17,25},{25,17},{2,10},{10... | collective-permute-start | bytes 1032200 | tf_op jit(solution)/shard_map/ppermute | solution.py:841
  345.4 19.2 %collective-permute-start.38 = (bf16[224,1152]{1,0:T(8,128)(2,1)}, bf16[224,1152]{1,0:T(8,128)(2,1)}, u32[]{:S(2)}, u32[]{:S(2)}) collective-permute-start(bf16[224,1152]{1,0:T(8,128)(2,1)} %get-tuple-element.250.refs_2_), channel_id=1, source_target_pairs={{0,2},{1,3},{2,0},{3,1},{4,6},{5,7},{6,4},{7,5},{8,10},{9,11},{10,... | collective-permute-start | bytes 1548296 | tf_op jit(solution)/shard_map/ppermute | solution.py:850
  345.4 38.6 %collective-permute-start.43 = (bf16[224,2304]{1,0:T(8,128)(2,1)}, bf16[224,2304]{1,0:T(8,128)(2,1)}, u32[]{:S(2)}, u32[]{:S(2)}) collective-permute-start(bf16[224,2304]{1,0:T(8,128)(2,1)} %get-tuple-element.259.refs_2_.refs_3_), channel_id=1, source_target_pairs={{0,1},{1,0},{2,3},{3,2},{4,5},{5,4},{6,7},{7,6},{8,9},{9,8},{10,11... | collective-permute-start | bytes 3096584 | tf_op jit(solution)/shard_map/ppermute | solution.py:847
  346.8 11.7 %collective-permute-start.39 = (bf16[224,896]{1,0:T(8,128)(2,1)}, bf16[224,896]{1,0:T(8,128)(2,1)}, u32[]{:S(2)}, u32[]{:S(2)}) collective-permute-start(bf16[224,896]{1,0:T(8,128)(2,1)} %get-tuple-element.252), channel_id=1, source_target_pairs={{0,16},{8,24},{16,0},{24,8},{1,17},{9,25},{17,1},{25,9},{2,18},{10... | collective-permute-start | bytes 1204232 | tf_op jit(solution)/shard_map/ppermute | solution.py:844
  350.4 31.9 %collective-permute-start.44 = (bf16[112,2304]{1,0:T(8,128)(2,1)}, bf16[112,2304]{1,0:T(8,128)(2,1)}, u32[]{:S(2)}, u32[]{:S(2)}) collective-permute-start(bf16[112,2304]{1,0:T(8,128)(2,1)} %get-tuple-element.260.refs_4_), channel_id=1, source_target_pairs={{0,4},{1,5},{2,6},{3,7},{4,0},{5,1},{6,2},{7,3},{8,12},{9,13},{10,... | collective-permute-start | bytes 1548296 | tf_op jit(solution)/shard_map/ppermute | solution.py:850
  368.0 16.0 %collective-permute-start.45 = (bf16[224,1152]{1,0:T(8,128)(2,1)}, bf16[224,1152]{1,0:T(8,128)(2,1)}, u32[]{:S(2)}, u32[]{:S(2)}) collective-permute-start(bf16[224,1152]{1,0:T(8,128)(2,1)} %get-tuple-element.262), channel_id=1, source_target_pairs={{0,16},{8,24},{16,0},{24,8},{1,17},{9,25},{17,1},{25,9},{2,18},{10... | collective-permute-start | bytes 1548296 | tf_op jit(solution)/shard_map/ppermute | solution.py:844
  387.2 14.1 %collective-permute-start.47 = (bf16[112,2304]{1,0:T(8,128)(2,1)}, bf16[112,2304]{1,0:T(8,128)(2,1)}, u32[]{:S(2)}, u32[]{:S(2)}) collective-permute-start(bf16[112,2304]{1,0:T(8,128)(2,1)} %get-tuple-element.268.refs_2_), channel_id=1, source_target_pairs={{0,2},{1,3},{2,0},{3,1},{4,6},{5,7},{6,4},{7,5},{8,10},{9,11},{10,... | collective-permute-start | bytes 1548296 | tf_op jit(solution)/shard_map/ppermute | solution.py:850
  387.2 13.6 %collective-permute-start.49 = (bf16[112,1152]{1,0:T(8,128)(2,1)}, bf16[112,1152]{1,0:T(8,128)(2,1)}, u32[]{:S(2)}, u32[]{:S(2)}) collective-permute-start(bf16[112,1152]{1,0:T(8,128)(2,1)} %get-tuple-element.272), channel_id=1, source_target_pairs={{0,1},{1,0},{2,3},{3,2},{4,5},{5,4},{6,7},{7,6},{8,9},{9,8},{10,11... | collective-permute-start | bytes 774152 | tf_op jit(solution)/shard_map/ppermute | solution.py:847
  389.6 11.2 %collective-permute-start.48 = (bf16[112,896]{1,0:T(8,128)(2,1)}, bf16[112,896]{1,0:T(8,128)(2,1)}, u32[]{:S(2)}, u32[]{:S(2)}) collective-permute-start(bf16[112,896]{1,0:T(8,128)(2,1)} %get-tuple-element.270), channel_id=1, source_target_pairs={{0,1},{1,0},{2,3},{3,2},{4,5},{5,4},{6,7},{7,6},{8,9},{9,8},{10,11... | collective-permute-start | bytes 602120 | tf_op jit(solution)/shard_map/ppermute | solution.py:847
  404.0 35.5 %collective-permute-start.58 = (bf16[224,2304]{1,0:T(8,128)(2,1)}, bf16[224,2304]{1,0:T(8,128)(2,1)}, u32[]{:S(2)}, u32[]{:S(2)}) collective-permute-start(bf16[224,2304]{1,0:T(8,128)(2,1)} %get-tuple-element.273.refs_0_.refs_2_.refs_4_), channel_id=1, source_target_pairs={{0,1},{1,0},{2,3},{3,2},{4,5},{5,4},{6,7},{7,6},{8,9},{9,8},{10,11... | collective-permute-start | bytes 3096584 | tf_op jit(solution)/shard_map/ppermute | solution.py:847
  406.9 25.9 %collective-permute-start.54 = (bf16[224,1152]{1,0:T(8,128)(2,1)}, bf16[224,1152]{1,0:T(8,128)(2,1)}, u32[]{:S(2)}, u32[]{:S(2)}) collective-permute-start(bf16[224,1152]{1,0:T(8,128)(2,1)} %get-tuple-element.256.refs_0_.refs_2_), channel_id=1, source_target_pairs={{0,4},{1,5},{2,6},{3,7},{4,0},{5,1},{6,2},{7,3},{8,12},{9,13},{10,... | collective-permute-start | bytes 1548296 | tf_op jit(solution)/shard_map/ppermute | solution.py:850
  408.6 24.3 %collective-permute-start.56 = (bf16[112,1152]{1,0:T(8,128)(2,1)}, bf16[112,1152]{1,0:T(8,128)(2,1)}, u32[]{:S(2)}, u32[]{:S(2)}) collective-permute-start(bf16[112,1152]{1,0:T(8,128)(2,1)} %get-tuple-element.278.refs_6_), channel_id=1, source_target_pairs={{0,2},{1,3},{2,0},{3,1},{4,6},{5,7},{6,4},{7,5},{8,10},{9,11},{10,... | collective-permute-start | bytes 774152 | tf_op jit(solution)/shard_map/ppermute | solution.py:850
  409.3 23.6 %collective-permute-start.55 = (bf16[112,896]{1,0:T(8,128)(2,1)}, bf16[112,896]{1,0:T(8,128)(2,1)}, u32[]{:S(2)}, u32[]{:S(2)}) collective-permute-start(bf16[112,896]{1,0:T(8,128)(2,1)} %get-tuple-element.277.refs_4_), channel_id=1, source_target_pairs={{0,2},{1,3},{2,0},{3,1},{4,6},{5,7},{6,4},{7,5},{8,10},{9,11},{10,... | collective-permute-start | bytes 602120 | tf_op jit(solution)/shard_map/ppermute | solution.py:850
  410.6 22.3 %collective-permute-start.57 = (f32[1,2944]{1,0:T(1,128)}, f32[1,2944]{1,0:T(1,128)}, u32[]{:S(2)}, u32[]{:S(2)}) collective-permute-start(f32[1,2944]{1,0:T(1,128)} %get-tuple-element.279.refs_8_), channel_id=1, source_target_pairs={{0,1},{1,0},{2,3},{3,2},{4,5},{5,4},{6,7},{7,6},{8,9},{9,8},{10,11... | collective-permute-start | bytes 35336 | tf_op jit(solution)/shard_map/ppermute | solution.py:847
  435.4 23.4 %collective-permute-start.60 = (bf16[224,1152]{1,0:T(8,128)(2,1)}, bf16[224,1152]{1,0:T(8,128)(2,1)}, u32[]{:S(2)}, u32[]{:S(2)}) collective-permute-start(bf16[224,1152]{1,0:T(8,128)(2,1)} %get-tuple-element.280.refs_0_.refs_2_.refs_5_), channel_id=1, source_target_pairs={{0,1},{1,0},{2,3},{3,2},{4,5},{5,4},{6,7},{7,6},{8,9},{9,8},{10,11... | collective-permute-start | bytes 1548296 | tf_op jit(solution)/shard_map/ppermute | solution.py:847
  435.5 32.2 %collective-permute-start.65 = (bf16[224,1536]{1,0:T(8,128)(2,1)}, bf16[224,1536]{1,0:T(8,128)(2,1)}, u32[]{:S(2)}, u32[]{:S(2)}) collective-permute-start(bf16[224,1536]{1,0:T(8,128)(2,1)} %get-tuple-element.266.refs_0_), channel_id=1, source_target_pairs={{0,8},{8,0},{16,24},{24,16},{1,9},{9,1},{17,25},{25,17},{2,10},{10... | collective-permute-start | bytes 2064392 | tf_op jit(solution)/shard_map/ppermute | solution.py:841
  435.6 23.3 %collective-permute-start.62 = (bf16[112,1152]{1,0:T(8,128)(2,1)}, bf16[112,1152]{1,0:T(8,128)(2,1)}, u32[]{:S(2)}, u32[]{:S(2)}) collective-permute-start(bf16[112,1152]{1,0:T(8,128)(2,1)} %get-tuple-element.284.refs_6_), channel_id=1, source_target_pairs={{0,4},{1,5},{2,6},{3,7},{4,0},{5,1},{6,2},{7,3},{8,12},{9,13},{10,... | collective-permute-start | bytes 774152 | tf_op jit(solution)/shard_map/ppermute | solution.py:850
  441.7 26.1 %collective-permute-start.66 = (bf16[224,1536]{1,0:T(8,128)(2,1)}, bf16[224,1536]{1,0:T(8,128)(2,1)}, u32[]{:S(2)}, u32[]{:S(2)}) collective-permute-start(bf16[224,1536]{1,0:T(8,128)(2,1)} %get-tuple-element.282.refs_0_), channel_id=1, source_target_pairs={{0,8},{8,0},{16,24},{24,16},{1,9},{9,1},{17,25},{25,17},{2,10},{10... | collective-permute-start | bytes 2064392 | tf_op jit(solution)/shard_map/ppermute | solution.py:841
  441.7 17.1 %collective-permute-start.61 = (bf16[112,896]{1,0:T(8,128)(2,1)}, bf16[112,896]{1,0:T(8,128)(2,1)}, u32[]{:S(2)}, u32[]{:S(2)}) collective-permute-start(bf16[112,896]{1,0:T(8,128)(2,1)} %get-tuple-element.283.refs_4_), channel_id=1, source_target_pairs={{0,4},{1,5},{2,6},{3,7},{4,0},{5,1},{6,2},{7,3},{8,12},{9,13},{10,... | collective-permute-start | bytes 602120 | tf_op jit(solution)/shard_map/ppermute | solution.py:850
  465.2 13.4 %collective-permute-start.70 = (f32[1,2944]{1,0:T(1,128)}, f32[1,2944]{1,0:T(1,128)}, u32[]{:S(2)}, u32[]{:S(2)}) collective-permute-start(f32[1,2944]{1,0:T(1,128)} %get-tuple-element.290.refs_6_), channel_id=1, source_target_pairs={{0,4},{1,5},{2,6},{3,7},{4,0},{5,1},{6,2},{7,3},{8,12},{9,13},{10,... | collective-permute-start | bytes 35336 | tf_op jit(solution)/shard_map/ppermute | solution.py:850
  465.8 12.8 %collective-permute-start.68 = (bf16[112,896]{1,0:T(8,128)(2,1)}, bf16[112,896]{1,0:T(8,128)(2,1)}, u32[]{:S(2)}, u32[]{:S(2)}) collective-permute-start(bf16[112,896]{1,0:T(8,128)(2,1)} %get-tuple-element.288.refs_2_), channel_id=1, source_target_pairs={{0,1},{1,0},{2,3},{3,2},{4,5},{5,4},{6,7},{7,6},{8,9},{9,8},{10,11... | collective-permute-start | bytes 602120 | tf_op jit(solution)/shard_map/ppermute | solution.py:847
  (25 other events, 105.4 us)

commit v4 on v3

--- a/solution.py
+++ b/solution.py
@@ -241,7 +241,9 @@
         c, s = cos[...], sin[...]
         for p in range(width // 128):
             at = slice(p * 128, p * 128 + 128)
-            u = nn(n, w[:, at]) + bias[:, at]
+            if p % 2 == 0:
+                two = nn(n, w[:, p * 128 : p * 128 + 256])
+            u = two[:, p % 2 * 128 : p % 2 * 128 + 128] + bias[:, at]
             if p * 128 < qw + kw:
                 u = (u * c + swap_halves(u, lanes) * s).astype(bf16)
             if p * 128 < qw:
@@ -357,7 +359,7 @@
     )
 
 
-def attend_back(order, q, do, o, o_rest, kx, vz, cos, sin, probs, first, last, running=()):
+def attend_back(order, q, do, o, o_rest, kx, vz, cos, sin, probs, base, first, last, running=(), finish=False):
     t = q.shape[0]
     tiles = t // TILE
     count = last - first
@@ -402,28 +404,29 @@
         @pl.when(step == count - 1)
         def _():
             one = lambda a: jnp.where(left, a[0] + pltpu.roll(a[1], HD, 1), pltpu.roll(a[2], HD, 1) + a[3])
-            if not running:
-                dk[...] = one(dkacc)
-                dv[...] = one(dvacc)
-                return
-            lanes = lax.broadcasted_iota(jnp.int32, (t, 2 * HD), 1)
-            g = one(dkacc) + dk_in[...]
-            dk[...] = (g * cos[...] - swap_halves(g, lanes) * sin[...]).astype(bf16)
-            dv[...] = (one(dvacc) + dv_in[...]).astype(bf16)
+            g, gv = one(dkacc), one(dvacc)
+            if running:
+                g, gv = g + dk_in[...], gv + dv_in[...]
+            if finish:
+                lanes = lax.broadcasted_iota(jnp.int32, (t, 2 * HD), 1)
+                g = g * cos[...] - swap_halves(g, lanes) * sin[...]
+            dk[...] = g.astype(dk.dtype)
+            dv[...] = gv.astype(dv.dtype)
 
     lane = pl.BlockSpec((t, 2 * HD), lambda p: (0, p + first))
     out_lane = pl.BlockSpec((t, 2 * HD), lambda p: (0, p))
+    part_lane = pl.BlockSpec((t, 2 * HD), lambda p: (0, p + first - base))
     wide = (4, t, 2 * HD)
-    sums = (shaped((t, 2 * HD), bf16 if running else f32), fixed((t, 2 * HD)))
+    sums = (shaped((t, 2 * HD), bf16 if finish else f32), fixed((t, 2 * HD)))
     return call(
         order,
         body,
         "attend_back",
-        1 + count,
+        0.1,
         count,
-        [(q, lane), (do, out_lane), (o, out_lane), (o_rest, out_lane), (kx, fixed(wide)), (vz, fixed(wide))]
+        [(q, lane), (do, part_lane), (o, part_lane), (o_rest, part_lane), (kx, fixed(wide)), (vz, fixed(wide))]
         + [(cos, fixed(cos.shape)), (sin, fixed(sin.shape))]
-        + [(p, pl.BlockSpec((2,) + p.shape[1:], lambda i: (i, 0, 0))) for p in probs]
+        + [(p, pl.BlockSpec((2,) + p.shape[1:], lambda i: (i + first - base, 0, 0))) for p in probs]
         + [(r, fixed(r.shape)) for r in running],
         [(shaped((t, count * 2 * HD)), out_lane), sums, sums],
         [pltpu.VMEM((t, t), bf16)] * 2 + [pltpu.VMEM(wide, f32)] * 2,
@@ -486,15 +489,23 @@
     steps = t // tt
 
     def body(where, dya, dyb, mine, core_rows, x_rows, y_rows, down, *refs):
-        n2, (hid, dgu, keep, send, weights, acc, wt, tokens, copied) = refs[: len(refs) - 9], refs[-9:]
+        n2, (hid, dgu, keep, send, weights, acc, wt, tokens, copied, arrived) = refs[: len(refs) - 10], refs[-10:]
         step = pl.program_id(0)
         x, c, y = where[0], where[1], where[2]
         copy_out = pltpu.make_async_copy(wt, weights, copied)
-        for k, ref in enumerate(n2):
-
-            @pl.when(step == k)
+
+        def fetch(k):
+            return pltpu.make_async_copy(n2[k], tokens.at[k % 2], arrived.at[k % 2])
+
+        @pl.when(step == 0)
+        def _():
+            fetch(0).start()
+
+        for k in range(1, len(n2)):
+
+            @pl.when(step == k - 1)
             def _():
-                tokens[...] = ref[...]
+                fetch(k).start()
 
         @pl.when(step == 0)
         def _():
@@ -517,9 +528,15 @@
                             wt[at, lo : lo + w] = ref[:, at6 + (4 + part) * w : at6 + (5 + part) * w]
 
             copy_out.start()
-            acc[...] = jnp.zeros_like(acc)
-
-        a = tokens[...]
+
+        for k in range(len(n2)):
+
+            @pl.when(step == k)
+            def _():
+                fetch(k).wait()
+
+        a = tokens[lax.rem(step, 2)]
+        old = lambda at: jnp.where(step == 0, 0.0, acc[:, at])
         b = jnp.where(step < steps, dya[...], dyb[...])
         for lo in range(0, 2 * w, BLK):
             hi = min(lo + BLK, 2 * w)
@@ -533,9 +550,9 @@
             hid[:, g] = h
             dgu[:, g] = d_gate
             dgu[:, u] = d_up
-            acc[:, v] += tn(b, h)
-            acc[:, g] += tn(a, d_gate)
-            acc[:, u] += tn(a, d_up)
+            acc[:, v] = old(v) + tn(b, h)
+            acc[:, g] = old(g) + tn(a, d_gate)
+            acc[:, u] = old(u) + tn(a, d_up)
 
         @pl.when(step == 2 * steps - 1)
         def _():
@@ -562,7 +579,8 @@
         5 + w // 16 if off else 0.1,
         2 * steps,
         [(where, SCALARS), (dy[0], early), (dy[1], late)]
-        + [whole(a) for a in (mine, core_rows, x_rows, y_rows, down, *n2)],
+        + [whole(a) for a in (mine, core_rows, x_rows, y_rows, down)]
+        + [(a, pl.BlockSpec(memory_space=pl.ANY)) for a in n2],
         [
             (shaped((2 * t, 2 * w)), by_rows(tt, 2 * w)),
             (shaped((2 * t, 4 * w)), by_rows(tt, 4 * w)),
@@ -573,8 +591,9 @@
         [
             pltpu.VMEM((d, 6 * w), f32),
             pltpu.VMEM((d, 6 * w), bf16),
-            pltpu.VMEM((tt, d), bf16),
+            pltpu.VMEM((2, tt, d), bf16),
             pltpu.SemaphoreType.DMA(()),
+            pltpu.SemaphoreType.DMA((2,)),
         ],
     )
 
@@ -945,7 +964,7 @@
 GATE = "gate"
 
 
-def advance(order, where, chains):
+def advance(order, where, chains, us=2):
     chains = [chain for chain in chains if chain.asked is not None]
     for chain in [chain for chain in chains if chain.asked[0] == GATE]:
         chains.remove(chain)
@@ -965,7 +984,7 @@
         order,
         body,
         "sums",
-        2,
+        us,
         1,
         [(where, SCALARS)] + [pair for _, i, _ in asked for pair in i],
         [(shape, fixed(shape.shape)) for _, _, o in asked for shape in o],
@@ -1010,7 +1029,8 @@
     mine, send = yield split_sum(Y, keep, links.across(send))
     half, other = yield from replica_steps(order, links, mine, send, how)
     (rows,) = yield rows_for_core(half, other, 4 * w)
-    return half, other, links.core(rows)
+    (cores,) = yield GATE, links.core(rows)
+    return half, other, cores
 
 
 def owned_steps(order, links, keep, sends, how, widths):
@@ -1020,9 +1040,22 @@
     return (yield in_order_lanes(Y, half, other, widths))
 
 
-def small_steps(links, v, widths):
-    moves = [links.core, links.beside, links.across]
+def beside_each_other(parts):
+    def body(where, *refs):
+        lo = 0
+        for ref in refs[:-1]:
+            refs[-1][:, lo : lo + ref.shape[1]] = ref[...]
+            lo += ref.shape[1]
+
+    width = sum(p.shape[1] for p in parts)
+    return body, [(p, fixed(p.shape)) for p in parts], [shaped((parts[0].shape[0], width), parts[0].dtype)]
+
+
+def small_steps(links, parts, widths):
+    (v,) = yield beside_each_other(parts)
+    moves = [links.core, links.across]
     moves += [functools.partial(links.far, bit=bit) for bit in links.bits()]
+    moves.append(links.beside)
     for move in moves[:-1]:
         (v,) = yield whole_sum(v, move(v))
     return (yield lanes_sum(v, moves[-1](v), widths))
@@ -1149,8 +1182,8 @@
     chains, hids, dgus, weights = [], [], [], []
     how = ["whole"] + ["halves"] * (len(cuts) - 2) + ["whole"]
 
-    def step(*which):
-        advance(order, where, [chains[n] for n in which if n < len(chains)])
+    def step(*which, us=2):
+        advance(order, where, [chains[n] for n in which if n < len(chains)], us)
 
     for n in pieces:
         g = group_of[n]
@@ -1174,44 +1207,39 @@
     )
     step(1)
 
-    both = [
-        (queries, scaled[n], mixed[n], mixed_rest[n], kx, vz, cos, sin, probs[n], *span)
-        for n, span in enumerate(((0, middle), (middle, PAIRS)))
-    ]
-    dq_first, *running = attend_back(order, *both[0], ())
-    step(1, 2, 3)
     out_keep, *out_sends = weight_grads(order, where, [(mixed, d_attn)], [d // 2 // 128 * 128, d - d // 2 // 128 * 128])
-    out_chain = Chain(owned_steps(order, links, out_keep, out_sends, "whole", [d]))
-    dq_second, d_key, d_value = attend_back(order, *both[1], running)
-    chains.append(out_chain)
-    n_out = len(chains) - 1
-    step(0, 1, 2, 3, n_out)
-    d_parts = [dq_first, dq_second, d_key, d_value]
+    n_out, n_qkv, n_small = (len(cuts) + n for n in range(3))
+    chains.append(Chain(owned_steps(order, links, out_keep, out_sends, "whole", [d])))
+
+    both = [(queries, scaled[n], mixed[n], mixed_rest[n], kx, vz, cos, sin, probs[n]) for n in (0, 1)]
+    late = middle + (PAIRS - middle) // 2
+    dq_first, *running = attend_back(order, *both[0], 0, 0, middle)
+    step(2, 3, n_out, us=0.1)
+    dq_second, *running = attend_back(order, *both[1], middle, middle, late, running)
+    step(1, 2, us=0.1)
+    dq_third, d_key, d_value = attend_back(order, *both[1], middle, late, PAIRS, running, True)
+    d_parts = [dq_first, dq_second, dq_third, d_key, d_value]
     share = (qw + 2 * kw) // 3 // 128 * 128
     qkv_keep, *qkv_sends = weight_grads(
         order, where, [((normed,), p) for p in d_parts], [share, share, qw + 2 * kw - 2 * share]
     )
     chains.append(Chain(owned_steps(order, links, qkv_keep, qkv_sends, "whole", [qw, kw, kw])))
-    n_qkv = n_out + 1
-    step(3, n_out, n_qkv)
+    step(0, 1, 2, 3, n_out, us=0.1)
+    step(n_qkv, us=0.1)
     grad_tokens, grad_gain_attn, grad_biases = finish_tokens(order, tokens, gain_attn, d_parts, full_qkv, d_resid)
-    chains.append(
-        Chain(small_steps(links, jnp.concatenate([grad_gain_attn, grad_gain_ffn, grad_biases], 1), [d, d, qw, kw, kw]))
-    )
-    n_small = n_qkv + 1
-    step(1, 2, n_qkv, n_small)
+    chains.append(Chain(small_steps(links, [grad_gain_attn, grad_gain_ffn, grad_biases], [d, d, qw, kw, kw])))
     down_lanes = [2 * w for w, _ in cuts]
     out_other = [links.core(v) for v in sum_parts(order, "down_tokens", 0.1, hids, weights, down_lanes, 2, (1,), True)]
-    step(2, n_out, n_qkv)
-    (output,) = sum_parts(order, "down_tokens", 0.1, hids, weights, down_lanes, 2, (0,), False, residual, out_other)
-    step(3, n_out, n_qkv, n_small)
-    step(2, n_small)
-    step(3, n_out, n_qkv, n_small)
+    step(0, 1, 2, 3, n_out, n_qkv, n_small, us=0.1)
+    (output,) = sum_parts(order, "down_tokens", 20, hids, weights, down_lanes, 2, (0,), False, residual, out_other)
+    step(n_qkv, n_small, us=20)
+    step(1, 2, 3, n_qkv, n_small, us=20)
+    step(3, n_out, n_qkv, n_small, us=20)
     while any(chain.result is None for chain in chains[: len(cuts)]):
-        step(*range(len(chains)))
+        step(*range(len(cuts)), us=20)
     grad_gate, grad_up, grad_down = assemble(order, where, *zip(*(chain.result for chain in chains[: len(cuts)])), cuts, ff)
     while any(chain.result is None for chain in chains):
-        step(*range(len(chains)))
+        step(*range(len(chains)), us=20)
     (grad_output,), grad_qkv, small = (chain.result for chain in chains[len(cuts) :])
     return (
         output,

time: 490 us -> 472 us (0.963)
  waiting for transfers between devices: 69.8 us -> 42.2 us
  starting transfers between devices: 46.8 us -> 56 us
    ppermute x16, waiting for transfers between devices: 45.3 us -> 21.6 us  [far(): lax.ppermute(v, 'replica', [(i, i ^ bit) for i in range(self.replicas)])]
    ppermute x16, starting transfers between devices: 11.8 us -> 19.8 us  [far(): lax.ppermute(v, 'replica', [(i, i ^ bit) for i in range(self.replicas)])]
    ppermute x11, waiting for transfers between devices: 17.3 us -> 10.7 us  [across(): return lax.ppermute(v, 'shard', [(i, i ^ 2) for i in range(self.shards)])]
    ppermute x16, waiting for transfers between devices: 0.68 us -> 6.71 us  [beside(): lax.ppermute(v, 'replica', [(i, i ^ 1) for i in range(self.replicas)])]
    pallas_call x41 -> x47, Pallas kernels: 350 us -> 354 us  [call(): pl.pallas_call(kernel, grid=(grid,), in_specs=[pl.BlockSpec(memory_space=...]
  transfers between devices with their start and end apart: 71 -> 71, of which waited for: 19 -> 15; matrix products, arithmetic and copies ran while one was open for 3% -> 2% of each run, Pallas kernels for 68% -> 73%
where the time goes in v4:
time: 472 us; the launch traced here: 464 us
  Pallas kernels  354 us (75%)
  starting transfers between devices  56 us (12%)
  waiting for transfers between devices  42.2 us (9%)
  local copies, waits for them, and re-layouts  6.96 us (1%)
    pallas_call x47, Pallas kernels, call(): pl.pallas_call(kernel, grid=(grid,), in_specs=[pl.BlockSpec(memory_space=...  354 us
    ppermute x16, waiting for transfers between devices, far(): lax.ppermute(v, 'replica', [(i, i ^ bit) for i in range(self.replicas)])  21.6 us
    ppermute x16, starting transfers between devices, far(): lax.ppermute(v, 'replica', [(i, i ^ bit) for i in range(self.replicas)])  19.8 us
    ppermute x16, starting transfers between devices, beside(): lax.ppermute(v, 'replica', [(i, i ^ 1) for i in range(self.replicas)])  16.6 us
    ppermute x11, starting transfers between devices, across(): return lax.ppermute(v, 'shard', [(i, i ^ 2) for i in range(self.shards)])  14 us
    ppermute x11, waiting for transfers between devices, across(): return lax.ppermute(v, 'shard', [(i, i ^ 2) for i in range(self.shards)])  10.7 us
  transfers between devices with their start and end apart: 71, of which 15 were waited for; matrix products, arithmetic and copies ran while one was open for 2% of the time, Pallas kernels for 73%

profile of v4, /device:TPU:0, one launch (start us, length us, event | category | flops | bytes accessed | tf_op | source)
XLA Modules:
  0.0 464.0 jit_solution(97879921057873308)
XLA Ops:
  2.5 2.9 collective-permute-start
  10.1 4.4 split_weights.2
  15.0 2.5 collective-permute-done.refs_1_
  17.5 2.8 pack_weights.2.refs_0_
  25.2 9.0 %project.1 = (bf16[1024,896]{1,0:T(8,128)(2,1)}, bf16[1024,896]{1,0:T(8,128)(2,1)}, bf16[4,1024,128]{2,1,0:T(8,128)(2,1)}, bf16[4,1024,128]{2,1,0:T(8,128)(2,1)}...) custom-call(bf16[224,3328]{1,0:T(8,128)(2,1)} %pack_weights.2.refs_0_, ...), custom_call_target="tpu_custom_call" | custom-call | flops 50000000 | bytes 100000 | tf_op jit(solution)/shard_map/project/pallas_call | solution.py:67
  34.2 6.1 %split_weights.3 = (bf16[224,1536]{1,0:T(8,128)(2,1)}, bf16[224,1536]{1,0:T(8,128)(2,1)}, bf16[224,768]{1,0:T(8,128)(2,1)}, bf16[224,1536]{1,0:T(8,128)(2,1)}, b...) custom-call(bf16[1024,896]{1,0:T(8,128)(2,1)} %get-tuple-element.165, ...), custom_call_target="tpu_custom_call" | custom-call | flops 50000000 | bytes 100000 | tf_op jit(solution)/shard_map/split_weights/pallas_call | solution.py:67
  42.5 13.8 %attend.2 = (bf16[1024,384]{1,0:T(8,128)(2,1)}, bf16[1024,384]{1,0:T(8,128)(2,1)}, f32[1024,384]{1,0:T(8,128)}, bf16[6,1024,256]{2,1,0:T(8,128)(2,1)}, bf16[6,76...) custom-call(bf16[224,1536]{1,0:T(8,128)(2,1)} %get-tuple-element.166.refs_0_, ...), custom_call_target="tpu_custom_call" | custom-call | flops 50000000 | bytes 100000 | tf_op jit(solution)/shard_map/attend/pallas_call | solution.py:67
  58.3 4.3 pack_weights.3
  67.4 17.1 %attend.3 = (bf16[1024,512]{1,0:T(8,128)(2,1)}, bf16[1024,512]{1,0:T(8,128)(2,1)}, f32[1024,512]{1,0:T(8,128)}, bf16[8,1024,256]{2,1,0:T(8,128)(2,1)}, bf16[8,76...) custom-call(bf16[224,2304]{1,0:T(8,128)(2,1)} %get-tuple-element.179.refs_0_, ...), custom_call_target="tpu_custom_call" | custom-call | flops 50000000 | bytes 100000 | tf_op jit(solution)/shard_map/attend/pallas_call | solution.py:67
  84.5 8.3 %join_output.1 = (f32[1024,896]{1,0:T(8,128)}, bf16[896,896]{1,0:T(8,128)(2,1)}, bf16[512,896]{1,0:T(8,128)(2,1)}, bf16[512,896]{1,0:T(8,128)(2,1)}) custom-call(bf16[1024,512]{1,0:T(8,128)(2,1)} %get-tuple-element.180.refs_0_.refs_9_.refs_3_, bf16[224,1536]{1,0:T(8,128)(2,1)} %collective-permute-done.10.refs_1_.refs_7_, ...), custom_call_target="tpu_custom_call" | custom-call | flops 50000000 | bytes 100000 | tf_op jit(solution)/shard_map/join_output/pallas_call | solution.py:67
  97.0 20.8 %ffn_part.4 = (bf16[2048,512]{1,0:T(8,128)(2,1)}, bf16[2048,1024]{1,0:T(8,128)(2,1)}, bf16[448,1536]{1,0:T(8,128)(2,1)}, bf16[448,1536]{1,0:T(8,128)(2,1)}, bf16[896,1536]{1,0:T(8,128)(2,1)}) custom-call(bf16[224,2304]{1,0:T(8,128)(2,1)} %gate.8.refs_0_.refs_6_, s32[4]{0:T(128)} %pad_add_fusion.refs_3_.refs_1_.refs_2_, bf16[1024,896]{1,0:T(8,128)(2,1)} %refs_3_.7, ...), custom_call_target="tpu_custom_call" | custom-call | flops 50000000 | bytes 100000 | tf_op jit(solution)/shard_map/ffn_part/pallas_call | solution.py:67
  117.8 3.5 collective-permute-done.14.refs_1_
  123.4 28.4 %ffn_part.5 = (bf16[2048,768]{1,0:T(8,128)(2,1)}, bf16[2048,1536]{1,0:T(8,128)(2,1)}, bf16[448,2304]{1,0:T(8,128)(2,1)}, bf16[448,2304]{1,0:T(8,128)(2,1)}, bf16[896,2304]{1,0:T(8,128)(2,1)}) custom-call(bf16[224,3456]{1,0:T(8,128)(2,1)} %gate.9.refs_0_.refs_6_, s32[4]{0:T(128)} %pad_add_fusion.refs_3_.refs_1_.refs_2_, bf16[1024,896]{1,0:T(8,128)(2,1)} %refs_3_.7, ...), custom_call_target="tpu_custom_call" | custom-call | flops 14499999744 | bytes 100000 | tf_op jit(solution)/shard_map/ffn_part/pallas_call | solution.py:67
  155.4 3.1 sums.15
  159.3 28.3 %ffn_part.6 = (bf16[2048,768]{1,0:T(8,128)(2,1)}, bf16[2048,1536]{1,0:T(8,128)(2,1)}, bf16[448,2304]{1,0:T(8,128)(2,1)}, bf16[448,2304]{1,0:T(8,128)(2,1)}, bf16[896,2304]{1,0:T(8,128)(2,1)}) custom-call(bf16[224,1536]{1,0:T(8,128)(2,1)} %get-tuple-element.189.refs_0_.refs_2_, s32[4]{0:T(128)} %pad_add_fusion.refs_3_.refs_1_.refs_2_, ...), custom_call_target="tpu_custom_call" | custom-call | flops 14499999744 | bytes 100000 | tf_op jit(solution)/shard_map/ffn_part/pallas_call | solution.py:67
  187.7 2.4 sums.16.refs_0_.refs_2_
  191.4 20.3 %ffn_part.7 = (bf16[2048,384]{1,0:T(8,128)(2,1)}, bf16[2048,768]{1,0:T(8,128)(2,1)}, bf16[448,1152]{1,0:T(8,128)(2,1)}, bf16[448,1152]{1,0:T(8,128)(2,1)}, bf16[896,1152]{1,0:T(8,128)(2,1)}) custom-call(bf16[224,1536]{1,0:T(8,128)(2,1)} %sums.16.refs_0_.refs_2_, s32[4]{0:T(128)} %pad_add_fusion.refs_3_.refs_1_.refs_2_, bf16[1024,896]{1,0:T(8,128)(2,1)} %refs_3_.7, ...), custom_call_target="tpu_custom_call" | custom-call | flops 8499999744 | bytes 100000 | tf_op jit(solution)/shard_map/ffn_part/pallas_call | solution.py:67
  211.7 4.4 sums.17
  216.1 2.6 collective-permute-start.21
  220.2 29.2 %back_tokens.1 = (bf16[256,896]{1,0:T(8,128)(2,1)}, bf16[256,896]{1,0:T(8,128)(2,1)}, bf16[256,896]{1,0:T(8,128)(2,1)}, bf16[256,896]{1,0:T(8,128)(2,1)}, f32[1024,896]{1,0:T(8,128)}) custom-call(bf16[224,1536]{1,0:T(8,128)(2,1)} %get-tuple-element.195.refs_0_.refs_2_, bf16[2048,1024]{1,0:T(8,128)(2,1)} %get-tuple-element.196.refs_1_, ...), custom_call_target="tpu_custom_call" | custom-call | flops 12000000000 | bytes 100000 | tf_op jit(solution)/shard_map/back_tokens/pallas_call | solution.py:67
  250.5 5.4 %sums.18 = (bf16[224,1536]{1,0:T(8,128)(2,1)}, bf16[112,2304]{1,0:T(8,128)(2,1)}, bf16[112,2304]{1,0:T(8,128)(2,1)}, bf16[224,2304]{1,0:T(8,128)(2,1)}, bf16[224,2304]{1,0:T(8,128)(2,1)}) custom-call(bf16[256,896]{1,0:T(8,128)(2,1)} %get-tuple-element.204.refs_0_, s32[4]{0:T(128)} %pad_add_fusion.refs_3_.refs_1_.refs_2_, ...), custom_call_target="tpu_custom_call" | custom-call | flops 1000000000 | bytes 100000 | tf_op jit(solution)/shard_map/sums/pallas_call | solution.py:67
  258.9 10.1 %turn_back.1 = (f32[1024,896]{1,0:T(8,128)}, bf16[1024,896]{1,0:T(8,128)(2,1)}, f32[1,896]{1,0:T(1,128)}, bf16[1024,384]{1,0:T(8,128)(2,1)}, bf16[1024,512]{1,0:T(8,128)(2,1)}) custom-call(bf16[224,1536]{1,0:T(8,128)(2,1)} %get-tuple-element.209.refs_0_.refs_2_, f32[1024,896]{1,0:T(8,128)} %get-tuple-element.210.refs_1_, ...), custom_call_target="tpu_custom_call" | custom-call | flops 4000000000 | bytes 100000 | tf_op jit(solution)/shard_map/turn_back/pallas_call | solution.py:67
  272.1 5.3 %weight_grads.2 = (bf16[448,896]{1,0:T(8,128)(2,1)}, bf16[448,384]{1,0:T(8,128)(2,1)}, bf16[448,512]{1,0:T(8,128)(2,1)}) custom-call(bf16[112,2304]{1,0:T(8,128)(2,1)} %sums.19.refs_0_.refs_2_, s32[4]{0:T(128)} %pad_add_fusion.refs_3_.refs_1_.refs_2_, bf16[1024,384]{1,0:T(8,128)(2,1)} %get-tuple-element.170.refs_0_.refs_8_.refs_2_.refs_3_, ...), custom_call_target="tpu_custom_call" | custom-call | flops 50000000 | bytes 100000 | tf_op jit(solution)/shard_map/weight_grads/pallas_call | solution.py:67
  278.3 17.8 %attend_back.3 = (bf16[1024,384]{1,0:T(8,128)(2,1)}, f32[1024,128]{1,0:T(8,128)}, f32[1024,128]{1,0:T(8,128)}) custom-call(bf16[448,896]{1,0:T(8,128)(2,1)} %get-tuple-element.221.refs_0_.refs_6_, bf16[1024,896]{1,0:T(8,128)(2,1)} %get-tuple-element.167.refs_3_.refs_1_, bf16[1024,384]{1,0:T(8,128)(2,1)} %get-tuple-element.222.refs_2_, ...), custom_call_target="tpu_custom_call" | custom-call | flops 50000000 | bytes 100000 | tf_op jit(solution)/shard_map/attend_back/pallas_call | solution.py:67
  296.1 4.7 %sums.20 = (bf16[112,2304]{1,0:T(8,128)(2,1)}, bf16[112,2304]{1,0:T(8,128)(2,1)}, bf16[224,1152]{1,0:T(8,128)(2,1)}, bf16[224,1152]{1,0:T(8,128)(2,1)}, bf16[224...) custom-call(bf16[1024,384]{1,0:T(8,128)(2,1)} %get-tuple-element.229.refs_0_.refs_3_.refs_5_, ...), custom_call_target="tpu_custom_call" | custom-call | flops 50000000 | bytes 100000 | tf_op jit(solution)/shard_map/sums/pallas_call | solution.py:67
  305.2 13.8 %attend_back.4 = (bf16[1024,256]{1,0:T(8,128)(2,1)}, f32[1024,128]{1,0:T(8,128)}, f32[1024,128]{1,0:T(8,128)}) custom-call(bf16[112,2304]{1,0:T(8,128)(2,1)} %get-tuple-element.236.refs_0_.refs_4_, bf16[1024,896]{1,0:T(8,128)(2,1)} %get-tuple-element.167.refs_3_.refs_1_, bf16[1024,512]{1,0:T(8,128)(2,1)} %get-tuple-element.237.refs_2_, ...), custom_call_target="tpu_custom_call" | custom-call | flops 50000000 | bytes 100000 | tf_op jit(solution)/shard_map/attend_back/pallas_call | solution.py:67
  319.0 2.6 sums.21
  321.7 2.6 collective-permute-start.37
  325.9 14.2 %attend_back.5 = (bf16[1024,256]{1,0:T(8,128)(2,1)}, bf16[1024,128]{1,0:T(8,128)(2,1)}, bf16[1024,128]{1,0:T(8,128)(2,1)}) custom-call(bf16[112,2304]{1,0:T(8,128)(2,1)} %get-tuple-element.247.refs_0_.refs_4_, bf16[1024,896]{1,0:T(8,128)(2,1)} %get-tuple-element.167.refs_3_.refs_1_, bf16[1024,512]{1,0:T(8,128)(2,1)} %get-tuple-element.237.refs_2_, ...), custom_call_target="tpu_custom_call" | custom-call | flops 50000000 | bytes 100000 | tf_op jit(solution)/shard_map/attend_back/pallas_call | solution.py:67
  340.1 6.5 %weight_grads.3 = (bf16[448,1152]{1,0:T(8,128)(2,1)}, bf16[448,384]{1,0:T(8,128)(2,1)}, bf16[448,384]{1,0:T(8,128)(2,1)}, bf16[448,384]{1,0:T(8,128)(2,1)}) custom-call(bf16[1024,256]{1,0:T(8,128)(2,1)} %get-tuple-element.250.refs_0_.refs_5_.refs_7_, s32[4]{0:T(128)} %pad_add_fusion.refs_3_.refs_1_.refs_2_, ...), custom_call_target="tpu_custom_call" | custom-call | flops 50000000 | bytes 100000 | tf_op jit(solution)/shard_map/weight_grads/pallas_call | solution.py:67
  347.2 4.0 sums.22
  353.3 2.6 sums.23
  359.4 9.4 %finish_tokens.1 = (f32[1024,896]{1,0:T(8,128)}, f32[1,896]{1,0:T(1,128)}, f32[1,1152]{1,0:T(1,128)}) custom-call(bf16[224,1152]{1,0:T(8,128)(2,1)} %get-tuple-element.263.refs_0_.refs_10_, bf16[1024,896]{1,0:T(8,128)(2,1)} %refs_1_.3, f32[1,896]{1,0:T(1,128)} %broadcast_in_dim.11.refs_4_.refs_2_, bf16[896,1152]{1,0:T(8,128)(2,1)} %get-tuple-element.264.refs_3_, ...), custom_call_target="tpu_custom_call" | custom-call | flops 50000000 | bytes 100000 | tf_op jit(solution)/shard_map/finish_tokens/pallas_call | solution.py:67
  368.8 10.7 %down_tokens.2 = (bf16[256,896]{1,0:T(8,128)(2,1)}, bf16[256,896]{1,0:T(8,128)(2,1)}, bf16[256,896]{1,0:T(8,128)(2,1)}, bf16[256,896]{1,0:T(8,128)(2,1)}) custom-call(f32[1024,896]{1,0:T(8,128)} %get-tuple-element.149.refs_0_, bf16[2048,512]{1,0:T(8,128)(2,1)} %get-tuple-element.184.refs_0_.refs_1_, bf16[2048,768]{1,0:T(8,128)(2,1)} %get-tuple-element.186.refs_0_.refs_2_, ...), custom_call_target="tpu_custom_call" | custom-call | flops 50000000 | bytes 100000 | tf_op jit(solution)/shard_map/down_tokens/pallas_call | solution.py:67
  381.0 4.1 sums.24
  388.5 12.1 %down_tokens.3.refs_0_ = bf16[1024,896]{1,0:T(8,128)(2,1)} custom-call(bf16[224,1536]{1,0:T(8,128)(2,1)} %get-tuple-element.276.refs_0_, bf16[2048,512]{1,0:T(8,128)(2,1)} %get-tuple-element.184.refs_0_.refs_1_, bf16[2048,768]{1,0:T(8,128)(2,1)} %get-tuple-element.186.refs_0_.refs_2_, bf16[2048,768]{1,0:T(8,128)(2,1)} %get-tuple-element.190.refs_0_.refs_3_, ...), custom_call_target="tpu_custom_call" | custom-call | flops 10000000000 | bytes 100000 | tf_op jit(solution)/shard_map/down_tokens/pallas_call | solution.py:67
  405.9 2.5 collective-permute-done.59.refs_9_
  408.4 3.5 collective-permute-done.57.refs_5_
  411.9 5.4 %collective-permute-done.58.refs_7_ = bf16[112,1152]{1,0:T(8,128)(2,1)} collective-permute-done((bf16[112,1152]{1,0:T(8,128)(2,1)}, bf16[112,1152]{1,0:T(8,128)(2,1)}, u32[]{:S(2)}, u32[]{:S(2)}) %collective-permute-start.58) | collective-permute-done | bytes 258080 | tf_op jit(solution)/shard_map/ppermute | solution.py:869
  417.3 2.9 sums.26
  421.6 2.4 collective-permute-start.61
  424.1 8.1 %collective-permute-done.61.refs_5_ = bf16[112,896]{1,0:T(8,128)(2,1)} collective-permute-done((bf16[112,896]{1,0:T(8,128)(2,1)}, bf16[112,896]{1,0:T(8,128)(2,1)}, u32[]{:S(2)}, u32[]{:S(2)}) %collective-permute-start.61) | collective-permute-done | bytes 200736 | tf_op jit(solution)/shard_map/ppermute | solution.py:869
  432.2 3.3 collective-permute-done.62.refs_7_
  435.5 2.4 sums.27
  437.9 2.9 collective-permute-start.66
  441.3 10.8 %assemble.1 = (f32[224,4864]{1,0:T(8,128)}, f32[224,4864]{1,0:T(8,128)}, f32[1216,896]{1,0:T(8,128)}) custom-call(bf16[224,768]{1,0:T(8,128)(2,1)} %gate.13.refs_0_.refs_13_, s32[4]{0:T(128)} %pad_add_fusion.refs_3_.refs_1_.refs_2_, bf16[224,1536]{1,0:T(8,128)(2,1)} %get-tuple-element.209.refs_0_.refs_2_, ...), custom_call_target="tpu_custom_call" | custom-call | flops 5500000256 | bytes 100000 | tf_op jit(solution)/shard_map/assemble/pallas_call | solution.py:67
  452.1 2.4 sums.28
  456.5 5.1 %collective-permute-done.70.refs_5_ = f32[1,2944]{1,0:T(1,128)} collective-permute-done((f32[1,2944]{1,0:T(1,128)}, f32[1,2944]{1,0:T(1,128)}, u32[]{:S(2)}, u32[]{:S(2)}) %collective-permute-start.70) | collective-permute-done | bytes 11808 | tf_op jit(solution)/shard_map/ppermute | solution.py:866
  (156 shorter events, 70.9 us)
Async XLA Ops:
  2.5 15.0 %collective-permute-start = (bf16[224,1152]{1,0:T(8,128)(2,1)}, bf16[224,1152]{1,0:T(8,128)(2,1)}, u32[]{:S(2)}, u32[]{:S(2)}) collective-permute-start(bf16[224,1152]{1,0:T(8,128)(2,1)} %side_by_side.1.refs_0_.refs_5_), channel_id=1, source_target_pairs={{0,16},{8,24},{16,0},{24,8},{1,17},{9,25},{17,1},{25,9},{2,18},{10... | collective-permute-start | bytes 1548296 | tf_op jit(solution)/shard_map/ppermute | solution.py:863
  5.5 19.7 %collective-permute-start.3 = (bf16[1024,896]{1,0:T(8,128)(2,1)}, bf16[1024,896]{1,0:T(8,128)(2,1)}, u32[]{:S(2)}, u32[]{:S(2)}) collective-permute-start(bf16[1024,896]{1,0:T(8,128)(2,1)} %refs_3_.7), channel_id=1, source_target_pairs={{0,8},{8,0},{16,24},{24,16},{1,9},{9,1},{17,25},{25,17},{2,10},{10... | collective-permute-start | bytes 5505032 | tf_op jit(solution)/shard_map/ppermute | solution.py:860
  20.3 35.9 %collective-permute-start.6 = (bf16[224,3328]{1,0:T(8,128)(2,1)}, bf16[224,3328]{1,0:T(8,128)(2,1)}, u32[]{:S(2)}, u32[]{:S(2)}) collective-permute-start(bf16[224,3328]{1,0:T(8,128)(2,1)} %pack_weights.2.refs_0_), channel_id=1, source_target_pairs={{0,16},{8,24},{16,0},{24,8},{1,17},{9,25},{17,1},{25,9},{2,18},{10... | collective-permute-start | bytes 4472840 | tf_op jit(solution)/shard_map/ppermute | solution.py:863
  40.2 18.0 %collective-permute-start.8 = (bf16[224,1536]{1,0:T(8,128)(2,1)}, bf16[224,1536]{1,0:T(8,128)(2,1)}, u32[]{:S(2)}, u32[]{:S(2)}) collective-permute-start(bf16[224,1536]{1,0:T(8,128)(2,1)} %get-tuple-element.171), channel_id=1, source_target_pairs={{0,8},{8,0},{16,24},{24,16},{1,9},{9,1},{17,25},{25,17},{2,10},{10... | collective-permute-start | bytes 2064392 | tf_op jit(solution)/shard_map/ppermute | solution.py:860
  40.2 18.0 %collective-permute-start.7 = (bf16[224,1536]{1,0:T(8,128)(2,1)}, bf16[224,1536]{1,0:T(8,128)(2,1)}, u32[]{:S(2)}, u32[]{:S(2)}) collective-permute-start(bf16[224,1536]{1,0:T(8,128)(2,1)} %get-tuple-element.166.refs_0_), channel_id=1, source_target_pairs={{0,8},{8,0},{16,24},{24,16},{1,9},{9,1},{17,25},{25,17},{2,10},{10... | collective-permute-start | bytes 2064392 | tf_op jit(solution)/shard_map/ppermute | solution.py:860
  40.7 17.5 %collective-permute-start.9 = (bf16[224,768]{1,0:T(8,128)(2,1)}, bf16[224,768]{1,0:T(8,128)(2,1)}, u32[]{:S(2)}, u32[]{:S(2)}) collective-permute-start(bf16[224,768]{1,0:T(8,128)(2,1)} %get-tuple-element.172), channel_id=1, source_target_pairs={{0,8},{8,0},{16,24},{24,16},{1,9},{9,1},{17,25},{25,17},{2,10},{10... | collective-permute-start | bytes 1032200 | tf_op jit(solution)/shard_map/ppermute | solution.py:860
  62.6 30.7 %collective-permute-start.11 = (bf16[224,2304]{1,0:T(8,128)(2,1)}, bf16[224,2304]{1,0:T(8,128)(2,1)}, u32[]{:S(2)}, u32[]{:S(2)}) collective-permute-start(bf16[224,2304]{1,0:T(8,128)(2,1)} %get-tuple-element.179.refs_0_), channel_id=1, source_target_pairs={{0,16},{8,24},{16,0},{24,8},{1,17},{9,25},{17,1},{25,9},{2,18},{10... | collective-permute-start | bytes 3096584 | tf_op jit(solution)/shard_map/ppermute | solution.py:863
  62.9 21.6 %collective-permute-start.10 = (bf16[224,1536]{1,0:T(8,128)(2,1)}, bf16[224,1536]{1,0:T(8,128)(2,1)}, u32[]{:S(2)}, u32[]{:S(2)}) collective-permute-start(bf16[224,1536]{1,0:T(8,128)(2,1)} %first_lanes.1.refs_0_), channel_id=1, source_target_pairs={{0,1},{1,0},{2,3},{3,2},{4,5},{5,4},{6,7},{7,6},{8,9},{9,8},{10,11... | collective-permute-start | bytes 2064392 | tf_op jit(solution)/shard_map/ppermute | solution.py:866
  64.7 56.7 %collective-permute-start.14 = (bf16[224,3456]{1,0:T(8,128)(2,1)}, bf16[224,3456]{1,0:T(8,128)(2,1)}, u32[]{:S(2)}, u32[]{:S(2)}) collective-permute-start(bf16[224,3456]{1,0:T(8,128)(2,1)} %get-tuple-element.185), channel_id=1, source_target_pairs={{0,16},{8,24},{16,0},{24,8},{1,17},{9,25},{17,1},{25,9},{2,18},{10... | collective-permute-start | bytes 4644872 | tf_op jit(solution)/shard_map/ppermute | solution.py:863
  93.3 30.0 %collective-permute-start.15 = (bf16[224,2304]{1,0:T(8,128)(2,1)}, bf16[224,2304]{1,0:T(8,128)(2,1)}, u32[]{:S(2)}, u32[]{:S(2)}) collective-permute-start(bf16[224,2304]{1,0:T(8,128)(2,1)} %gate.8.refs_0_.refs_6_), channel_id=1, source_target_pairs={{0,1},{1,0},{2,3},{3,2},{4,5},{5,4},{6,7},{7,6},{8,9},{9,8},{10,11... | collective-permute-start | bytes 3096584 | tf_op jit(solution)/shard_map/ppermute | solution.py:866
  121.3 37.9 %collective-permute-start.17 = (bf16[224,3456]{1,0:T(8,128)(2,1)}, bf16[224,3456]{1,0:T(8,128)(2,1)}, u32[]{:S(2)}, u32[]{:S(2)}) collective-permute-start(bf16[224,3456]{1,0:T(8,128)(2,1)} %gate.9.refs_0_.refs_6_), channel_id=1, source_target_pairs={{0,1},{1,0},{2,3},{3,2},{4,5},{5,4},{6,7},{7,6},{8,9},{9,8},{10,11... | collective-permute-start | bytes 4644872 | tf_op jit(solution)/shard_map/ppermute | solution.py:866
  122.8 32.6 %collective-permute-start.16 = (bf16[448,1536]{1,0:T(8,128)(2,1)}, bf16[448,1536]{1,0:T(8,128)(2,1)}, u32[]{:S(2)}, u32[]{:S(2)}) collective-permute-start(bf16[448,1536]{1,0:T(8,128)(2,1)} %get-tuple-element.188), channel_id=1, source_target_pairs={{0,16},{8,24},{16,0},{24,8},{1,17},{9,25},{17,1},{25,9},{2,18},{10... | collective-permute-start | bytes 4128776 | tf_op jit(solution)/shard_map/ppermute | solution.py:863
  151.7 59.9 %collective-permute-start.20 = (bf16[448,2304]{1,0:T(8,128)(2,1)}, bf16[448,2304]{1,0:T(8,128)(2,1)}, u32[]{:S(2)}, u32[]{:S(2)}) collective-permute-start(bf16[448,2304]{1,0:T(8,128)(2,1)} %get-tuple-element.194), channel_id=1, source_target_pairs={{0,16},{8,24},{16,0},{24,8},{1,17},{9,25},{17,1},{25,9},{2,18},{10... | collective-permute-start | bytes 6193160 | tf_op jit(solution)/shard_map/ppermute | solution.py:863
  158.5 29.2 %collective-permute-start.18 = (bf16[224,1536]{1,0:T(8,128)(2,1)}, bf16[224,1536]{1,0:T(8,128)(2,1)}, u32[]{:S(2)}, u32[]{:S(2)}) collective-permute-start(bf16[224,1536]{1,0:T(8,128)(2,1)} %get-tuple-element.191), channel_id=1, source_target_pairs={{0,1},{1,0},{2,3},{3,2},{4,5},{5,4},{6,7},{7,6},{8,9},{9,8},{10,11... | collective-permute-start | bytes 2064392 | tf_op jit(solution)/shard_map/ppermute | solution.py:866
  187.6 62.9 %collective-permute-start.23 = (bf16[448,2304]{1,0:T(8,128)(2,1)}, bf16[448,2304]{1,0:T(8,128)(2,1)}, u32[]{:S(2)}, u32[]{:S(2)}) collective-permute-start(bf16[448,2304]{1,0:T(8,128)(2,1)} %get-tuple-element.208), channel_id=1, source_target_pairs={{0,16},{8,24},{16,0},{24,8},{1,17},{9,25},{17,1},{25,9},{2,18},{10... | collective-permute-start | bytes 6193160 | tf_op jit(solution)/shard_map/ppermute | solution.py:863
  190.0 21.6 %collective-permute-start.19 = (bf16[224,1536]{1,0:T(8,128)(2,1)}, bf16[224,1536]{1,0:T(8,128)(2,1)}, u32[]{:S(2)}, u32[]{:S(2)}) collective-permute-start(bf16[224,1536]{1,0:T(8,128)(2,1)} %sums.16.refs_0_.refs_2_), channel_id=1, source_target_pairs={{0,2},{1,3},{2,0},{3,1},{4,6},{5,7},{6,4},{7,5},{8,10},{9,11},{10,... | collective-permute-start | bytes 2064392 | tf_op jit(solution)/shard_map/ppermute | solution.py:869
  216.1 33.9 %collective-permute-start.21 = (bf16[224,1536]{1,0:T(8,128)(2,1)}, bf16[224,1536]{1,0:T(8,128)(2,1)}, u32[]{:S(2)}, u32[]{:S(2)}) collective-permute-start(bf16[224,1536]{1,0:T(8,128)(2,1)} %get-tuple-element.195.refs_0_.refs_2_), channel_id=1, source_target_pairs={{0,4},{1,5},{2,6},{3,7},{4,0},{5,1},{6,2},{7,3},{8,12},{9,13},{10,... | collective-permute-start | bytes 2064392 | tf_op jit(solution)/shard_map/ppermute | solution.py:869
  218.7 31.4 %collective-permute-start.22 = (bf16[224,2304]{1,0:T(8,128)(2,1)}, bf16[224,2304]{1,0:T(8,128)(2,1)}, u32[]{:S(2)}, u32[]{:S(2)}) collective-permute-start(bf16[224,2304]{1,0:T(8,128)(2,1)} %get-tuple-element.206), channel_id=1, source_target_pairs={{0,1},{1,0},{2,3},{3,2},{4,5},{5,4},{6,7},{7,6},{8,9},{9,8},{10,11... | collective-permute-start | bytes 3096584 | tf_op jit(solution)/shard_map/ppermute | solution.py:866
  255.9 14.0 %collective-permute-start.28 = (bf16[112,2304]{1,0:T(8,128)(2,1)}, bf16[112,2304]{1,0:T(8,128)(2,1)}, u32[]{:S(2)}, u32[]{:S(2)}) collective-permute-start(bf16[112,2304]{1,0:T(8,128)(2,1)} %get-tuple-element.219), channel_id=1, source_target_pairs={{0,2},{1,3},{2,0},{3,1},{4,6},{5,7},{6,4},{7,5},{8,10},{9,11},{10,... | collective-permute-start | bytes 1548296 | tf_op jit(solution)/shard_map/ppermute | solution.py:869
  256.4 39.7 %collective-permute-start.30 = (bf16[448,1152]{1,0:T(8,128)(2,1)}, bf16[448,1152]{1,0:T(8,128)(2,1)}, u32[]{:S(2)}, u32[]{:S(2)}) collective-permute-start(bf16[448,1152]{1,0:T(8,128)(2,1)} %get-tuple-element.233), channel_id=1, source_target_pairs={{0,16},{8,24},{16,0},{24,8},{1,17},{9,25},{17,1},{25,9},{2,18},{10... | collective-permute-start | bytes 3096584 | tf_op jit(solution)/shard_map/ppermute | solution.py:863
  258.4 37.7 %collective-permute-start.29 = (bf16[224,2304]{1,0:T(8,128)(2,1)}, bf16[224,2304]{1,0:T(8,128)(2,1)}, u32[]{:S(2)}, u32[]{:S(2)}) collective-permute-start(bf16[224,2304]{1,0:T(8,128)(2,1)} %get-tuple-element.231), channel_id=1, source_target_pairs={{0,1},{1,0},{2,3},{3,2},{4,5},{5,4},{6,7},{7,6},{8,9},{9,8},{10,11... | collective-permute-start | bytes 3096584 | tf_op jit(solution)/shard_map/ppermute | solution.py:866
  277.4 18.6 %collective-permute-start.32 = (bf16[448,512]{1,0:T(8,128)(2,1)}, bf16[448,512]{1,0:T(8,128)(2,1)}, u32[]{:S(2)}, u32[]{:S(2)}) collective-permute-start(bf16[448,512]{1,0:T(8,128)(2,1)} %get-tuple-element.235), channel_id=1, source_target_pairs={{0,8},{8,0},{16,24},{24,16},{1,9},{9,1},{17,25},{25,17},{2,10},{10... | collective-permute-start | bytes 1376264 | tf_op jit(solution)/shard_map/ppermute | solution.py:860
  277.4 18.6 %collective-permute-start.31 = (bf16[448,384]{1,0:T(8,128)(2,1)}, bf16[448,384]{1,0:T(8,128)(2,1)}, u32[]{:S(2)}, u32[]{:S(2)}) collective-permute-start(bf16[448,384]{1,0:T(8,128)(2,1)} %get-tuple-element.234), channel_id=1, source_target_pairs={{0,8},{8,0},{16,24},{24,16},{1,9},{9,1},{17,25},{25,17},{2,10},{10... | collective-permute-start | bytes 1032200 | tf_op jit(solution)/shard_map/ppermute | solution.py:860
  278.0 41.0 %collective-permute-start.33 = (bf16[112,2304]{1,0:T(8,128)(2,1)}, bf16[112,2304]{1,0:T(8,128)(2,1)}, u32[]{:S(2)}, u32[]{:S(2)}) collective-permute-start(bf16[112,2304]{1,0:T(8,128)(2,1)} %sums.19.refs_0_.refs_2_), channel_id=1, source_target_pairs={{0,4},{1,5},{2,6},{3,7},{4,0},{5,1},{6,2},{7,3},{8,12},{9,13},{10,... | collective-permute-start | bytes 1548296 | tf_op jit(solution)/shard_map/ppermute | solution.py:869
  300.8 18.2 %collective-permute-start.34 = (bf16[112,2304]{1,0:T(8,128)(2,1)}, bf16[112,2304]{1,0:T(8,128)(2,1)}, u32[]{:S(2)}, u32[]{:S(2)}) collective-permute-start(bf16[112,2304]{1,0:T(8,128)(2,1)} %get-tuple-element.246), channel_id=1, source_target_pairs={{0,2},{1,3},{2,0},{3,1},{4,6},{5,7},{6,4},{7,5},{8,10},{9,11},{10,... | collective-permute-start | bytes 1548296 | tf_op jit(solution)/shard_map/ppermute | solution.py:869
  301.4 45.2 %collective-permute-start.35 = (bf16[224,1536]{1,0:T(8,128)(2,1)}, bf16[224,1536]{1,0:T(8,128)(2,1)}, u32[]{:S(2)}, u32[]{:S(2)}) collective-permute-start(bf16[224,1536]{1,0:T(8,128)(2,1)} %get-tuple-element.209.refs_0_.refs_2_), channel_id=1, source_target_pairs={{0,1},{1,0},{2,3},{3,2},{4,5},{5,4},{6,7},{7,6},{8,9},{9,8},{10,11... | collective-permute-start | bytes 2064392 | tf_op jit(solution)/shard_map/ppermute | solution.py:866
  302.9 44.2 %collective-permute-start.38 = (bf16[224,1152]{1,0:T(8,128)(2,1)}, bf16[224,1152]{1,0:T(8,128)(2,1)}, u32[]{:S(2)}, u32[]{:S(2)}) collective-permute-start(bf16[224,1152]{1,0:T(8,128)(2,1)} %get-tuple-element.256), channel_id=1, source_target_pairs={{0,1},{1,0},{2,3},{3,2},{4,5},{5,4},{6,7},{7,6},{8,9},{9,8},{10,11... | collective-permute-start | bytes 1548296 | tf_op jit(solution)/shard_map/ppermute | solution.py:866
  303.4 43.2 %collective-permute-start.39 = (bf16[224,896]{1,0:T(8,128)(2,1)}, bf16[224,896]{1,0:T(8,128)(2,1)}, u32[]{:S(2)}, u32[]{:S(2)}) collective-permute-start(bf16[224,896]{1,0:T(8,128)(2,1)} %get-tuple-element.258), channel_id=1, source_target_pairs={{0,16},{8,24},{16,0},{24,8},{1,17},{9,25},{17,1},{25,9},{2,18},{10... | collective-permute-start | bytes 1204232 | tf_op jit(solution)/shard_map/ppermute | solution.py:863
  321.7 25.5 %collective-permute-start.37 = (bf16[112,2304]{1,0:T(8,128)(2,1)}, bf16[112,2304]{1,0:T(8,128)(2,1)}, u32[]{:S(2)}, u32[]{:S(2)}) collective-permute-start(bf16[112,2304]{1,0:T(8,128)(2,1)} %get-tuple-element.254.refs_6_), channel_id=1, source_target_pairs={{0,4},{1,5},{2,6},{3,7},{4,0},{5,1},{6,2},{7,3},{8,12},{9,13},{10,... | collective-permute-start | bytes 1548296 | tf_op jit(solution)/shard_map/ppermute | solution.py:869
  324.3 22.9 %collective-permute-start.36 = (bf16[112,2304]{1,0:T(8,128)(2,1)}, bf16[112,2304]{1,0:T(8,128)(2,1)}, u32[]{:S(2)}, u32[]{:S(2)}) collective-permute-start(bf16[112,2304]{1,0:T(8,128)(2,1)} %get-tuple-element.247.refs_0_.refs_4_), channel_id=1, source_target_pairs={{0,2},{1,3},{2,0},{3,1},{4,6},{5,7},{6,4},{7,5},{8,10},{9,11},{10,... | collective-permute-start | bytes 1548296 | tf_op jit(solution)/shard_map/ppermute | solution.py:869
  351.7 29.3 %collective-permute-start.44 = (bf16[224,2304]{1,0:T(8,128)(2,1)}, bf16[224,2304]{1,0:T(8,128)(2,1)}, u32[]{:S(2)}, u32[]{:S(2)}) collective-permute-start(bf16[224,2304]{1,0:T(8,128)(2,1)} %get-tuple-element.267.refs_2_.refs_3_), channel_id=1, source_target_pairs={{0,1},{1,0},{2,3},{3,2},{4,5},{5,4},{6,7},{7,6},{8,9},{9,8},{10,11... | collective-permute-start | bytes 3096584 | tf_op jit(solution)/shard_map/ppermute | solution.py:866
  355.9 24.1 %collective-permute-start.48 = (bf16[224,1152]{1,0:T(8,128)(2,1)}, bf16[224,1152]{1,0:T(8,128)(2,1)}, u32[]{:S(2)}, u32[]{:S(2)}) collective-permute-start(bf16[224,1152]{1,0:T(8,128)(2,1)} %get-tuple-element.272), channel_id=1, source_target_pairs={{0,16},{8,24},{16,0},{24,8},{1,17},{9,25},{17,1},{25,9},{2,18},{10... | collective-permute-start | bytes 1548296 | tf_op jit(solution)/shard_map/ppermute | solution.py:863
  355.9 24.2 %collective-permute-start.45 = (bf16[112,2304]{1,0:T(8,128)(2,1)}, bf16[112,2304]{1,0:T(8,128)(2,1)}, u32[]{:S(2)}, u32[]{:S(2)}) collective-permute-start(bf16[112,2304]{1,0:T(8,128)(2,1)} %get-tuple-element.268.refs_4_), channel_id=1, source_target_pairs={{0,2},{1,3},{2,0},{3,1},{4,6},{5,7},{6,4},{7,5},{8,10},{9,11},{10,... | collective-permute-start | bytes 1548296 | tf_op jit(solution)/shard_map/ppermute | solution.py:869
  356.9 23.9 %collective-permute-start.46 = (bf16[224,1152]{1,0:T(8,128)(2,1)}, bf16[224,1152]{1,0:T(8,128)(2,1)}, u32[]{:S(2)}, u32[]{:S(2)}) collective-permute-start(bf16[224,1152]{1,0:T(8,128)(2,1)} %get-tuple-element.269.refs_6_), channel_id=1, source_target_pairs={{0,2},{1,3},{2,0},{3,1},{4,6},{5,7},{6,4},{7,5},{8,10},{9,11},{10,... | collective-permute-start | bytes 1548296 | tf_op jit(solution)/shard_map/ppermute | solution.py:869
  359.3 20.1 %collective-permute-start.43 = (bf16[224,1024]{1,0:T(8,128)(2,1)}, bf16[224,1024]{1,0:T(8,128)(2,1)}, u32[]{:S(2)}, u32[]{:S(2)}) collective-permute-start(bf16[224,1024]{1,0:T(8,128)(2,1)} %get-tuple-element.259.refs_0_), channel_id=1, source_target_pairs={{0,8},{8,0},{16,24},{24,16},{1,9},{9,1},{17,25},{25,17},{2,10},{10... | collective-permute-start | bytes 1376264 | tf_op jit(solution)/shard_map/ppermute | solution.py:860
  385.1 15.5 %collective-permute-start.54 = (f32[1,2944]{1,0:T(1,128)}, f32[1,2944]{1,0:T(1,128)}, u32[]{:S(2)}, u32[]{:S(2)}) collective-permute-start(f32[1,2944]{1,0:T(1,128)} %get-tuple-element.282.refs_4_), channel_id=1, source_target_pairs={{0,8},{8,0},{16,24},{24,16},{1,9},{9,1},{17,25},{25,17},{2,10},{10... | collective-permute-start | bytes 35336 | tf_op jit(solution)/shard_map/ppermute | solution.py:860
  385.4 15.1 %collective-permute-start.53 = (bf16[112,1152]{1,0:T(8,128)(2,1)}, bf16[112,1152]{1,0:T(8,128)(2,1)}, u32[]{:S(2)}, u32[]{:S(2)}) collective-permute-start(bf16[112,1152]{1,0:T(8,128)(2,1)} %get-tuple-element.281), channel_id=1, source_target_pairs={{0,1},{1,0},{2,3},{3,2},{4,5},{5,4},{6,7},{7,6},{8,9},{9,8},{10,11... | collective-permute-start | bytes 774152 | tf_op jit(solution)/shard_map/ppermute | solution.py:866
  385.9 26.0 %collective-permute-start.57 = (bf16[224,1152]{1,0:T(8,128)(2,1)}, bf16[224,1152]{1,0:T(8,128)(2,1)}, u32[]{:S(2)}, u32[]{:S(2)}) collective-permute-start(bf16[224,1152]{1,0:T(8,128)(2,1)} %get-tuple-element.285.refs_4_), channel_id=1, source_target_pairs={{0,4},{1,5},{2,6},{3,7},{4,0},{5,1},{6,2},{7,3},{8,12},{9,13},{10,... | collective-permute-start | bytes 1548296 | tf_op jit(solution)/shard_map/ppermute | solution.py:869
  386.8 19.1 %collective-permute-start.55 = (bf16[224,1536]{1,0:T(8,128)(2,1)}, bf16[224,1536]{1,0:T(8,128)(2,1)}, u32[]{:S(2)}, u32[]{:S(2)}) collective-permute-start(bf16[224,1536]{1,0:T(8,128)(2,1)} %get-tuple-element.276.refs_0_), channel_id=1, source_target_pairs={{0,8},{8,0},{16,24},{24,16},{1,9},{9,1},{17,25},{25,17},{2,10},{10... | collective-permute-start | bytes 2064392 | tf_op jit(solution)/shard_map/ppermute | solution.py:860
  386.9 30.5 %collective-permute-start.56 = (bf16[224,2304]{1,0:T(8,128)(2,1)}, bf16[224,2304]{1,0:T(8,128)(2,1)}, u32[]{:S(2)}, u32[]{:S(2)}) collective-permute-start(bf16[224,2304]{1,0:T(8,128)(2,1)} %get-tuple-element.284.refs_2_.refs_4_), channel_id=1, source_target_pairs={{0,1},{1,0},{2,3},{3,2},{4,5},{5,4},{6,7},{7,6},{8,9},{9,8},{10,11... | collective-permute-start | bytes 3096584 | tf_op jit(solution)/shard_map/ppermute | solution.py:866
  402.4 14.9 %collective-permute-start.58 = (bf16[112,1152]{1,0:T(8,128)(2,1)}, bf16[112,1152]{1,0:T(8,128)(2,1)}, u32[]{:S(2)}, u32[]{:S(2)}) collective-permute-start(bf16[112,1152]{1,0:T(8,128)(2,1)} %get-tuple-element.283.refs_0_.refs_6_), channel_id=1, source_target_pairs={{0,2},{1,3},{2,0},{3,1},{4,6},{5,7},{6,4},{7,5},{8,10},{9,11},{10,... | collective-permute-start | bytes 774152 | tf_op jit(solution)/shard_map/ppermute | solution.py:869
  420.2 15.2 %collective-permute-start.60 = (bf16[224,1152]{1,0:T(8,128)(2,1)}, bf16[224,1152]{1,0:T(8,128)(2,1)}, u32[]{:S(2)}, u32[]{:S(2)}) collective-permute-start(bf16[224,1152]{1,0:T(8,128)(2,1)} %get-tuple-element.288.refs_2_.refs_5_), channel_id=1, source_target_pairs={{0,1},{1,0},{2,3},{3,2},{4,5},{5,4},{6,7},{7,6},{8,9},{9,8},{10,11... | collective-permute-start | bytes 1548296 | tf_op jit(solution)/shard_map/ppermute | solution.py:866
  421.6 13.8 %collective-permute-start.62 = (bf16[112,1152]{1,0:T(8,128)(2,1)}, bf16[112,1152]{1,0:T(8,128)(2,1)}, u32[]{:S(2)}, u32[]{:S(2)}) collective-permute-start(bf16[112,1152]{1,0:T(8,128)(2,1)} %get-tuple-element.290.refs_6_), channel_id=1, source_target_pairs={{0,4},{1,5},{2,6},{3,7},{4,0},{5,1},{6,2},{7,3},{8,12},{9,13},{10,... | collective-permute-start | bytes 774152 | tf_op jit(solution)/shard_map/ppermute | solution.py:869
  421.6 10.5 %collective-permute-start.61 = (bf16[112,896]{1,0:T(8,128)(2,1)}, bf16[112,896]{1,0:T(8,128)(2,1)}, u32[]{:S(2)}, u32[]{:S(2)}) collective-permute-start(bf16[112,896]{1,0:T(8,128)(2,1)} %get-tuple-element.289.refs_4_), channel_id=1, source_target_pairs={{0,2},{1,3},{2,0},{3,1},{4,6},{5,7},{6,4},{7,5},{8,10},{9,11},{10,... | collective-permute-start | bytes 602120 | tf_op jit(solution)/shard_map/ppermute | solution.py:869
  424.1 17.2 %collective-permute-start.64 = (bf16[224,1536]{1,0:T(8,128)(2,1)}, bf16[224,1536]{1,0:T(8,128)(2,1)}, u32[]{:S(2)}, u32[]{:S(2)}) collective-permute-start(bf16[224,1536]{1,0:T(8,128)(2,1)} %get-tuple-element.287.refs_0_), channel_id=1, source_target_pairs={{0,8},{8,0},{16,24},{24,16},{1,9},{9,1},{17,25},{25,17},{2,10},{10... | collective-permute-start | bytes 2064392 | tf_op jit(solution)/shard_map/ppermute | solution.py:860
  437.8 14.3 %collective-permute-start.68 = (f32[1,2944]{1,0:T(1,128)}, f32[1,2944]{1,0:T(1,128)}, u32[]{:S(2)}, u32[]{:S(2)}) collective-permute-start(f32[1,2944]{1,0:T(1,128)} %get-tuple-element.296.refs_6_), channel_id=1, source_target_pairs={{0,4},{1,5},{2,6},{3,7},{4,0},{5,1},{6,2},{7,3},{8,12},{9,13},{10,... | collective-permute-start | bytes 35336 | tf_op jit(solution)/shard_map/ppermute | solution.py:869
  437.9 14.2 %collective-permute-start.66 = (bf16[112,896]{1,0:T(8,128)(2,1)}, bf16[112,896]{1,0:T(8,128)(2,1)}, u32[]{:S(2)}, u32[]{:S(2)}) collective-permute-start(bf16[112,896]{1,0:T(8,128)(2,1)} %get-tuple-element.294.refs_2_), channel_id=1, source_target_pairs={{0,4},{1,5},{2,6},{3,7},{4,0},{5,1},{6,2},{7,3},{8,12},{9,13},{10,... | collective-permute-start | bytes 602120 | tf_op jit(solution)/shard_map/ppermute | solution.py:869
  440.8 11.3 %collective-permute-start.67 = (bf16[112,1152]{1,0:T(8,128)(2,1)}, bf16[112,1152]{1,0:T(8,128)(2,1)}, u32[]{:S(2)}, u32[]{:S(2)}) collective-permute-start(bf16[112,1152]{1,0:T(8,128)(2,1)} %get-tuple-element.295.refs_4_), channel_id=1, source_target_pairs={{0,1},{1,0},{2,3},{3,2},{4,5},{5,4},{6,7},{7,6},{8,9},{9,8},{10,11... | collective-permute-start | bytes 774152 | tf_op jit(solution)/shard_map/ppermute | solution.py:866
  (23 other events, 132.9 us)

commit v5 on v4

--- a/solution.py
+++ b/solution.py
@@ -541,7 +541,8 @@
         for lo in range(0, 2 * w, BLK):
             hi = min(lo + BLK, 2 * w)
             g, u, v = slice(lo, hi), slice(2 * w + lo, 2 * w + hi), slice(4 * w + lo, 4 * w + hi)
-            gate, up, dh = nn(a, wt[:, g]), nn(a, wt[:, u]), nn(b, wt[:, v])
+            both = nn(a, jnp.concatenate([wt[:, g], wt[:, u]], 1))
+            gate, up, dh = both[:, : hi - lo], both[:, hi - lo :], nn(b, wt[:, v])
             sig = jax.nn.sigmoid(gate)
             silu = gate * sig
             h = (silu * up).astype(bf16)

time: 472 us -> 472 us (level)
  no operation moved by 1% of the time
where the time goes in v5:
time: 472 us; the launch traced here: 463 us
  Pallas kernels  354 us (75%)
  starting transfers between devices  56 us (12%)
  waiting for transfers between devices  42.2 us (9%)
  local copies, waits for them, and re-layouts  6.96 us (1%)
    pallas_call x47, Pallas kernels, call(): pl.pallas_call(kernel, grid=(grid,), in_specs=[pl.BlockSpec(memory_space=...  354 us
    ppermute x16, waiting for transfers between devices, far(): lax.ppermute(v, 'replica', [(i, i ^ bit) for i in range(self.replicas)])  21.6 us
    ppermute x16, starting transfers between devices, far(): lax.ppermute(v, 'replica', [(i, i ^ bit) for i in range(self.replicas)])  19.8 us
    ppermute x16, starting transfers between devices, beside(): lax.ppermute(v, 'replica', [(i, i ^ 1) for i in range(self.replicas)])  16.7 us
    ppermute x11, starting transfers between devices, across(): return lax.ppermute(v, 'shard', [(i, i ^ 2) for i in range(self.shards)])  14 us
    ppermute x11, waiting for transfers between devices, across(): return lax.ppermute(v, 'shard', [(i, i ^ 2) for i in range(self.shards)])  10.7 us
  transfers between devices with their start and end apart: 71, of which 15 were waited for; matrix products, arithmetic and copies ran while one was open for 2% of the time, Pallas kernels for 73%

profile of v5, /device:TPU:0, one launch (start us, length us, event | category | flops | bytes accessed | tf_op | source)
XLA Modules:
  0.0 463.4 jit_solution(9212157714022152437)
XLA Ops:
  2.5 2.9 collective-permute-start
  10.1 4.4 split_weights.2
  15.0 2.5 collective-permute-done.refs_1_
  17.5 2.8 pack_weights.2.refs_0_
  25.2 9.0 %project.1 = (bf16[1024,896]{1,0:T(8,128)(2,1)}, bf16[1024,896]{1,0:T(8,128)(2,1)}, bf16[4,1024,128]{2,1,0:T(8,128)(2,1)}, bf16[4,1024,128]{2,1,0:T(8,128)(2,1)}...) custom-call(bf16[224,3328]{1,0:T(8,128)(2,1)} %pack_weights.2.refs_0_, ...), custom_call_target="tpu_custom_call" | custom-call | flops 50000000 | bytes 100000 | tf_op jit(solution)/shard_map/project/pallas_call | solution.py:67
  34.2 6.1 %split_weights.3 = (bf16[224,1536]{1,0:T(8,128)(2,1)}, bf16[224,1536]{1,0:T(8,128)(2,1)}, bf16[224,768]{1,0:T(8,128)(2,1)}, bf16[224,1536]{1,0:T(8,128)(2,1)}, b...) custom-call(bf16[1024,896]{1,0:T(8,128)(2,1)} %get-tuple-element.165, ...), custom_call_target="tpu_custom_call" | custom-call | flops 50000000 | bytes 100000 | tf_op jit(solution)/shard_map/split_weights/pallas_call | solution.py:67
  42.5 13.8 %attend.2 = (bf16[1024,384]{1,0:T(8,128)(2,1)}, bf16[1024,384]{1,0:T(8,128)(2,1)}, f32[1024,384]{1,0:T(8,128)}, bf16[6,1024,256]{2,1,0:T(8,128)(2,1)}, bf16[6,76...) custom-call(bf16[224,1536]{1,0:T(8,128)(2,1)} %get-tuple-element.166.refs_0_, ...), custom_call_target="tpu_custom_call" | custom-call | flops 50000000 | bytes 100000 | tf_op jit(solution)/shard_map/attend/pallas_call | solution.py:67
  58.3 4.3 pack_weights.3
  67.4 17.1 %attend.3 = (bf16[1024,512]{1,0:T(8,128)(2,1)}, bf16[1024,512]{1,0:T(8,128)(2,1)}, f32[1024,512]{1,0:T(8,128)}, bf16[8,1024,256]{2,1,0:T(8,128)(2,1)}, bf16[8,76...) custom-call(bf16[224,2304]{1,0:T(8,128)(2,1)} %get-tuple-element.179.refs_0_, ...), custom_call_target="tpu_custom_call" | custom-call | flops 50000000 | bytes 100000 | tf_op jit(solution)/shard_map/attend/pallas_call | solution.py:67
  84.5 8.3 %join_output.1 = (f32[1024,896]{1,0:T(8,128)}, bf16[896,896]{1,0:T(8,128)(2,1)}, bf16[512,896]{1,0:T(8,128)(2,1)}, bf16[512,896]{1,0:T(8,128)(2,1)}) custom-call(bf16[1024,512]{1,0:T(8,128)(2,1)} %get-tuple-element.180.refs_0_.refs_9_.refs_3_, bf16[224,1536]{1,0:T(8,128)(2,1)} %collective-permute-done.10.refs_1_.refs_7_, ...), custom_call_target="tpu_custom_call" | custom-call | flops 50000000 | bytes 100000 | tf_op jit(solution)/shard_map/join_output/pallas_call | solution.py:67
  97.0 20.8 %ffn_part.4 = (bf16[2048,512]{1,0:T(8,128)(2,1)}, bf16[2048,1024]{1,0:T(8,128)(2,1)}, bf16[448,1536]{1,0:T(8,128)(2,1)}, bf16[448,1536]{1,0:T(8,128)(2,1)}, bf16[896,1536]{1,0:T(8,128)(2,1)}) custom-call(bf16[224,2304]{1,0:T(8,128)(2,1)} %gate.8.refs_0_.refs_6_, s32[4]{0:T(128)} %pad_add_fusion.refs_3_.refs_1_.refs_2_, bf16[1024,896]{1,0:T(8,128)(2,1)} %refs_3_.7, ...), custom_call_target="tpu_custom_call" | custom-call | flops 50000000 | bytes 100000 | tf_op jit(solution)/shard_map/ffn_part/pallas_call | solution.py:67
  117.8 3.5 collective-permute-done.14.refs_1_
  123.4 28.4 %ffn_part.5 = (bf16[2048,768]{1,0:T(8,128)(2,1)}, bf16[2048,1536]{1,0:T(8,128)(2,1)}, bf16[448,2304]{1,0:T(8,128)(2,1)}, bf16[448,2304]{1,0:T(8,128)(2,1)}, bf16[896,2304]{1,0:T(8,128)(2,1)}) custom-call(bf16[224,3456]{1,0:T(8,128)(2,1)} %gate.9.refs_0_.refs_6_, s32[4]{0:T(128)} %pad_add_fusion.refs_3_.refs_1_.refs_2_, bf16[1024,896]{1,0:T(8,128)(2,1)} %refs_3_.7, ...), custom_call_target="tpu_custom_call" | custom-call | flops 14499999744 | bytes 100000 | tf_op jit(solution)/shard_map/ffn_part/pallas_call | solution.py:67
  155.4 3.1 sums.15
  159.3 28.3 %ffn_part.6 = (bf16[2048,768]{1,0:T(8,128)(2,1)}, bf16[2048,1536]{1,0:T(8,128)(2,1)}, bf16[448,2304]{1,0:T(8,128)(2,1)}, bf16[448,2304]{1,0:T(8,128)(2,1)}, bf16[896,2304]{1,0:T(8,128)(2,1)}) custom-call(bf16[224,1536]{1,0:T(8,128)(2,1)} %get-tuple-element.189.refs_0_.refs_2_, s32[4]{0:T(128)} %pad_add_fusion.refs_3_.refs_1_.refs_2_, ...), custom_call_target="tpu_custom_call" | custom-call | flops 14499999744 | bytes 100000 | tf_op jit(solution)/shard_map/ffn_part/pallas_call | solution.py:67
  187.7 2.4 sums.16.refs_0_.refs_2_
  191.4 19.6 %ffn_part.7 = (bf16[2048,384]{1,0:T(8,128)(2,1)}, bf16[2048,768]{1,0:T(8,128)(2,1)}, bf16[448,1152]{1,0:T(8,128)(2,1)}, bf16[448,1152]{1,0:T(8,128)(2,1)}, bf16[896,1152]{1,0:T(8,128)(2,1)}) custom-call(bf16[224,1536]{1,0:T(8,128)(2,1)} %sums.16.refs_0_.refs_2_, s32[4]{0:T(128)} %pad_add_fusion.refs_3_.refs_1_.refs_2_, bf16[1024,896]{1,0:T(8,128)(2,1)} %refs_3_.7, ...), custom_call_target="tpu_custom_call" | custom-call | flops 8499999744 | bytes 100000 | tf_op jit(solution)/shard_map/ffn_part/pallas_call | solution.py:67
  211.0 4.4 sums.17
  215.5 2.6 collective-permute-start.21
  219.6 29.2 %back_tokens.1 = (bf16[256,896]{1,0:T(8,128)(2,1)}, bf16[256,896]{1,0:T(8,128)(2,1)}, bf16[256,896]{1,0:T(8,128)(2,1)}, bf16[256,896]{1,0:T(8,128)(2,1)}, f32[1024,896]{1,0:T(8,128)}) custom-call(bf16[224,1536]{1,0:T(8,128)(2,1)} %get-tuple-element.195.refs_0_.refs_2_, bf16[2048,1024]{1,0:T(8,128)(2,1)} %get-tuple-element.196.refs_1_, ...), custom_call_target="tpu_custom_call" | custom-call | flops 12000000000 | bytes 100000 | tf_op jit(solution)/shard_map/back_tokens/pallas_call | solution.py:67
  249.8 5.4 %sums.18 = (bf16[224,1536]{1,0:T(8,128)(2,1)}, bf16[112,2304]{1,0:T(8,128)(2,1)}, bf16[112,2304]{1,0:T(8,128)(2,1)}, bf16[224,2304]{1,0:T(8,128)(2,1)}, bf16[224,2304]{1,0:T(8,128)(2,1)}) custom-call(bf16[256,896]{1,0:T(8,128)(2,1)} %get-tuple-element.204.refs_0_, s32[4]{0:T(128)} %pad_add_fusion.refs_3_.refs_1_.refs_2_, ...), custom_call_target="tpu_custom_call" | custom-call | flops 1000000000 | bytes 100000 | tf_op jit(solution)/shard_map/sums/pallas_call | solution.py:67
  258.2 10.1 %turn_back.1 = (f32[1024,896]{1,0:T(8,128)}, bf16[1024,896]{1,0:T(8,128)(2,1)}, f32[1,896]{1,0:T(1,128)}, bf16[1024,384]{1,0:T(8,128)(2,1)}, bf16[1024,512]{1,0:T(8,128)(2,1)}) custom-call(bf16[224,1536]{1,0:T(8,128)(2,1)} %get-tuple-element.209.refs_0_.refs_2_, f32[1024,896]{1,0:T(8,128)} %get-tuple-element.210.refs_1_, ...), custom_call_target="tpu_custom_call" | custom-call | flops 4000000000 | bytes 100000 | tf_op jit(solution)/shard_map/turn_back/pallas_call | solution.py:67
  271.4 5.3 %weight_grads.2 = (bf16[448,896]{1,0:T(8,128)(2,1)}, bf16[448,384]{1,0:T(8,128)(2,1)}, bf16[448,512]{1,0:T(8,128)(2,1)}) custom-call(bf16[112,2304]{1,0:T(8,128)(2,1)} %sums.19.refs_0_.refs_2_, s32[4]{0:T(128)} %pad_add_fusion.refs_3_.refs_1_.refs_2_, bf16[1024,384]{1,0:T(8,128)(2,1)} %get-tuple-element.170.refs_0_.refs_8_.refs_2_.refs_3_, ...), custom_call_target="tpu_custom_call" | custom-call | flops 50000000 | bytes 100000 | tf_op jit(solution)/shard_map/weight_grads/pallas_call | solution.py:67
  277.6 17.8 %attend_back.3 = (bf16[1024,384]{1,0:T(8,128)(2,1)}, f32[1024,128]{1,0:T(8,128)}, f32[1024,128]{1,0:T(8,128)}) custom-call(bf16[448,896]{1,0:T(8,128)(2,1)} %get-tuple-element.221.refs_0_.refs_6_, bf16[1024,896]{1,0:T(8,128)(2,1)} %get-tuple-element.167.refs_3_.refs_1_, bf16[1024,384]{1,0:T(8,128)(2,1)} %get-tuple-element.222.refs_2_, ...), custom_call_target="tpu_custom_call" | custom-call | flops 50000000 | bytes 100000 | tf_op jit(solution)/shard_map/attend_back/pallas_call | solution.py:67
  295.5 4.7 %sums.20 = (bf16[112,2304]{1,0:T(8,128)(2,1)}, bf16[112,2304]{1,0:T(8,128)(2,1)}, bf16[224,1152]{1,0:T(8,128)(2,1)}, bf16[224,1152]{1,0:T(8,128)(2,1)}, bf16[224...) custom-call(bf16[1024,384]{1,0:T(8,128)(2,1)} %get-tuple-element.229.refs_0_.refs_3_.refs_5_, ...), custom_call_target="tpu_custom_call" | custom-call | flops 50000000 | bytes 100000 | tf_op jit(solution)/shard_map/sums/pallas_call | solution.py:67
  304.6 13.8 %attend_back.4 = (bf16[1024,256]{1,0:T(8,128)(2,1)}, f32[1024,128]{1,0:T(8,128)}, f32[1024,128]{1,0:T(8,128)}) custom-call(bf16[112,2304]{1,0:T(8,128)(2,1)} %get-tuple-element.236.refs_0_.refs_4_, bf16[1024,896]{1,0:T(8,128)(2,1)} %get-tuple-element.167.refs_3_.refs_1_, bf16[1024,512]{1,0:T(8,128)(2,1)} %get-tuple-element.237.refs_2_, ...), custom_call_target="tpu_custom_call" | custom-call | flops 50000000 | bytes 100000 | tf_op jit(solution)/shard_map/attend_back/pallas_call | solution.py:67
  318.4 2.6 sums.21
  321.0 2.6 collective-permute-start.37
  325.2 14.2 %attend_back.5 = (bf16[1024,256]{1,0:T(8,128)(2,1)}, bf16[1024,128]{1,0:T(8,128)(2,1)}, bf16[1024,128]{1,0:T(8,128)(2,1)}) custom-call(bf16[112,2304]{1,0:T(8,128)(2,1)} %get-tuple-element.247.refs_0_.refs_4_, bf16[1024,896]{1,0:T(8,128)(2,1)} %get-tuple-element.167.refs_3_.refs_1_, bf16[1024,512]{1,0:T(8,128)(2,1)} %get-tuple-element.237.refs_2_, ...), custom_call_target="tpu_custom_call" | custom-call | flops 50000000 | bytes 100000 | tf_op jit(solution)/shard_map/attend_back/pallas_call | solution.py:67
  339.4 6.5 %weight_grads.3 = (bf16[448,1152]{1,0:T(8,128)(2,1)}, bf16[448,384]{1,0:T(8,128)(2,1)}, bf16[448,384]{1,0:T(8,128)(2,1)}, bf16[448,384]{1,0:T(8,128)(2,1)}) custom-call(bf16[1024,256]{1,0:T(8,128)(2,1)} %get-tuple-element.250.refs_0_.refs_5_.refs_7_, s32[4]{0:T(128)} %pad_add_fusion.refs_3_.refs_1_.refs_2_, ...), custom_call_target="tpu_custom_call" | custom-call | flops 50000000 | bytes 100000 | tf_op jit(solution)/shard_map/weight_grads/pallas_call | solution.py:67
  346.6 4.0 sums.22
  352.6 2.6 sums.23
  358.7 9.4 %finish_tokens.1 = (f32[1024,896]{1,0:T(8,128)}, f32[1,896]{1,0:T(1,128)}, f32[1,1152]{1,0:T(1,128)}) custom-call(bf16[224,1152]{1,0:T(8,128)(2,1)} %get-tuple-element.263.refs_0_.refs_10_, bf16[1024,896]{1,0:T(8,128)(2,1)} %refs_1_.3, f32[1,896]{1,0:T(1,128)} %broadcast_in_dim.11.refs_4_.refs_2_, bf16[896,1152]{1,0:T(8,128)(2,1)} %get-tuple-element.264.refs_3_, ...), custom_call_target="tpu_custom_call" | custom-call | flops 50000000 | bytes 100000 | tf_op jit(solution)/shard_map/finish_tokens/pallas_call | solution.py:67
  368.1 10.7 %down_tokens.2 = (bf16[256,896]{1,0:T(8,128)(2,1)}, bf16[256,896]{1,0:T(8,128)(2,1)}, bf16[256,896]{1,0:T(8,128)(2,1)}, bf16[256,896]{1,0:T(8,128)(2,1)}) custom-call(f32[1024,896]{1,0:T(8,128)} %get-tuple-element.149.refs_0_, bf16[2048,512]{1,0:T(8,128)(2,1)} %get-tuple-element.184.refs_0_.refs_1_, bf16[2048,768]{1,0:T(8,128)(2,1)} %get-tuple-element.186.refs_0_.refs_2_, ...), custom_call_target="tpu_custom_call" | custom-call | flops 50000000 | bytes 100000 | tf_op jit(solution)/shard_map/down_tokens/pallas_call | solution.py:67
  380.4 4.1 sums.24
  387.8 12.1 %down_tokens.3.refs_0_ = bf16[1024,896]{1,0:T(8,128)(2,1)} custom-call(bf16[224,1536]{1,0:T(8,128)(2,1)} %get-tuple-element.276.refs_0_, bf16[2048,512]{1,0:T(8,128)(2,1)} %get-tuple-element.184.refs_0_.refs_1_, bf16[2048,768]{1,0:T(8,128)(2,1)} %get-tuple-element.186.refs_0_.refs_2_, bf16[2048,768]{1,0:T(8,128)(2,1)} %get-tuple-element.190.refs_0_.refs_3_, ...), custom_call_target="tpu_custom_call" | custom-call | flops 10000000000 | bytes 100000 | tf_op jit(solution)/shard_map/down_tokens/pallas_call | solution.py:67
  405.3 2.5 collective-permute-done.59.refs_9_
  407.7 3.5 collective-permute-done.57.refs_5_
  411.2 5.4 %collective-permute-done.58.refs_7_ = bf16[112,1152]{1,0:T(8,128)(2,1)} collective-permute-done((bf16[112,1152]{1,0:T(8,128)(2,1)}, bf16[112,1152]{1,0:T(8,128)(2,1)}, u32[]{:S(2)}, u32[]{:S(2)}) %collective-permute-start.58) | collective-permute-done | bytes 258080 | tf_op jit(solution)/shard_map/ppermute | solution.py:870
  416.7 2.9 sums.26
  421.0 2.4 collective-permute-start.61
  423.4 8.1 %collective-permute-done.61.refs_5_ = bf16[112,896]{1,0:T(8,128)(2,1)} collective-permute-done((bf16[112,896]{1,0:T(8,128)(2,1)}, bf16[112,896]{1,0:T(8,128)(2,1)}, u32[]{:S(2)}, u32[]{:S(2)}) %collective-permute-start.61) | collective-permute-done | bytes 200736 | tf_op jit(solution)/shard_map/ppermute | solution.py:870
  431.5 3.3 collective-permute-done.62.refs_7_
  434.8 2.4 sums.27
  437.2 2.9 collective-permute-start.66
  440.7 10.8 %assemble.1 = (f32[224,4864]{1,0:T(8,128)}, f32[224,4864]{1,0:T(8,128)}, f32[1216,896]{1,0:T(8,128)}) custom-call(bf16[224,768]{1,0:T(8,128)(2,1)} %gate.13.refs_0_.refs_13_, s32[4]{0:T(128)} %pad_add_fusion.refs_3_.refs_1_.refs_2_, bf16[224,1536]{1,0:T(8,128)(2,1)} %get-tuple-element.209.refs_0_.refs_2_, ...), custom_call_target="tpu_custom_call" | custom-call | flops 5500000256 | bytes 100000 | tf_op jit(solution)/shard_map/assemble/pallas_call | solution.py:67
  451.5 2.4 sums.28
  455.9 5.1 %collective-permute-done.70.refs_5_ = f32[1,2944]{1,0:T(1,128)} collective-permute-done((f32[1,2944]{1,0:T(1,128)}, f32[1,2944]{1,0:T(1,128)}, u32[]{:S(2)}, u32[]{:S(2)}) %collective-permute-start.70) | collective-permute-done | bytes 11808 | tf_op jit(solution)/shard_map/ppermute | solution.py:867
  (156 shorter events, 70.9 us)
Async XLA Ops:
  2.5 15.0 %collective-permute-start = (bf16[224,1152]{1,0:T(8,128)(2,1)}, bf16[224,1152]{1,0:T(8,128)(2,1)}, u32[]{:S(2)}, u32[]{:S(2)}) collective-permute-start(bf16[224,1152]{1,0:T(8,128)(2,1)} %side_by_side.1.refs_0_.refs_5_), channel_id=1, source_target_pairs={{0,16},{8,24},{16,0},{24,8},{1,17},{9,25},{17,1},{25,9},{2,18},{10... | collective-permute-start | bytes 1548296 | tf_op jit(solution)/shard_map/ppermute | solution.py:864
  5.5 19.7 %collective-permute-start.3 = (bf16[1024,896]{1,0:T(8,128)(2,1)}, bf16[1024,896]{1,0:T(8,128)(2,1)}, u32[]{:S(2)}, u32[]{:S(2)}) collective-permute-start(bf16[1024,896]{1,0:T(8,128)(2,1)} %refs_3_.7), channel_id=1, source_target_pairs={{0,8},{8,0},{16,24},{24,16},{1,9},{9,1},{17,25},{25,17},{2,10},{10... | collective-permute-start | bytes 5505032 | tf_op jit(solution)/shard_map/ppermute | solution.py:861
  20.3 35.9 %collective-permute-start.6 = (bf16[224,3328]{1,0:T(8,128)(2,1)}, bf16[224,3328]{1,0:T(8,128)(2,1)}, u32[]{:S(2)}, u32[]{:S(2)}) collective-permute-start(bf16[224,3328]{1,0:T(8,128)(2,1)} %pack_weights.2.refs_0_), channel_id=1, source_target_pairs={{0,16},{8,24},{16,0},{24,8},{1,17},{9,25},{17,1},{25,9},{2,18},{10... | collective-permute-start | bytes 4472840 | tf_op jit(solution)/shard_map/ppermute | solution.py:864
  40.2 18.0 %collective-permute-start.8 = (bf16[224,1536]{1,0:T(8,128)(2,1)}, bf16[224,1536]{1,0:T(8,128)(2,1)}, u32[]{:S(2)}, u32[]{:S(2)}) collective-permute-start(bf16[224,1536]{1,0:T(8,128)(2,1)} %get-tuple-element.171), channel_id=1, source_target_pairs={{0,8},{8,0},{16,24},{24,16},{1,9},{9,1},{17,25},{25,17},{2,10},{10... | collective-permute-start | bytes 2064392 | tf_op jit(solution)/shard_map/ppermute | solution.py:861
  40.2 18.0 %collective-permute-start.7 = (bf16[224,1536]{1,0:T(8,128)(2,1)}, bf16[224,1536]{1,0:T(8,128)(2,1)}, u32[]{:S(2)}, u32[]{:S(2)}) collective-permute-start(bf16[224,1536]{1,0:T(8,128)(2,1)} %get-tuple-element.166.refs_0_), channel_id=1, source_target_pairs={{0,8},{8,0},{16,24},{24,16},{1,9},{9,1},{17,25},{25,17},{2,10},{10... | collective-permute-start | bytes 2064392 | tf_op jit(solution)/shard_map/ppermute | solution.py:861
  40.7 17.5 %collective-permute-start.9 = (bf16[224,768]{1,0:T(8,128)(2,1)}, bf16[224,768]{1,0:T(8,128)(2,1)}, u32[]{:S(2)}, u32[]{:S(2)}) collective-permute-start(bf16[224,768]{1,0:T(8,128)(2,1)} %get-tuple-element.172), channel_id=1, source_target_pairs={{0,8},{8,0},{16,24},{24,16},{1,9},{9,1},{17,25},{25,17},{2,10},{10... | collective-permute-start | bytes 1032200 | tf_op jit(solution)/shard_map/ppermute | solution.py:861
  62.6 30.7 %collective-permute-start.11 = (bf16[224,2304]{1,0:T(8,128)(2,1)}, bf16[224,2304]{1,0:T(8,128)(2,1)}, u32[]{:S(2)}, u32[]{:S(2)}) collective-permute-start(bf16[224,2304]{1,0:T(8,128)(2,1)} %get-tuple-element.179.refs_0_), channel_id=1, source_target_pairs={{0,16},{8,24},{16,0},{24,8},{1,17},{9,25},{17,1},{25,9},{2,18},{10... | collective-permute-start | bytes 3096584 | tf_op jit(solution)/shard_map/ppermute | solution.py:864
  62.9 21.6 %collective-permute-start.10 = (bf16[224,1536]{1,0:T(8,128)(2,1)}, bf16[224,1536]{1,0:T(8,128)(2,1)}, u32[]{:S(2)}, u32[]{:S(2)}) collective-permute-start(bf16[224,1536]{1,0:T(8,128)(2,1)} %first_lanes.1.refs_0_), channel_id=1, source_target_pairs={{0,1},{1,0},{2,3},{3,2},{4,5},{5,4},{6,7},{7,6},{8,9},{9,8},{10,11... | collective-permute-start | bytes 2064392 | tf_op jit(solution)/shard_map/ppermute | solution.py:867
  64.7 56.7 %collective-permute-start.14 = (bf16[224,3456]{1,0:T(8,128)(2,1)}, bf16[224,3456]{1,0:T(8,128)(2,1)}, u32[]{:S(2)}, u32[]{:S(2)}) collective-permute-start(bf16[224,3456]{1,0:T(8,128)(2,1)} %get-tuple-element.185), channel_id=1, source_target_pairs={{0,16},{8,24},{16,0},{24,8},{1,17},{9,25},{17,1},{25,9},{2,18},{10... | collective-permute-start | bytes 4644872 | tf_op jit(solution)/shard_map/ppermute | solution.py:864
  93.3 30.0 %collective-permute-start.15 = (bf16[224,2304]{1,0:T(8,128)(2,1)}, bf16[224,2304]{1,0:T(8,128)(2,1)}, u32[]{:S(2)}, u32[]{:S(2)}) collective-permute-start(bf16[224,2304]{1,0:T(8,128)(2,1)} %gate.8.refs_0_.refs_6_), channel_id=1, source_target_pairs={{0,1},{1,0},{2,3},{3,2},{4,5},{5,4},{6,7},{7,6},{8,9},{9,8},{10,11... | collective-permute-start | bytes 3096584 | tf_op jit(solution)/shard_map/ppermute | solution.py:867
  121.3 37.9 %collective-permute-start.17 = (bf16[224,3456]{1,0:T(8,128)(2,1)}, bf16[224,3456]{1,0:T(8,128)(2,1)}, u32[]{:S(2)}, u32[]{:S(2)}) collective-permute-start(bf16[224,3456]{1,0:T(8,128)(2,1)} %gate.9.refs_0_.refs_6_), channel_id=1, source_target_pairs={{0,1},{1,0},{2,3},{3,2},{4,5},{5,4},{6,7},{7,6},{8,9},{9,8},{10,11... | collective-permute-start | bytes 4644872 | tf_op jit(solution)/shard_map/ppermute | solution.py:867
  122.8 32.6 %collective-permute-start.16 = (bf16[448,1536]{1,0:T(8,128)(2,1)}, bf16[448,1536]{1,0:T(8,128)(2,1)}, u32[]{:S(2)}, u32[]{:S(2)}) collective-permute-start(bf16[448,1536]{1,0:T(8,128)(2,1)} %get-tuple-element.188), channel_id=1, source_target_pairs={{0,16},{8,24},{16,0},{24,8},{1,17},{9,25},{17,1},{25,9},{2,18},{10... | collective-permute-start | bytes 4128776 | tf_op jit(solution)/shard_map/ppermute | solution.py:864
  151.7 59.3 %collective-permute-start.20 = (bf16[448,2304]{1,0:T(8,128)(2,1)}, bf16[448,2304]{1,0:T(8,128)(2,1)}, u32[]{:S(2)}, u32[]{:S(2)}) collective-permute-start(bf16[448,2304]{1,0:T(8,128)(2,1)} %get-tuple-element.194), channel_id=1, source_target_pairs={{0,16},{8,24},{16,0},{24,8},{1,17},{9,25},{17,1},{25,9},{2,18},{10... | collective-permute-start | bytes 6193160 | tf_op jit(solution)/shard_map/ppermute | solution.py:864
  158.5 29.2 %collective-permute-start.18 = (bf16[224,1536]{1,0:T(8,128)(2,1)}, bf16[224,1536]{1,0:T(8,128)(2,1)}, u32[]{:S(2)}, u32[]{:S(2)}) collective-permute-start(bf16[224,1536]{1,0:T(8,128)(2,1)} %get-tuple-element.191), channel_id=1, source_target_pairs={{0,1},{1,0},{2,3},{3,2},{4,5},{5,4},{6,7},{7,6},{8,9},{9,8},{10,11... | collective-permute-start | bytes 2064392 | tf_op jit(solution)/shard_map/ppermute | solution.py:867
  187.6 62.2 %collective-permute-start.23 = (bf16[448,2304]{1,0:T(8,128)(2,1)}, bf16[448,2304]{1,0:T(8,128)(2,1)}, u32[]{:S(2)}, u32[]{:S(2)}) collective-permute-start(bf16[448,2304]{1,0:T(8,128)(2,1)} %get-tuple-element.208), channel_id=1, source_target_pairs={{0,16},{8,24},{16,0},{24,8},{1,17},{9,25},{17,1},{25,9},{2,18},{10... | collective-permute-start | bytes 6193160 | tf_op jit(solution)/shard_map/ppermute | solution.py:864
  190.0 21.0 %collective-permute-start.19 = (bf16[224,1536]{1,0:T(8,128)(2,1)}, bf16[224,1536]{1,0:T(8,128)(2,1)}, u32[]{:S(2)}, u32[]{:S(2)}) collective-permute-start(bf16[224,1536]{1,0:T(8,128)(2,1)} %sums.16.refs_0_.refs_2_), channel_id=1, source_target_pairs={{0,2},{1,3},{2,0},{3,1},{4,6},{5,7},{6,4},{7,5},{8,10},{9,11},{10,... | collective-permute-start | bytes 2064392 | tf_op jit(solution)/shard_map/ppermute | solution.py:870
  215.5 33.9 %collective-permute-start.21 = (bf16[224,1536]{1,0:T(8,128)(2,1)}, bf16[224,1536]{1,0:T(8,128)(2,1)}, u32[]{:S(2)}, u32[]{:S(2)}) collective-permute-start(bf16[224,1536]{1,0:T(8,128)(2,1)} %get-tuple-element.195.refs_0_.refs_2_), channel_id=1, source_target_pairs={{0,4},{1,5},{2,6},{3,7},{4,0},{5,1},{6,2},{7,3},{8,12},{9,13},{10,... | collective-permute-start | bytes 2064392 | tf_op jit(solution)/shard_map/ppermute | solution.py:870
  218.0 31.4 %collective-permute-start.22 = (bf16[224,2304]{1,0:T(8,128)(2,1)}, bf16[224,2304]{1,0:T(8,128)(2,1)}, u32[]{:S(2)}, u32[]{:S(2)}) collective-permute-start(bf16[224,2304]{1,0:T(8,128)(2,1)} %get-tuple-element.206), channel_id=1, source_target_pairs={{0,1},{1,0},{2,3},{3,2},{4,5},{5,4},{6,7},{7,6},{8,9},{9,8},{10,11... | collective-permute-start | bytes 3096584 | tf_op jit(solution)/shard_map/ppermute | solution.py:867
  255.3 14.0 %collective-permute-start.28 = (bf16[112,2304]{1,0:T(8,128)(2,1)}, bf16[112,2304]{1,0:T(8,128)(2,1)}, u32[]{:S(2)}, u32[]{:S(2)}) collective-permute-start(bf16[112,2304]{1,0:T(8,128)(2,1)} %get-tuple-element.219), channel_id=1, source_target_pairs={{0,2},{1,3},{2,0},{3,1},{4,6},{5,7},{6,4},{7,5},{8,10},{9,11},{10,... | collective-permute-start | bytes 1548296 | tf_op jit(solution)/shard_map/ppermute | solution.py:870
  255.7 39.7 %collective-permute-start.30 = (bf16[448,1152]{1,0:T(8,128)(2,1)}, bf16[448,1152]{1,0:T(8,128)(2,1)}, u32[]{:S(2)}, u32[]{:S(2)}) collective-permute-start(bf16[448,1152]{1,0:T(8,128)(2,1)} %get-tuple-element.233), channel_id=1, source_target_pairs={{0,16},{8,24},{16,0},{24,8},{1,17},{9,25},{17,1},{25,9},{2,18},{10... | collective-permute-start | bytes 3096584 | tf_op jit(solution)/shard_map/ppermute | solution.py:864
  257.7 37.7 %collective-permute-start.29 = (bf16[224,2304]{1,0:T(8,128)(2,1)}, bf16[224,2304]{1,0:T(8,128)(2,1)}, u32[]{:S(2)}, u32[]{:S(2)}) collective-permute-start(bf16[224,2304]{1,0:T(8,128)(2,1)} %get-tuple-element.231), channel_id=1, source_target_pairs={{0,1},{1,0},{2,3},{3,2},{4,5},{5,4},{6,7},{7,6},{8,9},{9,8},{10,11... | collective-permute-start | bytes 3096584 | tf_op jit(solution)/shard_map/ppermute | solution.py:867
  276.8 18.7 %collective-permute-start.32 = (bf16[448,512]{1,0:T(8,128)(2,1)}, bf16[448,512]{1,0:T(8,128)(2,1)}, u32[]{:S(2)}, u32[]{:S(2)}) collective-permute-start(bf16[448,512]{1,0:T(8,128)(2,1)} %get-tuple-element.235), channel_id=1, source_target_pairs={{0,8},{8,0},{16,24},{24,16},{1,9},{9,1},{17,25},{25,17},{2,10},{10... | collective-permute-start | bytes 1376264 | tf_op jit(solution)/shard_map/ppermute | solution.py:861
  276.8 18.6 %collective-permute-start.31 = (bf16[448,384]{1,0:T(8,128)(2,1)}, bf16[448,384]{1,0:T(8,128)(2,1)}, u32[]{:S(2)}, u32[]{:S(2)}) collective-permute-start(bf16[448,384]{1,0:T(8,128)(2,1)} %get-tuple-element.234), channel_id=1, source_target_pairs={{0,8},{8,0},{16,24},{24,16},{1,9},{9,1},{17,25},{25,17},{2,10},{10... | collective-permute-start | bytes 1032200 | tf_op jit(solution)/shard_map/ppermute | solution.py:861
  277.3 41.1 %collective-permute-start.33 = (bf16[112,2304]{1,0:T(8,128)(2,1)}, bf16[112,2304]{1,0:T(8,128)(2,1)}, u32[]{:S(2)}, u32[]{:S(2)}) collective-permute-start(bf16[112,2304]{1,0:T(8,128)(2,1)} %sums.19.refs_0_.refs_2_), channel_id=1, source_target_pairs={{0,4},{1,5},{2,6},{3,7},{4,0},{5,1},{6,2},{7,3},{8,12},{9,13},{10,... | collective-permute-start | bytes 1548296 | tf_op jit(solution)/shard_map/ppermute | solution.py:870
  300.1 18.3 %collective-permute-start.34 = (bf16[112,2304]{1,0:T(8,128)(2,1)}, bf16[112,2304]{1,0:T(8,128)(2,1)}, u32[]{:S(2)}, u32[]{:S(2)}) collective-permute-start(bf16[112,2304]{1,0:T(8,128)(2,1)} %get-tuple-element.246), channel_id=1, source_target_pairs={{0,2},{1,3},{2,0},{3,1},{4,6},{5,7},{6,4},{7,5},{8,10},{9,11},{10,... | collective-permute-start | bytes 1548296 | tf_op jit(solution)/shard_map/ppermute | solution.py:870
  300.7 45.2 %collective-permute-start.35 = (bf16[224,1536]{1,0:T(8,128)(2,1)}, bf16[224,1536]{1,0:T(8,128)(2,1)}, u32[]{:S(2)}, u32[]{:S(2)}) collective-permute-start(bf16[224,1536]{1,0:T(8,128)(2,1)} %get-tuple-element.209.refs_0_.refs_2_), channel_id=1, source_target_pairs={{0,1},{1,0},{2,3},{3,2},{4,5},{5,4},{6,7},{7,6},{8,9},{9,8},{10,11... | collective-permute-start | bytes 2064392 | tf_op jit(solution)/shard_map/ppermute | solution.py:867
  302.3 44.2 %collective-permute-start.38 = (bf16[224,1152]{1,0:T(8,128)(2,1)}, bf16[224,1152]{1,0:T(8,128)(2,1)}, u32[]{:S(2)}, u32[]{:S(2)}) collective-permute-start(bf16[224,1152]{1,0:T(8,128)(2,1)} %get-tuple-element.256), channel_id=1, source_target_pairs={{0,1},{1,0},{2,3},{3,2},{4,5},{5,4},{6,7},{7,6},{8,9},{9,8},{10,11... | collective-permute-start | bytes 1548296 | tf_op jit(solution)/shard_map/ppermute | solution.py:867
  302.8 43.2 %collective-permute-start.39 = (bf16[224,896]{1,0:T(8,128)(2,1)}, bf16[224,896]{1,0:T(8,128)(2,1)}, u32[]{:S(2)}, u32[]{:S(2)}) collective-permute-start(bf16[224,896]{1,0:T(8,128)(2,1)} %get-tuple-element.258), channel_id=1, source_target_pairs={{0,16},{8,24},{16,0},{24,8},{1,17},{9,25},{17,1},{25,9},{2,18},{10... | collective-permute-start | bytes 1204232 | tf_op jit(solution)/shard_map/ppermute | solution.py:864
  321.0 25.5 %collective-permute-start.37 = (bf16[112,2304]{1,0:T(8,128)(2,1)}, bf16[112,2304]{1,0:T(8,128)(2,1)}, u32[]{:S(2)}, u32[]{:S(2)}) collective-permute-start(bf16[112,2304]{1,0:T(8,128)(2,1)} %get-tuple-element.254.refs_6_), channel_id=1, source_target_pairs={{0,4},{1,5},{2,6},{3,7},{4,0},{5,1},{6,2},{7,3},{8,12},{9,13},{10,... | collective-permute-start | bytes 1548296 | tf_op jit(solution)/shard_map/ppermute | solution.py:870
  323.6 22.9 %collective-permute-start.36 = (bf16[112,2304]{1,0:T(8,128)(2,1)}, bf16[112,2304]{1,0:T(8,128)(2,1)}, u32[]{:S(2)}, u32[]{:S(2)}) collective-permute-start(bf16[112,2304]{1,0:T(8,128)(2,1)} %get-tuple-element.247.refs_0_.refs_4_), channel_id=1, source_target_pairs={{0,2},{1,3},{2,0},{3,1},{4,6},{5,7},{6,4},{7,5},{8,10},{9,11},{10,... | collective-permute-start | bytes 1548296 | tf_op jit(solution)/shard_map/ppermute | solution.py:870
  351.1 29.3 %collective-permute-start.44 = (bf16[224,2304]{1,0:T(8,128)(2,1)}, bf16[224,2304]{1,0:T(8,128)(2,1)}, u32[]{:S(2)}, u32[]{:S(2)}) collective-permute-start(bf16[224,2304]{1,0:T(8,128)(2,1)} %get-tuple-element.267.refs_2_.refs_3_), channel_id=1, source_target_pairs={{0,1},{1,0},{2,3},{3,2},{4,5},{5,4},{6,7},{7,6},{8,9},{9,8},{10,11... | collective-permute-start | bytes 3096584 | tf_op jit(solution)/shard_map/ppermute | solution.py:867
  355.2 24.1 %collective-permute-start.48 = (bf16[224,1152]{1,0:T(8,128)(2,1)}, bf16[224,1152]{1,0:T(8,128)(2,1)}, u32[]{:S(2)}, u32[]{:S(2)}) collective-permute-start(bf16[224,1152]{1,0:T(8,128)(2,1)} %get-tuple-element.272), channel_id=1, source_target_pairs={{0,16},{8,24},{16,0},{24,8},{1,17},{9,25},{17,1},{25,9},{2,18},{10... | collective-permute-start | bytes 1548296 | tf_op jit(solution)/shard_map/ppermute | solution.py:864
  355.3 24.2 %collective-permute-start.45 = (bf16[112,2304]{1,0:T(8,128)(2,1)}, bf16[112,2304]{1,0:T(8,128)(2,1)}, u32[]{:S(2)}, u32[]{:S(2)}) collective-permute-start(bf16[112,2304]{1,0:T(8,128)(2,1)} %get-tuple-element.268.refs_4_), channel_id=1, source_target_pairs={{0,2},{1,3},{2,0},{3,1},{4,6},{5,7},{6,4},{7,5},{8,10},{9,11},{10,... | collective-permute-start | bytes 1548296 | tf_op jit(solution)/shard_map/ppermute | solution.py:870
  356.3 23.9 %collective-permute-start.46 = (bf16[224,1152]{1,0:T(8,128)(2,1)}, bf16[224,1152]{1,0:T(8,128)(2,1)}, u32[]{:S(2)}, u32[]{:S(2)}) collective-permute-start(bf16[224,1152]{1,0:T(8,128)(2,1)} %get-tuple-element.269.refs_6_), channel_id=1, source_target_pairs={{0,2},{1,3},{2,0},{3,1},{4,6},{5,7},{6,4},{7,5},{8,10},{9,11},{10,... | collective-permute-start | bytes 1548296 | tf_op jit(solution)/shard_map/ppermute | solution.py:870
  358.7 20.1 %collective-permute-start.43 = (bf16[224,1024]{1,0:T(8,128)(2,1)}, bf16[224,1024]{1,0:T(8,128)(2,1)}, u32[]{:S(2)}, u32[]{:S(2)}) collective-permute-start(bf16[224,1024]{1,0:T(8,128)(2,1)} %get-tuple-element.259.refs_0_), channel_id=1, source_target_pairs={{0,8},{8,0},{16,24},{24,16},{1,9},{9,1},{17,25},{25,17},{2,10},{10... | collective-permute-start | bytes 1376264 | tf_op jit(solution)/shard_map/ppermute | solution.py:861
  384.5 15.5 %collective-permute-start.54 = (f32[1,2944]{1,0:T(1,128)}, f32[1,2944]{1,0:T(1,128)}, u32[]{:S(2)}, u32[]{:S(2)}) collective-permute-start(f32[1,2944]{1,0:T(1,128)} %get-tuple-element.282.refs_4_), channel_id=1, source_target_pairs={{0,8},{8,0},{16,24},{24,16},{1,9},{9,1},{17,25},{25,17},{2,10},{10... | collective-permute-start | bytes 35336 | tf_op jit(solution)/shard_map/ppermute | solution.py:861
  384.8 15.1 %collective-permute-start.53 = (bf16[112,1152]{1,0:T(8,128)(2,1)}, bf16[112,1152]{1,0:T(8,128)(2,1)}, u32[]{:S(2)}, u32[]{:S(2)}) collective-permute-start(bf16[112,1152]{1,0:T(8,128)(2,1)} %get-tuple-element.281), channel_id=1, source_target_pairs={{0,1},{1,0},{2,3},{3,2},{4,5},{5,4},{6,7},{7,6},{8,9},{9,8},{10,11... | collective-permute-start | bytes 774152 | tf_op jit(solution)/shard_map/ppermute | solution.py:867
  385.3 26.0 %collective-permute-start.57 = (bf16[224,1152]{1,0:T(8,128)(2,1)}, bf16[224,1152]{1,0:T(8,128)(2,1)}, u32[]{:S(2)}, u32[]{:S(2)}) collective-permute-start(bf16[224,1152]{1,0:T(8,128)(2,1)} %get-tuple-element.285.refs_4_), channel_id=1, source_target_pairs={{0,4},{1,5},{2,6},{3,7},{4,0},{5,1},{6,2},{7,3},{8,12},{9,13},{10,... | collective-permute-start | bytes 1548296 | tf_op jit(solution)/shard_map/ppermute | solution.py:870
  386.2 19.1 %collective-permute-start.55 = (bf16[224,1536]{1,0:T(8,128)(2,1)}, bf16[224,1536]{1,0:T(8,128)(2,1)}, u32[]{:S(2)}, u32[]{:S(2)}) collective-permute-start(bf16[224,1536]{1,0:T(8,128)(2,1)} %get-tuple-element.276.refs_0_), channel_id=1, source_target_pairs={{0,8},{8,0},{16,24},{24,16},{1,9},{9,1},{17,25},{25,17},{2,10},{10... | collective-permute-start | bytes 2064392 | tf_op jit(solution)/shard_map/ppermute | solution.py:861
  386.2 30.5 %collective-permute-start.56 = (bf16[224,2304]{1,0:T(8,128)(2,1)}, bf16[224,2304]{1,0:T(8,128)(2,1)}, u32[]{:S(2)}, u32[]{:S(2)}) collective-permute-start(bf16[224,2304]{1,0:T(8,128)(2,1)} %get-tuple-element.284.refs_2_.refs_4_), channel_id=1, source_target_pairs={{0,1},{1,0},{2,3},{3,2},{4,5},{5,4},{6,7},{7,6},{8,9},{9,8},{10,11... | collective-permute-start | bytes 3096584 | tf_op jit(solution)/shard_map/ppermute | solution.py:867
  401.8 14.9 %collective-permute-start.58 = (bf16[112,1152]{1,0:T(8,128)(2,1)}, bf16[112,1152]{1,0:T(8,128)(2,1)}, u32[]{:S(2)}, u32[]{:S(2)}) collective-permute-start(bf16[112,1152]{1,0:T(8,128)(2,1)} %get-tuple-element.283.refs_0_.refs_6_), channel_id=1, source_target_pairs={{0,2},{1,3},{2,0},{3,1},{4,6},{5,7},{6,4},{7,5},{8,10},{9,11},{10,... | collective-permute-start | bytes 774152 | tf_op jit(solution)/shard_map/ppermute | solution.py:870
  419.6 15.2 %collective-permute-start.60 = (bf16[224,1152]{1,0:T(8,128)(2,1)}, bf16[224,1152]{1,0:T(8,128)(2,1)}, u32[]{:S(2)}, u32[]{:S(2)}) collective-permute-start(bf16[224,1152]{1,0:T(8,128)(2,1)} %get-tuple-element.288.refs_2_.refs_5_), channel_id=1, source_target_pairs={{0,1},{1,0},{2,3},{3,2},{4,5},{5,4},{6,7},{7,6},{8,9},{9,8},{10,11... | collective-permute-start | bytes 1548296 | tf_op jit(solution)/shard_map/ppermute | solution.py:867
  421.0 13.8 %collective-permute-start.62 = (bf16[112,1152]{1,0:T(8,128)(2,1)}, bf16[112,1152]{1,0:T(8,128)(2,1)}, u32[]{:S(2)}, u32[]{:S(2)}) collective-permute-start(bf16[112,1152]{1,0:T(8,128)(2,1)} %get-tuple-element.290.refs_6_), channel_id=1, source_target_pairs={{0,4},{1,5},{2,6},{3,7},{4,0},{5,1},{6,2},{7,3},{8,12},{9,13},{10,... | collective-permute-start | bytes 774152 | tf_op jit(solution)/shard_map/ppermute | solution.py:870
  421.0 10.5 %collective-permute-start.61 = (bf16[112,896]{1,0:T(8,128)(2,1)}, bf16[112,896]{1,0:T(8,128)(2,1)}, u32[]{:S(2)}, u32[]{:S(2)}) collective-permute-start(bf16[112,896]{1,0:T(8,128)(2,1)} %get-tuple-element.289.refs_4_), channel_id=1, source_target_pairs={{0,2},{1,3},{2,0},{3,1},{4,6},{5,7},{6,4},{7,5},{8,10},{9,11},{10,... | collective-permute-start | bytes 602120 | tf_op jit(solution)/shard_map/ppermute | solution.py:870
  423.4 17.2 %collective-permute-start.64 = (bf16[224,1536]{1,0:T(8,128)(2,1)}, bf16[224,1536]{1,0:T(8,128)(2,1)}, u32[]{:S(2)}, u32[]{:S(2)}) collective-permute-start(bf16[224,1536]{1,0:T(8,128)(2,1)} %get-tuple-element.287.refs_0_), channel_id=1, source_target_pairs={{0,8},{8,0},{16,24},{24,16},{1,9},{9,1},{17,25},{25,17},{2,10},{10... | collective-permute-start | bytes 2064392 | tf_op jit(solution)/shard_map/ppermute | solution.py:861
  437.2 14.3 %collective-permute-start.68 = (f32[1,2944]{1,0:T(1,128)}, f32[1,2944]{1,0:T(1,128)}, u32[]{:S(2)}, u32[]{:S(2)}) collective-permute-start(f32[1,2944]{1,0:T(1,128)} %get-tuple-element.296.refs_6_), channel_id=1, source_target_pairs={{0,4},{1,5},{2,6},{3,7},{4,0},{5,1},{6,2},{7,3},{8,12},{9,13},{10,... | collective-permute-start | bytes 35336 | tf_op jit(solution)/shard_map/ppermute | solution.py:870
  437.2 14.2 %collective-permute-start.66 = (bf16[112,896]{1,0:T(8,128)(2,1)}, bf16[112,896]{1,0:T(8,128)(2,1)}, u32[]{:S(2)}, u32[]{:S(2)}) collective-permute-start(bf16[112,896]{1,0:T(8,128)(2,1)} %get-tuple-element.294.refs_2_), channel_id=1, source_target_pairs={{0,4},{1,5},{2,6},{3,7},{4,0},{5,1},{6,2},{7,3},{8,12},{9,13},{10,... | collective-permute-start | bytes 602120 | tf_op jit(solution)/shard_map/ppermute | solution.py:870
  440.2 11.3 %collective-permute-start.67 = (bf16[112,1152]{1,0:T(8,128)(2,1)}, bf16[112,1152]{1,0:T(8,128)(2,1)}, u32[]{:S(2)}, u32[]{:S(2)}) collective-permute-start(bf16[112,1152]{1,0:T(8,128)(2,1)} %get-tuple-element.295.refs_4_), channel_id=1, source_target_pairs={{0,1},{1,0},{2,3},{3,2},{4,5},{5,4},{6,7},{7,6},{8,9},{9,8},{10,11... | collective-permute-start | bytes 774152 | tf_op jit(solution)/shard_map/ppermute | solution.py:867
  (23 other events, 133.0 us)
